TPU v7x, 256 devices: a whole 4x4x8 slice. The times are simulated.
256 devices in a mesh: seq: 64 (over y, z, core), chan: 4 (over x).
Axes of the slice: x: 4, y: 4, z: 8, core: 2. Of those that a mesh axis runs over, the one named last changes fastest.
Arguments:
- inputs: bfloat16 [32768, 1536], P('seq', 'chan'), may hold values from -16 to 16
- conv_weight: bfloat16 [1, 3, 1536, 1536], P(None, None, None, 'chan'), may hold values from -0.09375 to 0.09375
- head_weight: bfloat16 [1536, 4096], P(None, 'chan'), may hold values from -0.15625 to 0.15625
- head_cot: bfloat16 [32768, 4096], P('seq', 'chan'), may hold values from -6 to 6
- exon_blocks: int32 [512, 8], P('seq'), may hold values from 0 to 255
Outputs:
- tracks: bfloat16 [32768, 4096], P('seq', 'chan')
- coverage: float32 [512, 4096], P('seq', 'chan')
- input_grad: bfloat16 [32768, 1536], P('seq', 'chan')
- kernel_gradient: float32 [1, 3, 1536, 1536], P(None, None, 'seq', 'chan')
All inputs are finite; a program needn't handle non-finite values.
Results may differ from a plain program's by a relative error of at most 0.0059.
Values may be sent and summed in bfloat16 or wider, within the bound.
No kernel may reach another device: no remote copies, remote signals or barrier semaphores. Data moves between devices by JAX's collectives and lax.ppermute only.
A program may use at most 64 MiB of HBM per device.

v0:
```python
import jax
import jax.numpy as jnp
from jax import lax
from jax.sharding import PartitionSpec as P

BLOCK = 128
EXONS = 8


def shifted(value, axis, steps):
    count = lax.axis_size(axis)
    leading, last = (max(0, -steps), min(count, count - steps))
    return lax.ppermute(value, axis, [(source, source + steps) for source in range(leading, last)])


def activation_slope(point, cotan):
    _, back = jax.vjp(jax.nn.gelu, point)
    return back(cotan)[0]


def tap_input(values, steps):
    return shifted(values, "seq", steps)


def tap_grad(values, steps):
    return shifted(values, "seq", steps)


def times_t(left, right):
    return lax.dot_general(
        left, right, (((1,), (1,)), ((), ())), preferred_element_type=jnp.float32
    )


def inner_rows(left, right):
    return lax.dot_general(
        left, right, (((0,), (0,)), ((), ())), preferred_element_type=jnp.float32
    )


def shards(inputs, conv_weight, head_weight, head_cot, exon_blocks):
    rows = inputs.shape[0]
    state = inputs
    layer_number = 0
    steps = 2 * 2**layer_number
    acted = jax.nn.gelu(state.astype(jnp.float32)).astype(jnp.bfloat16)
    lower = tap_input(acted, steps)
    upper = tap_input(acted, -steps)
    whole = lax.all_gather(acted, "chan", axis=1, tiled=True)
    whole_low = lax.all_gather(lower, "chan", axis=1, tiled=True)
    whole_up = lax.all_gather(upper, "chan", axis=1, tiled=True)
    mixed = jnp.dot(whole_low, conv_weight[layer_number, 0], preferred_element_type=jnp.float32)
    mixed = mixed + jnp.dot(whole, conv_weight[layer_number, 1], preferred_element_type=jnp.float32)
    mixed = mixed + jnp.dot(
        whole_up, conv_weight[layer_number, 2], preferred_element_type=jnp.float32
    )
    saved = [(state, whole, steps)]
    state = (state.astype(jnp.float32) + mixed).astype(jnp.bfloat16)
    full_state = lax.all_gather(state, "chan", axis=1, tiled=True)
    logits = jnp.dot(full_state, head_weight, preferred_element_type=jnp.float32)
    tracks = jax.nn.softplus(logits).astype(jnp.bfloat16)
    head_term = (head_cot.astype(jnp.float32) * jax.nn.sigmoid(logits)).astype(jnp.bfloat16)
    grad = lax.psum_scatter(
        times_t(head_term, head_weight), "chan", scatter_dimension=1, tiled=True
    )
    grads = []
    for layer_number in reversed(range(conv_weight.shape[0])):
        before, whole, steps = saved[layer_number]
        grad_low = grad.astype(jnp.bfloat16)
        later = tap_grad(grad_low, -steps)
        earlier = tap_grad(grad_low, steps)
        partial_value = times_t(later, conv_weight[layer_number, 0])
        partial_value = partial_value + times_t(grad_low, conv_weight[layer_number, 1])
        partial_value = partial_value + times_t(earlier, conv_weight[layer_number, 2])
        back_u = lax.psum_scatter(partial_value, "chan", scatter_dimension=1, tiled=True)
        kernel = jnp.stack(
            [inner_rows(whole, later), inner_rows(whole, grad_low), inner_rows(whole, earlier)]
        )
        grads.append(lax.psum_scatter(kernel, "seq", scatter_dimension=1, tiled=True))
        grad = grad + activation_slope(before.astype(jnp.float32), back_u)
    kernel_gradient = jnp.stack(grads[::-1])
    resident_blocks = rows // BLOCK
    block_partial_sums = (
        tracks.astype(jnp.float32).reshape(resident_blocks, BLOCK, tracks.shape[1]).sum(axis=1)
    )
    scale = jnp.sqrt(jnp.float32(EXONS * BLOCK))
    all_blocks = lax.all_gather(block_partial_sums, "seq", axis=0, tiled=True)
    labels = jnp.arange(all_blocks.shape[0], dtype=jnp.int32)
    counts = jnp.sum((exon_blocks[:, :, None] == labels[None, None, :]).astype(jnp.float32), axis=1)
    coverage = jnp.dot(counts, all_blocks, precision=lax.Precision.HIGHEST) / scale
    return (tracks, coverage, grad.astype(jnp.bfloat16), kernel_gradient)


def solution(mesh):
    return jax.shard_map(
        shards,
        mesh=mesh,
        in_specs=(
            P("seq", "chan"),
            P(None, None, None, "chan"),
            P(None, "chan"),
            P("seq", "chan"),
            P("seq", None),
        ),
        out_specs=(
            P("seq", "chan"),
            P("seq", "chan"),
            P("seq", "chan"),
            P(None, None, "seq", "chan"),
        ),
        check_vma=False,
    )
```

profile of v0, /device:TPU:1, one launch (start us, length us, event | category | flops | bytes accessed | tf_op | source)
XLA Modules:
  0.0 465.0 jit_solution(14514463337364591084)
XLA Ops:
  7.2 0.0 copy-start
  7.2 0.0 all-gather.9.cloned.1.call-start
  7.2 2.2 fusion.30
  9.4 0.0 all-gather.9.cloned.1.call-update
  9.4 0.0 all-gather.11.cloned.1.call-start
  9.5 1.3 collective-permute-start.1
  10.8 10.2 %collective-permute-done.1 = bf16[512,384]{1,0:T(8,128)(2,1)S(1)} collective-permute-done((bf16[512,384]{1,0:T(8,128)(2,1)}, bf16[512,384]{1,0:T(8,128)(2,1)S(1)}, u32[]{:S(2)}, u32[]{:S(2)}) %collective-permute-start.1) | collective-permute-done | bytes 393248 | tf_op jit(solution)/shard_map/ppermute | solution.py:13
  21.0 0.7 copy-done.8
  21.7 0.0 all-gather.11.cloned.1.call-update
  21.7 0.0 all-gather.7.cloned.1.call-start
  21.8 5.4 %collective-permute-start = (bf16[512,384]{1,0:T(8,128)(2,1)}, bf16[512,384]{1,0:T(8,128)(2,1)S(1)}, u32[]{:S(2)}, u32[]{:S(2)}) collective-permute-start(bf16[512,384]{1,0:T(8,128)(2,1)} %fusion.30), channel_id=1, source_target_pairs={{0,8},{4,12},{8,16},{12,20},{16,24},{20,28},{24,32},{28,36},{32,40... | collective-permute-start | bytes 1179656 | tf_op jit(solution)/shard_map/ppermute | solution.py:13
  27.2 7.3 %collective-permute-done = bf16[512,384]{1,0:T(8,128)(2,1)S(1)} collective-permute-done((bf16[512,384]{1,0:T(8,128)(2,1)}, bf16[512,384]{1,0:T(8,128)(2,1)S(1)}, u32[]{:S(2)}, u32[]{:S(2)}) %collective-permute-start) | collective-permute-done | bytes 393248 | tf_op jit(solution)/shard_map/ppermute | solution.py:13
  34.5 0.7 copy-done.9
  35.3 0.0 all-gather.7.cloned.1.call-update
  35.3 0.0 all-gather.13.cloned.1.call-start
  35.3 8.0 %all-gather.9.cloned.1.call-done = bf16[512,1536]{1,0:T(8,128)(2,1)} async-done(((bf16[512,384]{1,0:T(8,128)(2,1)}), bf16[512,1536]{1,0:T(8,128)(2,1)}) %all-gather.9.cloned.1.call-update) | async-done | bytes 1572880 | tf_op jit(solution)/shard_map/all_gather | solution.py:49
  43.3 3.6 fusion.10
  46.9 27.9 %all-gather.11.cloned.1.call-done = bf16[512,1536]{1,0:T(8,128)(2,1)} async-done(((bf16[512,384]{1,0:T(8,128)(2,1)}), bf16[512,1536]{1,0:T(8,128)(2,1)}) %all-gather.11.cloned.1.call-update) | async-done | bytes 1572880 | tf_op jit(solution)/shard_map/all_gather | solution.py:51
  74.9 3.6 fusion.6
  78.5 27.4 %all-gather.7.cloned.1.call-done = bf16[512,1536]{1,0:T(8,128)(2,1)} async-done(((bf16[512,384]{1,0:T(8,128)(2,1)}), bf16[512,1536]{1,0:T(8,128)(2,1)}) %all-gather.7.cloned.1.call-update) | async-done | bytes 1572880 | tf_op jit(solution)/shard_map/all_gather | solution.py:50
  105.9 0.0 copy-done.2
  105.9 3.9 fusion.3
  109.8 0.0 all-gather.13.cloned.1.call-update
  109.9 0.0 reduce-scatter.4.cloned.1.call-start
  109.9 29.2 %all-gather.13.cloned.1.call-done = bf16[512,1536]{1,0:T(8,128)(2,1)} async-done(((bf16[512,384]{1,0:T(8,128)(2,1)}), bf16[512,1536]{1,0:T(8,128)(2,1)}) %all-gather.13.cloned.1.call-update) | async-done | bytes 1572880 | tf_op jit(solution)/shard_map/all_gather | solution.py:59
  139.1 0.0 copy-done
  139.1 5.8 %convert_reduce_fusion = (f32[4,1024]{1,0:T(4,128)}, bf16[512,1024]{1,0:T(8,128)(2,1)}, f32[512,1024]{1,0:T(8,128)S(1)}) fusion(bf16[512,1536]{1,0:T(8,128)(2,1)} %all-gather.13.cloned.1.call-done, bf16[1536,1024]{1,0:T(8,128)(2,1)S(1)} %copy-done), kind=kOutput, calls=%fused_computation.8 | convolution fusion | flops 1615327232 | bytes 7880704 | tf_op jit(solution)/shard_map/dot_general | solution.py:60
  145.0 0.0 copy-done.12
  145.0 3.5 fusion.15
  148.5 0.0 reduce-scatter.4.cloned.1.call-update
  148.5 0.0 all-gather.15.cloned.1.call-start
  148.5 0.5 all-gather.15.cloned.1.call-update
  149.1 0.0 reduce-scatter.6.cloned.1.call-start
  149.1 40.4 %reduce-scatter.4.cloned.1.call-done = f32[512,384]{1,0:T(8,128)} async-done(((f32[512,1536]{1,0:T(8,128)}), f32[512,384]{1,0:T(8,128)}) %reduce-scatter.4.cloned.1.call-update) | async-done | bytes 786448 | tf_op jit(solution)/shard_map/reduce_scatter | solution.py:63
  189.5 1.2 convert_element_type.37
  190.7 0.0 copy-start.3
  190.7 0.0 copy-start.1
  190.7 3.5 collective-permute-start.3
  194.2 1.3 collective-permute-start.2
  195.5 2.3 fusion.8
  197.8 0.0 copy-done.3
  197.8 4.2 collective-permute-done.3
  202.0 0.0 copy-done.1
  202.0 1.0 fusion.4
  203.1 2.8 collective-permute-done.2
  205.8 0.7 copy-done.4
  206.6 2.7 fusion
  209.3 0.0 reduce-scatter.6.cloned.1.call-update
  209.3 0.2 reduce-scatter.8.cloned.1.call-start
  209.6 0.0 copy-start.7
  209.6 2.6 convolution_bitcast_fusion.1
  212.3 1.0 convolution_bitcast_fusion
  213.3 0.0 copy-done.5
  213.3 1.0 convolution_bitcast_fusion.2
  214.3 3.3 pad_maximum_fusion
  217.6 0.0 reduce-scatter.8.cloned.1.call-update
  217.6 0.7 copy-done.10
  218.3 0.1 convert_reduce_fusion.1
  218.4 50.9 %all-gather.15.cloned.1.call-done = f32[64,4,1024]{2,1,0:T(4,128)} async-done(((f32[1,4,1024]{2,1,0:T(4,128)}), f32[64,4,1024]{2,1,0:T(4,128)}) %all-gather.15.cloned.1.call-update) | async-done | bytes 1048592 | tf_op jit(solution)/shard_map/all_gather | solution.py:87
  269.3 2.6 reshape.20
  271.9 2.4 convolution_multiply_fusion
  274.3 35.6 %reduce-scatter.6.cloned.1.call-done = f32[512,384]{1,0:T(8,128)} async-done(((f32[512,1536]{1,0:T(8,128)}), f32[512,384]{1,0:T(8,128)}) %reduce-scatter.6.cloned.1.call-update) | async-done | bytes 786448 | tf_op jit(solution)/shard_map/reduce_scatter | solution.py:75
  310.0 2.7 fusion.26
  312.7 145.5 %reduce-scatter.8.cloned.1.call-done = f32[3,24,384]{2,1,0:T(8,128)} async-done(((f32[3,1536,384]{2,1,0:T(8,128)}), f32[3,24,384]{2,1,0:T(8,128)}) %reduce-scatter.8.cloned.1.call-update) | async-done | bytes 110608 | tf_op jit(solution)/shard_map/reduce_scatter | solution.py:79
  (12 shorter events, 0.0 us)
Async XLA Ops:
  7.2 132.0 %copy-start = (bf16[1536,1024]{1,0:T(8,128)(2,1)S(1)}, bf16[1536,1024]{1,0:T(8,128)(2,1)}, u32[]{:S(2)}) copy-start(bf16[1536,1024]{1,0:T(8,128)(2,1)} %param.7) | copy-start | bytes 9437188
  7.2 36.1 %all-gather.9.cloned.1.call-start = ((), (), s32[]{:S(2)}) async-start(), calls=%async_computation.4 | async-start | bytes 1966080 | tf_op jit(solution)/shard_map/all_gather | solution.py:49
  9.4 65.5 %all-gather.11.cloned.1.call-start = ((), (), s32[]{:S(2)}) async-start(), calls=%async_computation.5 | async-start | bytes 1966080 | tf_op jit(solution)/shard_map/all_gather | solution.py:51
  9.5 11.5 %collective-permute-start.1 = (bf16[512,384]{1,0:T(8,128)(2,1)}, bf16[512,384]{1,0:T(8,128)(2,1)S(1)}, u32[]{:S(2)}, u32[]{:S(2)}) collective-permute-start(bf16[512,384]{1,0:T(8,128)(2,1)} %fusion.30), channel_id=1, source_target_pairs={{8,0},{12,4},{16,8},{20,12},{24,16},{28,20},{32,24},{36,28},{40,32... | collective-permute-start | bytes 1179656 | tf_op jit(solution)/shard_map/ppermute | solution.py:13
  21.0 0.7 copy-start.8
  21.7 84.2 %all-gather.7.cloned.1.call-start = ((), (), s32[]{:S(2)}) async-start(), calls=%async_computation.3 | async-start | bytes 1966080 | tf_op jit(solution)/shard_map/all_gather | solution.py:50
  21.8 12.7 %collective-permute-start = (bf16[512,384]{1,0:T(8,128)(2,1)}, bf16[512,384]{1,0:T(8,128)(2,1)S(1)}, u32[]{:S(2)}, u32[]{:S(2)}) collective-permute-start(bf16[512,384]{1,0:T(8,128)(2,1)} %fusion.30), channel_id=1, source_target_pairs={{0,8},{4,12},{8,16},{12,20},{16,24},{20,28},{24,32},{28,36},{32,40... | collective-permute-start | bytes 1179656 | tf_op jit(solution)/shard_map/ppermute | solution.py:13
  34.5 0.7 copy-start.9
  35.3 103.9 %all-gather.13.cloned.1.call-start = ((), (), s32[]{:S(2)}) async-start(), calls=%async_computation.6 | async-start | bytes 1966080 | tf_op jit(solution)/shard_map/all_gather | solution.py:59
  46.9 59.0 %copy-start.2 = (bf16[512,384]{1,0:T(8,128)(2,1)S(1)}, bf16[512,384]{1,0:T(8,128)(2,1)}, u32[]{:S(2)}) copy-start(bf16[512,384]{1,0:T(8,128)(2,1)} %param.5) | copy-start | bytes 1179652
  109.9 79.7 %reduce-scatter.4.cloned.1.call-start = ((), (), s32[]{:S(2)}) async-start(), calls=%async_computation.7 | async-start | bytes 3932160 | tf_op jit(solution)/shard_map/reduce_scatter | solution.py:63
  139.1 5.8 %copy-start.12 = (bf16[512,1024]{1,0:T(8,128)(2,1)S(1)}, bf16[512,1024]{1,0:T(8,128)(2,1)}, u32[]{:S(2)}) copy-start(bf16[512,1024]{1,0:T(8,128)(2,1)} %param.8) | copy-start | bytes 3145732
  148.5 120.8 %all-gather.15.cloned.1.call-start = ((), (), s32[]{:S(2)}) async-start(), calls=%async_computation.10 | async-start | bytes 1064960 | tf_op jit(solution)/shard_map/all_gather | solution.py:87
  149.1 160.9 %reduce-scatter.6.cloned.1.call-start = ((), (), s32[]{:S(2)}) async-start(), calls=%async_computation.8 | async-start | bytes 3932160 | tf_op jit(solution)/shard_map/reduce_scatter | solution.py:75
  190.7 7.1 %copy-start.3 = (bf16[512,384]{1,0:T(8,128)(2,1)}, bf16[512,384]{1,0:T(8,128)(2,1)S(1)}, u32[]{:S(2)}) copy-start(bf16[512,384]{1,0:T(8,128)(2,1)S(1)} %convert_element_type.37) | copy-start | bytes 1179652
  190.7 11.3 %copy-start.1 = (bf16[1,3,1536,384]{3,2,1,0:T(8,128)(2,1)S(1)}, bf16[1,3,1536,384]{3,2,1,0:T(8,128)(2,1)}, u32[]{:S(2)}) copy-start(bf16[1,3,1536,384]{3,2,1,0:T(8,128)(2,1)} %param.6) | copy-start | bytes 10616836
  190.7 11.3 %collective-permute-start.3 = (bf16[512,384]{1,0:T(8,128)(2,1)S(1)}, bf16[512,384]{1,0:T(8,128)(2,1)S(1)}, u32[]{:S(2)}, u32[]{:S(2)}) collective-permute-start(bf16[512,384]{1,0:T(8,128)(2,1)S(1)} %convert_element_type.37), channel_id=1, source_target_pairs={{0,8},{4,12},{8,16},{12,20},{16,24},{20,28},{24,32},{28,36},{32,40... | collective-permute-start | bytes 1179656 | tf_op jit(solution)/shard_map/ppermute | solution.py:13
  194.2 11.6 %collective-permute-start.2 = (bf16[512,384]{1,0:T(8,128)(2,1)S(1)}, bf16[512,384]{1,0:T(8,128)(2,1)S(1)}, u32[]{:S(2)}, u32[]{:S(2)}) collective-permute-start(bf16[512,384]{1,0:T(8,128)(2,1)S(1)} %convert_element_type.37), channel_id=1, source_target_pairs={{8,0},{12,4},{16,8},{20,12},{24,16},{28,20},{32,24},{36,28},{40,32... | collective-permute-start | bytes 1179656 | tf_op jit(solution)/shard_map/ppermute | solution.py:13
  202.0 1.0 copy-start.6
  205.8 0.7 copy-start.4
  209.3 248.8 %reduce-scatter.8.cloned.1.call-start = ((), (), s32[]{:S(2)}) async-start(), calls=%async_computation.9 | async-start | bytes 7188480 | tf_op jit(solution)/shard_map/reduce_scatter | solution.py:79
  209.6 2.7 copy-start.7
  209.6 2.7 copy-start.11
  212.2 1.0 copy-start.5
  217.6 0.7 copy-start.10
Sparse Core Ops, SparseCore 0:
  10.4 32.8 all-gather.8
  45.7 29.1 all-gather.10
  76.7 29.1 all-gather.6
  110.0 29.1 all-gather.12
  148.6 40.8 reduce-scatter.3
  192.7 76.5 all-gather.14
  271.9 38.0 reduce-scatter.5
  314.8 143.2 reduce-scatter.7
where the time goes:
time: 469 us; the launch traced here: 465 us
  waiting for transfers between devices  390 us (83%)
  matrix products  33.6 us (7%)
  between operations  14.3 us (3%)
  starting transfers between devices  11.9 us (3%)
  other arithmetic  9.47 us (2%)
  local copies, waits for them, and re-layouts  5.52 us (1%)
    reduce_scatter x1, waiting for transfers between devices, shards(): lax.psum_scatter(kernel, 'seq', scatter_dimension=1, tiled=True)  145 us
    all_gather x1, waiting for transfers between devices, shards(): all_blocks = lax.all_gather(block_partial_sums, 'seq', axis=0, tiled=True)  50.9 us
    reduce_scatter x1, waiting for transfers between devices, shards(): lax.psum_scatter(times_t(head_term, head_weight), 'chan', scatter_dimensi...  40.4 us
    reduce_scatter x1, waiting for transfers between devices, shards(): lax.psum_scatter(partial_value, 'chan', scatter_dimension=1, tiled=True)  35.6 us
    all_gather x1, waiting for transfers between devices, shards(): full_state = lax.all_gather(state, 'chan', axis=1, tiled=True)  29.2 us
    all_gather x1, waiting for transfers between devices, shards(): whole_up = lax.all_gather(upper, 'chan', axis=1, tiled=True)  27.9 us
    all_gather x1, waiting for transfers between devices, shards(): whole_low = lax.all_gather(lower, 'chan', axis=1, tiled=True)  27.4 us
    ppermute x4, waiting for transfers between devices, shifted(): lax.ppermute(value, axis, [(source, source + steps) for source in range(l...  24.5 us
  transfers between devices with their start and end apart: 12, of which 12 were waited for; matrix products, arithmetic and copies ran while one was open for 7% of the time, Pallas kernels for 0%

commit v1 on v0

v1 whole, which is shorter than its diff:
```python
import jax
import jax.numpy as jnp
from jax import lax
from jax.experimental import pallas as pl
from jax.experimental.pallas import tpu as pltpu
from jax.sharding import PartitionSpec as P

BLOCK = 128
EXONS = 8
NX, NY, NZ = 4, 4, 8
TAPS = 3
GROUP = 24
F32 = jnp.float32
BF = jnp.bfloat16


def activation_slope(point, cotan):
    _, back = jax.vjp(jax.nn.gelu, point)
    return back(cotan)[0]


def seq_index(y, z, core):
    return (y * NZ + z) * 2 + core


def shifted(value, steps):
    count = lax.axis_size("seq")
    leading, last = (max(0, -steps), min(count, count - steps))
    return lax.ppermute(value, "seq", [(s, s + steps) for s in range(leading, last)])


def along_x(value, steps):
    return lax.ppermute(value, "chan", [(i, (i + steps) % NX) for i in range(NX)])


def along_seq(value, dy, dz, dcore):
    pairs = [
        (
            seq_index(y, z, core),
            seq_index((y + dy) % NY, (z + dz) % NZ, (core + dcore) % 2),
        )
        for y in range(NY)
        for z in range(NZ)
        for core in range(2)
    ]
    return lax.ppermute(value, "seq", pairs)


def from_all_x(value):
    return [value] + [along_x(value, -r) for r in range(1, NX)]


def times_t(left, right):
    return lax.dot_general(left, right, (((1,), (1,)), ((), ())), preferred_element_type=F32)


def call(body, place, operands, outs, scratch=(), after=(), limit=56, flops=0, moved=0):
    count = len(operands)

    def kernel(*refs):
        body(refs[0], *refs[1 : 1 + count], *refs[1 + count + len(after) :])

    vmem = pl.BlockSpec(memory_space=pltpu.VMEM)
    return pl.pallas_call(
        kernel,
        in_specs=[pl.BlockSpec(memory_space=pltpu.SMEM)]
        + [pl.BlockSpec(memory_space=space) for _, space in operands]
        + [pl.BlockSpec(memory_space=pl.ANY)] * len(after),
        out_specs=[vmem] * len(outs),
        scratch_shapes=list(scratch),
        out_shape=outs,
        cost_estimate=pl.CostEstimate(flops=flops, bytes_accessed=moved, transcendentals=0),
        compiler_params=pltpu.CompilerParams(vmem_limit_bytes=limit * 2**20),
    )(place, *[value for value, _ in operands], *after)


def local(values):
    return [(value, pltpu.VMEM) for value in values]


def like(shape, dtype):
    return jax.ShapeDtypeStruct(shape, dtype)


def slot(place, r, width):
    return pl.ds(pl.multiple_of(lax.rem(place[0] + r, NX) * width, 128), width)


def outer_products(place, blocks, conv_weight, after):
    size, width = blocks[0].shape
    tall = NX * width

    def body(place, b0, b1, b2, b3, weight, low, up, whole, held, sems):
        copies = [
            pltpu.make_async_copy(weight.at[0, tap], held.at[i], sems.at[i])
            for i, tap in enumerate((0, 2))
        ]
        for copy in copies:
            copy.start()
        for r, block in enumerate((b0, b1, b2, b3)):
            whole[:, slot(place, r, width)] = block[...]
        for i, ref in enumerate((low, up)):
            copies[i].wait()
            ref[...] = jnp.dot(whole[...], held[i], preferred_element_type=F32).astype(BF)

    block = (size, width)
    return call(
        body,
        place,
        local(blocks) + [(conv_weight, pl.ANY)],
        [like(block, BF), like(block, BF), like((size, tall), BF)],
        scratch=[pltpu.VMEM((2, tall, width), BF), pltpu.SemaphoreType.DMA((2,))],
        after=after,
        flops=4 * size * tall * width,
        moved=4 * tall * width,
    )


def turned_blocks(place, whole, after):
    size, tall = whole.shape
    width = tall // NY

    def body(place, whole, *outs):
        for m, out in enumerate(outs):
            at = pl.multiple_of(lax.rem(place[1] + m, NY) * width, 128)
            out[...] = whole[:, pl.ds(at, width)].T

    return call(
        body,
        place,
        local([whole]),
        [like((width, size), BF)] * NY,
        after=after,
        flops=size * tall,
        moved=4 * size * tall,
    )


def middle_product(place, whole, conv_weight, after):
    size, tall = whole.shape
    width = tall // NX

    def body(place, whole, weight, mid, held, sem):
        copy = pltpu.make_async_copy(weight.at[0, 1], held, sem)
        copy.start()
        copy.wait()
        mid[...] = jnp.dot(whole[...], held[...], preferred_element_type=F32)

    return call(
        body,
        place,
        local([whole]) + [(conv_weight, pl.ANY)],
        [like((size, width), F32)],
        scratch=[pltpu.VMEM((tall, width), BF), pltpu.SemaphoreType.DMA(())],
        after=after,
        flops=2 * size * tall * width,
        moved=2 * tall * width,
    )[0]


def track_head(place, blocks, head_weight, head_cot, after):
    size, width = blocks[0].shape
    tall, wide = head_weight.shape
    tile = 256
    groups = size // BLOCK

    def body(place, b0, b1, b2, b3, weight, cot, out, sums, o0, o1, o2, o3, whole, held, term, cots, sems):
        copies = []
        for j in range(wide // tile):
            cols = slice(j * tile, (j + 1) * tile)
            copies.append(
                (
                    pltpu.make_async_copy(weight.at[:, cols], held.at[:, cols], sems.at[0, j]),
                    pltpu.make_async_copy(cot.at[:, cols], cots.at[:, cols], sems.at[1, j]),
                )
            )
            for copy in copies[-1]:
                copy.start()
        for r, block in enumerate((b0, b1, b2, b3)):
            whole[:, slot(place, r, width)] = block[...]
        for j in range(wide // tile):
            cols = slice(j * tile, (j + 1) * tile)
            for copy in copies[j]:
                copy.wait()
            logits = jnp.dot(whole[...], held[:, cols], preferred_element_type=F32)
            decay = jnp.exp(-jnp.abs(logits))
            track = (jnp.maximum(logits, 0.0) + jnp.log1p(decay)).astype(BF)
            out[:, cols] = track
            sums[:, cols] = jnp.sum(track.astype(F32).reshape(groups, BLOCK, tile), axis=1)
            sigmoid = jnp.where(logits >= 0.0, 1.0, decay) / (1.0 + decay)
            term[:, cols] = (cots[:, cols].astype(F32) * sigmoid).astype(BF)
        for r, ref in ((2, o2), (1, o1), (3, o3), (0, o0)):
            ref[...] = times_t(term[...], held[slot(place, r, width), :]).astype(ref.dtype)

    block = (size, width)
    return call(
        body,
        place,
        local(blocks) + [(head_weight, pl.ANY), (head_cot, pl.ANY)],
        [like((size, wide), BF), like((groups, wide), F32), like(block, F32)] + [like(block, BF)] * 3,
        scratch=[
            pltpu.VMEM((size, tall), BF),
            pltpu.VMEM((tall, wide), BF),
            pltpu.VMEM((size, wide), BF),
            pltpu.VMEM((size, wide), BF),
            pltpu.SemaphoreType.DMA((2, wide // tile)),
        ],
        after=after,
        flops=4 * size * tall * wide,
        moved=2 * tall * wide,
    )


def add_up(place, own, came, after):
    def body(place, own, c1, c2, c3, total, low):
        value = own[...] + c1[...].astype(F32) + c2[...].astype(F32) + c3[...].astype(F32)
        total[...] = value
        low[...] = value.astype(BF)

    shape = own.shape
    return call(
        body,
        place,
        local([own] + came),
        [like(shape, F32), like(shape, BF)],
        after=after,
        flops=4 * own.size,
        moved=16 * own.size,
    )


def back_products(place, around, conv_weight, after):
    size, width = around[0].shape
    tall = NX * width
    cols = TAPS * width

    def body(place, d0, d1, d2, weight, o0, o1, o2, o3, held, joined, sems):
        copies = []
        for k in range(TAPS):
            at = slice(k * width, (k + 1) * width)
            copies.append(pltpu.make_async_copy(weight.at[0, k], held.at[:, at], sems.at[k]))
            copies[-1].start()
        for k, ref in enumerate((d0, d1, d2)):
            joined[:, k * width : (k + 1) * width] = ref[...]
        for copy in copies:
            copy.wait()
        for r, ref in ((2, o2), (1, o1), (3, o3), (0, o0)):
            ref[...] = times_t(joined[...], held[slot(place, r, width), :]).astype(ref.dtype)

    block = (size, width)
    return call(
        body,
        place,
        local(around) + [(conv_weight, pl.ANY)],
        [like(block, F32)] + [like(block, BF)] * 3,
        scratch=[
            pltpu.VMEM((tall, cols), BF),
            pltpu.VMEM((size, cols), BF),
            pltpu.SemaphoreType.DMA((TAPS,)),
        ],
        after=after,
        flops=2 * size * tall * cols,
        moved=2 * tall * cols,
    )


def kernel_terms(place, earlier, own, later, cots, after):
    _, width, size = own.shape
    half = width // 2
    cols = TAPS * width

    def body(place, earlier, own, later, d0, d1, d2, d3, kept, sent):
        y, z, core = place[1], place[2], place[3]
        first, last = z == 0, z == NZ - 1
        for k, left in enumerate((earlier, own, later)):
            total = jnp.zeros((width, width), F32)
            for m, right in enumerate((d0, d1, d2, d3)):
                if k == 0:
                    index = jnp.where(first, (m + 1) % NY, m)
                    valid = jnp.logical_not(jnp.logical_and(first, y == m))
                elif k == 2:
                    index = jnp.where(last, (m + NY - 1) % NY, m)
                    valid = jnp.logical_not(jnp.logical_and(last, y == (m + NY - 1) % NY))
                else:
                    index, valid = m, None
                product = jnp.dot(left[index], right[...], preferred_element_type=F32)
                total += product if valid is None else jnp.where(valid, product, 0.0)
            pairs = total.reshape(half // GROUP, 2, GROUP, width)
            one, two = (pairs[:, i].reshape(half, width) for i in range(2))
            at = slice(k * width, (k + 1) * width)
            kept[:, at] = jnp.where(core == 0, one, two)
            sent[:, at] = jnp.where(core == 0, two, one).astype(BF)

    return call(
        body,
        place,
        local([earlier, own, later] + cots),
        [like((half, cols), F32), like((half, cols), BF)],
        after=after,
        flops=2 * size * NY * width * cols,
        moved=8 * NY * width * size,
    )


def over_z(place, kept, came, after):
    rows, cols = kept.shape

    def body(place, kept, came, *refs):
        outs, total = refs[:NZ], refs[NZ]
        total[...] = kept[...] + came[...].astype(F32)
        for m, ref in enumerate(outs):
            at = pl.multiple_of(lax.rem(place[2] + m, NZ) * GROUP, 8)
            ref[...] = total[pl.ds(at, GROUP), :].astype(ref.dtype)

    block = (GROUP, cols)
    return call(
        body,
        place,
        local([kept, came]),
        [like(block, F32)] + [like(block, BF)] * (NZ - 1),
        scratch=[pltpu.VMEM((rows, cols), F32)],
        after=after,
        limit=16,
        flops=4 * rows * cols,
        moved=6 * rows * cols,
    )


def coverage_of(blocks, order, exon_blocks):
    count, lines, half = blocks.shape
    own = lines // 2
    line = jnp.arange(lines, dtype=jnp.int32)
    labels = order[:, None] * own + line[None] // 2
    hits = (exon_blocks[:, :, None, None] == labels[None, None]).astype(F32).sum(axis=1)
    counts = jnp.stack([jnp.where(line % 2 == side, hits, 0.0) for side in range(2)])
    total = jnp.dot(
        counts.astype(BF).reshape(-1, count * lines),
        blocks.reshape(count * lines, half),
        preferred_element_type=F32,
    )
    total = total.reshape(2, -1, half).transpose(1, 0, 2).reshape(-1, 2 * half)
    return total / jnp.sqrt(F32(EXONS * BLOCK))


def shards(inputs, conv_weight, head_weight, head_cot, exon_blocks):
    width = inputs.shape[1]
    x = lax.axis_index("chan")
    s = lax.axis_index("seq")
    core, z, y = s % 2, (s // 2) % NZ, s // (2 * NZ)
    place = jnp.stack([x, y, z, core]).astype(jnp.int32)
    steps = 2

    state = inputs.astype(F32)
    acted = from_all_x(jax.nn.gelu(state).astype(BF))
    low, up, whole = outer_products(place, acted, conv_weight, ())
    low, up = shifted(low, steps), shifted(up, -steps)
    mid = middle_product(place, whole, conv_weight, ())
    turned = turned_blocks(place, whole, (mid,))
    full = from_all_x((state + (mid + low.astype(F32) + up.astype(F32))).astype(BF))
    turned = jnp.stack([turned[0]] + [along_seq(turned[m], m, 0, 0) for m in range(1, NY)])
    before = along_seq(turned, 0, 1, 0)
    behind = along_seq(turned, 0, NZ - 1, 0)

    tracks, sums, *blocks = track_head(place, full, head_weight, head_cot, (turned,))
    came = [along_x(blocks[r], r) for r in range(1, NX)]
    sums = sums.astype(BF).reshape(1, -1, 512)
    z_groups = [[seq_index(j, i, c) for i in range(NZ)] for j in range(NY) for c in range(2)]
    other_groups = [[seq_index(j, i, c) for j in range(NY) for c in range(2)] for i in range(NZ)]
    sums = lax.all_gather(sums, "seq", axis=0, tiled=True, axis_index_groups=z_groups)
    gathered = lax.all_gather(sums, "seq", axis=0, tiled=True, axis_index_groups=other_groups)
    order = jnp.array([seq_index(j, i, c) for j in range(NY) for c in range(2) for i in range(NZ)], jnp.int32)

    grad, low = add_up(place, blocks[0], came, (before, behind, gathered))
    cots = [low] + [along_seq(low, m, 0, 0) for m in range(1, NY)]
    around = [shifted(low, -steps), low, shifted(low, steps)]
    blocks = back_products(place, around, conv_weight, ())
    came = [along_x(blocks[r], r) for r in range(1, NX)]
    kept, sent = kernel_terms(place, before, turned, behind, cots, (blocks[1],))
    kept, *parts = over_z(place, kept, along_seq(sent, 0, 0, 1), ())
    for m, part in enumerate(parts):
        kept = kept + along_seq(part, 0, m + 1, 0).astype(F32)
    kernel_gradient = kept.reshape(GROUP, TAPS, width).transpose(1, 0, 2)[None]

    back_u = blocks[0] + came[0].astype(F32) + came[1].astype(F32) + came[2].astype(F32)
    out = (grad + activation_slope(state, back_u)).astype(BF)
    coverage = coverage_of(gathered, order, exon_blocks)
    return (tracks, coverage, out, kernel_gradient)


def solution(mesh):
    return jax.shard_map(
        shards,
        mesh=mesh,
        in_specs=(
            P("seq", "chan"),
            P(None, None, None, "chan"),
            P(None, "chan"),
            P("seq", "chan"),
            P("seq", None),
        ),
        out_specs=(
            P("seq", "chan"),
            P("seq", "chan"),
            P("seq", "chan"),
            P(None, None, "seq", "chan"),
        ),
        check_vma=False,
    )
```

time: 469 us -> 233 us (0.50)
  waiting for transfers between devices: 390 us -> 91.7 us
  blocking collectives: 0 us -> 42 us
  Pallas kernels: 0 us -> 40.9 us
  matrix products: 33.6 us -> 0.8 us
  starting transfers between devices: 11.9 us -> 41.7 us
  between operations: 14.3 us -> 1.07 us
    reduce_scatter x3 -> x0, waiting for transfers between devices: 222 us -> none  [the longest x1 145 us: shards(): lax.psum_scatter(kernel, 'seq', scatter_dimension=1, tiled=True)]
    all_gather x5 -> x0, waiting for transfers between devices: 143 us -> none  [the longest x1 50.9 us: shards(): all_blocks = lax.all_gather(block_partial_sums, 'seq', axis=0, tiled=True)]
    ppermute x4 -> x32, waiting for transfers between devices: 24.5 us -> 91.7 us  [the longest x12 52.6 us: along_x(): lax.ppermute(value, 'chan', [(i, (i + steps) % NX) for i in range(NX)])]
    all_gather x0 -> x2, blocking collectives: none -> 42 us  [the longest x1 22.4 us: shards(): lax.all_gather(sums, 'seq', axis=0, tiled=True, axis_index_groups=other_g...]
    pallas_call x0 -> x8, Pallas kernels: none -> 40.9 us  [call(): pl.pallas_call(kernel, in_specs=[pl.BlockSpec(memory_space=pltpu.SMEM)] +...]
    dot_general x12 -> x1, matrix products: 33.6 us -> 0.8 us  [coverage_of(): jnp.dot(counts.astype(BF).reshape(-1, count * lines), blocks.reshape(coun...]
    ppermute x4 -> x32, starting transfers between devices: 11.4 us -> 41.7 us  [the longest x16 18.2 us: along_seq(): return lax.ppermute(value, 'seq', pairs)]
  transfers between devices with their start and end apart: 12 -> 32, of which waited for: 12 -> 15; matrix products, arithmetic and copies ran while one was open for 7% -> 3% of each run, Pallas kernels for 0% -> 8%
where the time goes in v1:
time: 233 us; the launch traced here: 231 us
  waiting for transfers between devices  91.7 us (39%)
  blocking collectives  42 us (18%)
  starting transfers between devices  41.7 us (18%)
  Pallas kernels  40.9 us (18%)
  local copies, waits for them, and re-layouts  7.22 us (3%)
  other arithmetic  5.86 us (3%)
    ppermute x12, waiting for transfers between devices, along_x(): lax.ppermute(value, 'chan', [(i, (i + steps) % NX) for i in range(NX)])  52.6 us
    pallas_call x8, Pallas kernels, call(): pl.pallas_call(kernel, in_specs=[pl.BlockSpec(memory_space=pltpu.SMEM)] +...  40.9 us
    ppermute x16, waiting for transfers between devices, along_seq(): return lax.ppermute(value, 'seq', pairs)  36.1 us
    all_gather x1, blocking collectives, shards(): lax.all_gather(sums, 'seq', axis=0, tiled=True, axis_index_groups=other_g...  22.4 us
    all_gather x1, blocking collectives, shards(): lax.all_gather(sums, 'seq', axis=0, tiled=True, axis_index_groups=z_groups)  19.6 us
    ppermute x16, starting transfers between devices, along_seq(): return lax.ppermute(value, 'seq', pairs)  18.2 us
    ppermute x12, starting transfers between devices, along_x(): lax.ppermute(value, 'chan', [(i, (i + steps) % NX) for i in range(NX)])  12.8 us
    ppermute x4, starting transfers between devices, shifted(): lax.ppermute(value, 'seq', [(s, s + steps) for s in range(leading, last)])  10.8 us
  transfers between devices with their start and end apart: 32, of which 15 were waited for; matrix products, arithmetic and copies ran while one was open for 3% of the time, Pallas kernels for 8%

profile of v1, /device:TPU:1, one launch (start us, length us, event | category | flops | bytes accessed | tf_op | source)
XLA Modules:
  0.0 231.4 jit_solution(1882812956967334208)
XLA Ops:
  0.6 1.3 fusion.8.refs_1_
  1.9 3.4 %collective-permute-start = (bf16[512,384]{1,0:T(8,128)(2,1)S(1)}, bf16[512,384]{1,0:T(8,128)(2,1)S(1)}, u32[]{:S(2)}, u32[]{:S(2)}) collective-permute-start(bf16[512,384]{1,0:T(8,128)(2,1)S(1)} %fusion.8.refs_1_), channel_id=1, source_target_pairs={{0,3},{1,0},{2,1},{3,2},{4,7},{5,4},{6,5},{7,6},{8,11},{9,8},{10,9... | collective-permute-start | bytes 1179656 | tf_op jit(solution)/shard_map/ppermute | solution.py:33
  5.3 0.5 collective-permute-start.1
  5.8 0.6 collective-permute-start.2
  6.4 0.6 pad_add_fusion.refs_0_
  7.0 9.1 %collective-permute-done.refs_2_ = bf16[512,384]{1,0:T(8,128)(2,1)S(1)} collective-permute-done((bf16[512,384]{1,0:T(8,128)(2,1)S(1)}, bf16[512,384]{1,0:T(8,128)(2,1)S(1)}, u32[]{:S(2)}, u32[]{:S(2)}) %collective-permute-start) | collective-permute-done | bytes 393248 | tf_op jit(solution)/shard_map/ppermute | solution.py:33
  16.1 0.4 collective-permute-done.1.refs_3_
  16.5 9.8 %collective-permute-done.2.refs_4_ = bf16[512,384]{1,0:T(8,128)(2,1)S(1)} collective-permute-done((bf16[512,384]{1,0:T(8,128)(2,1)S(1)}, bf16[512,384]{1,0:T(8,128)(2,1)S(1)}, u32[]{:S(2)}, u32[]{:S(2)}) %collective-permute-start.2) | collective-permute-done | bytes 393248 | tf_op jit(solution)/shard_map/ppermute | solution.py:33
  26.3 0.7 copy-done.15
  27.0 5.9 %shard_map.93 = (bf16[512,384]{1,0:T(8,128)(2,1)}, bf16[512,384]{1,0:T(8,128)(2,1)}, bf16[512,1536]{1,0:T(8,128)(2,1)}) custom-call(s32[4]{0:T(128)} %pad_add_fusion.refs_0_, bf16[512,384]{1,0:T(8,128)(2,1)} %copy-done.6, bf16[512,384]{1,0:T(8,128)(2,1)} %copy-done.13, bf16[512,384]{1,0:T(8,128)(2,1)} %copy-done.14, bf16[512,384]{1,0:T(8,128)(2,1)} %copy-done.15, ...), custom_call_target="tpu_custom_call" | custom-call | flops 1207959552 | bytes 2359296 | tf_op jit(solution)/shard_map/pallas_call | solution.py:64
  33.0 4.6 %shard_map.94.refs_2_ = f32[512,384]{1,0:T(8,128)} custom-call(s32[4]{0:T(128)} %pad_add_fusion.refs_0_, bf16[512,1536]{1,0:T(8,128)(2,1)} %get-tuple-element.33.refs_1_, bf16[1,3,1536,384]{3,2,1,0:T(8,128)(2,1)} %refs_4_.1), custom_call_target="tpu_custom_call" | custom-call | flops 603979776 | bytes 1179648 | tf_op jit(solution)/shard_map/pallas_call | solution.py:64
  37.6 2.8 %shard_map.95 = (bf16[384,512]{1,0:T(8,128)(2,1)}, bf16[384,512]{1,0:T(8,128)(2,1)}, bf16[384,512]{1,0:T(8,128)(2,1)}, bf16[384,512]{1,0:T(8,128)(2,1)}) custom-call(s32[4]{0:T(128)} %pad_add_fusion.refs_0_, bf16[512,1536]{1,0:T(8,128)(2,1)} %get-tuple-element.33.refs_1_, f32[512,384]{1,0:T(8,128)} %shard_map.94.refs_2_), custom_call_target="tpu_custom_call" | custom-call | flops 786432 | bytes 3145728 | tf_op jit(solution)/shard_map/pallas_call | solution.py:64
  40.3 2.7 %collective-permute-start.10 = (bf16[384,512]{1,0:T(8,128)(2,1)}, bf16[384,512]{1,0:T(8,128)(2,1)S(1)}, u32[]{:S(2)}, u32[]{:S(2)}) collective-permute-start(bf16[384,512]{1,0:T(8,128)(2,1)} %get-tuple-element.39), channel_id=1, source_target_pairs={{0,192},{4,196},{8,200},{12,204},{16,208},{20,212},{24,216},{28,22... | collective-permute-start | bytes 1179656 | tf_op jit(solution)/shard_map/ppermute | solution.py:46
  43.1 0.3 collective-permute-start.9
  43.4 0.7 collective-permute-start.8
  44.1 1.3 collective-permute-start.4
  45.4 4.2 %collective-permute-start.3 = (bf16[512,384]{1,0:T(8,128)(2,1)S(1)}, bf16[512,384]{1,0:T(8,128)(2,1)S(1)}, u32[]{:S(2)}, u32[]{:S(2)}) collective-permute-start(bf16[512,384]{1,0:T(8,128)(2,1)S(1)} %copy-done.19), channel_id=1, source_target_pairs={{0,8},{4,12},{8,16},{12,20},{16,24},{20,28},{24,32},{28,36},{32,40... | collective-permute-start | bytes 1179656 | tf_op jit(solution)/shard_map/ppermute | solution.py:29
  49.6 10.0 %collective-permute-done.10 = bf16[384,512]{1,0:T(8,128)(2,1)S(1)} collective-permute-done((bf16[384,512]{1,0:T(8,128)(2,1)}, bf16[384,512]{1,0:T(8,128)(2,1)S(1)}, u32[]{:S(2)}, u32[]{:S(2)}) %collective-permute-start.10) | collective-permute-done | bytes 393248 | tf_op jit(solution)/shard_map/ppermute | solution.py:46
  59.7 8.6 %collective-permute-done.8 = bf16[384,512]{1,0:T(8,128)(2,1)S(1)} collective-permute-done((bf16[384,512]{1,0:T(8,128)(2,1)}, bf16[384,512]{1,0:T(8,128)(2,1)S(1)}, u32[]{:S(2)}, u32[]{:S(2)}) %collective-permute-start.8) | collective-permute-done | bytes 393248 | tf_op jit(solution)/shard_map/ppermute | solution.py:46
  68.3 1.3 pad_maximum_fusion.refs_7_.refs_2_
  69.7 2.7 %collective-permute-start.15 = (bf16[4,384,512]{2,1,0:T(8,128)(2,1)S(1)}, bf16[4,384,512]{2,1,0:T(8,128)(2,1)}, u32[]{:S(2)}, u32[]{:S(2)}) collective-permute-start(bf16[4,384,512]{2,1,0:T(8,128)(2,1)S(1)} %pad_maximum_fusion.refs_7_.refs_2_), channel_id=1, source_target_pairs={{0,56},{4,60},{8,0},{12,4},{16,8},{20,12},{24,16},{28,20},{32,24},... | collective-permute-start | bytes 4718600 | tf_op jit(solution)/shard_map/ppermute | solution.py:46
  72.4 0.2 fusion.9.refs_1_
  72.7 0.6 collective-permute-start.6
  73.3 0.8 collective-permute-start.7
  74.1 7.0 %collective-permute-done.5.refs_2_ = bf16[512,384]{1,0:T(8,128)(2,1)S(1)} collective-permute-done((bf16[512,384]{1,0:T(8,128)(2,1)S(1)}, bf16[512,384]{1,0:T(8,128)(2,1)S(1)}, u32[]{:S(2)}, u32[]{:S(2)}) %collective-permute-start.5) | collective-permute-done | bytes 393248 | tf_op jit(solution)/shard_map/ppermute | solution.py:33
  81.2 1.6 collective-permute-done.6.refs_3_
  82.8 11.1 %collective-permute-done.7.refs_4_ = bf16[512,384]{1,0:T(8,128)(2,1)S(1)} collective-permute-done((bf16[512,384]{1,0:T(8,128)(2,1)S(1)}, bf16[512,384]{1,0:T(8,128)(2,1)S(1)}, u32[]{:S(2)}, u32[]{:S(2)}) %collective-permute-start.7) | collective-permute-done | bytes 393248 | tf_op jit(solution)/shard_map/ppermute | solution.py:33
  93.9 0.8 copy-done.28
  94.7 10.7 %shard_map.96 = (bf16[512,1024]{1,0:T(8,128)(2,1)}, f32[4,1024]{1,0:T(4,128)}, f32[512,384]{1,0:T(8,128)}, bf16[512,384]{1,0:T(8,128)(2,1)}, bf16[512,384]{1,0:T(8,128)(2,1)}, /*index=5*/bf16[512,384]{1,0:T(8,128)(2,1)}) custom-call(s32[4]{0:T(128)} %pad_add_fusion.refs_0_, bf16[512,384]{1,0:T(8,128)(2,1)} %copy-done.12, bf16[512,384]{1,0:T(8,128)(2,1)} %copy-done.26, ...), custom_call_target="tpu_custom_call" | custom-call | flops 3221225472 | bytes 3145728 | tf_op jit(solution)/shard_map/pallas_call | solution.py:64
  105.5 0.6 collective-permute-start.12
  106.1 2.1 collective-permute-start.13
  108.1 0.7 convert_element_type.63
  108.9 19.6 %all_gather.6 = bf16[8,8,512]{2,1,0:T(8,128)(2,1)S(1)} all-gather(bf16[1,8,512]{2,1,0:T(8,128)(2,1)S(1)} %reshape.138), channel_id=1, replica_groups={{0,8,16,24,32,40,48,56},{4,12,20,28,36,44,52,60},{64,72,80,88,96,104,11..., dimensions={0}, use_global_device_ids=true | all-gather | bytes 73728 | tf_op jit(solution)/shard_map/all_gather | solution.py:369
  128.5 22.4 %all_gather.7.refs_7_ = bf16[64,8,512]{2,1,0:T(8,128)(2,1)} all-gather(bf16[8,8,512]{2,1,0:T(8,128)(2,1)S(1)} %all_gather.6), channel_id=1, replica_groups={{0,4,64,68,128,132,192,196},{8,12,72,76,136,140,200,204},{16,20,80,84,1..., dimensions={0}, use_global_device_ids=true | all-gather | bytes 589824 | tf_op jit(solution)/shard_map/all_gather | solution.py:370
  151.0 0.7 copy-done.9
  151.9 2.7 %shard_map.97 = (f32[512,384]{1,0:T(8,128)}, bf16[512,384]{1,0:T(8,128)(2,1)}) custom-call(s32[4]{0:T(128)} %pad_add_fusion.refs_0_, f32[512,384]{1,0:T(8,128)} %get-tuple-element.42.refs_1_, bf16[512,384]{1,0:T(8,128)(2,1)} %copy-done.9, bf16[512,384]{1,0:T(8,128)(2,1)} %copy-done.10, bf16[512,384]{1,0:T(8,128)(2,1)} %copy-done.11, ...), custom_call_target="tpu_custom_call" | custom-call | flops 786432 | bytes 3145728 | tf_op jit(solution)/shard_map/pallas_call | solution.py:64
  154.6 1.3 collective-permute-start.16
  155.9 4.0 %collective-permute-start.17 = (bf16[512,384]{1,0:T(8,128)(2,1)}, bf16[512,384]{1,0:T(8,128)(2,1)S(1)}, u32[]{:S(2)}, u32[]{:S(2)}) collective-permute-start(bf16[512,384]{1,0:T(8,128)(2,1)} %get-tuple-element.47.refs_2_.refs_4_), channel_id=1, source_target_pairs={{0,8},{4,12},{8,16},{12,20},{16,24},{20,28},{24,32},{28,36},{32,40... | collective-permute-start | bytes 1179656 | tf_op jit(solution)/shard_map/ppermute | solution.py:29
  160.0 1.2 collective-permute-start.21
  161.1 2.4 %collective-permute-start.22 = (bf16[512,384]{1,0:T(8,128)(2,1)}, bf16[512,384]{1,0:T(8,128)(2,1)S(1)}, u32[]{:S(2)}, u32[]{:S(2)}) collective-permute-start(bf16[512,384]{1,0:T(8,128)(2,1)} %get-tuple-element.47.refs_2_.refs_4_), channel_id=1, source_target_pairs={{0,128},{4,132},{8,136},{12,140},{16,144},{20,148},{24,152},{28,15... | collective-permute-start | bytes 1179656 | tf_op jit(solution)/shard_map/ppermute | solution.py:46
  163.5 1.1 collective-permute-start.23
  165.0 0.2 reduce_sum.12
  165.2 2.1 collective-permute-done.16.refs_1_
  167.3 1.0 collective-permute-done.17.refs_3_
  168.3 0.8 copy-done.25
  169.0 6.9 %shard_map.98 = (f32[512,384]{1,0:T(8,128)}, bf16[512,384]{1,0:T(8,128)(2,1)}, bf16[512,384]{1,0:T(8,128)(2,1)}, bf16[512,384]{1,0:T(8,128)(2,1)}) custom-call(s32[4]{0:T(128)} %pad_add_fusion.refs_0_, bf16[512,384]{1,0:T(8,128)(2,1)} %copy-done.24, bf16[512,384]{1,0:T(8,128)(2,1)} %get-tuple-element.47.refs_2_.refs_4_, bf16[512,384]{1,0:T(8,128)(2,1)} %copy-done.25, ...), custom_call_target="tpu_custom_call" | custom-call | flops 1811939328 | bytes 3538944 | tf_op jit(solution)/shard_map/pallas_call | solution.py:64
  176.0 1.7 collective-permute-done.21.refs_5_
  177.6 12.0 %collective-permute-done.22.refs_6_ = bf16[512,384]{1,0:T(8,128)(2,1)S(1)} collective-permute-done((bf16[512,384]{1,0:T(8,128)(2,1)}, bf16[512,384]{1,0:T(8,128)(2,1)S(1)}, u32[]{:S(2)}, u32[]{:S(2)}) %collective-permute-start.22) | collective-permute-done | bytes 393248 | tf_op jit(solution)/shard_map/ppermute | solution.py:46
  189.6 0.7 copy-done.22
  190.4 0.7 copy-done.23
  191.1 6.7 %shard_map.99 = (f32[192,1152]{1,0:T(8,128)}, bf16[192,1152]{1,0:T(8,128)(2,1)}) custom-call(s32[4]{0:T(128)} %pad_add_fusion.refs_0_, bf16[4,384,512]{2,1,0:T(8,128)(2,1)} %collective-permute-done.14.refs_5_.refs_1_, bf16[4,384,512]{2,1,0:T(8,128)(2,1)} %copy-done.5, bf16[4,384,512]{2,1,0:T(8,128)(2,1)} %collective-permute-done.15.refs_6_.refs_3_, ...), custom_call_target="tpu_custom_call" | custom-call | flops 1811939328 | bytes 6291456 | tf_op jit(solution)/shard_map/pallas_call | solution.py:64
  197.8 1.1 collective-permute-start.24
  199.1 1.7 collective-permute-start.18
  200.8 1.1 collective-permute-start.20
  201.8 1.2 collective-permute-start.19
  203.1 1.2 copy-done
  204.3 0.7 shard_map.100
  205.2 0.8 convolution_multiply_fusion
  206.0 5.5 %collective-permute-done.20 = bf16[512,384]{1,0:T(8,128)(2,1)S(1)} collective-permute-done((bf16[512,384]{1,0:T(8,128)(2,1)}, bf16[512,384]{1,0:T(8,128)(2,1)S(1)}, u32[]{:S(2)}, u32[]{:S(2)}) %collective-permute-start.20) | collective-permute-done | bytes 393248 | tf_op jit(solution)/shard_map/ppermute | solution.py:33
  211.4 8.1 %collective-permute-done.19 = bf16[512,384]{1,0:T(8,128)(2,1)S(1)} collective-permute-done((bf16[512,384]{1,0:T(8,128)(2,1)}, bf16[512,384]{1,0:T(8,128)(2,1)S(1)}, u32[]{:S(2)}, u32[]{:S(2)}) %collective-permute-start.19) | collective-permute-done | bytes 393248 | tf_op jit(solution)/shard_map/ppermute | solution.py:33
  219.7 5.6 %collective-permute-start.25 = (bf16[24,1152]{1,0:T(8,128)(2,1)S(1)}, bf16[24,1152]{1,0:T(8,128)(2,1)S(1)}, u32[]{:S(2)}, u32[]{:S(2)}) collective-permute-start(bf16[24,1152]{1,0:T(8,128)(2,1)S(1)} %get-tuple-element.55), channel_id=1, source_target_pairs={{0,8},{4,12},{8,16},{12,20},{16,24},{20,28},{24,32},{28,36},{32,40... | collective-permute-start | bytes 165896 | tf_op jit(solution)/shard_map/ppermute | solution.py:46
  225.3 1.5 fusion.4
  226.9 3.7 %collective-permute-done.25 = bf16[24,1152]{1,0:T(8,128)(2,1)S(1)} collective-permute-done((bf16[24,1152]{1,0:T(8,128)(2,1)S(1)}, bf16[24,1152]{1,0:T(8,128)(2,1)S(1)}, u32[]{:S(2)}, u32[]{:S(2)}) %collective-permute-start.25) | collective-permute-done | bytes 55328 | tf_op jit(solution)/shard_map/ppermute | solution.py:46
  230.7 0.7 copy.14
  (91 shorter events, 1.6 us)
Async XLA Ops:
  1.9 24.4 %copy-start.6 = (bf16[512,384]{1,0:T(8,128)(2,1)}, bf16[512,384]{1,0:T(8,128)(2,1)S(1)}, u32[]{:S(2)}) copy-start(bf16[512,384]{1,0:T(8,128)(2,1)S(1)} %fusion.8.refs_1_) | copy-start | bytes 1179652
  1.9 14.2 %collective-permute-start = (bf16[512,384]{1,0:T(8,128)(2,1)S(1)}, bf16[512,384]{1,0:T(8,128)(2,1)S(1)}, u32[]{:S(2)}, u32[]{:S(2)}) collective-permute-start(bf16[512,384]{1,0:T(8,128)(2,1)S(1)} %fusion.8.refs_1_), channel_id=1, source_target_pairs={{0,3},{1,0},{2,1},{3,2},{4,7},{5,4},{6,5},{7,6},{8,11},{9,8},{10,9... | collective-permute-start | bytes 1179656 | tf_op jit(solution)/shard_map/ppermute | solution.py:33
  5.3 11.2 %collective-permute-start.1 = (bf16[512,384]{1,0:T(8,128)(2,1)S(1)}, bf16[512,384]{1,0:T(8,128)(2,1)S(1)}, u32[]{:S(2)}, u32[]{:S(2)}) collective-permute-start(bf16[512,384]{1,0:T(8,128)(2,1)S(1)} %fusion.8.refs_1_), channel_id=1, source_target_pairs={{0,2},{1,3},{2,0},{3,1},{4,6},{5,7},{6,4},{7,5},{8,10},{9,11},{10,... | collective-permute-start | bytes 1179656 | tf_op jit(solution)/shard_map/ppermute | solution.py:33
  5.8 20.4 %collective-permute-start.2 = (bf16[512,384]{1,0:T(8,128)(2,1)S(1)}, bf16[512,384]{1,0:T(8,128)(2,1)S(1)}, u32[]{:S(2)}, u32[]{:S(2)}) collective-permute-start(bf16[512,384]{1,0:T(8,128)(2,1)S(1)} %fusion.8.refs_1_), channel_id=1, source_target_pairs={{0,1},{1,2},{2,3},{3,0},{4,5},{5,6},{6,7},{7,4},{8,9},{9,10},{10,1... | collective-permute-start | bytes 1179656 | tf_op jit(solution)/shard_map/ppermute | solution.py:33
  16.1 10.1 %copy-start.13 = (bf16[512,384]{1,0:T(8,128)(2,1)}, bf16[512,384]{1,0:T(8,128)(2,1)S(1)}, u32[]{:S(2)}) copy-start(bf16[512,384]{1,0:T(8,128)(2,1)S(1)} %collective-permute-done.refs_2_) | copy-start | bytes 1179652
  16.5 9.8 %copy-start.14 = (bf16[512,384]{1,0:T(8,128)(2,1)}, bf16[512,384]{1,0:T(8,128)(2,1)S(1)}, u32[]{:S(2)}) copy-start(bf16[512,384]{1,0:T(8,128)(2,1)S(1)} %collective-permute-done.1.refs_3_) | copy-start | bytes 1179652
  26.3 0.8 copy-start.15
  37.5 6.6 %copy-start.20 = (bf16[512,384]{1,0:T(8,128)(2,1)S(1)}, bf16[512,384]{1,0:T(8,128)(2,1)}, u32[]{:S(2)}) copy-start(bf16[512,384]{1,0:T(8,128)(2,1)} %get-tuple-element.35) | copy-start | bytes 1179652
  37.6 7.9 %copy-start.19 = (bf16[512,384]{1,0:T(8,128)(2,1)S(1)}, bf16[512,384]{1,0:T(8,128)(2,1)}, u32[]{:S(2)}) copy-start(bf16[512,384]{1,0:T(8,128)(2,1)} %get-tuple-element.34) | copy-start | bytes 1179652
  40.3 19.3 %collective-permute-start.10 = (bf16[384,512]{1,0:T(8,128)(2,1)}, bf16[384,512]{1,0:T(8,128)(2,1)S(1)}, u32[]{:S(2)}, u32[]{:S(2)}) collective-permute-start(bf16[384,512]{1,0:T(8,128)(2,1)} %get-tuple-element.39), channel_id=1, source_target_pairs={{0,192},{4,196},{8,200},{12,204},{16,208},{20,212},{24,216},{28,22... | collective-permute-start | bytes 1179656 | tf_op jit(solution)/shard_map/ppermute | solution.py:46
  43.1 16.6 %collective-permute-start.9 = (bf16[384,512]{1,0:T(8,128)(2,1)}, bf16[384,512]{1,0:T(8,128)(2,1)S(1)}, u32[]{:S(2)}, u32[]{:S(2)}) collective-permute-start(bf16[384,512]{1,0:T(8,128)(2,1)} %get-tuple-element.38), channel_id=1, source_target_pairs={{0,128},{4,132},{8,136},{12,140},{16,144},{20,148},{24,152},{28,15... | collective-permute-start | bytes 1179656 | tf_op jit(solution)/shard_map/ppermute | solution.py:46
  43.4 24.9 %collective-permute-start.8 = (bf16[384,512]{1,0:T(8,128)(2,1)}, bf16[384,512]{1,0:T(8,128)(2,1)S(1)}, u32[]{:S(2)}, u32[]{:S(2)}) collective-permute-start(bf16[384,512]{1,0:T(8,128)(2,1)} %get-tuple-element.37), channel_id=1, source_target_pairs={{0,64},{4,68},{8,72},{12,76},{16,80},{20,84},{24,88},{28,92},{32,9... | collective-permute-start | bytes 1179656 | tf_op jit(solution)/shard_map/ppermute | solution.py:46
  44.1 28.2 %collective-permute-start.4 = (bf16[512,384]{1,0:T(8,128)(2,1)S(1)}, bf16[512,384]{1,0:T(8,128)(2,1)S(1)}, u32[]{:S(2)}, u32[]{:S(2)}) collective-permute-start(bf16[512,384]{1,0:T(8,128)(2,1)S(1)} %copy-done.20), channel_id=1, source_target_pairs={{8,0},{12,4},{16,8},{20,12},{24,16},{28,20},{32,24},{36,28},{40,32... | collective-permute-start | bytes 1179656 | tf_op jit(solution)/shard_map/ppermute | solution.py:29
  45.4 27.0 %collective-permute-start.3 = (bf16[512,384]{1,0:T(8,128)(2,1)S(1)}, bf16[512,384]{1,0:T(8,128)(2,1)S(1)}, u32[]{:S(2)}, u32[]{:S(2)}) collective-permute-start(bf16[512,384]{1,0:T(8,128)(2,1)S(1)} %copy-done.19), channel_id=1, source_target_pairs={{0,8},{4,12},{8,16},{12,20},{16,24},{20,28},{24,32},{28,36},{32,40... | collective-permute-start | bytes 1179656 | tf_op jit(solution)/shard_map/ppermute | solution.py:29
  68.3 4.1 %copy-start.2 = (f32[512,384]{1,0:T(8,128)S(1)}, f32[512,384]{1,0:T(8,128)}, u32[]{:S(2)}) copy-start(f32[512,384]{1,0:T(8,128)} %shard_map.94.refs_2_) | copy-start | bytes 2359300
  68.3 4.1 %copy-start.4 = (bf16[512,384]{1,0:T(8,128)(2,1)S(1)}, bf16[512,384]{1,0:T(8,128)(2,1)}, u32[]{:S(2)}) copy-start(bf16[512,384]{1,0:T(8,128)(2,1)} %param.6) | copy-start | bytes 1179652
  69.6 24.2 %copy-start.5 = (bf16[4,384,512]{2,1,0:T(8,128)(2,1)}, bf16[4,384,512]{2,1,0:T(8,128)(2,1)S(1)}, u32[]{:S(2)}) copy-start(bf16[4,384,512]{2,1,0:T(8,128)(2,1)S(1)} %pad_maximum_fusion.refs_7_.refs_2_) | copy-start | bytes 4718596
  69.6 81.3 %collective-permute-start.14 = (bf16[4,384,512]{2,1,0:T(8,128)(2,1)S(1)}, bf16[4,384,512]{2,1,0:T(8,128)(2,1)}, u32[]{:S(2)}, u32[]{:S(2)}) collective-permute-start(bf16[4,384,512]{2,1,0:T(8,128)(2,1)S(1)} %pad_maximum_fusion.refs_7_.refs_2_), channel_id=1, source_target_pairs={{0,8},{4,12},{8,16},{12,20},{16,24},{20,28},{24,32},{28,36},{32,40... | collective-permute-start | bytes 4718600 | tf_op jit(solution)/shard_map/ppermute | solution.py:46
  69.7 81.2 %collective-permute-start.15 = (bf16[4,384,512]{2,1,0:T(8,128)(2,1)S(1)}, bf16[4,384,512]{2,1,0:T(8,128)(2,1)}, u32[]{:S(2)}, u32[]{:S(2)}) collective-permute-start(bf16[4,384,512]{2,1,0:T(8,128)(2,1)S(1)} %pad_maximum_fusion.refs_7_.refs_2_), channel_id=1, source_target_pairs={{0,56},{4,60},{8,0},{12,4},{16,8},{20,12},{24,16},{28,20},{32,24},... | collective-permute-start | bytes 4718600 | tf_op jit(solution)/shard_map/ppermute | solution.py:46
  72.6 21.3 %copy-start.12 = (bf16[512,384]{1,0:T(8,128)(2,1)}, bf16[512,384]{1,0:T(8,128)(2,1)S(1)}, u32[]{:S(2)}) copy-start(bf16[512,384]{1,0:T(8,128)(2,1)S(1)} %fusion.9.refs_1_) | copy-start | bytes 1179652
  72.6 8.6 %collective-permute-start.5 = (bf16[512,384]{1,0:T(8,128)(2,1)S(1)}, bf16[512,384]{1,0:T(8,128)(2,1)S(1)}, u32[]{:S(2)}, u32[]{:S(2)}) collective-permute-start(bf16[512,384]{1,0:T(8,128)(2,1)S(1)} %fusion.9.refs_1_), channel_id=1, source_target_pairs={{0,3},{1,0},{2,1},{3,2},{4,7},{5,4},{6,5},{7,6},{8,11},{9,8},{10,9... | collective-permute-start | bytes 1179656 | tf_op jit(solution)/shard_map/ppermute | solution.py:33
  72.7 10.1 %collective-permute-start.6 = (bf16[512,384]{1,0:T(8,128)(2,1)S(1)}, bf16[512,384]{1,0:T(8,128)(2,1)S(1)}, u32[]{:S(2)}, u32[]{:S(2)}) collective-permute-start(bf16[512,384]{1,0:T(8,128)(2,1)S(1)} %fusion.9.refs_1_), channel_id=1, source_target_pairs={{0,2},{1,3},{2,0},{3,1},{4,6},{5,7},{6,4},{7,5},{8,10},{9,11},{10,... | collective-permute-start | bytes 1179656 | tf_op jit(solution)/shard_map/ppermute | solution.py:33
  73.3 20.6 %collective-permute-start.7 = (bf16[512,384]{1,0:T(8,128)(2,1)S(1)}, bf16[512,384]{1,0:T(8,128)(2,1)S(1)}, u32[]{:S(2)}, u32[]{:S(2)}) collective-permute-start(bf16[512,384]{1,0:T(8,128)(2,1)S(1)} %fusion.9.refs_1_), channel_id=1, source_target_pairs={{0,1},{1,2},{2,3},{3,0},{4,5},{5,6},{6,7},{7,4},{8,9},{9,10},{10,1... | collective-permute-start | bytes 1179656 | tf_op jit(solution)/shard_map/ppermute | solution.py:33
  81.2 12.7 %copy-start.26 = (bf16[512,384]{1,0:T(8,128)(2,1)}, bf16[512,384]{1,0:T(8,128)(2,1)S(1)}, u32[]{:S(2)}) copy-start(bf16[512,384]{1,0:T(8,128)(2,1)S(1)} %collective-permute-done.5.refs_2_) | copy-start | bytes 1179652
  82.7 11.1 %copy-start.27 = (bf16[512,384]{1,0:T(8,128)(2,1)}, bf16[512,384]{1,0:T(8,128)(2,1)S(1)}, u32[]{:S(2)}) copy-start(bf16[512,384]{1,0:T(8,128)(2,1)S(1)} %collective-permute-done.6.refs_3_) | copy-start | bytes 1179652
  93.9 0.8 copy-start.28
  105.4 45.5 %collective-permute-start.11 = (bf16[512,384]{1,0:T(8,128)(2,1)}, bf16[512,384]{1,0:T(8,128)(2,1)S(1)}, u32[]{:S(2)}, u32[]{:S(2)}) collective-permute-start(bf16[512,384]{1,0:T(8,128)(2,1)} %get-tuple-element.43), channel_id=1, source_target_pairs={{0,1},{1,2},{2,3},{3,0},{4,5},{5,6},{6,7},{7,4},{8,9},{9,10},{10,1... | collective-permute-start | bytes 1179656 | tf_op jit(solution)/shard_map/ppermute | solution.py:33
  105.5 45.4 %collective-permute-start.12 = (bf16[512,384]{1,0:T(8,128)(2,1)}, bf16[512,384]{1,0:T(8,128)(2,1)S(1)}, u32[]{:S(2)}, u32[]{:S(2)}) collective-permute-start(bf16[512,384]{1,0:T(8,128)(2,1)} %get-tuple-element.44), channel_id=1, source_target_pairs={{0,2},{1,3},{2,0},{3,1},{4,6},{5,7},{6,4},{7,5},{8,10},{9,11},{10,... | collective-permute-start | bytes 1179656 | tf_op jit(solution)/shard_map/ppermute | solution.py:33
  106.1 44.9 %collective-permute-start.13 = (bf16[512,384]{1,0:T(8,128)(2,1)}, bf16[512,384]{1,0:T(8,128)(2,1)S(1)}, u32[]{:S(2)}, u32[]{:S(2)}) collective-permute-start(bf16[512,384]{1,0:T(8,128)(2,1)} %get-tuple-element.45), channel_id=1, source_target_pairs={{0,3},{1,0},{2,1},{3,2},{4,7},{5,4},{6,5},{7,6},{8,11},{9,8},{10,9... | collective-permute-start | bytes 1179656 | tf_op jit(solution)/shard_map/ppermute | solution.py:33
  150.9 0.7 copy-start.9
  150.9 0.9 copy-start.10
  150.9 1.0 copy-start.11
  151.9 12.7 %copy-start.17 = (s32[64]{0:T(128)S(1)}, s32[64]{0:T(128)}, u32[]{:S(2)}) copy-start(s32[64]{0:T(128)} %constant.101) | copy-start | bytes 772
  151.9 12.8 %copy-start.16 = (s32[8,8]{1,0:T(8,128)S(1)}, s32[8,8]{1,0:T(8,128)}, u32[]{:S(2)}) copy-start(s32[8,8]{1,0:T(8,128)} %param.10) | copy-start | bytes 772
  154.6 12.7 %collective-permute-start.16 = (bf16[512,384]{1,0:T(8,128)(2,1)}, bf16[512,384]{1,0:T(8,128)(2,1)S(1)}, u32[]{:S(2)}, u32[]{:S(2)}) collective-permute-start(bf16[512,384]{1,0:T(8,128)(2,1)} %get-tuple-element.47.refs_2_.refs_4_), channel_id=1, source_target_pairs={{8,0},{12,4},{16,8},{20,12},{24,16},{28,20},{32,24},{36,28},{40,32... | collective-permute-start | bytes 1179656 | tf_op jit(solution)/shard_map/ppermute | solution.py:29
  155.9 12.3 %collective-permute-start.17 = (bf16[512,384]{1,0:T(8,128)(2,1)}, bf16[512,384]{1,0:T(8,128)(2,1)S(1)}, u32[]{:S(2)}, u32[]{:S(2)}) collective-permute-start(bf16[512,384]{1,0:T(8,128)(2,1)} %get-tuple-element.47.refs_2_.refs_4_), channel_id=1, source_target_pairs={{0,8},{4,12},{8,16},{12,20},{16,24},{20,28},{24,32},{28,36},{32,40... | collective-permute-start | bytes 1179656 | tf_op jit(solution)/shard_map/ppermute | solution.py:29
  160.0 17.7 %collective-permute-start.21 = (bf16[512,384]{1,0:T(8,128)(2,1)}, bf16[512,384]{1,0:T(8,128)(2,1)S(1)}, u32[]{:S(2)}, u32[]{:S(2)}) collective-permute-start(bf16[512,384]{1,0:T(8,128)(2,1)} %get-tuple-element.47.refs_2_.refs_4_), channel_id=1, source_target_pairs={{0,64},{4,68},{8,72},{12,76},{16,80},{20,84},{24,88},{28,92},{32,9... | collective-permute-start | bytes 1179656 | tf_op jit(solution)/shard_map/ppermute | solution.py:46
  161.1 28.5 %collective-permute-start.22 = (bf16[512,384]{1,0:T(8,128)(2,1)}, bf16[512,384]{1,0:T(8,128)(2,1)S(1)}, u32[]{:S(2)}, u32[]{:S(2)}) collective-permute-start(bf16[512,384]{1,0:T(8,128)(2,1)} %get-tuple-element.47.refs_2_.refs_4_), channel_id=1, source_target_pairs={{0,128},{4,132},{8,136},{12,140},{16,144},{20,148},{24,152},{28,15... | collective-permute-start | bytes 1179656 | tf_op jit(solution)/shard_map/ppermute | solution.py:46
  163.5 26.1 %collective-permute-start.23 = (bf16[512,384]{1,0:T(8,128)(2,1)}, bf16[512,384]{1,0:T(8,128)(2,1)S(1)}, u32[]{:S(2)}, u32[]{:S(2)}) collective-permute-start(bf16[512,384]{1,0:T(8,128)(2,1)} %get-tuple-element.47.refs_2_.refs_4_), channel_id=1, source_target_pairs={{0,192},{4,196},{8,200},{12,204},{16,208},{20,212},{24,216},{28,22... | collective-permute-start | bytes 1179656 | tf_op jit(solution)/shard_map/ppermute | solution.py:46
  167.3 1.0 copy-start.24
  168.3 0.8 copy-start.25
  177.6 13.5 %copy-start.21 = (bf16[512,384]{1,0:T(8,128)(2,1)}, bf16[512,384]{1,0:T(8,128)(2,1)S(1)}, u32[]{:S(2)}) copy-start(bf16[512,384]{1,0:T(8,128)(2,1)S(1)} %collective-permute-done.21.refs_5_) | copy-start | bytes 1179652
  189.6 0.8 copy-start.22
  190.4 0.7 copy-start.23
  191.1 8.0 %copy-start.18 = (bf16[512,384]{1,0:T(8,128)(2,1)S(1)}, bf16[512,384]{1,0:T(8,128)(2,1)}, u32[]{:S(2)}) copy-start(bf16[512,384]{1,0:T(8,128)(2,1)} %get-tuple-element.49.refs_8_) | copy-start | bytes 1179652
  191.1 12.0 %copy-start.1 = (s32[4]{0:T(128)S(1)}, s32[4]{0:T(128)}, u32[]{:S(2)}) copy-start(s32[4]{0:T(128)} %pad_add_fusion.refs_0_) | copy-start | bytes 52
  191.1 14.1 %copy-start.3 = (bf16[64,8,512]{2,1,0:T(8,128)(2,1)S(1)}, bf16[64,8,512]{2,1,0:T(8,128)(2,1)}, u32[]{:S(2)}) copy-start(bf16[64,8,512]{2,1,0:T(8,128)(2,1)} %all_gather.7.refs_7_) | copy-start | bytes 1572868
  191.1 34.2 %copy-start.7 = (f32[512,384]{1,0:T(8,128)S(1)}, f32[512,384]{1,0:T(8,128)}, u32[]{:S(2)}) copy-start(f32[512,384]{1,0:T(8,128)} %get-tuple-element.46) | copy-start | bytes 2359300
  191.1 34.2 %copy-start.8 = (f32[512,384]{1,0:T(8,128)S(1)}, f32[512,384]{1,0:T(8,128)}, u32[]{:S(2)}) copy-start(f32[512,384]{1,0:T(8,128)} %get-tuple-element.48) | copy-start | bytes 2359300
  197.8 5.3 %collective-permute-start.24 = (bf16[192,1152]{1,0:T(8,128)(2,1)}, bf16[192,1152]{1,0:T(8,128)(2,1)S(1)}, u32[]{:S(2)}, u32[]{:S(2)}) collective-permute-start(bf16[192,1152]{1,0:T(8,128)(2,1)} %get-tuple-element.53), channel_id=1, source_target_pairs={{0,4},{4,0},{8,12},{12,8},{16,20},{20,16},{24,28},{28,24},{32,36},... | collective-permute-start | bytes 1327112 | tf_op jit(solution)/shard_map/ppermute | solution.py:46
  199.1 20.5 %collective-permute-start.18 = (bf16[512,384]{1,0:T(8,128)(2,1)S(1)}, bf16[512,384]{1,0:T(8,128)(2,1)S(1)}, u32[]{:S(2)}, u32[]{:S(2)}) collective-permute-start(bf16[512,384]{1,0:T(8,128)(2,1)S(1)} %copy-done.18), channel_id=1, source_target_pairs={{0,1},{1,2},{2,3},{3,0},{4,5},{5,6},{6,7},{7,4},{8,9},{9,10},{10,1... | collective-permute-start | bytes 1179656 | tf_op jit(solution)/shard_map/ppermute | solution.py:33
  200.8 10.6 %collective-permute-start.20 = (bf16[512,384]{1,0:T(8,128)(2,1)}, bf16[512,384]{1,0:T(8,128)(2,1)S(1)}, u32[]{:S(2)}, u32[]{:S(2)}) collective-permute-start(bf16[512,384]{1,0:T(8,128)(2,1)} %get-tuple-element.51), channel_id=1, source_target_pairs={{0,3},{1,0},{2,1},{3,2},{4,7},{5,4},{6,5},{7,6},{8,11},{9,8},{10,9... | collective-permute-start | bytes 1179656 | tf_op jit(solution)/shard_map/ppermute | solution.py:33
  201.8 17.7 %collective-permute-start.19 = (bf16[512,384]{1,0:T(8,128)(2,1)}, bf16[512,384]{1,0:T(8,128)(2,1)S(1)}, u32[]{:S(2)}, u32[]{:S(2)}) collective-permute-start(bf16[512,384]{1,0:T(8,128)(2,1)} %get-tuple-element.50), channel_id=1, source_target_pairs={{0,2},{1,3},{2,0},{3,1},{4,6},{5,7},{6,4},{7,5},{8,10},{9,11},{10,... | collective-permute-start | bytes 1179656 | tf_op jit(solution)/shard_map/ppermute | solution.py:33
  203.1 1.2 copy-start
  205.0 14.6 %collective-permute-start.31 = (bf16[24,1152]{1,0:T(8,128)(2,1)S(1)}, bf16[24,1152]{1,0:T(8,128)(2,1)S(1)}, u32[]{:S(2)}, u32[]{:S(2)}) collective-permute-start(bf16[24,1152]{1,0:T(8,128)(2,1)S(1)} %get-tuple-element.61), channel_id=1, source_target_pairs={{0,56},{4,60},{8,0},{12,4},{16,8},{20,12},{24,16},{28,20},{32,24},... | collective-permute-start | bytes 165896 | tf_op jit(solution)/shard_map/ppermute | solution.py:46
  205.1 14.6 %collective-permute-start.30 = (bf16[24,1152]{1,0:T(8,128)(2,1)S(1)}, bf16[24,1152]{1,0:T(8,128)(2,1)S(1)}, u32[]{:S(2)}, u32[]{:S(2)}) collective-permute-start(bf16[24,1152]{1,0:T(8,128)(2,1)S(1)} %get-tuple-element.60), channel_id=1, source_target_pairs={{0,48},{4,52},{8,56},{12,60},{16,0},{20,4},{24,8},{28,12},{32,16},... | collective-permute-start | bytes 165896 | tf_op jit(solution)/shard_map/ppermute | solution.py:46
  211.4 15.4 %collective-permute-start.29 = (bf16[24,1152]{1,0:T(8,128)(2,1)S(1)}, bf16[24,1152]{1,0:T(8,128)(2,1)S(1)}, u32[]{:S(2)}, u32[]{:S(2)}) collective-permute-start(bf16[24,1152]{1,0:T(8,128)(2,1)S(1)} %get-tuple-element.59), channel_id=1, source_target_pairs={{0,40},{4,44},{8,48},{12,52},{16,56},{20,60},{24,0},{28,4},{32,8},... | collective-permute-start | bytes 165896 | tf_op jit(solution)/shard_map/ppermute | solution.py:46
  219.6 7.3 %collective-permute-start.28 = (bf16[24,1152]{1,0:T(8,128)(2,1)S(1)}, bf16[24,1152]{1,0:T(8,128)(2,1)S(1)}, u32[]{:S(2)}, u32[]{:S(2)}) collective-permute-start(bf16[24,1152]{1,0:T(8,128)(2,1)S(1)} %get-tuple-element.58), channel_id=1, source_target_pairs={{0,32},{4,36},{8,40},{12,44},{16,48},{20,52},{24,56},{28,60},{32,0... | collective-permute-start | bytes 165896 | tf_op jit(solution)/shard_map/ppermute | solution.py:46
  219.6 7.3 %collective-permute-start.27 = (bf16[24,1152]{1,0:T(8,128)(2,1)S(1)}, bf16[24,1152]{1,0:T(8,128)(2,1)S(1)}, u32[]{:S(2)}, u32[]{:S(2)}) collective-permute-start(bf16[24,1152]{1,0:T(8,128)(2,1)S(1)} %get-tuple-element.57), channel_id=1, source_target_pairs={{0,24},{4,28},{8,32},{12,36},{16,40},{20,44},{24,48},{28,52},{32,5... | collective-permute-start | bytes 165896 | tf_op jit(solution)/shard_map/ppermute | solution.py:46
  219.6 7.2 %collective-permute-start.26 = (bf16[24,1152]{1,0:T(8,128)(2,1)S(1)}, bf16[24,1152]{1,0:T(8,128)(2,1)S(1)}, u32[]{:S(2)}, u32[]{:S(2)}) collective-permute-start(bf16[24,1152]{1,0:T(8,128)(2,1)S(1)} %get-tuple-element.56), channel_id=1, source_target_pairs={{0,16},{4,20},{8,24},{12,28},{16,32},{20,36},{24,40},{28,44},{32,4... | collective-permute-start | bytes 165896 | tf_op jit(solution)/shard_map/ppermute | solution.py:46
  219.7 10.9 %collective-permute-start.25 = (bf16[24,1152]{1,0:T(8,128)(2,1)S(1)}, bf16[24,1152]{1,0:T(8,128)(2,1)S(1)}, u32[]{:S(2)}, u32[]{:S(2)}) collective-permute-start(bf16[24,1152]{1,0:T(8,128)(2,1)S(1)} %get-tuple-element.55), channel_id=1, source_target_pairs={{0,8},{4,12},{8,16},{12,20},{16,24},{20,28},{24,32},{28,36},{32,40... | collective-permute-start | bytes 165896 | tf_op jit(solution)/shard_map/ppermute | solution.py:46

commit v2 on v1

v2 whole, which is shorter than its diff:
```python
import jax
import jax.numpy as jnp
from jax import lax
from jax.experimental import pallas as pl
from jax.experimental.pallas import tpu as pltpu
from jax.sharding import PartitionSpec as P

BLOCK = 128
EXONS = 8
NX, NY, NZ = 4, 4, 8
TAPS = 3
GROUP = 24
F32 = jnp.float32
BF = jnp.bfloat16


def activation_slope(point, cotan):
    _, back = jax.vjp(jax.nn.gelu, point)
    return back(cotan)[0]


def seq_index(y, z, core):
    return (y * NZ + z) * 2 + core


def shifted(value, steps):
    count = lax.axis_size("seq")
    leading, last = (max(0, -steps), min(count, count - steps))
    return lax.ppermute(value, "seq", [(s, s + steps) for s in range(leading, last)])


def along_x(value, steps):
    return lax.ppermute(value, "chan", [(i, (i + steps) % NX) for i in range(NX)])


def along_seq(value, dy, dz, dcore):
    pairs = [
        (
            seq_index(y, z, core),
            seq_index((y + dy) % NY, (z + dz) % NZ, (core + dcore) % 2),
        )
        for y in range(NY)
        for z in range(NZ)
        for core in range(2)
    ]
    return lax.ppermute(value, "seq", pairs)


def from_all_x(value):
    return [value] + [along_x(value, -r) for r in range(1, NX)]


def times_t(left, right):
    return lax.dot_general(left, right, (((1,), (1,)), ((), ())), preferred_element_type=F32)


def call(body, place, operands, outs, scratch=(), after=(), limit=16, flops=0, moved=0):
    count = len(operands)

    def kernel(*refs):
        body(refs[0], *refs[1 : 1 + count], *refs[1 + count + len(after) :])

    vmem = pl.BlockSpec(memory_space=pltpu.VMEM)
    return pl.pallas_call(
        kernel,
        in_specs=[pl.BlockSpec(memory_space=pltpu.SMEM)]
        + [pl.BlockSpec(memory_space=space) for _, space in operands]
        + [pl.BlockSpec(memory_space=pl.ANY)] * len(after),
        out_specs=[vmem] * len(outs),
        scratch_shapes=list(scratch),
        out_shape=outs,
        cost_estimate=pl.CostEstimate(flops=flops, bytes_accessed=moved, transcendentals=0),
        compiler_params=pltpu.CompilerParams(vmem_limit_bytes=limit * 2**20),
    )(place, *[value for value, _ in operands], *after)


def local(values):
    return [(value, pltpu.VMEM) for value in values]


def like(shape, dtype):
    return jax.ShapeDtypeStruct(shape, dtype)


def slot(place, r, width):
    return pl.ds(pl.multiple_of(lax.rem(place[0] + r, NX) * width, 128), width)


def conv_products(place, blocks, conv_weight, after):
    size, width = blocks[0].shape
    tall = NX * width

    def body(place, b0, b1, b2, b3, weight, low, mid, up, whole):
        for r, block in enumerate((b0, b1, b2, b3)):
            whole[:, slot(place, r, width)] = block[...]
        for k, ref in ((0, low), (2, up), (1, mid)):
            product = jnp.dot(whole[...], weight[0, k], preferred_element_type=F32)
            ref[...] = product.astype(ref.dtype)

    block = (size, width)
    return call(
        body,
        place,
        local(blocks + [conv_weight]),
        [like(block, BF), like(block, F32), like(block, BF), like((size, tall), BF)],
        after=after,
        flops=2 * size * tall * TAPS * width,
        moved=2 * tall * TAPS * width,
    )


def turned_blocks(place, whole, after):
    size, tall = whole.shape
    width = tall // NY

    def body(place, whole, *outs):
        for m, out in enumerate(outs):
            at = pl.multiple_of(lax.rem(place[1] + m, NY) * width, 128)
            out[...] = whole[:, pl.ds(at, width)].T

    return call(
        body,
        place,
        local([whole]),
        [like((width, size), BF)] * NY,
        after=after,
        flops=size * tall,
        moved=4 * size * tall,
    )


def stacked(place, values, after):
    shape = values[0].shape

    def body(place, *refs):
        for i in range(len(values)):
            refs[-1][i] = refs[i][...]

    return call(
        body,
        place,
        local(values),
        [like((len(values),) + shape, BF)],
        after=after,
        moved=4 * len(values) * values[0].size,
    )[0]


def token(value):
    return value[(0,) * (value.ndim - 2) + (slice(8), slice(128))]


def track_head(place, blocks, head_weight, head_cot, after):
    size, width = blocks[0].shape
    tall, wide = head_weight.shape
    tile = 256
    groups = size // BLOCK

    def body(place, b0, b1, b2, b3, weight, cot, out, sums, o0, o1, o2, o3, whole, term):
        for r, block in enumerate((b0, b1, b2, b3)):
            whole[:, slot(place, r, width)] = block[...]
        for j in range(wide // tile):
            cols = slice(j * tile, (j + 1) * tile)
            logits = jnp.dot(whole[...], weight[:, cols], preferred_element_type=F32)
            decay = jnp.exp(-jnp.abs(logits))
            above = 1.0 + decay
            log = jnp.where(decay < 1e-3, decay - 0.5 * decay * decay, jnp.log(above))
            track = (jnp.maximum(logits, 0.0) + log).astype(BF)
            out[:, cols] = track
            sums[:, cols] = jnp.sum(track.astype(F32).reshape(groups, BLOCK, tile), axis=1)
            part = pl.reciprocal(above, approx=True)
            part = part * (2.0 - above * part)
            sigmoid = jnp.where(logits >= 0.0, part, decay * part)
            term[:, cols] = (cot[:, cols].astype(F32) * sigmoid).astype(BF)
        for r, ref in ((2, o2), (1, o1), (3, o3), (0, o0)):
            ref[...] = times_t(term[...], weight[slot(place, r, width), :]).astype(ref.dtype)

    block = (size, width)
    return call(
        body,
        place,
        local(blocks + [head_weight, head_cot]),
        [like((size, wide), BF), like((groups, wide), F32), like(block, F32)] + [like(block, BF)] * 3,
        scratch=[pltpu.VMEM((size, tall), BF), pltpu.VMEM((size, wide), BF)],
        after=after,
        flops=4 * size * tall * wide,
        moved=2 * tall * wide,
    )


EXTRA = 16


def add_up(place, own, came, sums, after):
    size, width = own.shape
    groups, wide = sums.shape

    def body(place, own, c1, c2, c3, sums, total, low, long, below):
        value = own[...] + c1[...].astype(F32) + c2[...].astype(F32) + c3[...].astype(F32)
        total[...] = value
        low[...] = value.astype(BF)
        long[:size, :] = value.astype(BF)
        below[...] = jnp.zeros((EXTRA, width), F32)
        for i in range(TAPS):
            cols = min(width, wide - i * width)
            below[i * groups : (i + 1) * groups, :cols] = sums[:, i * width : i * width + cols]
        long[size:, :] = below[...].astype(BF)

    return call(
        body,
        place,
        local([own] + came + [sums]),
        [like((size, width), F32), like((size, width), BF), like((size + EXTRA, width), BF)],
        scratch=[pltpu.VMEM((EXTRA, width), F32)],
        after=after,
        flops=4 * own.size,
        moved=16 * own.size,
    )


def back_products(place, around, conv_weight, after):
    size, width = around[0].shape
    tall = NX * width
    cols = TAPS * width

    def body(place, d0, d1, d2, weight, o0, o1, o2, o3):
        for r, ref in ((2, o2), (1, o1), (3, o3), (0, o0)):
            at = slot(place, r, width)
            total = times_t(d0[...], weight[0, 0, at, :])
            total += times_t(d1[...], weight[0, 1, at, :])
            total += times_t(d2[...], weight[0, 2, at, :])
            ref[...] = total.astype(ref.dtype)

    block = (size, width)
    return call(
        body,
        place,
        local(around + [conv_weight]),
        [like(block, F32)] + [like(block, BF)] * 3,
        after=after,
        flops=2 * size * tall * cols,
        moved=2 * tall * cols,
    )


def kernel_terms(place, earlier, own, later, cots, after):
    _, width, size = own.shape
    half = width // 2
    cols = TAPS * width

    def body(place, earlier, own, later, d0, d1, d2, d3, kept, sent):
        y, z, core = place[1], place[2], place[3]
        first, last = z == 0, z == NZ - 1
        for k, left in enumerate((earlier, own, later)):
            total = jnp.zeros((width, width), F32)
            for m, right in enumerate((d0, d1, d2, d3)):
                if k == 0:
                    index = jnp.where(first, (m + 1) % NY, m)
                    valid = jnp.logical_not(jnp.logical_and(first, y == m))
                elif k == 2:
                    index = jnp.where(last, (m + NY - 1) % NY, m)
                    valid = jnp.logical_not(jnp.logical_and(last, y == (m + NY - 1) % NY))
                else:
                    index, valid = m, None
                product = jnp.dot(left[index], right[:size, :], preferred_element_type=F32)
                total += product if valid is None else jnp.where(valid, product, 0.0)
            pairs = total.reshape(half // GROUP, 2, GROUP, width)
            one, two = (pairs[:, i].reshape(half, width) for i in range(2))
            at = slice(k * width, (k + 1) * width)
            kept[:, at] = jnp.where(core == 0, one, two)
            sent[:, at] = jnp.where(core == 0, two, one).astype(BF)

    return call(
        body,
        place,
        local([earlier, own, later] + cots),
        [like((half, cols), F32), like((half, cols), BF)],
        after=after,
        flops=2 * size * NY * width * cols,
        moved=8 * NY * width * size,
    )


def over_z(place, kept, came, cover, after):
    rows, cols = kept.shape

    def body(place, kept, came, cover, *refs):
        outs, total, message = refs[:NZ], refs[NZ], refs[NZ + 1]
        total[...] = kept[...] + came[...].astype(F32)
        message[:EXTRA, :] = cover[...].astype(F32)
        for m, ref in enumerate(outs):
            at = pl.multiple_of(lax.rem(place[2] + m, NZ) * GROUP, 8)
            if m == 0:
                ref[...] = total[pl.ds(at, GROUP), :]
            else:
                message[EXTRA:, :] = total[pl.ds(at, GROUP), :]
                ref[...] = message[...].astype(BF)

    return call(
        body,
        place,
        local([kept, came, cover]),
        [like((GROUP, cols), F32)] + [like((EXTRA + GROUP, cols), BF)] * (NZ - 1),
        scratch=[pltpu.VMEM((rows, cols), F32), pltpu.VMEM((EXTRA + GROUP, cols), F32)],
        after=after,
        flops=4 * rows * cols,
        moved=6 * rows * cols,
    )


def coverage_of(blocks, place, exon_blocks, own):
    _, y, z, core = (place[i] for i in range(4))
    flip, dz, dy, part = jnp.meshgrid(
        *(jnp.arange(n, dtype=jnp.int32) for n in (2, NZ, NY, own)), indexing="ij"
    )
    labels = seq_index((y + NY - dy) % NY, (z + NZ - dz) % NZ, core ^ flip) * own + part
    labels = labels.reshape(-1)
    counts = (exon_blocks[:, :, None] == labels[None, None]).astype(F32).sum(axis=1)
    total = jnp.dot(
        counts.astype(BF), blocks.reshape(labels.shape[0], -1), preferred_element_type=F32
    )
    return total / jnp.sqrt(F32(EXONS * BLOCK))


def shards(inputs, conv_weight, head_weight, head_cot, exon_blocks):
    size, width = inputs.shape
    wide = head_cot.shape[1]
    own = size // BLOCK
    x = lax.axis_index("chan")
    s = lax.axis_index("seq")
    core, z, y = s % 2, (s // 2) % NZ, s // (2 * NZ)
    place = jnp.stack([x, y, z, core]).astype(jnp.int32)
    steps = 2

    state = inputs.astype(F32)
    acted = from_all_x(jax.nn.gelu(state).astype(BF))
    low, mid, up, whole = conv_products(place, acted, conv_weight, ())
    low, up = shifted(low, steps), shifted(up, -steps)
    after_conv = (state + (mid + low.astype(F32) + up.astype(F32))).astype(BF)
    full = from_all_x(after_conv)
    turned = turned_blocks(place, whole, (token(after_conv),))
    turned = [turned[0]] + [along_seq(turned[m], m, 0, 0) for m in range(1, NY)]
    turned = stacked(place, turned, tuple(token(value) for value in full[1:]))
    before = along_seq(turned, 0, 1, 0)
    behind = along_seq(turned, 0, NZ - 1, 0)

    tracks, sums, *blocks = track_head(place, full, head_weight, head_cot, (token(turned),))
    came = [along_x(blocks[r], r) for r in range(1, NX)]
    grad, low, long = add_up(place, blocks[0], came, sums, (token(before), token(behind)))
    cots = [long] + [along_seq(long, m, 0, 0) for m in range(1, NY)]
    around = [shifted(low, -steps), low, shifted(low, steps)]
    blocks = back_products(place, around, conv_weight, ())
    came = [along_x(blocks[r], r) for r in range(1, NX)]
    kept, sent = kernel_terms(place, before, turned, behind, cots, (token(blocks[1]),))
    cover = [
        cot[size : size + TAPS * own].reshape(TAPS, own, width).transpose(1, 0, 2).reshape(own, -1)
        for cot in cots
    ]
    cover = jnp.concatenate(cover, axis=0)
    kept, *parts = over_z(place, kept, along_seq(sent, 0, 0, 1), cover, ())
    parts = [along_seq(part, 0, m + 1, 0) for m, part in enumerate(parts)]
    for part in parts:
        kept = kept + part[EXTRA:].astype(F32)
    kernel_gradient = kept.reshape(GROUP, TAPS, width).transpose(1, 0, 2)[None]

    cover = jnp.stack([cover] + [part[:EXTRA] for part in parts])[:, :, :wide]
    cover = jnp.stack([cover, along_seq(cover, 0, 0, 1)])
    coverage = coverage_of(cover, place, exon_blocks, own)
    back_u = blocks[0] + came[0].astype(F32) + came[1].astype(F32) + came[2].astype(F32)
    out = (grad + activation_slope(state, back_u)).astype(BF)
    return (tracks, coverage, out, kernel_gradient)


def solution(mesh):
    return jax.shard_map(
        shards,
        mesh=mesh,
        in_specs=(
            P("seq", "chan"),
            P(None, None, None, "chan"),
            P(None, "chan"),
            P("seq", "chan"),
            P("seq", None),
        ),
        out_specs=(
            P("seq", "chan"),
            P("seq", "chan"),
            P("seq", "chan"),
            P(None, None, "seq", "chan"),
        ),
        check_vma=False,
    )
```

time: 233 us -> 193 us (0.83)
  blocking collectives: 42 us -> 0 us
  starting transfers between devices: 41.7 us -> 60 us
  Pallas kernels: 40.9 us -> 23.4 us
  local copies, waits for them, and re-layouts: 7.22 us -> 22.7 us
  waiting for transfers between devices: 91.7 us -> 79.8 us
    all_gather x2 -> x0, blocking collectives: 42 us -> none  [the longest x1 22.4 us: shards(): lax.all_gather(sums, 'seq', axis=0, tiled=True, axis_index_groups=other_g...]
    ppermute x12, waiting for transfers between devices: 52.6 us -> 29 us  [along_x(): lax.ppermute(value, 'chan', [(i, (i + steps) % NX) for i in range(NX)])]
    pallas_call x8, Pallas kernels: 40.9 us -> 23.4 us  [call(): pl.pallas_call(kernel, in_specs=[pl.BlockSpec(memory_space=pltpu.SMEM)] +...]
    ppermute x16 -> x17, starting transfers between devices: 18.2 us -> 33.3 us  [along_seq(): return lax.ppermute(value, 'seq', pairs)]
    ppermute x4, waiting for transfers between devices: 3.09 us -> 10.8 us  [shifted(): lax.ppermute(value, 'seq', [(s, s + steps) for s in range(leading, last)])]
    unnamed x59 -> x37, local copies, waits for them, and re-layouts: 6.64 us -> 11.3 us
    slice x0 -> x9, local copies, waits for them, and re-layouts: none -> 4.64 us  [the longest x4 4.63 us: shards(): cot[size:size + TAPS * own].reshape(TAPS, own, width).transpose(1, 0, 2)]
    reshape x1 -> x4, local copies, waits for them, and re-layouts: 0.01 us -> 4.56 us  [shards(): cot[size:size + TAPS * own].reshape(TAPS, own, width).transpose(1, 0, 2)]
  transfers between devices with their start and end apart: 32 -> 33, of which waited for: 15 -> 16; matrix products, arithmetic and copies ran while one was open for 3% -> 8% of each run, Pallas kernels for 8% -> 9%
where the time goes in v2:
time: 193 us; the launch traced here: 192 us
  waiting for transfers between devices  79.8 us (41%)
  starting transfers between devices  60 us (31%)
  Pallas kernels  23.4 us (12%)
  local copies, waits for them, and re-layouts  22.7 us (12%)
  other arithmetic  4.55 us (2%)
    ppermute x17, waiting for transfers between devices, along_seq(): return lax.ppermute(value, 'seq', pairs)  39.9 us
    ppermute x17, starting transfers between devices, along_seq(): return lax.ppermute(value, 'seq', pairs)  33.3 us
    ppermute x12, waiting for transfers between devices, along_x(): lax.ppermute(value, 'chan', [(i, (i + steps) % NX) for i in range(NX)])  29 us
    pallas_call x8, Pallas kernels, call(): pl.pallas_call(kernel, in_specs=[pl.BlockSpec(memory_space=pltpu.SMEM)] +...  23.4 us
    ppermute x12, starting transfers between devices, along_x(): lax.ppermute(value, 'chan', [(i, (i + steps) % NX) for i in range(NX)])  15.8 us
    unnamed x37, local copies, waits for them, and re-layouts  11.3 us
    ppermute x4, starting transfers between devices, shifted(): lax.ppermute(value, 'seq', [(s, s + steps) for s in range(leading, last)])  10.9 us
    ppermute x4, waiting for transfers between devices, shifted(): lax.ppermute(value, 'seq', [(s, s + steps) for s in range(leading, last)])  10.8 us
  transfers between devices with their start and end apart: 33, of which 16 were waited for; matrix products, arithmetic and copies ran while one was open for 8% of the time, Pallas kernels for 9%

profile of v2, /device:TPU:1, one launch (start us, length us, event | category | flops | bytes accessed | tf_op | source)
XLA Modules:
  0.0 192.1 jit_solution(8225618870622633320)
XLA Ops:
  0.6 1.3 fusion.8.refs_1_
  1.9 3.4 %collective-permute-start = (bf16[512,384]{1,0:T(8,128)(2,1)S(1)}, bf16[512,384]{1,0:T(8,128)(2,1)S(1)}, u32[]{:S(2)}, u32[]{:S(2)}) collective-permute-start(bf16[512,384]{1,0:T(8,128)(2,1)S(1)} %fusion.8.refs_1_), channel_id=1, source_target_pairs={{0,3},{1,0},{2,1},{3,2},{4,7},{5,4},{6,5},{7,6},{8,11},{9,8},{10,9... | collective-permute-start | bytes 1179656 | tf_op jit(solution)/shard_map/ppermute | solution.py:33
  6.5 9.6 %collective-permute-done.refs_2_ = bf16[512,384]{1,0:T(8,128)(2,1)S(1)} collective-permute-done((bf16[512,384]{1,0:T(8,128)(2,1)S(1)}, bf16[512,384]{1,0:T(8,128)(2,1)S(1)}, u32[]{:S(2)}, u32[]{:S(2)}) %collective-permute-start) | collective-permute-done | bytes 393248 | tf_op jit(solution)/shard_map/ppermute | solution.py:33
  16.5 9.8 %collective-permute-done.2.refs_4_ = bf16[512,384]{1,0:T(8,128)(2,1)S(1)} collective-permute-done((bf16[512,384]{1,0:T(8,128)(2,1)S(1)}, bf16[512,384]{1,0:T(8,128)(2,1)S(1)}, u32[]{:S(2)}, u32[]{:S(2)}) %collective-permute-start.2) | collective-permute-done | bytes 393248 | tf_op jit(solution)/shard_map/ppermute | solution.py:33
  26.3 2.0 %copy-done = bf16[1,3,1536,384]{3,2,1,0:T(8,128)(2,1)S(1)} copy-done((bf16[1,3,1536,384]{3,2,1,0:T(8,128)(2,1)S(1)}, bf16[1,3,1536,384]{3,2,1,0:T(8,128)(2,1)}, u32[]{:S(2)}) %copy-start) | copy-done | bytes 3538968
  28.3 3.2 %shard_map.84 = (bf16[512,384]{1,0:T(8,128)(2,1)S(1)}, f32[512,384]{1,0:T(8,128)S(1)}, bf16[512,384]{1,0:T(8,128)(2,1)S(1)}, bf16[512,1536]{1,0:T(8,128)(2,1)S(1)}) custom-call(s32[4]{0:T(128)S(1)} %pad_add_fusion.refs_0_, bf16[512,384]{1,0:T(8,128)(2,1)S(1)} %fusion.8.refs_1_, bf16[512,384]{1,0:T(8,128)(2,1)S(1)} %collective-permute-done.refs_2_, ...), custom_call_target="tpu_custom_call" | custom-call | flops 1811939328 | bytes 3538944 | tf_op jit(solution)/shard_map/pallas_call | solution.py:64
  31.5 3.6 %collective-permute-start.3 = (bf16[512,384]{1,0:T(8,128)(2,1)S(1)}, bf16[512,384]{1,0:T(8,128)(2,1)S(1)}, u32[]{:S(2)}, u32[]{:S(2)}) collective-permute-start(bf16[512,384]{1,0:T(8,128)(2,1)S(1)} %get-tuple-element.36), channel_id=1, source_target_pairs={{0,8},{4,12},{8,16},{12,20},{16,24},{20,28},{24,32},{28,36},{32,40... | collective-permute-start | bytes 1179656 | tf_op jit(solution)/shard_map/ppermute | solution.py:29
  35.1 1.3 collective-permute-start.4
  36.4 6.6 %collective-permute-done.3 = bf16[512,384]{1,0:T(8,128)(2,1)S(1)} collective-permute-done((bf16[512,384]{1,0:T(8,128)(2,1)S(1)}, bf16[512,384]{1,0:T(8,128)(2,1)S(1)}, u32[]{:S(2)}, u32[]{:S(2)}) %collective-permute-start.3) | collective-permute-done | bytes 393248 | tf_op jit(solution)/shard_map/ppermute | solution.py:29
  43.0 4.2 %collective-permute-done.4 = bf16[512,384]{1,0:T(8,128)(2,1)S(1)} collective-permute-done((bf16[512,384]{1,0:T(8,128)(2,1)S(1)}, bf16[512,384]{1,0:T(8,128)(2,1)S(1)}, u32[]{:S(2)}, u32[]{:S(2)}) %collective-permute-start.4) | collective-permute-done | bytes 393248 | tf_op jit(solution)/shard_map/ppermute | solution.py:29
  48.1 0.8 collective-permute-start.7
  48.9 1.0 shard_map.85
  49.9 4.7 %collective-permute-start.10 = (bf16[384,512]{1,0:T(8,128)(2,1)S(1)}, bf16[384,512]{1,0:T(8,128)(2,1)S(1)}, u32[]{:S(2)}, u32[]{:S(2)}) collective-permute-start(bf16[384,512]{1,0:T(8,128)(2,1)S(1)} %get-tuple-element.42), channel_id=1, source_target_pairs={{0,192},{4,196},{8,200},{12,204},{16,208},{20,212},{24,216},{28,22... | collective-permute-start | bytes 1179656 | tf_op jit(solution)/shard_map/ppermute | solution.py:46
  54.6 2.0 %collective-permute-done.5.refs_2_ = bf16[512,384]{1,0:T(8,128)(2,1)S(1)} collective-permute-done((bf16[512,384]{1,0:T(8,128)(2,1)S(1)}, bf16[512,384]{1,0:T(8,128)(2,1)S(1)}, u32[]{:S(2)}, u32[]{:S(2)}) %collective-permute-start.5) | collective-permute-done | bytes 393248 | tf_op jit(solution)/shard_map/ppermute | solution.py:33
  56.6 4.7 %collective-permute-start.9 = (bf16[384,512]{1,0:T(8,128)(2,1)S(1)}, bf16[384,512]{1,0:T(8,128)(2,1)S(1)}, u32[]{:S(2)}, u32[]{:S(2)}) collective-permute-start(bf16[384,512]{1,0:T(8,128)(2,1)S(1)} %get-tuple-element.41), channel_id=1, source_target_pairs={{0,128},{4,132},{8,136},{12,140},{16,144},{20,148},{24,152},{28,15... | collective-permute-start | bytes 1179656 | tf_op jit(solution)/shard_map/ppermute | solution.py:46
  61.2 7.3 %collective-permute-done.7.refs_4_ = bf16[512,384]{1,0:T(8,128)(2,1)S(1)} collective-permute-done((bf16[512,384]{1,0:T(8,128)(2,1)S(1)}, bf16[512,384]{1,0:T(8,128)(2,1)S(1)}, u32[]{:S(2)}, u32[]{:S(2)}) %collective-permute-start.7) | collective-permute-done | bytes 393248 | tf_op jit(solution)/shard_map/ppermute | solution.py:33
  68.5 2.7 %collective-permute-done.9.refs_3_ = bf16[384,512]{1,0:T(8,128)(2,1)S(1)} collective-permute-done((bf16[384,512]{1,0:T(8,128)(2,1)S(1)}, bf16[384,512]{1,0:T(8,128)(2,1)S(1)}, u32[]{:S(2)}, u32[]{:S(2)}) %collective-permute-start.9) | collective-permute-done | bytes 393248 | tf_op jit(solution)/shard_map/ppermute | solution.py:46
  71.9 4.4 %collective-permute-start.15 = (bf16[4,384,512]{2,1,0:T(8,128)(2,1)S(1)}, bf16[4,384,512]{2,1,0:T(8,128)(2,1)}, u32[]{:S(2)}, u32[]{:S(2)}) collective-permute-start(bf16[4,384,512]{2,1,0:T(8,128)(2,1)S(1)} %shard_map.86.refs_2_), channel_id=1, source_target_pairs={{0,56},{4,60},{8,0},{12,4},{16,8},{20,12},{24,16},{28,20},{32,24},... | collective-permute-start | bytes 4718600 | tf_op jit(solution)/shard_map/ppermute | solution.py:46
  76.3 1.9 copy-done.2
  78.2 1.2 copy-done.3
  79.4 6.6 %shard_map.87 = (bf16[512,1024]{1,0:T(8,128)(2,1)}, f32[4,1024]{1,0:T(4,128)S(1)}, f32[512,384]{1,0:T(8,128)S(1)}, bf16[512,384]{1,0:T(8,128)(2,1)S(1)}, bf16[51...) custom-call(s32[4]{0:T(128)S(1)} %pad_add_fusion.refs_0_, bf16[512,384]{1,0:T(8,128)(2,1)S(1)} %fusion.9.refs_1_, ...), custom_call_target="tpu_custom_call" | custom-call | flops 3221225472 | bytes 3145728 | tf_op jit(solution)/shard_map/pallas_call | solution.py:64
  86.1 1.5 collective-permute-start.11
  87.6 2.3 %collective-permute-start.12 = (bf16[512,384]{1,0:T(8,128)(2,1)S(1)}, bf16[512,384]{1,0:T(8,128)(2,1)S(1)}, u32[]{:S(2)}, u32[]{:S(2)}) collective-permute-start(bf16[512,384]{1,0:T(8,128)(2,1)S(1)} %get-tuple-element.46), channel_id=1, source_target_pairs={{0,2},{1,3},{2,0},{3,1},{4,6},{5,7},{6,4},{7,5},{8,10},{9,11},{10,... | collective-permute-start | bytes 1179656 | tf_op jit(solution)/shard_map/ppermute | solution.py:33
  89.8 1.8 collective-permute-start.13
  91.6 15.1 %collective-permute-done.15.refs_3_ = bf16[4,384,512]{2,1,0:T(8,128)(2,1)} collective-permute-done((bf16[4,384,512]{2,1,0:T(8,128)(2,1)S(1)}, bf16[4,384,512]{2,1,0:T(8,128)(2,1)}, u32[]{:S(2)}, u32[]{:S(2)}) %collective-permute-start.15) | collective-permute-done | bytes 1572896 | tf_op jit(solution)/shard_map/ppermute | solution.py:46
  106.7 0.7 slice_bitcast_fusion.7.refs_7_
  107.4 2.6 %collective-permute-done.14.refs_1_ = bf16[4,384,512]{2,1,0:T(8,128)(2,1)} collective-permute-done((bf16[4,384,512]{2,1,0:T(8,128)(2,1)S(1)}, bf16[4,384,512]{2,1,0:T(8,128)(2,1)}, u32[]{:S(2)}, u32[]{:S(2)}) %collective-permute-start.14) | collective-permute-done | bytes 1572896 | tf_op jit(solution)/shard_map/ppermute | solution.py:46
  109.9 0.7 slice_bitcast_fusion.8.refs_6_
  110.6 1.7 shard_map.88
  112.3 1.3 collective-permute-start.19
  113.6 4.7 %collective-permute-start.20 = (bf16[512,384]{1,0:T(8,128)(2,1)S(1)}, bf16[512,384]{1,0:T(8,128)(2,1)}, u32[]{:S(2)}, u32[]{:S(2)}) collective-permute-start(bf16[512,384]{1,0:T(8,128)(2,1)S(1)} %get-tuple-element.50.refs_2_), channel_id=1, source_target_pairs={{0,8},{4,12},{8,16},{12,20},{16,24},{20,28},{24,32},{28,36},{32,40... | collective-permute-start | bytes 1179656 | tf_op jit(solution)/shard_map/ppermute | solution.py:29
  118.3 0.8 copy-done.4
  120.3 3.1 %collective-permute-start.17 = (bf16[528,384]{1,0:T(8,128)(2,1)}, bf16[528,384]{1,0:T(8,128)(2,1)}, u32[]{:S(2)}, u32[]{:S(2)}) collective-permute-start(bf16[528,384]{1,0:T(8,128)(2,1)} %get-tuple-element.49.refs_4_), channel_id=1, source_target_pairs={{0,128},{4,132},{8,136},{12,140},{16,144},{20,148},{24,152},{28,15... | collective-permute-start | bytes 1216520 | tf_op jit(solution)/shard_map/ppermute | solution.py:46
  123.4 1.4 collective-permute-start.18
  124.9 0.7 slice.88
  126.2 0.7 copy-done.6
  127.0 2.0 %copy-done.1 = bf16[1,3,1536,384]{3,2,1,0:T(8,128)(2,1)S(1)} copy-done((bf16[1,3,1536,384]{3,2,1,0:T(8,128)(2,1)S(1)}, bf16[1,3,1536,384]{3,2,1,0:T(8,128)(2,1)}, u32[]{:S(2)}) %copy-start.1) | copy-done | bytes 3538968
  129.0 1.0 copy-done.5
  130.0 1.0 copy-done.7
  131.0 4.5 %shard_map.89 = (f32[512,384]{1,0:T(8,128)S(1)}, bf16[512,384]{1,0:T(8,128)(2,1)S(1)}, bf16[512,384]{1,0:T(8,128)(2,1)}, bf16[512,384]{1,0:T(8,128)(2,1)}) custom-call(s32[4]{0:T(128)S(1)} %pad_add_fusion.refs_0_, bf16[512,384]{1,0:T(8,128)(2,1)S(1)} %copy-done.7, bf16[512,384]{1,0:T(8,128)(2,1)S(1)} %copy-done.5, ...), custom_call_target="tpu_custom_call" | custom-call | flops 1811939328 | bytes 3538944 | tf_op jit(solution)/shard_map/pallas_call | solution.py:64
  135.5 2.1 %collective-permute-start.31 = (bf16[512,384]{1,0:T(8,128)(2,1)}, bf16[512,384]{1,0:T(8,128)(2,1)}, u32[]{:S(2)}, u32[]{:S(2)}) collective-permute-start(bf16[512,384]{1,0:T(8,128)(2,1)} %get-tuple-element.63), channel_id=1, source_target_pairs={{0,2},{1,3},{2,0},{3,1},{4,6},{5,7},{6,4},{7,5},{8,10},{9,11},{10,... | collective-permute-start | bytes 1179656 | tf_op jit(solution)/shard_map/ppermute | solution.py:33
  137.6 2.1 %collective-permute-start.32 = (bf16[512,384]{1,0:T(8,128)(2,1)}, bf16[512,384]{1,0:T(8,128)(2,1)}, u32[]{:S(2)}, u32[]{:S(2)}) collective-permute-start(bf16[512,384]{1,0:T(8,128)(2,1)} %get-tuple-element.64), channel_id=1, source_target_pairs={{0,3},{1,0},{2,1},{3,2},{4,7},{5,4},{6,5},{7,6},{8,11},{9,8},{10,9... | collective-permute-start | bytes 1179656 | tf_op jit(solution)/shard_map/ppermute | solution.py:33
  139.7 1.3 slice.115
  141.0 1.3 reshape.105
  142.3 7.9 %collective-permute-done.17.refs_6_ = bf16[528,384]{1,0:T(8,128)(2,1)} collective-permute-done((bf16[528,384]{1,0:T(8,128)(2,1)}, bf16[528,384]{1,0:T(8,128)(2,1)}, u32[]{:S(2)}, u32[]{:S(2)}) %collective-permute-start.17) | collective-permute-done | bytes 405536 | tf_op jit(solution)/shard_map/ppermute | solution.py:46
  150.3 1.3 slice.116
  151.6 1.3 reshape.107
  152.9 1.3 slice.117
  154.2 1.3 reshape.109
  155.5 5.0 %shard_map.90 = (f32[192,1152]{1,0:T(8,128)S(1)}, bf16[192,1152]{1,0:T(8,128)(2,1)S(1)}) custom-call(s32[4]{0:T(128)S(1)} %pad_add_fusion.refs_0_, bf16[4,384,512]{2,1,0:T(8,128)(2,1)} %collective-permute-done.14.refs_1_, bf16[4,384,512]{2,1,0:T(8,128)(2,1)S(1)} %shard_map.86.refs_2_, bf16[4,384,512]{2,1,0:T(8,128)(2,1)} %collective-permute-done.15.refs_3_, ...), custom_call_target="tpu_custom_call" | custom-call | flops 1811939328 | bytes 6291456 | tf_op jit(solution)/shard_map/pallas_call | solution.py:64
  160.6 1.0 collective-permute-start.21
  161.6 1.3 collective-permute-done.21.refs_2_
  162.9 0.7 shard_map.91
  163.8 2.7 %fusion.4 = bf16[512,384]{1,0:T(8,128)(2,1)} fusion(f32[512,384]{1,0:T(8,128)S(1)} %get-tuple-element.61, bf16[512,384]{1,0:T(8,128)(2,1)S(1)} %copy-done.9, bf16[512,384]{1,0:T(8,128)(2,1)} %collective-permute-done.32, bf16[512,384]{1,0:T(8,128)(2,1)} %collective-permute-done.31, f32[512,384]{1,0:T(8,128)S(1)} %get-tuple-element.62, ...), kind=kLoop, calls=%fused_computation.11 | loop fusion | flops 5505024 | bytes 3538944 | tf_op jit(solution)/shard_map/convert_element_type | solution.py:370
  166.6 5.6 %collective-permute-start.25 = (bf16[40,1152]{1,0:T(8,128)(2,1)S(1)}, bf16[40,1152]{1,0:T(8,128)(2,1)S(1)}, u32[]{:S(2)}, u32[]{:S(2)}) collective-permute-start(bf16[40,1152]{1,0:T(8,128)(2,1)S(1)} %get-tuple-element.57), channel_id=1, source_target_pairs={{0,32},{4,36},{8,40},{12,44},{16,48},{20,52},{24,56},{28,60},{32,0... | collective-permute-start | bytes 276488 | tf_op jit(solution)/shard_map/ppermute | solution.py:46
  172.1 0.9 collective-permute-start.26
  173.0 2.7 %collective-permute-start.27 = (bf16[40,1152]{1,0:T(8,128)(2,1)S(1)}, bf16[40,1152]{1,0:T(8,128)(2,1)S(1)}, u32[]{:S(2)}, u32[]{:S(2)}) collective-permute-start(bf16[40,1152]{1,0:T(8,128)(2,1)S(1)} %get-tuple-element.59), channel_id=1, source_target_pairs={{0,48},{4,52},{8,56},{12,60},{16,0},{20,4},{24,8},{28,12},{32,16},... | collective-permute-start | bytes 276488 | tf_op jit(solution)/shard_map/ppermute | solution.py:46
  175.7 3.6 %collective-permute-start.28 = (bf16[40,1152]{1,0:T(8,128)(2,1)S(1)}, bf16[40,1152]{1,0:T(8,128)(2,1)S(1)}, u32[]{:S(2)}, u32[]{:S(2)}) collective-permute-start(bf16[40,1152]{1,0:T(8,128)(2,1)S(1)} %get-tuple-element.60), channel_id=1, source_target_pairs={{0,56},{4,60},{8,0},{12,4},{16,8},{20,12},{24,16},{28,20},{32,24},... | collective-permute-start | bytes 276488 | tf_op jit(solution)/shard_map/ppermute | solution.py:46
  179.3 2.8 %collective-permute-done.24 = bf16[40,1152]{1,0:T(8,128)(2,1)S(1)} collective-permute-done((bf16[40,1152]{1,0:T(8,128)(2,1)S(1)}, bf16[40,1152]{1,0:T(8,128)(2,1)S(1)}, u32[]{:S(2)}, u32[]{:S(2)}) %collective-permute-start.24) | collective-permute-done | bytes 92192 | tf_op jit(solution)/shard_map/ppermute | solution.py:46
  182.2 4.4 %collective-permute-done.27 = bf16[40,1152]{1,0:T(8,128)(2,1)S(1)} collective-permute-done((bf16[40,1152]{1,0:T(8,128)(2,1)S(1)}, bf16[40,1152]{1,0:T(8,128)(2,1)S(1)}, u32[]{:S(2)}, u32[]{:S(2)}) %collective-permute-start.27) | collective-permute-done | bytes 92192 | tf_op jit(solution)/shard_map/ppermute | solution.py:46
  186.6 2.7 %collective-permute-done.28 = bf16[40,1152]{1,0:T(8,128)(2,1)S(1)} collective-permute-done((bf16[40,1152]{1,0:T(8,128)(2,1)S(1)}, bf16[40,1152]{1,0:T(8,128)(2,1)S(1)}, u32[]{:S(2)}, u32[]{:S(2)}) %collective-permute-start.28) | collective-permute-done | bytes 92192 | tf_op jit(solution)/shard_map/ppermute | solution.py:46
  189.4 0.7 collective-permute-start.29
  190.2 0.7 copy.15
  191.3 0.8 convolution_multiply_fusion
  (88 shorter events, 6.0 us)
Async XLA Ops:
  1.9 14.2 %collective-permute-start = (bf16[512,384]{1,0:T(8,128)(2,1)S(1)}, bf16[512,384]{1,0:T(8,128)(2,1)S(1)}, u32[]{:S(2)}, u32[]{:S(2)}) collective-permute-start(bf16[512,384]{1,0:T(8,128)(2,1)S(1)} %fusion.8.refs_1_), channel_id=1, source_target_pairs={{0,3},{1,0},{2,1},{3,2},{4,7},{5,4},{6,5},{7,6},{8,11},{9,8},{10,9... | collective-permute-start | bytes 1179656 | tf_op jit(solution)/shard_map/ppermute | solution.py:33
  5.3 11.2 %collective-permute-start.1 = (bf16[512,384]{1,0:T(8,128)(2,1)S(1)}, bf16[512,384]{1,0:T(8,128)(2,1)S(1)}, u32[]{:S(2)}, u32[]{:S(2)}) collective-permute-start(bf16[512,384]{1,0:T(8,128)(2,1)S(1)} %fusion.8.refs_1_), channel_id=1, source_target_pairs={{0,2},{1,3},{2,0},{3,1},{4,6},{5,7},{6,4},{7,5},{8,10},{9,11},{10,... | collective-permute-start | bytes 1179656 | tf_op jit(solution)/shard_map/ppermute | solution.py:33
  5.8 20.4 %collective-permute-start.2 = (bf16[512,384]{1,0:T(8,128)(2,1)S(1)}, bf16[512,384]{1,0:T(8,128)(2,1)S(1)}, u32[]{:S(2)}, u32[]{:S(2)}) collective-permute-start(bf16[512,384]{1,0:T(8,128)(2,1)S(1)} %fusion.8.refs_1_), channel_id=1, source_target_pairs={{0,1},{1,2},{2,3},{3,0},{4,5},{5,6},{6,7},{7,4},{8,9},{9,10},{10,1... | collective-permute-start | bytes 1179656 | tf_op jit(solution)/shard_map/ppermute | solution.py:33
  26.3 2.0 %copy-start = (bf16[1,3,1536,384]{3,2,1,0:T(8,128)(2,1)S(1)}, bf16[1,3,1536,384]{3,2,1,0:T(8,128)(2,1)}, u32[]{:S(2)}) copy-start(bf16[1,3,1536,384]{3,2,1,0:T(8,128)(2,1)} %refs_4_.1) | copy-start | bytes 10616836
  28.3 18.9 %copy-start.8 = (bf16[512,384]{1,0:T(8,128)(2,1)S(1)}, bf16[512,384]{1,0:T(8,128)(2,1)}, u32[]{:S(2)}) copy-start(bf16[512,384]{1,0:T(8,128)(2,1)} %param.5) | copy-start | bytes 1179652
  31.5 11.5 %collective-permute-start.3 = (bf16[512,384]{1,0:T(8,128)(2,1)S(1)}, bf16[512,384]{1,0:T(8,128)(2,1)S(1)}, u32[]{:S(2)}, u32[]{:S(2)}) collective-permute-start(bf16[512,384]{1,0:T(8,128)(2,1)S(1)} %get-tuple-element.36), channel_id=1, source_target_pairs={{0,8},{4,12},{8,16},{12,20},{16,24},{20,28},{24,32},{28,36},{32,40... | collective-permute-start | bytes 1179656 | tf_op jit(solution)/shard_map/ppermute | solution.py:29
  35.1 12.1 %collective-permute-start.4 = (bf16[512,384]{1,0:T(8,128)(2,1)S(1)}, bf16[512,384]{1,0:T(8,128)(2,1)S(1)}, u32[]{:S(2)}, u32[]{:S(2)}) collective-permute-start(bf16[512,384]{1,0:T(8,128)(2,1)S(1)} %get-tuple-element.37), channel_id=1, source_target_pairs={{8,0},{12,4},{16,8},{20,12},{24,16},{28,20},{32,24},{36,28},{40,32... | collective-permute-start | bytes 1179656 | tf_op jit(solution)/shard_map/ppermute | solution.py:29
  47.3 9.2 %collective-permute-start.5 = (bf16[512,384]{1,0:T(8,128)(2,1)S(1)}, bf16[512,384]{1,0:T(8,128)(2,1)S(1)}, u32[]{:S(2)}, u32[]{:S(2)}) collective-permute-start(bf16[512,384]{1,0:T(8,128)(2,1)S(1)} %fusion.9.refs_1_), channel_id=1, source_target_pairs={{0,3},{1,0},{2,1},{3,2},{4,7},{5,4},{6,5},{7,6},{8,11},{9,8},{10,9... | collective-permute-start | bytes 1179656 | tf_op jit(solution)/shard_map/ppermute | solution.py:33
  47.4 13.8 %collective-permute-start.6 = (bf16[512,384]{1,0:T(8,128)(2,1)S(1)}, bf16[512,384]{1,0:T(8,128)(2,1)S(1)}, u32[]{:S(2)}, u32[]{:S(2)}) collective-permute-start(bf16[512,384]{1,0:T(8,128)(2,1)S(1)} %fusion.9.refs_1_), channel_id=1, source_target_pairs={{0,2},{1,3},{2,0},{3,1},{4,6},{5,7},{6,4},{7,5},{8,10},{9,11},{10,... | collective-permute-start | bytes 1179656 | tf_op jit(solution)/shard_map/ppermute | solution.py:33
  48.1 20.4 %collective-permute-start.7 = (bf16[512,384]{1,0:T(8,128)(2,1)S(1)}, bf16[512,384]{1,0:T(8,128)(2,1)S(1)}, u32[]{:S(2)}, u32[]{:S(2)}) collective-permute-start(bf16[512,384]{1,0:T(8,128)(2,1)S(1)} %fusion.9.refs_1_), channel_id=1, source_target_pairs={{0,1},{1,2},{2,3},{3,0},{4,5},{5,6},{6,7},{7,4},{8,9},{9,10},{10,1... | collective-permute-start | bytes 1179656 | tf_op jit(solution)/shard_map/ppermute | solution.py:33
  49.9 18.6 %collective-permute-start.10 = (bf16[384,512]{1,0:T(8,128)(2,1)S(1)}, bf16[384,512]{1,0:T(8,128)(2,1)S(1)}, u32[]{:S(2)}, u32[]{:S(2)}) collective-permute-start(bf16[384,512]{1,0:T(8,128)(2,1)S(1)} %get-tuple-element.42), channel_id=1, source_target_pairs={{0,192},{4,196},{8,200},{12,204},{16,208},{20,212},{24,216},{28,22... | collective-permute-start | bytes 1179656 | tf_op jit(solution)/shard_map/ppermute | solution.py:46
  54.6 13.9 %collective-permute-start.8 = (bf16[384,512]{1,0:T(8,128)(2,1)S(1)}, bf16[384,512]{1,0:T(8,128)(2,1)S(1)}, u32[]{:S(2)}, u32[]{:S(2)}) collective-permute-start(bf16[384,512]{1,0:T(8,128)(2,1)S(1)} %get-tuple-element.40), channel_id=1, source_target_pairs={{0,64},{4,68},{8,72},{12,76},{16,80},{20,84},{24,88},{28,92},{32,9... | collective-permute-start | bytes 1179656 | tf_op jit(solution)/shard_map/ppermute | solution.py:46
  56.6 14.7 %collective-permute-start.9 = (bf16[384,512]{1,0:T(8,128)(2,1)S(1)}, bf16[384,512]{1,0:T(8,128)(2,1)S(1)}, u32[]{:S(2)}, u32[]{:S(2)}) collective-permute-start(bf16[384,512]{1,0:T(8,128)(2,1)S(1)} %get-tuple-element.41), channel_id=1, source_target_pairs={{0,128},{4,132},{8,136},{12,140},{16,144},{20,148},{24,152},{28,15... | collective-permute-start | bytes 1179656 | tf_op jit(solution)/shard_map/ppermute | solution.py:46
  71.9 34.8 %collective-permute-start.15 = (bf16[4,384,512]{2,1,0:T(8,128)(2,1)S(1)}, bf16[4,384,512]{2,1,0:T(8,128)(2,1)}, u32[]{:S(2)}, u32[]{:S(2)}) collective-permute-start(bf16[4,384,512]{2,1,0:T(8,128)(2,1)S(1)} %shard_map.86.refs_2_), channel_id=1, source_target_pairs={{0,56},{4,60},{8,0},{12,4},{16,8},{20,12},{24,16},{28,20},{32,24},... | collective-permute-start | bytes 4718600 | tf_op jit(solution)/shard_map/ppermute | solution.py:46
  76.3 33.6 %collective-permute-start.14 = (bf16[4,384,512]{2,1,0:T(8,128)(2,1)S(1)}, bf16[4,384,512]{2,1,0:T(8,128)(2,1)}, u32[]{:S(2)}, u32[]{:S(2)}) collective-permute-start(bf16[4,384,512]{2,1,0:T(8,128)(2,1)S(1)} %shard_map.86.refs_2_), channel_id=1, source_target_pairs={{0,8},{4,12},{8,16},{12,20},{16,24},{20,28},{24,32},{28,36},{32,40... | collective-permute-start | bytes 4718600 | tf_op jit(solution)/shard_map/ppermute | solution.py:46
  76.3 1.9 copy-start.2
  78.2 1.2 copy-start.3
  86.1 38.7 %copy-start.14 = (s32[8,8]{1,0:T(8,128)S(1)}, s32[8,8]{1,0:T(8,128)}, u32[]{:S(2)}) copy-start(s32[8,8]{1,0:T(8,128)} %param.9) | copy-start | bytes 772
  86.1 24.5 %collective-permute-start.11 = (bf16[512,384]{1,0:T(8,128)(2,1)S(1)}, bf16[512,384]{1,0:T(8,128)(2,1)S(1)}, u32[]{:S(2)}, u32[]{:S(2)}) collective-permute-start(bf16[512,384]{1,0:T(8,128)(2,1)S(1)} %get-tuple-element.45), channel_id=1, source_target_pairs={{0,1},{1,2},{2,3},{3,0},{4,5},{5,6},{6,7},{7,4},{8,9},{9,10},{10,1... | collective-permute-start | bytes 1179656 | tf_op jit(solution)/shard_map/ppermute | solution.py:33
  87.6 23.1 %collective-permute-start.12 = (bf16[512,384]{1,0:T(8,128)(2,1)S(1)}, bf16[512,384]{1,0:T(8,128)(2,1)S(1)}, u32[]{:S(2)}, u32[]{:S(2)}) collective-permute-start(bf16[512,384]{1,0:T(8,128)(2,1)S(1)} %get-tuple-element.46), channel_id=1, source_target_pairs={{0,2},{1,3},{2,0},{3,1},{4,6},{5,7},{6,4},{7,5},{8,10},{9,11},{10,... | collective-permute-start | bytes 1179656 | tf_op jit(solution)/shard_map/ppermute | solution.py:33
  89.8 20.8 %collective-permute-start.13 = (bf16[512,384]{1,0:T(8,128)(2,1)S(1)}, bf16[512,384]{1,0:T(8,128)(2,1)S(1)}, u32[]{:S(2)}, u32[]{:S(2)}) collective-permute-start(bf16[512,384]{1,0:T(8,128)(2,1)S(1)} %get-tuple-element.47), channel_id=1, source_target_pairs={{0,3},{1,0},{2,1},{3,2},{4,7},{5,4},{6,5},{7,6},{8,11},{9,8},{10,9... | collective-permute-start | bytes 1179656 | tf_op jit(solution)/shard_map/ppermute | solution.py:33
  112.3 13.9 %collective-permute-start.19 = (bf16[512,384]{1,0:T(8,128)(2,1)S(1)}, bf16[512,384]{1,0:T(8,128)(2,1)S(1)}, u32[]{:S(2)}, u32[]{:S(2)}) collective-permute-start(bf16[512,384]{1,0:T(8,128)(2,1)S(1)} %get-tuple-element.50.refs_2_), channel_id=1, source_target_pairs={{8,0},{12,4},{16,8},{20,12},{24,16},{28,20},{32,24},{36,28},{40,32... | collective-permute-start | bytes 1179656 | tf_op jit(solution)/shard_map/ppermute | solution.py:29
  113.6 13.4 %collective-permute-start.20 = (bf16[512,384]{1,0:T(8,128)(2,1)S(1)}, bf16[512,384]{1,0:T(8,128)(2,1)}, u32[]{:S(2)}, u32[]{:S(2)}) collective-permute-start(bf16[512,384]{1,0:T(8,128)(2,1)S(1)} %get-tuple-element.50.refs_2_), channel_id=1, source_target_pairs={{0,8},{4,12},{8,16},{12,20},{16,24},{20,28},{24,32},{28,36},{32,40... | collective-permute-start | bytes 1179656 | tf_op jit(solution)/shard_map/ppermute | solution.py:29
  118.3 0.8 copy-start.4
  119.8 17.9 %collective-permute-start.16 = (bf16[528,384]{1,0:T(8,128)(2,1)}, bf16[528,384]{1,0:T(8,128)(2,1)}, u32[]{:S(2)}, u32[]{:S(2)}) collective-permute-start(bf16[528,384]{1,0:T(8,128)(2,1)} %get-tuple-element.49.refs_4_), channel_id=1, source_target_pairs={{0,64},{4,68},{8,72},{12,76},{16,80},{20,84},{24,88},{28,92},{32,9... | collective-permute-start | bytes 1216520 | tf_op jit(solution)/shard_map/ppermute | solution.py:46
  120.3 30.0 %collective-permute-start.17 = (bf16[528,384]{1,0:T(8,128)(2,1)}, bf16[528,384]{1,0:T(8,128)(2,1)}, u32[]{:S(2)}, u32[]{:S(2)}) collective-permute-start(bf16[528,384]{1,0:T(8,128)(2,1)} %get-tuple-element.49.refs_4_), channel_id=1, source_target_pairs={{0,128},{4,132},{8,136},{12,140},{16,144},{20,148},{24,152},{28,15... | collective-permute-start | bytes 1216520 | tf_op jit(solution)/shard_map/ppermute | solution.py:46
  123.4 29.5 %collective-permute-start.18 = (bf16[528,384]{1,0:T(8,128)(2,1)}, bf16[528,384]{1,0:T(8,128)(2,1)}, u32[]{:S(2)}, u32[]{:S(2)}) collective-permute-start(bf16[528,384]{1,0:T(8,128)(2,1)} %get-tuple-element.49.refs_4_), channel_id=1, source_target_pairs={{0,192},{4,196},{8,200},{12,204},{16,208},{20,212},{24,216},{28,22... | collective-permute-start | bytes 1216520 | tf_op jit(solution)/shard_map/ppermute | solution.py:46
  126.2 0.7 copy-start.6
  127.0 2.0 %copy-start.1 = (bf16[1,3,1536,384]{3,2,1,0:T(8,128)(2,1)S(1)}, bf16[1,3,1536,384]{3,2,1,0:T(8,128)(2,1)}, u32[]{:S(2)}) copy-start(bf16[1,3,1536,384]{3,2,1,0:T(8,128)(2,1)} %refs_4_.1) | copy-start | bytes 10616836
  129.0 1.0 copy-start.5
  130.0 1.0 copy-start.7
  135.5 28.2 %collective-permute-start.30 = (bf16[512,384]{1,0:T(8,128)(2,1)S(1)}, bf16[512,384]{1,0:T(8,128)(2,1)}, u32[]{:S(2)}, u32[]{:S(2)}) collective-permute-start(bf16[512,384]{1,0:T(8,128)(2,1)S(1)} %get-tuple-element.51), channel_id=1, source_target_pairs={{0,1},{1,2},{2,3},{3,0},{4,5},{5,6},{6,7},{7,4},{8,9},{9,10},{10,1... | collective-permute-start | bytes 1179656 | tf_op jit(solution)/shard_map/ppermute | solution.py:33
  135.5 28.2 %collective-permute-start.31 = (bf16[512,384]{1,0:T(8,128)(2,1)}, bf16[512,384]{1,0:T(8,128)(2,1)}, u32[]{:S(2)}, u32[]{:S(2)}) collective-permute-start(bf16[512,384]{1,0:T(8,128)(2,1)} %get-tuple-element.63), channel_id=1, source_target_pairs={{0,2},{1,3},{2,0},{3,1},{4,6},{5,7},{6,4},{7,5},{8,10},{9,11},{10,... | collective-permute-start | bytes 1179656 | tf_op jit(solution)/shard_map/ppermute | solution.py:33
  137.6 26.1 %collective-permute-start.32 = (bf16[512,384]{1,0:T(8,128)(2,1)}, bf16[512,384]{1,0:T(8,128)(2,1)}, u32[]{:S(2)}, u32[]{:S(2)}) collective-permute-start(bf16[512,384]{1,0:T(8,128)(2,1)} %get-tuple-element.64), channel_id=1, source_target_pairs={{0,3},{1,0},{2,1},{3,2},{4,7},{5,4},{6,5},{7,6},{8,11},{9,8},{10,9... | collective-permute-start | bytes 1179656 | tf_op jit(solution)/shard_map/ppermute | solution.py:33
  155.5 6.0 %copy-start.10 = (bf16[3,4,384]{2,1,0:T(4,128)(2,1)S(1)}, bf16[3,4,384]{2,1,0:T(4,128)(2,1)}, u32[]{:S(2)}) copy-start(bf16[3,4,384]{2,1,0:T(4,128)(2,1)} %reshape.103) | copy-start | bytes 27652
  155.5 6.0 %copy-start.11 = (bf16[3,4,384]{2,1,0:T(4,128)(2,1)S(1)}, bf16[3,4,384]{2,1,0:T(4,128)(2,1)}, u32[]{:S(2)}) copy-start(bf16[3,4,384]{2,1,0:T(4,128)(2,1)} %reshape.105) | copy-start | bytes 27652
  155.5 6.0 %copy-start.12 = (bf16[3,4,384]{2,1,0:T(4,128)(2,1)S(1)}, bf16[3,4,384]{2,1,0:T(4,128)(2,1)}, u32[]{:S(2)}) copy-start(bf16[3,4,384]{2,1,0:T(4,128)(2,1)} %reshape.107) | copy-start | bytes 27652
  155.5 6.0 %copy-start.13 = (bf16[3,4,384]{2,1,0:T(4,128)(2,1)S(1)}, bf16[3,4,384]{2,1,0:T(4,128)(2,1)}, u32[]{:S(2)}) copy-start(bf16[3,4,384]{2,1,0:T(4,128)(2,1)} %reshape.109) | copy-start | bytes 27652
  160.5 3.2 %copy-start.9 = (bf16[512,384]{1,0:T(8,128)(2,1)S(1)}, bf16[512,384]{1,0:T(8,128)(2,1)}, u32[]{:S(2)}) copy-start(bf16[512,384]{1,0:T(8,128)(2,1)} %param.5) | copy-start | bytes 1179652
  160.6 2.4 %collective-permute-start.21 = (bf16[192,1152]{1,0:T(8,128)(2,1)S(1)}, bf16[192,1152]{1,0:T(8,128)(2,1)S(1)}, u32[]{:S(2)}, u32[]{:S(2)}) collective-permute-start(bf16[192,1152]{1,0:T(8,128)(2,1)S(1)} %get-tuple-element.53), channel_id=1, source_target_pairs={{0,4},{4,0},{8,12},{12,8},{16,20},{20,16},{24,28},{28,24},{32,36},... | collective-permute-start | bytes 1327112 | tf_op jit(solution)/shard_map/ppermute | solution.py:46
  163.7 9.4 %collective-permute-start.22 = (bf16[40,1152]{1,0:T(8,128)(2,1)S(1)}, bf16[40,1152]{1,0:T(8,128)(2,1)S(1)}, u32[]{:S(2)}, u32[]{:S(2)}) collective-permute-start(bf16[40,1152]{1,0:T(8,128)(2,1)S(1)} %get-tuple-element.54), channel_id=1, source_target_pairs={{0,8},{4,12},{8,16},{12,20},{16,24},{20,28},{24,32},{28,36},{32,40... | collective-permute-start | bytes 276488 | tf_op jit(solution)/shard_map/ppermute | solution.py:46
  166.5 9.2 %collective-permute-start.23 = (bf16[40,1152]{1,0:T(8,128)(2,1)S(1)}, bf16[40,1152]{1,0:T(8,128)(2,1)S(1)}, u32[]{:S(2)}, u32[]{:S(2)}) collective-permute-start(bf16[40,1152]{1,0:T(8,128)(2,1)S(1)} %get-tuple-element.55), channel_id=1, source_target_pairs={{0,16},{4,20},{8,24},{12,28},{16,32},{20,36},{24,40},{28,44},{32,4... | collective-permute-start | bytes 276488 | tf_op jit(solution)/shard_map/ppermute | solution.py:46
  166.5 15.6 %collective-permute-start.24 = (bf16[40,1152]{1,0:T(8,128)(2,1)S(1)}, bf16[40,1152]{1,0:T(8,128)(2,1)S(1)}, u32[]{:S(2)}, u32[]{:S(2)}) collective-permute-start(bf16[40,1152]{1,0:T(8,128)(2,1)S(1)} %get-tuple-element.56), channel_id=1, source_target_pairs={{0,24},{4,28},{8,32},{12,36},{16,40},{20,44},{24,48},{28,52},{32,5... | collective-permute-start | bytes 276488 | tf_op jit(solution)/shard_map/ppermute | solution.py:46
  166.6 15.6 %collective-permute-start.25 = (bf16[40,1152]{1,0:T(8,128)(2,1)S(1)}, bf16[40,1152]{1,0:T(8,128)(2,1)S(1)}, u32[]{:S(2)}, u32[]{:S(2)}) collective-permute-start(bf16[40,1152]{1,0:T(8,128)(2,1)S(1)} %get-tuple-element.57), channel_id=1, source_target_pairs={{0,32},{4,36},{8,40},{12,44},{16,48},{20,52},{24,56},{28,60},{32,0... | collective-permute-start | bytes 276488 | tf_op jit(solution)/shard_map/ppermute | solution.py:46
  172.1 10.0 %collective-permute-start.26 = (bf16[40,1152]{1,0:T(8,128)(2,1)S(1)}, bf16[40,1152]{1,0:T(8,128)(2,1)S(1)}, u32[]{:S(2)}, u32[]{:S(2)}) collective-permute-start(bf16[40,1152]{1,0:T(8,128)(2,1)S(1)} %get-tuple-element.58), channel_id=1, source_target_pairs={{0,40},{4,44},{8,48},{12,52},{16,56},{20,60},{24,0},{28,4},{32,8},... | collective-permute-start | bytes 276488 | tf_op jit(solution)/shard_map/ppermute | solution.py:46
  173.0 13.5 %collective-permute-start.27 = (bf16[40,1152]{1,0:T(8,128)(2,1)S(1)}, bf16[40,1152]{1,0:T(8,128)(2,1)S(1)}, u32[]{:S(2)}, u32[]{:S(2)}) collective-permute-start(bf16[40,1152]{1,0:T(8,128)(2,1)S(1)} %get-tuple-element.59), channel_id=1, source_target_pairs={{0,48},{4,52},{8,56},{12,60},{16,0},{20,4},{24,8},{28,12},{32,16},... | collective-permute-start | bytes 276488 | tf_op jit(solution)/shard_map/ppermute | solution.py:46
  175.7 13.5 %collective-permute-start.28 = (bf16[40,1152]{1,0:T(8,128)(2,1)S(1)}, bf16[40,1152]{1,0:T(8,128)(2,1)S(1)}, u32[]{:S(2)}, u32[]{:S(2)}) collective-permute-start(bf16[40,1152]{1,0:T(8,128)(2,1)S(1)} %get-tuple-element.60), channel_id=1, source_target_pairs={{0,56},{4,60},{8,0},{12,4},{16,8},{20,12},{24,16},{28,20},{32,24},... | collective-permute-start | bytes 276488 | tf_op jit(solution)/shard_map/ppermute | solution.py:46
  189.4 1.9 collective-permute-start.29

commit v3 on v2

--- a/solution.py
+++ b/solution.py
@@ -106,6 +106,28 @@
         after=after,
         flops=2 * size * tall * TAPS * width,
         moved=2 * tall * TAPS * width,
+    )
+
+
+def load(place, values, after):
+    count = len(values)
+
+    def body(place, *refs):
+        sems = refs[-1]
+        copies = [pltpu.make_async_copy(refs[i], refs[count + i], sems.at[i]) for i in range(count)]
+        for copy in copies:
+            copy.start()
+        for copy in copies:
+            copy.wait()
+
+    return call(
+        body,
+        place,
+        [(value, pl.ANY) for value in values],
+        [like(value.shape, value.dtype) for value in values],
+        scratch=[pltpu.SemaphoreType.DMA((count,))],
+        after=after,
+        moved=sum(4 * value.size for value in values),
     )
 
 
@@ -243,12 +265,12 @@
     )
 
 
-def kernel_terms(place, earlier, own, later, cots, after):
+def kernel_terms(place, earlier, own, later, cots, groups, after):
     _, width, size = own.shape
     half = width // 2
     cols = TAPS * width
 
-    def body(place, earlier, own, later, d0, d1, d2, d3, kept, sent):
+    def body(place, earlier, own, later, d0, d1, d2, d3, kept, sent, cover, below):
         y, z, core = place[1], place[2], place[3]
         first, last = z == 0, z == NZ - 1
         for k, left in enumerate((earlier, own, later)):
@@ -269,12 +291,19 @@
             at = slice(k * width, (k + 1) * width)
             kept[:, at] = jnp.where(core == 0, one, two)
             sent[:, at] = jnp.where(core == 0, two, one).astype(BF)
+        for m, right in enumerate((d0, d1, d2, d3)):
+            below[...] = right[size:, :].astype(F32)
+            for i in range(TAPS):
+                cover[m * groups : (m + 1) * groups, i * width : (i + 1) * width] = below[
+                    i * groups : (i + 1) * groups, :
+                ]
 
     return call(
         body,
         place,
         local([earlier, own, later] + cots),
-        [like((half, cols), F32), like((half, cols), BF)],
+        [like((half, cols), F32), like((half, cols), BF), like((NY * groups, cols), F32)],
+        scratch=[pltpu.VMEM((EXTRA, width), F32)],
         after=after,
         flops=2 * size * NY * width * cols,
         moved=8 * NY * width * size,
@@ -287,7 +316,7 @@
     def body(place, kept, came, cover, *refs):
         outs, total, message = refs[:NZ], refs[NZ], refs[NZ + 1]
         total[...] = kept[...] + came[...].astype(F32)
-        message[:EXTRA, :] = cover[...].astype(F32)
+        message[:EXTRA, :] = cover[...]
         for m, ref in enumerate(outs):
             at = pl.multiple_of(lax.rem(place[2] + m, NZ) * GROUP, 8)
             if m == 0:
@@ -306,6 +335,22 @@
         flops=4 * rows * cols,
         moved=6 * rows * cols,
     )
+
+
+def input_gradient(place, inputs, grad, own, came, after):
+    def body(place, state, grad, own, c1, c2, c3, out):
+        back_u = own[...] + c1[...].astype(F32) + c2[...].astype(F32) + c3[...].astype(F32)
+        out[...] = (grad[...] + activation_slope(state[...].astype(F32), back_u)).astype(BF)
+
+    return call(
+        body,
+        place,
+        local([inputs, grad, own] + came),
+        [like(inputs.shape, BF)],
+        after=after,
+        flops=20 * inputs.size,
+        moved=16 * inputs.size,
+    )[0]
 
 
 def coverage_of(blocks, place, exon_blocks, own):
@@ -334,40 +379,38 @@
 
     state = inputs.astype(F32)
     acted = from_all_x(jax.nn.gelu(state).astype(BF))
-    low, mid, up, whole = conv_products(place, acted, conv_weight, ())
+    (taps,) = load(place, [conv_weight], (token(acted[0]),))
+    low, mid, up, whole = conv_products(place, acted, taps, ())
     low, up = shifted(low, steps), shifted(up, -steps)
     after_conv = (state + (mid + low.astype(F32) + up.astype(F32))).astype(BF)
     full = from_all_x(after_conv)
     turned = turned_blocks(place, whole, (token(after_conv),))
     turned = [turned[0]] + [along_seq(turned[m], m, 0, 0) for m in range(1, NY)]
+
+    head, cot = load(place, [head_weight, head_cot], (token(after_conv),))
     turned = stacked(place, turned, tuple(token(value) for value in full[1:]))
     before = along_seq(turned, 0, 1, 0)
     behind = along_seq(turned, 0, NZ - 1, 0)
-
-    tracks, sums, *blocks = track_head(place, full, head_weight, head_cot, (token(turned),))
+    tracks, sums, *blocks = track_head(place, full, head, cot, (token(turned),))
     came = [along_x(blocks[r], r) for r in range(1, NX)]
+    (taps,) = load(place, [conv_weight], (token(blocks[1]),))
     grad, low, long = add_up(place, blocks[0], came, sums, (token(before), token(behind)))
+
     cots = [long] + [along_seq(long, m, 0, 0) for m in range(1, NY)]
     around = [shifted(low, -steps), low, shifted(low, steps)]
-    blocks = back_products(place, around, conv_weight, ())
+    blocks = back_products(place, around, taps, ())
     came = [along_x(blocks[r], r) for r in range(1, NX)]
-    kept, sent = kernel_terms(place, before, turned, behind, cots, (token(blocks[1]),))
-    cover = [
-        cot[size : size + TAPS * own].reshape(TAPS, own, width).transpose(1, 0, 2).reshape(own, -1)
-        for cot in cots
-    ]
-    cover = jnp.concatenate(cover, axis=0)
-    kept, *parts = over_z(place, kept, along_seq(sent, 0, 0, 1), cover, ())
+    kept, sent, cover = kernel_terms(place, before, turned, behind, cots, own, (token(blocks[1]),))
+    kept, *parts = over_z(place, kept, along_seq(sent, 0, 0, 1), cover, tuple(token(value) for value in came))
+    out = input_gradient(place, inputs, grad, blocks[0], came, (token(parts[-1]),))
     parts = [along_seq(part, 0, m + 1, 0) for m, part in enumerate(parts)]
     for part in parts:
         kept = kept + part[EXTRA:].astype(F32)
     kernel_gradient = kept.reshape(GROUP, TAPS, width).transpose(1, 0, 2)[None]
 
-    cover = jnp.stack([cover] + [part[:EXTRA] for part in parts])[:, :, :wide]
+    cover = jnp.stack([cover.astype(BF)] + [part[:EXTRA] for part in parts])[:, :, :wide]
     cover = jnp.stack([cover, along_seq(cover, 0, 0, 1)])
     coverage = coverage_of(cover, place, exon_blocks, own)
-    back_u = blocks[0] + came[0].astype(F32) + came[1].astype(F32) + came[2].astype(F32)
-    out = (grad + activation_slope(state, back_u)).astype(BF)
     return (tracks, coverage, out, kernel_gradient)
 
 

time: 193 us -> 185 us (0.959)
  local copies, waits for them, and re-layouts: 22.7 us -> 8.93 us
  waiting for transfers between devices: 79.8 us -> 86.8 us
  Pallas kernels: 23.4 us -> 28.8 us
  starting transfers between devices: 60 us -> 56 us
  other arithmetic: 4.55 us -> 1.77 us
    ppermute x17, waiting for transfers between devices: 39.9 us -> 49.9 us  [along_seq(): return lax.ppermute(value, 'seq', pairs)]
    unnamed x37 -> x39, local copies, waits for them, and re-layouts: 11.3 us -> 4.8 us
    pallas_call x8 -> x12, Pallas kernels: 23.4 us -> 28.8 us  [call(): pl.pallas_call(kernel, in_specs=[pl.BlockSpec(memory_space=pltpu.SMEM)] +...]
    slice x4 -> x0, local copies, waits for them, and re-layouts: 4.63 us -> none  [shards(): cot[size:size + TAPS * own].reshape(TAPS, own, width).transpose(1, 0, 2)]
    reshape x4 -> x0, local copies, waits for them, and re-layouts: 4.56 us -> none  [shards(): cot[size:size + TAPS * own].reshape(TAPS, own, width).transpose(1, 0, 2)]
    ppermute x17, starting transfers between devices: 33.3 us -> 29.9 us  [along_seq(): return lax.ppermute(value, 'seq', pairs)]
    slice x5 -> x11, local copies, waits for them, and re-layouts: 0.01 us -> 3.34 us  [token(): return value[(0,) * (value.ndim - 2) + (slice(8), slice(128))]]
    ppermute x12, waiting for transfers between devices: 29 us -> 26.1 us  [along_x(): lax.ppermute(value, 'chan', [(i, (i + steps) % NX) for i in range(NX)])]
  transfers between devices with their start and end apart: 33 -> 33, of which waited for: 16 -> 16; matrix products, arithmetic and copies ran while one was open for 8% -> 3% of each run, Pallas kernels for 9% -> 12%
where the time goes in v3:
time: 185 us; the launch traced here: 184 us
  waiting for transfers between devices  86.8 us (47%)
  starting transfers between devices  56 us (30%)
  Pallas kernels  28.8 us (16%)
  local copies, waits for them, and re-layouts  8.93 us (5%)
    ppermute x17, waiting for transfers between devices, along_seq(): return lax.ppermute(value, 'seq', pairs)  49.9 us
    ppermute x17, starting transfers between devices, along_seq(): return lax.ppermute(value, 'seq', pairs)  29.9 us
    pallas_call x12, Pallas kernels, call(): pl.pallas_call(kernel, in_specs=[pl.BlockSpec(memory_space=pltpu.SMEM)] +...  28.8 us
    ppermute x12, waiting for transfers between devices, along_x(): lax.ppermute(value, 'chan', [(i, (i + steps) % NX) for i in range(NX)])  26.1 us
    ppermute x12, starting transfers between devices, along_x(): lax.ppermute(value, 'chan', [(i, (i + steps) % NX) for i in range(NX)])  15.2 us
    ppermute x4, starting transfers between devices, shifted(): lax.ppermute(value, 'seq', [(s, s + steps) for s in range(leading, last)])  10.9 us
    ppermute x4, waiting for transfers between devices, shifted(): lax.ppermute(value, 'seq', [(s, s + steps) for s in range(leading, last)])  10.8 us
    unnamed x39, local copies, waits for them, and re-layouts  4.8 us
  transfers between devices with their start and end apart: 33, of which 16 were waited for; matrix products, arithmetic and copies ran while one was open for 3% of the time, Pallas kernels for 12%

profile of v3, /device:TPU:1, one launch (start us, length us, event | category | flops | bytes accessed | tf_op | source)
XLA Modules:
  0.0 184.1 jit_solution(2128723653808112457)
XLA Ops:
  0.6 1.3 fusion.5.refs_1_
  1.9 3.4 %collective-permute-start = (bf16[512,384]{1,0:T(8,128)(2,1)S(1)}, bf16[512,384]{1,0:T(8,128)(2,1)S(1)}, u32[]{:S(2)}, u32[]{:S(2)}) collective-permute-start(bf16[512,384]{1,0:T(8,128)(2,1)S(1)} %fusion.5.refs_1_), channel_id=1, source_target_pairs={{0,3},{1,0},{2,1},{3,2},{4,7},{5,4},{6,5},{7,6},{8,11},{9,8},{10,9... | collective-permute-start | bytes 1179656 | tf_op jit(solution)/shard_map/ppermute | solution.py:33
  5.3 0.5 collective-permute-start.1
  5.8 0.6 collective-permute-start.2
  6.5 2.0 %copy-done = bf16[1,3,1536,384]{3,2,1,0:T(8,128)(2,1)S(1)} copy-done((bf16[1,3,1536,384]{3,2,1,0:T(8,128)(2,1)S(1)}, bf16[1,3,1536,384]{3,2,1,0:T(8,128)(2,1)}, u32[]{:S(2)}) %copy-start) | copy-done | bytes 3538968
  8.5 1.0 shard_map.84.refs_5_
  9.5 6.7 %collective-permute-done.refs_2_ = bf16[512,384]{1,0:T(8,128)(2,1)S(1)} collective-permute-done((bf16[512,384]{1,0:T(8,128)(2,1)S(1)}, bf16[512,384]{1,0:T(8,128)(2,1)S(1)}, u32[]{:S(2)}, u32[]{:S(2)}) %collective-permute-start) | collective-permute-done | bytes 393248 | tf_op jit(solution)/shard_map/ppermute | solution.py:33
  16.1 0.4 collective-permute-done.1.refs_3_
  16.5 9.8 %collective-permute-done.2.refs_4_ = bf16[512,384]{1,0:T(8,128)(2,1)S(1)} collective-permute-done((bf16[512,384]{1,0:T(8,128)(2,1)S(1)}, bf16[512,384]{1,0:T(8,128)(2,1)S(1)}, u32[]{:S(2)}, u32[]{:S(2)}) %collective-permute-start.2) | collective-permute-done | bytes 393248 | tf_op jit(solution)/shard_map/ppermute | solution.py:33
  26.3 3.2 %shard_map.85 = (bf16[512,384]{1,0:T(8,128)(2,1)S(1)}, f32[512,384]{1,0:T(8,128)S(1)}, bf16[512,384]{1,0:T(8,128)(2,1)S(1)}, bf16[512,1536]{1,0:T(8,128)(2,1)S(1)}) custom-call(s32[4]{0:T(128)S(1)} %pad_add_fusion.refs_0_, bf16[512,384]{1,0:T(8,128)(2,1)S(1)} %fusion.5.refs_1_, bf16[512,384]{1,0:T(8,128)(2,1)S(1)} %collective-permute-done.refs_2_, ...), custom_call_target="tpu_custom_call" | custom-call | flops 1811939328 | bytes 3538944 | tf_op jit(solution)/shard_map/pallas_call | solution.py:64
  29.5 3.6 %collective-permute-start.3 = (bf16[512,384]{1,0:T(8,128)(2,1)S(1)}, bf16[512,384]{1,0:T(8,128)(2,1)S(1)}, u32[]{:S(2)}, u32[]{:S(2)}) collective-permute-start(bf16[512,384]{1,0:T(8,128)(2,1)S(1)} %get-tuple-element.39), channel_id=1, source_target_pairs={{0,8},{4,12},{8,16},{12,20},{16,24},{20,28},{24,32},{28,36},{32,40... | collective-permute-start | bytes 1179656 | tf_op jit(solution)/shard_map/ppermute | solution.py:29
  33.1 1.3 collective-permute-start.4
  34.4 6.6 %collective-permute-done.3 = bf16[512,384]{1,0:T(8,128)(2,1)S(1)} collective-permute-done((bf16[512,384]{1,0:T(8,128)(2,1)S(1)}, bf16[512,384]{1,0:T(8,128)(2,1)S(1)}, u32[]{:S(2)}, u32[]{:S(2)}) %collective-permute-start.3) | collective-permute-done | bytes 393248 | tf_op jit(solution)/shard_map/ppermute | solution.py:29
  41.0 4.2 %collective-permute-done.4 = bf16[512,384]{1,0:T(8,128)(2,1)S(1)} collective-permute-done((bf16[512,384]{1,0:T(8,128)(2,1)S(1)}, bf16[512,384]{1,0:T(8,128)(2,1)S(1)}, u32[]{:S(2)}, u32[]{:S(2)}) %collective-permute-start.4) | collective-permute-done | bytes 393248 | tf_op jit(solution)/shard_map/ppermute | solution.py:29
  45.5 0.6 collective-permute-start.6
  46.1 0.8 collective-permute-start.7
  46.9 1.0 shard_map.87
  47.9 4.7 %collective-permute-start.10 = (bf16[384,512]{1,0:T(8,128)(2,1)S(1)}, bf16[384,512]{1,0:T(8,128)(2,1)S(1)}, u32[]{:S(2)}, u32[]{:S(2)}) collective-permute-start(bf16[384,512]{1,0:T(8,128)(2,1)S(1)} %get-tuple-element.47), channel_id=1, source_target_pairs={{0,192},{4,196},{8,200},{12,204},{16,208},{20,212},{24,216},{28,22... | collective-permute-start | bytes 1179656 | tf_op jit(solution)/shard_map/ppermute | solution.py:46
  52.6 2.0 %collective-permute-done.5.refs_2_ = bf16[512,384]{1,0:T(8,128)(2,1)S(1)} collective-permute-done((bf16[512,384]{1,0:T(8,128)(2,1)S(1)}, bf16[512,384]{1,0:T(8,128)(2,1)S(1)}, u32[]{:S(2)}, u32[]{:S(2)}) %collective-permute-start.5) | collective-permute-done | bytes 393248 | tf_op jit(solution)/shard_map/ppermute | solution.py:33
  54.6 4.6 %collective-permute-start.9 = (bf16[384,512]{1,0:T(8,128)(2,1)S(1)}, bf16[384,512]{1,0:T(8,128)(2,1)S(1)}, u32[]{:S(2)}, u32[]{:S(2)}) collective-permute-start(bf16[384,512]{1,0:T(8,128)(2,1)S(1)} %get-tuple-element.46), channel_id=1, source_target_pairs={{0,128},{4,132},{8,136},{12,140},{16,144},{20,148},{24,152},{28,15... | collective-permute-start | bytes 1179656 | tf_op jit(solution)/shard_map/ppermute | solution.py:46
  59.2 7.3 %collective-permute-done.7.refs_4_ = bf16[512,384]{1,0:T(8,128)(2,1)S(1)} collective-permute-done((bf16[512,384]{1,0:T(8,128)(2,1)S(1)}, bf16[512,384]{1,0:T(8,128)(2,1)S(1)}, u32[]{:S(2)}, u32[]{:S(2)}) %collective-permute-start.7) | collective-permute-done | bytes 393248 | tf_op jit(solution)/shard_map/ppermute | solution.py:33
  66.5 2.7 %collective-permute-done.9.refs_3_ = bf16[384,512]{1,0:T(8,128)(2,1)S(1)} collective-permute-done((bf16[384,512]{1,0:T(8,128)(2,1)S(1)}, bf16[384,512]{1,0:T(8,128)(2,1)S(1)}, u32[]{:S(2)}, u32[]{:S(2)}) %collective-permute-start.9) | collective-permute-done | bytes 393248 | tf_op jit(solution)/shard_map/ppermute | solution.py:46
  69.2 0.6 shard_map.88.refs_2_
  69.9 4.4 %collective-permute-start.12 = (bf16[4,384,512]{2,1,0:T(8,128)(2,1)S(1)}, bf16[4,384,512]{2,1,0:T(8,128)(2,1)S(1)}, u32[]{:S(2)}, u32[]{:S(2)}) collective-permute-start(bf16[4,384,512]{2,1,0:T(8,128)(2,1)S(1)} %shard_map.88.refs_2_), channel_id=1, source_target_pairs={{0,56},{4,60},{8,0},{12,4},{16,8},{20,12},{24,16},{28,20},{32,24},... | collective-permute-start | bytes 4718600 | tf_op jit(solution)/shard_map/ppermute | solution.py:46
  74.3 0.8 shard_map.86
  75.2 6.6 %shard_map.89 = (bf16[512,1024]{1,0:T(8,128)(2,1)}, f32[4,1024]{1,0:T(4,128)S(1)}, f32[512,384]{1,0:T(8,128)S(1)}, bf16[512,384]{1,0:T(8,128)(2,1)S(1)}, bf16[51...) custom-call(s32[4]{0:T(128)S(1)} %pad_add_fusion.refs_0_, bf16[512,384]{1,0:T(8,128)(2,1)S(1)} %fusion.6.refs_1_, ...), custom_call_target="tpu_custom_call" | custom-call | flops 3221225472 | bytes 3145728 | tf_op jit(solution)/shard_map/pallas_call | solution.py:64
  81.8 1.5 collective-permute-start.13
  83.3 2.3 %collective-permute-start.14 = (bf16[512,384]{1,0:T(8,128)(2,1)S(1)}, bf16[512,384]{1,0:T(8,128)(2,1)S(1)}, u32[]{:S(2)}, u32[]{:S(2)}) collective-permute-start(bf16[512,384]{1,0:T(8,128)(2,1)S(1)} %get-tuple-element.51), channel_id=1, source_target_pairs={{0,2},{1,3},{2,0},{3,1},{4,6},{5,7},{6,4},{7,5},{8,10},{9,11},{10,... | collective-permute-start | bytes 1179656 | tf_op jit(solution)/shard_map/ppermute | solution.py:33
  85.6 1.8 collective-permute-start.15
  87.4 17.3 %collective-permute-done.12.refs_3_ = bf16[4,384,512]{2,1,0:T(8,128)(2,1)S(1)} collective-permute-done((bf16[4,384,512]{2,1,0:T(8,128)(2,1)S(1)}, bf16[4,384,512]{2,1,0:T(8,128)(2,1)S(1)}, u32[]{:S(2)}, u32[]{:S(2)}) %collective-permute-start.12) | collective-permute-done | bytes 1572896 | tf_op jit(solution)/shard_map/ppermute | solution.py:46
  104.7 3.1 %collective-permute-done.11.refs_1_ = bf16[4,384,512]{2,1,0:T(8,128)(2,1)S(1)} collective-permute-done((bf16[4,384,512]{2,1,0:T(8,128)(2,1)S(1)}, bf16[4,384,512]{2,1,0:T(8,128)(2,1)S(1)}, u32[]{:S(2)}, u32[]{:S(2)}) %collective-permute-start.11) | collective-permute-done | bytes 1572896 | tf_op jit(solution)/shard_map/ppermute | solution.py:46
  107.8 1.1 copy-done.13
  109.0 1.8 shard_map.90
  110.8 0.9 copy-done.8
  111.7 1.3 collective-permute-start.19
  112.9 4.7 %collective-permute-start.20 = (bf16[512,384]{1,0:T(8,128)(2,1)}, bf16[512,384]{1,0:T(8,128)(2,1)}, u32[]{:S(2)}, u32[]{:S(2)}) collective-permute-start(bf16[512,384]{1,0:T(8,128)(2,1)} %get-tuple-element.55.refs_2_), channel_id=1, source_target_pairs={{0,8},{4,12},{8,16},{12,20},{16,24},{20,28},{24,32},{28,36},{32,40... | collective-permute-start | bytes 1179656 | tf_op jit(solution)/shard_map/ppermute | solution.py:29
  117.7 0.5 collective-permute-start.16
  118.2 2.5 %collective-permute-start.17 = (bf16[528,384]{1,0:T(8,128)(2,1)}, bf16[528,384]{1,0:T(8,128)(2,1)}, u32[]{:S(2)}, u32[]{:S(2)}) collective-permute-start(bf16[528,384]{1,0:T(8,128)(2,1)} %get-tuple-element.54.refs_4_), channel_id=1, source_target_pairs={{0,128},{4,132},{8,136},{12,140},{16,144},{20,148},{24,152},{28,15... | collective-permute-start | bytes 1216520 | tf_op jit(solution)/shard_map/ppermute | solution.py:46
  120.7 2.0 %collective-permute-start.18 = (bf16[528,384]{1,0:T(8,128)(2,1)}, bf16[528,384]{1,0:T(8,128)(2,1)}, u32[]{:S(2)}, u32[]{:S(2)}) collective-permute-start(bf16[528,384]{1,0:T(8,128)(2,1)} %get-tuple-element.54.refs_4_), channel_id=1, source_target_pairs={{0,192},{4,196},{8,200},{12,204},{16,208},{20,212},{24,216},{28,22... | collective-permute-start | bytes 1216520 | tf_op jit(solution)/shard_map/ppermute | solution.py:46
  122.7 0.7 slice.96.refs_2_
  123.4 1.0 shard_map.91.refs_4_
  124.4 4.6 %shard_map.92 = (f32[512,384]{1,0:T(8,128)S(1)}, bf16[512,384]{1,0:T(8,128)(2,1)}, bf16[512,384]{1,0:T(8,128)(2,1)}, bf16[512,384]{1,0:T(8,128)(2,1)}) custom-call(s32[4]{0:T(128)S(1)} %pad_add_fusion.refs_0_, bf16[512,384]{1,0:T(8,128)(2,1)} %collective-permute-done.19.refs_1_, bf16[512,384]{1,0:T(8,128)(2,1)} %get-tuple-element.55.refs_2_, ...), custom_call_target="tpu_custom_call" | custom-call | flops 1811939328 | bytes 3538944 | tf_op jit(solution)/shard_map/pallas_call | solution.py:64
  129.0 0.7 slice.97.refs_8_
  129.7 1.8 collective-permute-start.23
  131.5 3.6 %collective-permute-done.16.refs_5_ = bf16[528,384]{1,0:T(8,128)(2,1)} collective-permute-done((bf16[528,384]{1,0:T(8,128)(2,1)}, bf16[528,384]{1,0:T(8,128)(2,1)}, u32[]{:S(2)}, u32[]{:S(2)}) %collective-permute-start.16) | collective-permute-done | bytes 405536 | tf_op jit(solution)/shard_map/ppermute | solution.py:46
  135.1 1.9 %collective-permute-start.24 = (bf16[512,384]{1,0:T(8,128)(2,1)}, bf16[512,384]{1,0:T(8,128)(2,1)}, u32[]{:S(2)}, u32[]{:S(2)}) collective-permute-start(bf16[512,384]{1,0:T(8,128)(2,1)} %get-tuple-element.61), channel_id=1, source_target_pairs={{0,3},{1,0},{2,1},{3,2},{4,7},{5,4},{6,5},{7,6},{8,11},{9,8},{10,9... | collective-permute-start | bytes 1179656 | tf_op jit(solution)/shard_map/ppermute | solution.py:33
  137.0 8.9 %collective-permute-done.17.refs_6_ = bf16[528,384]{1,0:T(8,128)(2,1)} collective-permute-done((bf16[528,384]{1,0:T(8,128)(2,1)}, bf16[528,384]{1,0:T(8,128)(2,1)}, u32[]{:S(2)}, u32[]{:S(2)}) %collective-permute-start.17) | collective-permute-done | bytes 405536 | tf_op jit(solution)/shard_map/ppermute | solution.py:46
  145.9 4.8 %shard_map.93 = (f32[192,1152]{1,0:T(8,128)S(1)}, bf16[192,1152]{1,0:T(8,128)(2,1)}, f32[16,1152]{1,0:T(8,128)S(1)}) custom-call(s32[4]{0:T(128)S(1)} %pad_add_fusion.refs_0_, bf16[4,384,512]{2,1,0:T(8,128)(2,1)S(1)} %copy-done.14, bf16[4,384,512]{2,1,0:T(8,128)(2,1)S(1)} %copy-done.6, bf16[4,384,512]{2,1,0:T(8,128)(2,1)S(1)} %copy-done.12, ...), custom_call_target="tpu_custom_call" | custom-call | flops 1811939328 | bytes 6291456 | tf_op jit(solution)/shard_map/pallas_call | solution.py:64
  150.7 2.6 %collective-permute-start.21 = (bf16[192,1152]{1,0:T(8,128)(2,1)}, bf16[192,1152]{1,0:T(8,128)(2,1)S(1)}, u32[]{:S(2)}, u32[]{:S(2)}) collective-permute-start(bf16[192,1152]{1,0:T(8,128)(2,1)} %get-tuple-element.59), channel_id=1, source_target_pairs={{0,4},{4,0},{8,12},{12,8},{16,20},{20,16},{24,28},{28,24},{32,36},... | collective-permute-start | bytes 1327112 | tf_op jit(solution)/shard_map/ppermute | solution.py:46
  154.1 0.6 slice.125.refs_4_
  154.7 0.7 slice.126.refs_5_
  155.4 0.7 slice.127.refs_6_
  156.1 0.7 shard_map.94
  156.9 2.7 %collective-permute-start.31 = (bf16[40,1152]{1,0:T(8,128)(2,1)S(1)}, bf16[40,1152]{1,0:T(8,128)(2,1)S(1)}, u32[]{:S(2)}, u32[]{:S(2)}) collective-permute-start(bf16[40,1152]{1,0:T(8,128)(2,1)S(1)} %get-tuple-element.68), channel_id=1, source_target_pairs={{0,56},{4,60},{8,0},{12,4},{16,8},{20,12},{24,16},{28,20},{32,24},... | collective-permute-start | bytes 276488 | tf_op jit(solution)/shard_map/ppermute | solution.py:46
  159.6 4.3 %collective-permute-start.28 = (bf16[40,1152]{1,0:T(8,128)(2,1)S(1)}, bf16[40,1152]{1,0:T(8,128)(2,1)S(1)}, u32[]{:S(2)}, u32[]{:S(2)}) collective-permute-start(bf16[40,1152]{1,0:T(8,128)(2,1)S(1)} %get-tuple-element.65), channel_id=1, source_target_pairs={{0,32},{4,36},{8,40},{12,44},{16,48},{20,52},{24,56},{28,60},{32,0... | collective-permute-start | bytes 276488 | tf_op jit(solution)/shard_map/ppermute | solution.py:46
  163.8 2.7 %shard_map.95 = bf16[512,384]{1,0:T(8,128)(2,1)} custom-call(s32[4]{0:T(128)S(1)} %pad_add_fusion.refs_0_, bf16[512,384]{1,0:T(8,128)(2,1)S(1)} %copy-done.3, f32[512,384]{1,0:T(8,128)S(1)} %copy-done.9, f32[512,384]{1,0:T(8,128)S(1)} %get-tuple-element.70.refs_3_, bf16[512,384]{1,0:T(8,128)(2,1)} %collective-permute-done.22.refs_4_, ...), custom_call_target="tpu_custom_call" | custom-call | flops 3932160 | bytes 3145728 | tf_op jit(solution)/shard_map/pallas_call | solution.py:64
  166.6 0.2 collective-permute-start.29
  166.8 6.2 %collective-permute-done.26 = bf16[40,1152]{1,0:T(8,128)(2,1)S(1)} collective-permute-done((bf16[40,1152]{1,0:T(8,128)(2,1)S(1)}, bf16[40,1152]{1,0:T(8,128)(2,1)S(1)}, u32[]{:S(2)}, u32[]{:S(2)}) %collective-permute-start.26) | collective-permute-done | bytes 92192 | tf_op jit(solution)/shard_map/ppermute | solution.py:46
  173.0 1.0 collective-permute-done.27
  174.0 6.7 %collective-permute-done.30 = bf16[40,1152]{1,0:T(8,128)(2,1)S(1)} collective-permute-done((bf16[40,1152]{1,0:T(8,128)(2,1)S(1)}, bf16[40,1152]{1,0:T(8,128)(2,1)S(1)}, u32[]{:S(2)}, u32[]{:S(2)}) %collective-permute-start.30) | collective-permute-done | bytes 92192 | tf_op jit(solution)/shard_map/ppermute | solution.py:46
  180.8 1.3 collective-permute-start.32
  182.2 0.7 copy.11
  182.9 0.4 collective-permute-done.32
  183.3 0.8 convolution_multiply_fusion
  (90 shorter events, 1.6 us)
Async XLA Ops:
  1.9 14.2 %collective-permute-start = (bf16[512,384]{1,0:T(8,128)(2,1)S(1)}, bf16[512,384]{1,0:T(8,128)(2,1)S(1)}, u32[]{:S(2)}, u32[]{:S(2)}) collective-permute-start(bf16[512,384]{1,0:T(8,128)(2,1)S(1)} %fusion.5.refs_1_), channel_id=1, source_target_pairs={{0,3},{1,0},{2,1},{3,2},{4,7},{5,4},{6,5},{7,6},{8,11},{9,8},{10,9... | collective-permute-start | bytes 1179656 | tf_op jit(solution)/shard_map/ppermute | solution.py:33
  5.3 11.2 %collective-permute-start.1 = (bf16[512,384]{1,0:T(8,128)(2,1)S(1)}, bf16[512,384]{1,0:T(8,128)(2,1)S(1)}, u32[]{:S(2)}, u32[]{:S(2)}) collective-permute-start(bf16[512,384]{1,0:T(8,128)(2,1)S(1)} %fusion.5.refs_1_), channel_id=1, source_target_pairs={{0,2},{1,3},{2,0},{3,1},{4,6},{5,7},{6,4},{7,5},{8,10},{9,11},{10,... | collective-permute-start | bytes 1179656 | tf_op jit(solution)/shard_map/ppermute | solution.py:33
  5.8 20.4 %collective-permute-start.2 = (bf16[512,384]{1,0:T(8,128)(2,1)S(1)}, bf16[512,384]{1,0:T(8,128)(2,1)S(1)}, u32[]{:S(2)}, u32[]{:S(2)}) collective-permute-start(bf16[512,384]{1,0:T(8,128)(2,1)S(1)} %fusion.5.refs_1_), channel_id=1, source_target_pairs={{0,1},{1,2},{2,3},{3,0},{4,5},{5,6},{6,7},{7,4},{8,9},{9,10},{10,1... | collective-permute-start | bytes 1179656 | tf_op jit(solution)/shard_map/ppermute | solution.py:33
  6.5 2.0 %copy-start = (bf16[1,3,1536,384]{3,2,1,0:T(8,128)(2,1)S(1)}, bf16[1,3,1536,384]{3,2,1,0:T(8,128)(2,1)}, u32[]{:S(2)}) copy-start(bf16[1,3,1536,384]{3,2,1,0:T(8,128)(2,1)} %refs_1_.6) | copy-start | bytes 10616836
  9.5 35.7 %copy-start.2 = (bf16[512,384]{1,0:T(8,128)(2,1)S(1)}, bf16[512,384]{1,0:T(8,128)(2,1)}, u32[]{:S(2)}) copy-start(bf16[512,384]{1,0:T(8,128)(2,1)} %refs_1_.7) | copy-start | bytes 1179652
  29.5 11.5 %collective-permute-start.3 = (bf16[512,384]{1,0:T(8,128)(2,1)S(1)}, bf16[512,384]{1,0:T(8,128)(2,1)S(1)}, u32[]{:S(2)}, u32[]{:S(2)}) collective-permute-start(bf16[512,384]{1,0:T(8,128)(2,1)S(1)} %get-tuple-element.39), channel_id=1, source_target_pairs={{0,8},{4,12},{8,16},{12,20},{16,24},{20,28},{24,32},{28,36},{32,40... | collective-permute-start | bytes 1179656 | tf_op jit(solution)/shard_map/ppermute | solution.py:29
  33.1 12.1 %collective-permute-start.4 = (bf16[512,384]{1,0:T(8,128)(2,1)S(1)}, bf16[512,384]{1,0:T(8,128)(2,1)S(1)}, u32[]{:S(2)}, u32[]{:S(2)}) collective-permute-start(bf16[512,384]{1,0:T(8,128)(2,1)S(1)} %get-tuple-element.40), channel_id=1, source_target_pairs={{8,0},{12,4},{16,8},{20,12},{24,16},{28,20},{32,24},{36,28},{40,32... | collective-permute-start | bytes 1179656 | tf_op jit(solution)/shard_map/ppermute | solution.py:29
  45.4 9.2 %collective-permute-start.5 = (bf16[512,384]{1,0:T(8,128)(2,1)S(1)}, bf16[512,384]{1,0:T(8,128)(2,1)S(1)}, u32[]{:S(2)}, u32[]{:S(2)}) collective-permute-start(bf16[512,384]{1,0:T(8,128)(2,1)S(1)} %fusion.6.refs_1_), channel_id=1, source_target_pairs={{0,3},{1,0},{2,1},{3,2},{4,7},{5,4},{6,5},{7,6},{8,11},{9,8},{10,9... | collective-permute-start | bytes 1179656 | tf_op jit(solution)/shard_map/ppermute | solution.py:33
  45.5 13.8 %collective-permute-start.6 = (bf16[512,384]{1,0:T(8,128)(2,1)S(1)}, bf16[512,384]{1,0:T(8,128)(2,1)S(1)}, u32[]{:S(2)}, u32[]{:S(2)}) collective-permute-start(bf16[512,384]{1,0:T(8,128)(2,1)S(1)} %fusion.6.refs_1_), channel_id=1, source_target_pairs={{0,2},{1,3},{2,0},{3,1},{4,6},{5,7},{6,4},{7,5},{8,10},{9,11},{10,... | collective-permute-start | bytes 1179656 | tf_op jit(solution)/shard_map/ppermute | solution.py:33
  46.1 20.4 %collective-permute-start.7 = (bf16[512,384]{1,0:T(8,128)(2,1)S(1)}, bf16[512,384]{1,0:T(8,128)(2,1)S(1)}, u32[]{:S(2)}, u32[]{:S(2)}) collective-permute-start(bf16[512,384]{1,0:T(8,128)(2,1)S(1)} %fusion.6.refs_1_), channel_id=1, source_target_pairs={{0,1},{1,2},{2,3},{3,0},{4,5},{5,6},{6,7},{7,4},{8,9},{9,10},{10,1... | collective-permute-start | bytes 1179656 | tf_op jit(solution)/shard_map/ppermute | solution.py:33
  46.9 27.4 %copy-start.7 = (bf16[512,1024]{1,0:T(8,128)(2,1)S(1)}, bf16[512,1024]{1,0:T(8,128)(2,1)}, u32[]{:S(2)}) copy-start(bf16[512,1024]{1,0:T(8,128)(2,1)} %refs_2_.1) | copy-start | bytes 3145732
  47.9 18.6 %collective-permute-start.10 = (bf16[384,512]{1,0:T(8,128)(2,1)S(1)}, bf16[384,512]{1,0:T(8,128)(2,1)S(1)}, u32[]{:S(2)}, u32[]{:S(2)}) collective-permute-start(bf16[384,512]{1,0:T(8,128)(2,1)S(1)} %get-tuple-element.47), channel_id=1, source_target_pairs={{0,192},{4,196},{8,200},{12,204},{16,208},{20,212},{24,216},{28,22... | collective-permute-start | bytes 1179656 | tf_op jit(solution)/shard_map/ppermute | solution.py:46
  52.6 13.9 %collective-permute-start.8 = (bf16[384,512]{1,0:T(8,128)(2,1)S(1)}, bf16[384,512]{1,0:T(8,128)(2,1)S(1)}, u32[]{:S(2)}, u32[]{:S(2)}) collective-permute-start(bf16[384,512]{1,0:T(8,128)(2,1)S(1)} %get-tuple-element.45), channel_id=1, source_target_pairs={{0,64},{4,68},{8,72},{12,76},{16,80},{20,84},{24,88},{28,92},{32,9... | collective-permute-start | bytes 1179656 | tf_op jit(solution)/shard_map/ppermute | solution.py:46
  54.6 14.6 %collective-permute-start.9 = (bf16[384,512]{1,0:T(8,128)(2,1)S(1)}, bf16[384,512]{1,0:T(8,128)(2,1)S(1)}, u32[]{:S(2)}, u32[]{:S(2)}) collective-permute-start(bf16[384,512]{1,0:T(8,128)(2,1)S(1)} %get-tuple-element.46), channel_id=1, source_target_pairs={{0,128},{4,132},{8,136},{12,140},{16,144},{20,148},{24,152},{28,15... | collective-permute-start | bytes 1179656 | tf_op jit(solution)/shard_map/ppermute | solution.py:46
  69.2 5.1 %copy-start.4 = (bf16[1536,1024]{1,0:T(8,128)(2,1)S(1)}, bf16[1536,1024]{1,0:T(8,128)(2,1)}, u32[]{:S(2)}) copy-start(bf16[1536,1024]{1,0:T(8,128)(2,1)} %refs_1_.5) | copy-start | bytes 9437188
  69.9 5.3 %copy-start.5 = (bf16[4,384,512]{2,1,0:T(8,128)(2,1)}, bf16[4,384,512]{2,1,0:T(8,128)(2,1)S(1)}, u32[]{:S(2)}) copy-start(bf16[4,384,512]{2,1,0:T(8,128)(2,1)S(1)} %shard_map.88.refs_2_) | copy-start | bytes 4718596
  69.9 34.8 %collective-permute-start.12 = (bf16[4,384,512]{2,1,0:T(8,128)(2,1)S(1)}, bf16[4,384,512]{2,1,0:T(8,128)(2,1)S(1)}, u32[]{:S(2)}, u32[]{:S(2)}) collective-permute-start(bf16[4,384,512]{2,1,0:T(8,128)(2,1)S(1)} %shard_map.88.refs_2_), channel_id=1, source_target_pairs={{0,56},{4,60},{8,0},{12,4},{16,8},{20,12},{24,16},{28,20},{32,24},... | collective-permute-start | bytes 4718600 | tf_op jit(solution)/shard_map/ppermute | solution.py:46
  74.3 33.5 %collective-permute-start.11 = (bf16[4,384,512]{2,1,0:T(8,128)(2,1)S(1)}, bf16[4,384,512]{2,1,0:T(8,128)(2,1)S(1)}, u32[]{:S(2)}, u32[]{:S(2)}) collective-permute-start(bf16[4,384,512]{2,1,0:T(8,128)(2,1)S(1)} %shard_map.88.refs_2_), channel_id=1, source_target_pairs={{0,8},{4,12},{8,16},{12,20},{16,24},{20,28},{24,32},{28,36},{32,40... | collective-permute-start | bytes 4718600 | tf_op jit(solution)/shard_map/ppermute | solution.py:46
  75.2 48.2 %copy-start.1 = (bf16[1,3,1536,384]{3,2,1,0:T(8,128)(2,1)S(1)}, bf16[1,3,1536,384]{3,2,1,0:T(8,128)(2,1)}, u32[]{:S(2)}) copy-start(bf16[1,3,1536,384]{3,2,1,0:T(8,128)(2,1)} %refs_1_.6) | copy-start | bytes 10616836
  81.8 28.9 %copy-start.10 = (bf16[512,384]{1,0:T(8,128)(2,1)}, bf16[512,384]{1,0:T(8,128)(2,1)S(1)}, u32[]{:S(2)}) copy-start(bf16[512,384]{1,0:T(8,128)(2,1)S(1)} %get-tuple-element.50) | copy-start | bytes 1179652
  81.8 27.1 %collective-permute-start.13 = (bf16[512,384]{1,0:T(8,128)(2,1)S(1)}, bf16[512,384]{1,0:T(8,128)(2,1)S(1)}, u32[]{:S(2)}, u32[]{:S(2)}) collective-permute-start(bf16[512,384]{1,0:T(8,128)(2,1)S(1)} %get-tuple-element.50), channel_id=1, source_target_pairs={{0,1},{1,2},{2,3},{3,0},{4,5},{5,6},{6,7},{7,4},{8,9},{9,10},{10,1... | collective-permute-start | bytes 1179656 | tf_op jit(solution)/shard_map/ppermute | solution.py:33
  83.3 25.7 %collective-permute-start.14 = (bf16[512,384]{1,0:T(8,128)(2,1)S(1)}, bf16[512,384]{1,0:T(8,128)(2,1)S(1)}, u32[]{:S(2)}, u32[]{:S(2)}) collective-permute-start(bf16[512,384]{1,0:T(8,128)(2,1)S(1)} %get-tuple-element.51), channel_id=1, source_target_pairs={{0,2},{1,3},{2,0},{3,1},{4,6},{5,7},{6,4},{7,5},{8,10},{9,11},{10,... | collective-permute-start | bytes 1179656 | tf_op jit(solution)/shard_map/ppermute | solution.py:33
  85.6 23.4 %collective-permute-start.15 = (bf16[512,384]{1,0:T(8,128)(2,1)S(1)}, bf16[512,384]{1,0:T(8,128)(2,1)S(1)}, u32[]{:S(2)}, u32[]{:S(2)}) collective-permute-start(bf16[512,384]{1,0:T(8,128)(2,1)S(1)} %get-tuple-element.52), channel_id=1, source_target_pairs={{0,3},{1,0},{2,1},{3,2},{4,7},{5,4},{6,5},{7,6},{8,11},{9,8},{10,9... | collective-permute-start | bytes 1179656 | tf_op jit(solution)/shard_map/ppermute | solution.py:33
  104.7 7.0 %copy-start.11 = (bf16[4,384,512]{2,1,0:T(8,128)(2,1)}, bf16[4,384,512]{2,1,0:T(8,128)(2,1)S(1)}, u32[]{:S(2)}) copy-start(bf16[4,384,512]{2,1,0:T(8,128)(2,1)S(1)} %collective-permute-done.12.refs_3_) | copy-start | bytes 4718596
  107.8 1.1 copy-start.13
  110.8 0.9 copy-start.8
  111.7 12.7 %collective-permute-start.19 = (bf16[512,384]{1,0:T(8,128)(2,1)}, bf16[512,384]{1,0:T(8,128)(2,1)}, u32[]{:S(2)}, u32[]{:S(2)}) collective-permute-start(bf16[512,384]{1,0:T(8,128)(2,1)} %get-tuple-element.55.refs_2_), channel_id=1, source_target_pairs={{8,0},{12,4},{16,8},{20,12},{24,16},{28,20},{32,24},{36,28},{40,32... | collective-permute-start | bytes 1179656 | tf_op jit(solution)/shard_map/ppermute | solution.py:29
  112.9 11.5 %collective-permute-start.20 = (bf16[512,384]{1,0:T(8,128)(2,1)}, bf16[512,384]{1,0:T(8,128)(2,1)}, u32[]{:S(2)}, u32[]{:S(2)}) collective-permute-start(bf16[512,384]{1,0:T(8,128)(2,1)} %get-tuple-element.55.refs_2_), channel_id=1, source_target_pairs={{0,8},{4,12},{8,16},{12,20},{16,24},{20,28},{24,32},{28,36},{32,40... | collective-permute-start | bytes 1179656 | tf_op jit(solution)/shard_map/ppermute | solution.py:29
  117.7 17.4 %collective-permute-start.16 = (bf16[528,384]{1,0:T(8,128)(2,1)}, bf16[528,384]{1,0:T(8,128)(2,1)}, u32[]{:S(2)}, u32[]{:S(2)}) collective-permute-start(bf16[528,384]{1,0:T(8,128)(2,1)} %get-tuple-element.54.refs_4_), channel_id=1, source_target_pairs={{0,64},{4,68},{8,72},{12,76},{16,80},{20,84},{24,88},{28,92},{32,9... | collective-permute-start | bytes 1216520 | tf_op jit(solution)/shard_map/ppermute | solution.py:46
  118.2 27.7 %collective-permute-start.17 = (bf16[528,384]{1,0:T(8,128)(2,1)}, bf16[528,384]{1,0:T(8,128)(2,1)}, u32[]{:S(2)}, u32[]{:S(2)}) collective-permute-start(bf16[528,384]{1,0:T(8,128)(2,1)} %get-tuple-element.54.refs_4_), channel_id=1, source_target_pairs={{0,128},{4,132},{8,136},{12,140},{16,144},{20,148},{24,152},{28,15... | collective-permute-start | bytes 1216520 | tf_op jit(solution)/shard_map/ppermute | solution.py:46
  120.7 25.2 %collective-permute-start.18 = (bf16[528,384]{1,0:T(8,128)(2,1)}, bf16[528,384]{1,0:T(8,128)(2,1)}, u32[]{:S(2)}, u32[]{:S(2)}) collective-permute-start(bf16[528,384]{1,0:T(8,128)(2,1)} %get-tuple-element.54.refs_4_), channel_id=1, source_target_pairs={{0,192},{4,196},{8,200},{12,204},{16,208},{20,212},{24,216},{28,22... | collective-permute-start | bytes 1216520 | tf_op jit(solution)/shard_map/ppermute | solution.py:46
  124.4 21.5 %copy-start.6 = (bf16[4,384,512]{2,1,0:T(8,128)(2,1)S(1)}, bf16[4,384,512]{2,1,0:T(8,128)(2,1)}, u32[]{:S(2)}) copy-start(bf16[4,384,512]{2,1,0:T(8,128)(2,1)} %copy-done.5) | copy-start | bytes 4718596
  124.4 21.5 %copy-start.12 = (bf16[4,384,512]{2,1,0:T(8,128)(2,1)S(1)}, bf16[4,384,512]{2,1,0:T(8,128)(2,1)}, u32[]{:S(2)}) copy-start(bf16[4,384,512]{2,1,0:T(8,128)(2,1)} %copy-done.11) | copy-start | bytes 4718596
  124.4 21.5 %copy-start.14 = (bf16[4,384,512]{2,1,0:T(8,128)(2,1)S(1)}, bf16[4,384,512]{2,1,0:T(8,128)(2,1)}, u32[]{:S(2)}) copy-start(bf16[4,384,512]{2,1,0:T(8,128)(2,1)} %copy-done.13) | copy-start | bytes 4718596
  129.7 24.4 %collective-permute-start.22 = (bf16[512,384]{1,0:T(8,128)(2,1)}, bf16[512,384]{1,0:T(8,128)(2,1)}, u32[]{:S(2)}, u32[]{:S(2)}) collective-permute-start(bf16[512,384]{1,0:T(8,128)(2,1)} %get-tuple-element.56), channel_id=1, source_target_pairs={{0,1},{1,2},{2,3},{3,0},{4,5},{5,6},{6,7},{7,4},{8,9},{9,10},{10,1... | collective-permute-start | bytes 1179656 | tf_op jit(solution)/shard_map/ppermute | solution.py:33
  129.7 25.0 %collective-permute-start.23 = (bf16[512,384]{1,0:T(8,128)(2,1)}, bf16[512,384]{1,0:T(8,128)(2,1)}, u32[]{:S(2)}, u32[]{:S(2)}) collective-permute-start(bf16[512,384]{1,0:T(8,128)(2,1)} %get-tuple-element.60), channel_id=1, source_target_pairs={{0,2},{1,3},{2,0},{3,1},{4,6},{5,7},{6,4},{7,5},{8,10},{9,11},{10,... | collective-permute-start | bytes 1179656 | tf_op jit(solution)/shard_map/ppermute | solution.py:33
  135.1 18.9 %copy-start.15 = (s32[8,8]{1,0:T(8,128)S(1)}, s32[8,8]{1,0:T(8,128)}, u32[]{:S(2)}) copy-start(s32[8,8]{1,0:T(8,128)} %param.9) | copy-start | bytes 772
  135.1 20.3 %collective-permute-start.24 = (bf16[512,384]{1,0:T(8,128)(2,1)}, bf16[512,384]{1,0:T(8,128)(2,1)}, u32[]{:S(2)}, u32[]{:S(2)}) collective-permute-start(bf16[512,384]{1,0:T(8,128)(2,1)} %get-tuple-element.61), channel_id=1, source_target_pairs={{0,3},{1,0},{2,1},{3,2},{4,7},{5,4},{6,5},{7,6},{8,11},{9,8},{10,9... | collective-permute-start | bytes 1179656 | tf_op jit(solution)/shard_map/ppermute | solution.py:33
  150.7 13.1 %copy-start.3 = (bf16[512,384]{1,0:T(8,128)(2,1)S(1)}, bf16[512,384]{1,0:T(8,128)(2,1)}, u32[]{:S(2)}) copy-start(bf16[512,384]{1,0:T(8,128)(2,1)} %refs_1_.7) | copy-start | bytes 1179652
  150.7 13.1 %copy-start.9 = (f32[512,384]{1,0:T(8,128)S(1)}, f32[512,384]{1,0:T(8,128)}, u32[]{:S(2)}) copy-start(f32[512,384]{1,0:T(8,128)} %copy-done.8) | copy-start | bytes 2359300
  150.7 5.4 %collective-permute-start.21 = (bf16[192,1152]{1,0:T(8,128)(2,1)}, bf16[192,1152]{1,0:T(8,128)(2,1)S(1)}, u32[]{:S(2)}, u32[]{:S(2)}) collective-permute-start(bf16[192,1152]{1,0:T(8,128)(2,1)} %get-tuple-element.59), channel_id=1, source_target_pairs={{0,4},{4,0},{8,12},{12,8},{16,20},{20,16},{24,28},{28,24},{32,36},... | collective-permute-start | bytes 1327112 | tf_op jit(solution)/shard_map/ppermute | solution.py:46
  156.8 9.8 %collective-permute-start.25 = (bf16[40,1152]{1,0:T(8,128)(2,1)S(1)}, bf16[40,1152]{1,0:T(8,128)(2,1)S(1)}, u32[]{:S(2)}, u32[]{:S(2)}) collective-permute-start(bf16[40,1152]{1,0:T(8,128)(2,1)S(1)} %get-tuple-element.62), channel_id=1, source_target_pairs={{0,8},{4,12},{8,16},{12,20},{16,24},{20,28},{24,32},{28,36},{32,40... | collective-permute-start | bytes 276488 | tf_op jit(solution)/shard_map/ppermute | solution.py:46
  156.9 23.8 %collective-permute-start.31 = (bf16[40,1152]{1,0:T(8,128)(2,1)S(1)}, bf16[40,1152]{1,0:T(8,128)(2,1)S(1)}, u32[]{:S(2)}, u32[]{:S(2)}) collective-permute-start(bf16[40,1152]{1,0:T(8,128)(2,1)S(1)} %get-tuple-element.68), channel_id=1, source_target_pairs={{0,56},{4,60},{8,0},{12,4},{16,8},{20,12},{24,16},{28,20},{32,24},... | collective-permute-start | bytes 276488 | tf_op jit(solution)/shard_map/ppermute | solution.py:46
  159.5 13.4 %collective-permute-start.26 = (bf16[40,1152]{1,0:T(8,128)(2,1)S(1)}, bf16[40,1152]{1,0:T(8,128)(2,1)S(1)}, u32[]{:S(2)}, u32[]{:S(2)}) collective-permute-start(bf16[40,1152]{1,0:T(8,128)(2,1)S(1)} %get-tuple-element.63), channel_id=1, source_target_pairs={{0,16},{4,20},{8,24},{12,28},{16,32},{20,36},{24,40},{28,44},{32,4... | collective-permute-start | bytes 276488 | tf_op jit(solution)/shard_map/ppermute | solution.py:46
  159.6 14.4 %collective-permute-start.27 = (bf16[40,1152]{1,0:T(8,128)(2,1)S(1)}, bf16[40,1152]{1,0:T(8,128)(2,1)S(1)}, u32[]{:S(2)}, u32[]{:S(2)}) collective-permute-start(bf16[40,1152]{1,0:T(8,128)(2,1)S(1)} %get-tuple-element.64), channel_id=1, source_target_pairs={{0,24},{4,28},{8,32},{12,36},{16,40},{20,44},{24,48},{28,52},{32,5... | collective-permute-start | bytes 276488 | tf_op jit(solution)/shard_map/ppermute | solution.py:46
  159.6 14.4 %collective-permute-start.28 = (bf16[40,1152]{1,0:T(8,128)(2,1)S(1)}, bf16[40,1152]{1,0:T(8,128)(2,1)S(1)}, u32[]{:S(2)}, u32[]{:S(2)}) collective-permute-start(bf16[40,1152]{1,0:T(8,128)(2,1)S(1)} %get-tuple-element.65), channel_id=1, source_target_pairs={{0,32},{4,36},{8,40},{12,44},{16,48},{20,52},{24,56},{28,60},{32,0... | collective-permute-start | bytes 276488 | tf_op jit(solution)/shard_map/ppermute | solution.py:46
  166.6 7.4 %collective-permute-start.29 = (bf16[40,1152]{1,0:T(8,128)(2,1)S(1)}, bf16[40,1152]{1,0:T(8,128)(2,1)S(1)}, u32[]{:S(2)}, u32[]{:S(2)}) collective-permute-start(bf16[40,1152]{1,0:T(8,128)(2,1)S(1)} %get-tuple-element.66), channel_id=1, source_target_pairs={{0,40},{4,44},{8,48},{12,52},{16,56},{20,60},{24,0},{28,4},{32,8},... | collective-permute-start | bytes 276488 | tf_op jit(solution)/shard_map/ppermute | solution.py:46
  173.0 7.7 %collective-permute-start.30 = (bf16[40,1152]{1,0:T(8,128)(2,1)S(1)}, bf16[40,1152]{1,0:T(8,128)(2,1)S(1)}, u32[]{:S(2)}, u32[]{:S(2)}) collective-permute-start(bf16[40,1152]{1,0:T(8,128)(2,1)S(1)} %get-tuple-element.67), channel_id=1, source_target_pairs={{0,48},{4,52},{8,56},{12,60},{16,0},{20,4},{24,8},{28,12},{32,16},... | collective-permute-start | bytes 276488 | tf_op jit(solution)/shard_map/ppermute | solution.py:46
  180.8 2.5 %collective-permute-start.32 = (bf16[8,16,1024]{2,1,0:T(8,128)(2,1)S(1)}, bf16[8,16,1024]{2,1,0:T(8,128)(2,1)S(1)}, u32[]{:S(2)}, u32[]{:S(2)}) collective-permute-start(bf16[8,16,1024]{2,1,0:T(8,128)(2,1)S(1)} %get-tuple-element.81), channel_id=1, source_target_pairs={{0,4},{4,0},{8,12},{12,8},{16,20},{20,16},{24,28},{28,24},{32,36},... | collective-permute-start | bytes 786440 | tf_op jit(solution)/shard_map/ppermute | solution.py:46

commit v4 on v3

--- a/solution.py
+++ b/solution.py
@@ -178,7 +178,7 @@
     tile = 256
     groups = size // BLOCK
 
-    def body(place, b0, b1, b2, b3, weight, cot, out, sums, o0, o1, o2, o3, whole, term):
+    def body(place, b0, b1, b2, b3, weight, cot, out, sums, o0, o1, o2, o3, done, whole, term):
         for r, block in enumerate((b0, b1, b2, b3)):
             whole[:, slot(place, r, width)] = block[...]
         for j in range(wide // tile):
@@ -196,13 +196,14 @@
             term[:, cols] = (cot[:, cols].astype(F32) * sigmoid).astype(BF)
         for r, ref in ((2, o2), (1, o1), (3, o3), (0, o0)):
             ref[...] = times_t(term[...], weight[slot(place, r, width), :]).astype(ref.dtype)
+        done[...] = jnp.zeros_like(done)
 
     block = (size, width)
     return call(
         body,
         place,
         local(blocks + [head_weight, head_cot]),
-        [like((size, wide), BF), like((groups, wide), F32), like(block, F32)] + [like(block, BF)] * 3,
+        [like((size, wide), BF), like((groups, wide), F32), like(block, F32)] + [like(block, BF)] * 3 + [like((8, 128), F32)],
         scratch=[pltpu.VMEM((size, tall), BF), pltpu.VMEM((size, wide), BF)],
         after=after,
         flops=4 * size * tall * wide,
@@ -217,10 +218,9 @@
     size, width = own.shape
     groups, wide = sums.shape
 
-    def body(place, own, c1, c2, c3, sums, total, low, long, below):
+    def body(place, own, c1, c2, c3, sums, total, long, below):
         value = own[...] + c1[...].astype(F32) + c2[...].astype(F32) + c3[...].astype(F32)
         total[...] = value
-        low[...] = value.astype(BF)
         long[:size, :] = value.astype(BF)
         below[...] = jnp.zeros((EXTRA, width), F32)
         for i in range(TAPS):
@@ -232,12 +232,27 @@
         body,
         place,
         local([own] + came + [sums]),
-        [like((size, width), F32), like((size, width), BF), like((size + EXTRA, width), BF)],
+        [like((size, width), F32), like((size + EXTRA, width), BF)],
         scratch=[pltpu.VMEM((EXTRA, width), F32)],
         after=after,
         flops=4 * own.size,
         moved=16 * own.size,
     )
+
+
+def rounded(place, value, after):
+    def body(place, value, out):
+        out[...] = value[...].astype(BF)
+
+    return call(
+        body,
+        place,
+        local([value]),
+        [like(value.shape, BF)],
+        after=after,
+        flops=value.size,
+        moved=200 * value.size,
+    )[0]
 
 
 def back_products(place, around, conv_weight, after):
@@ -245,20 +260,21 @@
     tall = NX * width
     cols = TAPS * width
 
-    def body(place, d0, d1, d2, weight, o0, o1, o2, o3):
+    def body(place, d0, d1, d2, weight, o0, o1, o2, o3, done):
         for r, ref in ((2, o2), (1, o1), (3, o3), (0, o0)):
             at = slot(place, r, width)
             total = times_t(d0[...], weight[0, 0, at, :])
             total += times_t(d1[...], weight[0, 1, at, :])
             total += times_t(d2[...], weight[0, 2, at, :])
             ref[...] = total.astype(ref.dtype)
+        done[...] = jnp.zeros_like(done)
 
     block = (size, width)
     return call(
         body,
         place,
         local(around + [conv_weight]),
-        [like(block, F32)] + [like(block, BF)] * 3,
+        [like(block, F32)] + [like(block, BF)] * 3 + [like((8, 128), F32)],
         after=after,
         flops=2 * size * tall * cols,
         moved=2 * tall * cols,
@@ -338,19 +354,20 @@
 
 
 def input_gradient(place, inputs, grad, own, came, after):
-    def body(place, state, grad, own, c1, c2, c3, out):
+    def body(place, state, grad, own, c1, c2, c3, out, done):
         back_u = own[...] + c1[...].astype(F32) + c2[...].astype(F32) + c3[...].astype(F32)
         out[...] = (grad[...] + activation_slope(state[...].astype(F32), back_u)).astype(BF)
+        done[...] = jnp.zeros_like(done)
 
     return call(
         body,
         place,
         local([inputs, grad, own] + came),
-        [like(inputs.shape, BF)],
+        [like(inputs.shape, BF), like((8, 128), F32)],
         after=after,
         flops=20 * inputs.size,
         moved=16 * inputs.size,
-    )[0]
+    )
 
 
 def coverage_of(blocks, place, exon_blocks, own):
@@ -388,21 +405,22 @@
     turned = [turned[0]] + [along_seq(turned[m], m, 0, 0) for m in range(1, NY)]
 
     head, cot = load(place, [head_weight, head_cot], (token(after_conv),))
-    turned = stacked(place, turned, tuple(token(value) for value in full[1:]))
+    tracks, sums, *blocks, done = track_head(place, full, head, cot, ())
+    turned = stacked(place, turned, (done,))
     before = along_seq(turned, 0, 1, 0)
     behind = along_seq(turned, 0, NZ - 1, 0)
-    tracks, sums, *blocks = track_head(place, full, head, cot, (token(turned),))
     came = [along_x(blocks[r], r) for r in range(1, NX)]
-    (taps,) = load(place, [conv_weight], (token(blocks[1]),))
-    grad, low, long = add_up(place, blocks[0], came, sums, (token(before), token(behind)))
-
+    (taps,) = load(place, [conv_weight], (done,))
+    grad, long = add_up(place, blocks[0], came, sums, ())
+
+    low = rounded(place, grad, (token(long),))
     cots = [long] + [along_seq(long, m, 0, 0) for m in range(1, NY)]
     around = [shifted(low, -steps), low, shifted(low, steps)]
-    blocks = back_products(place, around, taps, ())
+    *blocks, done = back_products(place, around, taps, (token(before), token(behind)))
     came = [along_x(blocks[r], r) for r in range(1, NX)]
-    kept, sent, cover = kernel_terms(place, before, turned, behind, cots, own, (token(blocks[1]),))
-    kept, *parts = over_z(place, kept, along_seq(sent, 0, 0, 1), cover, tuple(token(value) for value in came))
-    out = input_gradient(place, inputs, grad, blocks[0], came, (token(parts[-1]),))
+    kept, sent, cover = kernel_terms(place, before, turned, behind, cots, own, (done,))
+    out, done = input_gradient(place, inputs, grad, blocks[0], came, ())
+    kept, *parts = over_z(place, kept, along_seq(sent, 0, 0, 1), cover, (done,))
     parts = [along_seq(part, 0, m + 1, 0) for m, part in enumerate(parts)]
     for part in parts:
         kept = kept + part[EXTRA:].astype(F32)

time: 185 us -> 182 us (0.984)
  waiting for transfers between devices: 86.8 us -> 79.5 us
  starting transfers between devices: 56 us -> 61.8 us
  local copies, waits for them, and re-layouts: 8.93 us -> 4.88 us
  Pallas kernels: 28.8 us -> 31.5 us
    ppermute x17, waiting for transfers between devices: 49.9 us -> 23.6 us  [along_seq(): return lax.ppermute(value, 'seq', pairs)]
    ppermute x12, waiting for transfers between devices: 26.1 us -> 41.7 us  [along_x(): lax.ppermute(value, 'chan', [(i, (i + steps) % NX) for i in range(NX)])]
    ppermute x17, starting transfers between devices: 29.9 us -> 40 us  [along_seq(): return lax.ppermute(value, 'seq', pairs)]
    ppermute x12, starting transfers between devices: 15.2 us -> 11.7 us  [along_x(): lax.ppermute(value, 'chan', [(i, (i + steps) % NX) for i in range(NX)])]
    ppermute x4, waiting for transfers between devices: 10.8 us -> 14.2 us  [shifted(): lax.ppermute(value, 'seq', [(s, s + steps) for s in range(leading, last)])]
    slice x11 -> x3, local copies, waits for them, and re-layouts: 3.34 us -> 0.01 us  [token(): return value[(0,) * (value.ndim - 2) + (slice(8), slice(128))]]
    pallas_call x12 -> x13, Pallas kernels: 28.8 us -> 31.5 us  [call(): pl.pallas_call(kernel, in_specs=[pl.BlockSpec(memory_space=pltpu.SMEM)] +...]
    unnamed x39 -> x29, local copies, waits for them, and re-layouts: 4.8 us -> 2.75 us
  transfers between devices with their start and end apart: 33 -> 33, of which waited for: 16 -> 18; matrix products, arithmetic and copies ran while one was open for 3% -> 2% of each run, Pallas kernels for 12% -> 14%
where the time goes in v4:
time: 182 us; the launch traced here: 181 us
  waiting for transfers between devices  79.5 us (44%)
  starting transfers between devices  61.8 us (34%)
  Pallas kernels  31.5 us (17%)
  local copies, waits for them, and re-layouts  4.88 us (3%)
    ppermute x12, waiting for transfers between devices, along_x(): lax.ppermute(value, 'chan', [(i, (i + steps) % NX) for i in range(NX)])  41.7 us
    ppermute x17, starting transfers between devices, along_seq(): return lax.ppermute(value, 'seq', pairs)  40 us
    pallas_call x13, Pallas kernels, call(): pl.pallas_call(kernel, in_specs=[pl.BlockSpec(memory_space=pltpu.SMEM)] +...  31.5 us
    ppermute x17, waiting for transfers between devices, along_seq(): return lax.ppermute(value, 'seq', pairs)  23.6 us
    ppermute x4, waiting for transfers between devices, shifted(): lax.ppermute(value, 'seq', [(s, s + steps) for s in range(leading, last)])  14.2 us
    ppermute x12, starting transfers between devices, along_x(): lax.ppermute(value, 'chan', [(i, (i + steps) % NX) for i in range(NX)])  11.7 us
    ppermute x4, starting transfers between devices, shifted(): lax.ppermute(value, 'seq', [(s, s + steps) for s in range(leading, last)])  10.2 us
  transfers between devices with their start and end apart: 33, of which 18 were waited for; matrix products, arithmetic and copies ran while one was open for 2% of the time, Pallas kernels for 14%

profile of v4, /device:TPU:1, one launch (start us, length us, event | category | flops | bytes accessed | tf_op | source)
XLA Modules:
  0.0 181.3 jit_solution(11462956208857067387)
XLA Ops:
  0.6 1.3 fusion.5.refs_1_
  1.9 3.4 %collective-permute-start = (bf16[512,384]{1,0:T(8,128)(2,1)S(1)}, bf16[512,384]{1,0:T(8,128)(2,1)S(1)}, u32[]{:S(2)}, u32[]{:S(2)}) collective-permute-start(bf16[512,384]{1,0:T(8,128)(2,1)S(1)} %fusion.5.refs_1_), channel_id=1, source_target_pairs={{0,3},{1,0},{2,1},{3,2},{4,7},{5,4},{6,5},{7,6},{8,11},{9,8},{10,9... | collective-permute-start | bytes 1179656 | tf_op jit(solution)/shard_map/ppermute | solution.py:33
  5.3 0.5 collective-permute-start.1
  5.8 0.6 collective-permute-start.2
  6.5 2.0 %copy-done = bf16[1,3,1536,384]{3,2,1,0:T(8,128)(2,1)S(1)} copy-done((bf16[1,3,1536,384]{3,2,1,0:T(8,128)(2,1)S(1)}, bf16[1,3,1536,384]{3,2,1,0:T(8,128)(2,1)}, u32[]{:S(2)}) %copy-start) | copy-done | bytes 3538968
  8.5 1.0 shard_map.84.refs_5_
  9.5 6.7 %collective-permute-done.refs_2_ = bf16[512,384]{1,0:T(8,128)(2,1)S(1)} collective-permute-done((bf16[512,384]{1,0:T(8,128)(2,1)S(1)}, bf16[512,384]{1,0:T(8,128)(2,1)S(1)}, u32[]{:S(2)}, u32[]{:S(2)}) %collective-permute-start) | collective-permute-done | bytes 393248 | tf_op jit(solution)/shard_map/ppermute | solution.py:33
  16.1 0.4 collective-permute-done.1.refs_3_
  16.5 9.8 %collective-permute-done.2.refs_4_ = bf16[512,384]{1,0:T(8,128)(2,1)S(1)} collective-permute-done((bf16[512,384]{1,0:T(8,128)(2,1)S(1)}, bf16[512,384]{1,0:T(8,128)(2,1)S(1)}, u32[]{:S(2)}, u32[]{:S(2)}) %collective-permute-start.2) | collective-permute-done | bytes 393248 | tf_op jit(solution)/shard_map/ppermute | solution.py:33
  26.3 3.2 %shard_map.85 = (bf16[512,384]{1,0:T(8,128)(2,1)S(1)}, f32[512,384]{1,0:T(8,128)S(1)}, bf16[512,384]{1,0:T(8,128)(2,1)S(1)}, bf16[512,1536]{1,0:T(8,128)(2,1)S(1)}) custom-call(s32[4]{0:T(128)S(1)} %pad_add_fusion.refs_0_, bf16[512,384]{1,0:T(8,128)(2,1)S(1)} %fusion.5.refs_1_, bf16[512,384]{1,0:T(8,128)(2,1)S(1)} %collective-permute-done.refs_2_, ...), custom_call_target="tpu_custom_call" | custom-call | flops 1811939328 | bytes 3538944 | tf_op jit(solution)/shard_map/pallas_call | solution.py:64
  29.5 3.6 %collective-permute-start.3 = (bf16[512,384]{1,0:T(8,128)(2,1)S(1)}, bf16[512,384]{1,0:T(8,128)(2,1)S(1)}, u32[]{:S(2)}, u32[]{:S(2)}) collective-permute-start(bf16[512,384]{1,0:T(8,128)(2,1)S(1)} %get-tuple-element.42), channel_id=1, source_target_pairs={{0,8},{4,12},{8,16},{12,20},{16,24},{20,28},{24,32},{28,36},{32,40... | collective-permute-start | bytes 1179656 | tf_op jit(solution)/shard_map/ppermute | solution.py:29
  33.0 1.3 collective-permute-start.4
  34.4 6.6 %collective-permute-done.3 = bf16[512,384]{1,0:T(8,128)(2,1)S(1)} collective-permute-done((bf16[512,384]{1,0:T(8,128)(2,1)S(1)}, bf16[512,384]{1,0:T(8,128)(2,1)S(1)}, u32[]{:S(2)}, u32[]{:S(2)}) %collective-permute-start.3) | collective-permute-done | bytes 393248 | tf_op jit(solution)/shard_map/ppermute | solution.py:29
  41.0 4.2 %collective-permute-done.4 = bf16[512,384]{1,0:T(8,128)(2,1)S(1)} collective-permute-done((bf16[512,384]{1,0:T(8,128)(2,1)S(1)}, bf16[512,384]{1,0:T(8,128)(2,1)S(1)}, u32[]{:S(2)}, u32[]{:S(2)}) %collective-permute-start.4) | collective-permute-done | bytes 393248 | tf_op jit(solution)/shard_map/ppermute | solution.py:29
  45.5 0.6 collective-permute-start.6
  46.1 0.9 collective-permute-start.7
  46.9 1.0 shard_map.88
  47.9 4.7 %collective-permute-start.10 = (bf16[384,512]{1,0:T(8,128)(2,1)S(1)}, bf16[384,512]{1,0:T(8,128)(2,1)S(1)}, u32[]{:S(2)}, u32[]{:S(2)}) collective-permute-start(bf16[384,512]{1,0:T(8,128)(2,1)S(1)} %get-tuple-element.51), channel_id=1, source_target_pairs={{0,192},{4,196},{8,200},{12,204},{16,208},{20,212},{24,216},{28,22... | collective-permute-start | bytes 1179656 | tf_op jit(solution)/shard_map/ppermute | solution.py:46
  52.6 2.0 %collective-permute-done.5.refs_2_ = bf16[512,384]{1,0:T(8,128)(2,1)S(1)} collective-permute-done((bf16[512,384]{1,0:T(8,128)(2,1)S(1)}, bf16[512,384]{1,0:T(8,128)(2,1)S(1)}, u32[]{:S(2)}, u32[]{:S(2)}) %collective-permute-start.5) | collective-permute-done | bytes 393248 | tf_op jit(solution)/shard_map/ppermute | solution.py:33
  54.6 4.6 %collective-permute-start.9 = (bf16[384,512]{1,0:T(8,128)(2,1)S(1)}, bf16[384,512]{1,0:T(8,128)(2,1)S(1)}, u32[]{:S(2)}, u32[]{:S(2)}) collective-permute-start(bf16[384,512]{1,0:T(8,128)(2,1)S(1)} %get-tuple-element.50), channel_id=1, source_target_pairs={{0,128},{4,132},{8,136},{12,140},{16,144},{20,148},{24,152},{28,15... | collective-permute-start | bytes 1179656 | tf_op jit(solution)/shard_map/ppermute | solution.py:46
  59.2 0.8 shard_map.86
  60.1 6.4 %collective-permute-done.7.refs_4_ = bf16[512,384]{1,0:T(8,128)(2,1)S(1)} collective-permute-done((bf16[512,384]{1,0:T(8,128)(2,1)S(1)}, bf16[512,384]{1,0:T(8,128)(2,1)S(1)}, u32[]{:S(2)}, u32[]{:S(2)}) %collective-permute-start.7) | collective-permute-done | bytes 393248 | tf_op jit(solution)/shard_map/ppermute | solution.py:33
  66.5 6.9 %shard_map.87 = (bf16[512,1024]{1,0:T(8,128)(2,1)}, f32[4,1024]{1,0:T(4,128)S(1)}, f32[512,384]{1,0:T(8,128)S(1)}, bf16[512,384]{1,0:T(8,128)(2,1)}, bf16[512,38...) custom-call(s32[4]{0:T(128)S(1)} %pad_add_fusion.refs_0_, bf16[512,384]{1,0:T(8,128)(2,1)S(1)} %fusion.6.refs_1_, ...), custom_call_target="tpu_custom_call" | custom-call | flops 3221225472 | bytes 3145728 | tf_op jit(solution)/shard_map/pallas_call | solution.py:64
  73.4 1.8 %shard_map.89.refs_2_ = bf16[4,384,512]{2,1,0:T(8,128)(2,1)} custom-call(s32[4]{0:T(128)S(1)} %pad_add_fusion.refs_0_, bf16[384,512]{1,0:T(8,128)(2,1)S(1)} %get-tuple-element.48.refs_1_, bf16[384,512]{1,0:T(8,128)(2,1)S(1)} %collective-permute-done.8.refs_2_, bf16[384,512]{1,0:T(8,128)(2,1)S(1)} %collective-permute-done.9.refs_3_, ...), custom_call_target="tpu_custom_call" | custom-call | bytes 3145728 | tf_op jit(solution)/shard_map/pallas_call | solution.py:64
  75.3 6.0 %collective-permute-start.12 = (bf16[4,384,512]{2,1,0:T(8,128)(2,1)}, bf16[4,384,512]{2,1,0:T(8,128)(2,1)}, u32[]{:S(2)}, u32[]{:S(2)}) collective-permute-start(bf16[4,384,512]{2,1,0:T(8,128)(2,1)} %shard_map.89.refs_2_), channel_id=1, source_target_pairs={{0,56},{4,60},{8,0},{12,4},{16,8},{20,12},{24,16},{28,20},{32,24},... | collective-permute-start | bytes 4718600 | tf_op jit(solution)/shard_map/ppermute | solution.py:46
  81.3 0.5 collective-permute-start.14
  81.8 2.2 %collective-permute-start.15 = (bf16[512,384]{1,0:T(8,128)(2,1)}, bf16[512,384]{1,0:T(8,128)(2,1)}, u32[]{:S(2)}, u32[]{:S(2)}) collective-permute-start(bf16[512,384]{1,0:T(8,128)(2,1)} %get-tuple-element.56), channel_id=1, source_target_pairs={{0,3},{1,0},{2,1},{3,2},{4,7},{5,4},{6,5},{7,6},{8,11},{9,8},{10,9... | collective-permute-start | bytes 1179656 | tf_op jit(solution)/shard_map/ppermute | solution.py:33
  84.0 1.0 shard_map.92.refs_4_
  85.0 16.2 %collective-permute-done.13.refs_2_ = bf16[512,384]{1,0:T(8,128)(2,1)} collective-permute-done((bf16[512,384]{1,0:T(8,128)(2,1)}, bf16[512,384]{1,0:T(8,128)(2,1)}, u32[]{:S(2)}, u32[]{:S(2)}) %collective-permute-start.13) | collective-permute-done | bytes 393248 | tf_op jit(solution)/shard_map/ppermute | solution.py:33
  101.1 0.3 collective-permute-done.15.refs_4_
  101.5 1.6 shard_map.90
  103.1 0.6 shard_map.91.refs_2_
  103.7 1.3 collective-permute-start.19
  105.0 4.0 %collective-permute-start.20 = (bf16[512,384]{1,0:T(8,128)(2,1)S(1)}, bf16[512,384]{1,0:T(8,128)(2,1)S(1)}, u32[]{:S(2)}, u32[]{:S(2)}) collective-permute-start(bf16[512,384]{1,0:T(8,128)(2,1)S(1)} %shard_map.91.refs_2_), channel_id=1, source_target_pairs={{0,8},{4,12},{8,16},{12,20},{16,24},{20,28},{24,32},{28,36},{32,40... | collective-permute-start | bytes 1179656 | tf_op jit(solution)/shard_map/ppermute | solution.py:29
  109.0 2.2 %collective-permute-start.16 = (bf16[528,384]{1,0:T(8,128)(2,1)S(1)}, bf16[528,384]{1,0:T(8,128)(2,1)S(1)}, u32[]{:S(2)}, u32[]{:S(2)}) collective-permute-start(bf16[528,384]{1,0:T(8,128)(2,1)S(1)} %get-tuple-element.58.refs_4_), channel_id=1, source_target_pairs={{0,64},{4,68},{8,72},{12,76},{16,80},{20,84},{24,88},{28,92},{32,9... | collective-permute-start | bytes 1216520 | tf_op jit(solution)/shard_map/ppermute | solution.py:46
  111.2 3.7 %collective-permute-done.12.refs_3_ = bf16[4,384,512]{2,1,0:T(8,128)(2,1)} collective-permute-done((bf16[4,384,512]{2,1,0:T(8,128)(2,1)}, bf16[4,384,512]{2,1,0:T(8,128)(2,1)}, u32[]{:S(2)}, u32[]{:S(2)}) %collective-permute-start.12) | collective-permute-done | bytes 1572896 | tf_op jit(solution)/shard_map/ppermute | solution.py:46
  114.9 2.9 %collective-permute-start.17 = (bf16[528,384]{1,0:T(8,128)(2,1)S(1)}, bf16[528,384]{1,0:T(8,128)(2,1)S(1)}, u32[]{:S(2)}, u32[]{:S(2)}) collective-permute-start(bf16[528,384]{1,0:T(8,128)(2,1)S(1)} %get-tuple-element.58.refs_4_), channel_id=1, source_target_pairs={{0,128},{4,132},{8,136},{12,140},{16,144},{20,148},{24,152},{28,15... | collective-permute-start | bytes 1216520 | tf_op jit(solution)/shard_map/ppermute | solution.py:46
  118.0 0.6 collective-permute-start.18
  118.5 0.7 slice_bitcast_fusion.7.refs_6_
  119.2 0.7 slice_bitcast_fusion.8.refs_5_
  119.9 3.4 %collective-permute-done.20.refs_3_ = bf16[512,384]{1,0:T(8,128)(2,1)S(1)} collective-permute-done((bf16[512,384]{1,0:T(8,128)(2,1)S(1)}, bf16[512,384]{1,0:T(8,128)(2,1)S(1)}, u32[]{:S(2)}, u32[]{:S(2)}) %collective-permute-start.20) | collective-permute-done | bytes 393248 | tf_op jit(solution)/shard_map/ppermute | solution.py:29
  123.2 4.4 %shard_map.93 = (f32[512,384]{1,0:T(8,128)S(1)}, bf16[512,384]{1,0:T(8,128)(2,1)}, bf16[512,384]{1,0:T(8,128)(2,1)}, bf16[512,384]{1,0:T(8,128)(2,1)}, f32[8,128]{1,0:T(8,128)S(1)}) custom-call(s32[4]{0:T(128)S(1)} %pad_add_fusion.refs_0_, bf16[512,384]{1,0:T(8,128)(2,1)S(1)} %collective-permute-done.19.refs_1_, bf16[512,384]{1,0:T(8,128)(2,1)S(1)} %shard_map.91.refs_2_, ...), custom_call_target="tpu_custom_call" | custom-call | flops 1811939328 | bytes 3538944 | tf_op jit(solution)/shard_map/pallas_call | solution.py:64
  127.6 0.5 collective-permute-start.23
  128.1 2.4 %collective-permute-start.24 = (bf16[512,384]{1,0:T(8,128)(2,1)}, bf16[512,384]{1,0:T(8,128)(2,1)}, u32[]{:S(2)}, u32[]{:S(2)}) collective-permute-start(bf16[512,384]{1,0:T(8,128)(2,1)} %get-tuple-element.67), channel_id=1, source_target_pairs={{0,3},{1,0},{2,1},{3,2},{4,7},{5,4},{6,5},{7,6},{8,11},{9,8},{10,9... | collective-permute-start | bytes 1179656 | tf_op jit(solution)/shard_map/ppermute | solution.py:33
  130.6 7.6 %collective-permute-done.17.refs_6_ = bf16[528,384]{1,0:T(8,128)(2,1)S(1)} collective-permute-done((bf16[528,384]{1,0:T(8,128)(2,1)S(1)}, bf16[528,384]{1,0:T(8,128)(2,1)S(1)}, u32[]{:S(2)}, u32[]{:S(2)}) %collective-permute-start.17) | collective-permute-done | bytes 405536 | tf_op jit(solution)/shard_map/ppermute | solution.py:46
  138.1 5.8 %shard_map.94 = (f32[192,1152]{1,0:T(8,128)S(1)}, bf16[192,1152]{1,0:T(8,128)(2,1)}, f32[16,1152]{1,0:T(8,128)S(1)}) custom-call(s32[4]{0:T(128)S(1)} %pad_add_fusion.refs_0_, bf16[4,384,512]{2,1,0:T(8,128)(2,1)} %collective-permute-done.11.refs_1_, bf16[4,384,512]{2,1,0:T(8,128)(2,1)} %shard_map.89.refs_2_, ...), custom_call_target="tpu_custom_call" | custom-call | flops 1811939328 | bytes 6291456 | tf_op jit(solution)/shard_map/pallas_call | solution.py:64
  144.0 3.4 %collective-permute-start.21 = (bf16[192,1152]{1,0:T(8,128)(2,1)}, bf16[192,1152]{1,0:T(8,128)(2,1)S(1)}, u32[]{:S(2)}, u32[]{:S(2)}) collective-permute-start(bf16[192,1152]{1,0:T(8,128)(2,1)} %get-tuple-element.63), channel_id=1, source_target_pairs={{0,4},{4,0},{8,12},{12,8},{16,20},{20,16},{24,28},{28,24},{32,36},... | collective-permute-start | bytes 1327112 | tf_op jit(solution)/shard_map/ppermute | solution.py:46
  148.3 2.7 %shard_map.95 = (bf16[512,384]{1,0:T(8,128)(2,1)}, f32[8,128]{1,0:T(8,128)S(1)}) custom-call(s32[4]{0:T(128)S(1)} %pad_add_fusion.refs_0_, bf16[512,384]{1,0:T(8,128)(2,1)S(1)} %copy-done.3, f32[512,384]{1,0:T(8,128)S(1)} %get-tuple-element.59.refs_1_.refs_2_, f32[512,384]{1,0:T(8,128)S(1)} %get-tuple-element.64.refs_3_, ...), custom_call_target="tpu_custom_call" | custom-call | flops 3932160 | bytes 3145728 | tf_op jit(solution)/shard_map/pallas_call | solution.py:64
  151.0 0.7 shard_map.96
  151.7 1.6 collective-permute-start.25
  153.3 1.8 %collective-permute-start.26 = (bf16[40,1152]{1,0:T(8,128)(2,1)S(1)}, bf16[40,1152]{1,0:T(8,128)(2,1)S(1)}, u32[]{:S(2)}, u32[]{:S(2)}) collective-permute-start(bf16[40,1152]{1,0:T(8,128)(2,1)S(1)} %get-tuple-element.70), channel_id=1, source_target_pairs={{0,16},{4,20},{8,24},{12,28},{16,32},{20,36},{24,40},{28,44},{32,4... | collective-permute-start | bytes 276488 | tf_op jit(solution)/shard_map/ppermute | solution.py:46
  155.1 2.2 %collective-permute-start.27 = (bf16[40,1152]{1,0:T(8,128)(2,1)S(1)}, bf16[40,1152]{1,0:T(8,128)(2,1)S(1)}, u32[]{:S(2)}, u32[]{:S(2)}) collective-permute-start(bf16[40,1152]{1,0:T(8,128)(2,1)S(1)} %get-tuple-element.71), channel_id=1, source_target_pairs={{0,24},{4,28},{8,32},{12,36},{16,40},{20,44},{24,48},{28,52},{32,5... | collective-permute-start | bytes 276488 | tf_op jit(solution)/shard_map/ppermute | solution.py:46
  157.2 2.5 %collective-permute-start.28 = (bf16[40,1152]{1,0:T(8,128)(2,1)S(1)}, bf16[40,1152]{1,0:T(8,128)(2,1)S(1)}, u32[]{:S(2)}, u32[]{:S(2)}) collective-permute-start(bf16[40,1152]{1,0:T(8,128)(2,1)S(1)} %get-tuple-element.72), channel_id=1, source_target_pairs={{0,32},{4,36},{8,40},{12,44},{16,48},{20,52},{24,56},{28,60},{32,0... | collective-permute-start | bytes 276488 | tf_op jit(solution)/shard_map/ppermute | solution.py:46
  159.8 4.5 %collective-permute-start.29 = (bf16[40,1152]{1,0:T(8,128)(2,1)S(1)}, bf16[40,1152]{1,0:T(8,128)(2,1)S(1)}, u32[]{:S(2)}, u32[]{:S(2)}) collective-permute-start(bf16[40,1152]{1,0:T(8,128)(2,1)S(1)} %get-tuple-element.73), channel_id=1, source_target_pairs={{0,40},{4,44},{8,48},{12,52},{16,56},{20,60},{24,0},{28,4},{32,8},... | collective-permute-start | bytes 276488 | tf_op jit(solution)/shard_map/ppermute | solution.py:46
  164.2 0.8 collective-permute-start.30
  165.0 1.4 collective-permute-start.31
  166.5 5.7 %collective-permute-done.28 = bf16[40,1152]{1,0:T(8,128)(2,1)S(1)} collective-permute-done((bf16[40,1152]{1,0:T(8,128)(2,1)S(1)}, bf16[40,1152]{1,0:T(8,128)(2,1)S(1)}, u32[]{:S(2)}, u32[]{:S(2)}) %collective-permute-start.28) | collective-permute-done | bytes 92192 | tf_op jit(solution)/shard_map/ppermute | solution.py:46
  172.2 1.0 collective-permute-done.29
  173.2 2.6 %collective-permute-done.30 = bf16[40,1152]{1,0:T(8,128)(2,1)S(1)} collective-permute-done((bf16[40,1152]{1,0:T(8,128)(2,1)S(1)}, bf16[40,1152]{1,0:T(8,128)(2,1)S(1)}, u32[]{:S(2)}, u32[]{:S(2)}) %collective-permute-start.30) | collective-permute-done | bytes 92192 | tf_op jit(solution)/shard_map/ppermute | solution.py:46
  175.9 2.4 %collective-permute-done.31 = bf16[40,1152]{1,0:T(8,128)(2,1)S(1)} collective-permute-done((bf16[40,1152]{1,0:T(8,128)(2,1)S(1)}, bf16[40,1152]{1,0:T(8,128)(2,1)S(1)}, u32[]{:S(2)}, u32[]{:S(2)}) %collective-permute-start.31) | collective-permute-done | bytes 92192 | tf_op jit(solution)/shard_map/ppermute | solution.py:46
  178.3 0.9 collective-permute-start.32
  179.4 0.7 copy.11
  180.0 0.4 collective-permute-done.32
  180.5 0.8 convolution_multiply_fusion
  (72 shorter events, 1.7 us)
Async XLA Ops:
  1.9 14.2 %collective-permute-start = (bf16[512,384]{1,0:T(8,128)(2,1)S(1)}, bf16[512,384]{1,0:T(8,128)(2,1)S(1)}, u32[]{:S(2)}, u32[]{:S(2)}) collective-permute-start(bf16[512,384]{1,0:T(8,128)(2,1)S(1)} %fusion.5.refs_1_), channel_id=1, source_target_pairs={{0,3},{1,0},{2,1},{3,2},{4,7},{5,4},{6,5},{7,6},{8,11},{9,8},{10,9... | collective-permute-start | bytes 1179656 | tf_op jit(solution)/shard_map/ppermute | solution.py:33
  5.3 11.2 %collective-permute-start.1 = (bf16[512,384]{1,0:T(8,128)(2,1)S(1)}, bf16[512,384]{1,0:T(8,128)(2,1)S(1)}, u32[]{:S(2)}, u32[]{:S(2)}) collective-permute-start(bf16[512,384]{1,0:T(8,128)(2,1)S(1)} %fusion.5.refs_1_), channel_id=1, source_target_pairs={{0,2},{1,3},{2,0},{3,1},{4,6},{5,7},{6,4},{7,5},{8,10},{9,11},{10,... | collective-permute-start | bytes 1179656 | tf_op jit(solution)/shard_map/ppermute | solution.py:33
  5.8 20.4 %collective-permute-start.2 = (bf16[512,384]{1,0:T(8,128)(2,1)S(1)}, bf16[512,384]{1,0:T(8,128)(2,1)S(1)}, u32[]{:S(2)}, u32[]{:S(2)}) collective-permute-start(bf16[512,384]{1,0:T(8,128)(2,1)S(1)} %fusion.5.refs_1_), channel_id=1, source_target_pairs={{0,1},{1,2},{2,3},{3,0},{4,5},{5,6},{6,7},{7,4},{8,9},{9,10},{10,1... | collective-permute-start | bytes 1179656 | tf_op jit(solution)/shard_map/ppermute | solution.py:33
  6.5 2.0 %copy-start = (bf16[1,3,1536,384]{3,2,1,0:T(8,128)(2,1)S(1)}, bf16[1,3,1536,384]{3,2,1,0:T(8,128)(2,1)}, u32[]{:S(2)}) copy-start(bf16[1,3,1536,384]{3,2,1,0:T(8,128)(2,1)} %refs_1_.6) | copy-start | bytes 10616836
  9.5 35.7 %copy-start.2 = (bf16[512,384]{1,0:T(8,128)(2,1)S(1)}, bf16[512,384]{1,0:T(8,128)(2,1)}, u32[]{:S(2)}) copy-start(bf16[512,384]{1,0:T(8,128)(2,1)} %refs_1_.7) | copy-start | bytes 1179652
  26.3 33.0 %copy-start.5 = (bf16[512,1024]{1,0:T(8,128)(2,1)S(1)}, bf16[512,1024]{1,0:T(8,128)(2,1)}, u32[]{:S(2)}) copy-start(bf16[512,1024]{1,0:T(8,128)(2,1)} %refs_2_.1) | copy-start | bytes 3145732
  29.5 11.5 %collective-permute-start.3 = (bf16[512,384]{1,0:T(8,128)(2,1)S(1)}, bf16[512,384]{1,0:T(8,128)(2,1)S(1)}, u32[]{:S(2)}, u32[]{:S(2)}) collective-permute-start(bf16[512,384]{1,0:T(8,128)(2,1)S(1)} %get-tuple-element.42), channel_id=1, source_target_pairs={{0,8},{4,12},{8,16},{12,20},{16,24},{20,28},{24,32},{28,36},{32,40... | collective-permute-start | bytes 1179656 | tf_op jit(solution)/shard_map/ppermute | solution.py:29
  33.0 12.1 %collective-permute-start.4 = (bf16[512,384]{1,0:T(8,128)(2,1)S(1)}, bf16[512,384]{1,0:T(8,128)(2,1)S(1)}, u32[]{:S(2)}, u32[]{:S(2)}) collective-permute-start(bf16[512,384]{1,0:T(8,128)(2,1)S(1)} %get-tuple-element.43), channel_id=1, source_target_pairs={{8,0},{12,4},{16,8},{20,12},{24,16},{28,20},{32,24},{36,28},{40,32... | collective-permute-start | bytes 1179656 | tf_op jit(solution)/shard_map/ppermute | solution.py:29
  45.2 14.1 %copy-start.4 = (bf16[1536,1024]{1,0:T(8,128)(2,1)S(1)}, bf16[1536,1024]{1,0:T(8,128)(2,1)}, u32[]{:S(2)}) copy-start(bf16[1536,1024]{1,0:T(8,128)(2,1)} %refs_1_.5) | copy-start | bytes 9437188
  45.4 9.2 %collective-permute-start.5 = (bf16[512,384]{1,0:T(8,128)(2,1)S(1)}, bf16[512,384]{1,0:T(8,128)(2,1)S(1)}, u32[]{:S(2)}, u32[]{:S(2)}) collective-permute-start(bf16[512,384]{1,0:T(8,128)(2,1)S(1)} %fusion.6.refs_1_), channel_id=1, source_target_pairs={{0,3},{1,0},{2,1},{3,2},{4,7},{5,4},{6,5},{7,6},{8,11},{9,8},{10,9... | collective-permute-start | bytes 1179656 | tf_op jit(solution)/shard_map/ppermute | solution.py:33
  45.5 14.6 %collective-permute-start.6 = (bf16[512,384]{1,0:T(8,128)(2,1)S(1)}, bf16[512,384]{1,0:T(8,128)(2,1)S(1)}, u32[]{:S(2)}, u32[]{:S(2)}) collective-permute-start(bf16[512,384]{1,0:T(8,128)(2,1)S(1)} %fusion.6.refs_1_), channel_id=1, source_target_pairs={{0,2},{1,3},{2,0},{3,1},{4,6},{5,7},{6,4},{7,5},{8,10},{9,11},{10,... | collective-permute-start | bytes 1179656 | tf_op jit(solution)/shard_map/ppermute | solution.py:33
  46.1 20.5 %collective-permute-start.7 = (bf16[512,384]{1,0:T(8,128)(2,1)S(1)}, bf16[512,384]{1,0:T(8,128)(2,1)S(1)}, u32[]{:S(2)}, u32[]{:S(2)}) collective-permute-start(bf16[512,384]{1,0:T(8,128)(2,1)S(1)} %fusion.6.refs_1_), channel_id=1, source_target_pairs={{0,1},{1,2},{2,3},{3,0},{4,5},{5,6},{6,7},{7,4},{8,9},{9,10},{10,1... | collective-permute-start | bytes 1179656 | tf_op jit(solution)/shard_map/ppermute | solution.py:33
  47.9 25.5 %collective-permute-start.10 = (bf16[384,512]{1,0:T(8,128)(2,1)S(1)}, bf16[384,512]{1,0:T(8,128)(2,1)S(1)}, u32[]{:S(2)}, u32[]{:S(2)}) collective-permute-start(bf16[384,512]{1,0:T(8,128)(2,1)S(1)} %get-tuple-element.51), channel_id=1, source_target_pairs={{0,192},{4,196},{8,200},{12,204},{16,208},{20,212},{24,216},{28,22... | collective-permute-start | bytes 1179656 | tf_op jit(solution)/shard_map/ppermute | solution.py:46
  52.6 20.8 %collective-permute-start.8 = (bf16[384,512]{1,0:T(8,128)(2,1)S(1)}, bf16[384,512]{1,0:T(8,128)(2,1)S(1)}, u32[]{:S(2)}, u32[]{:S(2)}) collective-permute-start(bf16[384,512]{1,0:T(8,128)(2,1)S(1)} %get-tuple-element.49), channel_id=1, source_target_pairs={{0,64},{4,68},{8,72},{12,76},{16,80},{20,84},{24,88},{28,92},{32,9... | collective-permute-start | bytes 1179656 | tf_op jit(solution)/shard_map/ppermute | solution.py:46
  54.6 18.8 %collective-permute-start.9 = (bf16[384,512]{1,0:T(8,128)(2,1)S(1)}, bf16[384,512]{1,0:T(8,128)(2,1)S(1)}, u32[]{:S(2)}, u32[]{:S(2)}) collective-permute-start(bf16[384,512]{1,0:T(8,128)(2,1)S(1)} %get-tuple-element.50), channel_id=1, source_target_pairs={{0,128},{4,132},{8,136},{12,140},{16,144},{20,148},{24,152},{28,15... | collective-permute-start | bytes 1179656 | tf_op jit(solution)/shard_map/ppermute | solution.py:46
  66.5 17.5 %copy-start.1 = (bf16[1,3,1536,384]{3,2,1,0:T(8,128)(2,1)S(1)}, bf16[1,3,1536,384]{3,2,1,0:T(8,128)(2,1)}, u32[]{:S(2)}) copy-start(bf16[1,3,1536,384]{3,2,1,0:T(8,128)(2,1)} %refs_1_.6) | copy-start | bytes 10616836
  73.4 1.9 %copy-start.6 = (f32[512,384]{1,0:T(8,128)}, f32[512,384]{1,0:T(8,128)S(1)}, u32[]{:S(2)}) copy-start(f32[512,384]{1,0:T(8,128)S(1)} %get-tuple-element.53.refs_1_) | copy-start | bytes 2359300
  73.4 1.9 %copy-start.8 = (f32[4,1024]{1,0:T(4,128)}, f32[4,1024]{1,0:T(4,128)S(1)}, u32[]{:S(2)}) copy-start(f32[4,1024]{1,0:T(4,128)S(1)} %get-tuple-element.57.refs_5_) | copy-start | bytes 49156
  75.3 39.6 %collective-permute-start.12 = (bf16[4,384,512]{2,1,0:T(8,128)(2,1)}, bf16[4,384,512]{2,1,0:T(8,128)(2,1)}, u32[]{:S(2)}, u32[]{:S(2)}) collective-permute-start(bf16[4,384,512]{2,1,0:T(8,128)(2,1)} %shard_map.89.refs_2_), channel_id=1, source_target_pairs={{0,56},{4,60},{8,0},{12,4},{16,8},{20,12},{24,16},{28,20},{32,24},... | collective-permute-start | bytes 4718600 | tf_op jit(solution)/shard_map/ppermute | solution.py:46
  81.3 36.7 %collective-permute-start.11 = (bf16[4,384,512]{2,1,0:T(8,128)(2,1)}, bf16[4,384,512]{2,1,0:T(8,128)(2,1)}, u32[]{:S(2)}, u32[]{:S(2)}) collective-permute-start(bf16[4,384,512]{2,1,0:T(8,128)(2,1)} %shard_map.89.refs_2_), channel_id=1, source_target_pairs={{0,8},{4,12},{8,16},{12,20},{16,24},{20,28},{24,32},{28,36},{32,40... | collective-permute-start | bytes 4718600 | tf_op jit(solution)/shard_map/ppermute | solution.py:46
  81.3 19.8 %collective-permute-start.13 = (bf16[512,384]{1,0:T(8,128)(2,1)}, bf16[512,384]{1,0:T(8,128)(2,1)}, u32[]{:S(2)}, u32[]{:S(2)}) collective-permute-start(bf16[512,384]{1,0:T(8,128)(2,1)} %get-tuple-element.54), channel_id=1, source_target_pairs={{0,1},{1,2},{2,3},{3,0},{4,5},{5,6},{6,7},{7,4},{8,9},{9,10},{10,1... | collective-permute-start | bytes 1179656 | tf_op jit(solution)/shard_map/ppermute | solution.py:33
  81.3 19.8 %collective-permute-start.14 = (bf16[512,384]{1,0:T(8,128)(2,1)}, bf16[512,384]{1,0:T(8,128)(2,1)}, u32[]{:S(2)}, u32[]{:S(2)}) collective-permute-start(bf16[512,384]{1,0:T(8,128)(2,1)} %get-tuple-element.55), channel_id=1, source_target_pairs={{0,2},{1,3},{2,0},{3,1},{4,6},{5,7},{6,4},{7,5},{8,10},{9,11},{10,... | collective-permute-start | bytes 1179656 | tf_op jit(solution)/shard_map/ppermute | solution.py:33
  81.8 19.7 %collective-permute-start.15 = (bf16[512,384]{1,0:T(8,128)(2,1)}, bf16[512,384]{1,0:T(8,128)(2,1)}, u32[]{:S(2)}, u32[]{:S(2)}) collective-permute-start(bf16[512,384]{1,0:T(8,128)(2,1)} %get-tuple-element.56), channel_id=1, source_target_pairs={{0,3},{1,0},{2,1},{3,2},{4,7},{5,4},{6,5},{7,6},{8,11},{9,8},{10,9... | collective-permute-start | bytes 1179656 | tf_op jit(solution)/shard_map/ppermute | solution.py:33
  84.0 17.5 %copy-start.7 = (f32[512,384]{1,0:T(8,128)S(1)}, f32[512,384]{1,0:T(8,128)}, u32[]{:S(2)}) copy-start(f32[512,384]{1,0:T(8,128)} %copy-done.6) | copy-start | bytes 2359300
  84.0 17.5 %copy-start.9 = (f32[4,1024]{1,0:T(4,128)S(1)}, f32[4,1024]{1,0:T(4,128)}, u32[]{:S(2)}) copy-start(f32[4,1024]{1,0:T(4,128)} %copy-done.8) | copy-start | bytes 49156
  103.7 16.2 %collective-permute-start.19 = (bf16[512,384]{1,0:T(8,128)(2,1)S(1)}, bf16[512,384]{1,0:T(8,128)(2,1)S(1)}, u32[]{:S(2)}, u32[]{:S(2)}) collective-permute-start(bf16[512,384]{1,0:T(8,128)(2,1)S(1)} %shard_map.91.refs_2_), channel_id=1, source_target_pairs={{8,0},{12,4},{16,8},{20,12},{24,16},{28,20},{32,24},{36,28},{40,32... | collective-permute-start | bytes 1179656 | tf_op jit(solution)/shard_map/ppermute | solution.py:29
  105.0 18.3 %collective-permute-start.20 = (bf16[512,384]{1,0:T(8,128)(2,1)S(1)}, bf16[512,384]{1,0:T(8,128)(2,1)S(1)}, u32[]{:S(2)}, u32[]{:S(2)}) collective-permute-start(bf16[512,384]{1,0:T(8,128)(2,1)S(1)} %shard_map.91.refs_2_), channel_id=1, source_target_pairs={{0,8},{4,12},{8,16},{12,20},{16,24},{20,28},{24,32},{28,36},{32,40... | collective-permute-start | bytes 1179656 | tf_op jit(solution)/shard_map/ppermute | solution.py:29
  109.0 19.1 %collective-permute-start.16 = (bf16[528,384]{1,0:T(8,128)(2,1)S(1)}, bf16[528,384]{1,0:T(8,128)(2,1)S(1)}, u32[]{:S(2)}, u32[]{:S(2)}) collective-permute-start(bf16[528,384]{1,0:T(8,128)(2,1)S(1)} %get-tuple-element.58.refs_4_), channel_id=1, source_target_pairs={{0,64},{4,68},{8,72},{12,76},{16,80},{20,84},{24,88},{28,92},{32,9... | collective-permute-start | bytes 1216520 | tf_op jit(solution)/shard_map/ppermute | solution.py:46
  114.9 23.2 %collective-permute-start.17 = (bf16[528,384]{1,0:T(8,128)(2,1)S(1)}, bf16[528,384]{1,0:T(8,128)(2,1)S(1)}, u32[]{:S(2)}, u32[]{:S(2)}) collective-permute-start(bf16[528,384]{1,0:T(8,128)(2,1)S(1)} %get-tuple-element.58.refs_4_), channel_id=1, source_target_pairs={{0,128},{4,132},{8,136},{12,140},{16,144},{20,148},{24,152},{28,15... | collective-permute-start | bytes 1216520 | tf_op jit(solution)/shard_map/ppermute | solution.py:46
  118.0 20.1 %collective-permute-start.18 = (bf16[528,384]{1,0:T(8,128)(2,1)S(1)}, bf16[528,384]{1,0:T(8,128)(2,1)S(1)}, u32[]{:S(2)}, u32[]{:S(2)}) collective-permute-start(bf16[528,384]{1,0:T(8,128)(2,1)S(1)} %get-tuple-element.58.refs_4_), channel_id=1, source_target_pairs={{0,192},{4,196},{8,200},{12,204},{16,208},{20,212},{24,216},{28,22... | collective-permute-start | bytes 1216520 | tf_op jit(solution)/shard_map/ppermute | solution.py:46
  127.6 20.6 %collective-permute-start.22 = (bf16[512,384]{1,0:T(8,128)(2,1)}, bf16[512,384]{1,0:T(8,128)(2,1)}, u32[]{:S(2)}, u32[]{:S(2)}) collective-permute-start(bf16[512,384]{1,0:T(8,128)(2,1)} %get-tuple-element.65), channel_id=1, source_target_pairs={{0,1},{1,2},{2,3},{3,0},{4,5},{5,6},{6,7},{7,4},{8,9},{9,10},{10,1... | collective-permute-start | bytes 1179656 | tf_op jit(solution)/shard_map/ppermute | solution.py:33
  127.6 20.6 %collective-permute-start.23 = (bf16[512,384]{1,0:T(8,128)(2,1)}, bf16[512,384]{1,0:T(8,128)(2,1)}, u32[]{:S(2)}, u32[]{:S(2)}) collective-permute-start(bf16[512,384]{1,0:T(8,128)(2,1)} %get-tuple-element.66), channel_id=1, source_target_pairs={{0,2},{1,3},{2,0},{3,1},{4,6},{5,7},{6,4},{7,5},{8,10},{9,11},{10,... | collective-permute-start | bytes 1179656 | tf_op jit(solution)/shard_map/ppermute | solution.py:33
  128.1 20.1 %collective-permute-start.24 = (bf16[512,384]{1,0:T(8,128)(2,1)}, bf16[512,384]{1,0:T(8,128)(2,1)}, u32[]{:S(2)}, u32[]{:S(2)}) collective-permute-start(bf16[512,384]{1,0:T(8,128)(2,1)} %get-tuple-element.67), channel_id=1, source_target_pairs={{0,3},{1,0},{2,1},{3,2},{4,7},{5,4},{6,5},{7,6},{8,11},{9,8},{10,9... | collective-permute-start | bytes 1179656 | tf_op jit(solution)/shard_map/ppermute | solution.py:33
  138.1 10.0 %copy-start.10 = (s32[8,8]{1,0:T(8,128)S(1)}, s32[8,8]{1,0:T(8,128)}, u32[]{:S(2)}) copy-start(s32[8,8]{1,0:T(8,128)} %param.9) | copy-start | bytes 772
  138.1 10.1 %copy-start.3 = (bf16[512,384]{1,0:T(8,128)(2,1)S(1)}, bf16[512,384]{1,0:T(8,128)(2,1)}, u32[]{:S(2)}) copy-start(bf16[512,384]{1,0:T(8,128)(2,1)} %refs_1_.7) | copy-start | bytes 1179652
  144.0 7.0 %collective-permute-start.21 = (bf16[192,1152]{1,0:T(8,128)(2,1)}, bf16[192,1152]{1,0:T(8,128)(2,1)S(1)}, u32[]{:S(2)}, u32[]{:S(2)}) collective-permute-start(bf16[192,1152]{1,0:T(8,128)(2,1)} %get-tuple-element.63), channel_id=1, source_target_pairs={{0,4},{4,0},{8,12},{12,8},{16,20},{20,16},{24,28},{28,24},{32,36},... | collective-permute-start | bytes 1327112 | tf_op jit(solution)/shard_map/ppermute | solution.py:46
  151.7 12.5 %collective-permute-start.25 = (bf16[40,1152]{1,0:T(8,128)(2,1)S(1)}, bf16[40,1152]{1,0:T(8,128)(2,1)S(1)}, u32[]{:S(2)}, u32[]{:S(2)}) collective-permute-start(bf16[40,1152]{1,0:T(8,128)(2,1)S(1)} %get-tuple-element.69), channel_id=1, source_target_pairs={{0,8},{4,12},{8,16},{12,20},{16,24},{20,28},{24,32},{28,36},{32,40... | collective-permute-start | bytes 276488 | tf_op jit(solution)/shard_map/ppermute | solution.py:46
  153.3 11.8 %collective-permute-start.26 = (bf16[40,1152]{1,0:T(8,128)(2,1)S(1)}, bf16[40,1152]{1,0:T(8,128)(2,1)S(1)}, u32[]{:S(2)}, u32[]{:S(2)}) collective-permute-start(bf16[40,1152]{1,0:T(8,128)(2,1)S(1)} %get-tuple-element.70), channel_id=1, source_target_pairs={{0,16},{4,20},{8,24},{12,28},{16,32},{20,36},{24,40},{28,44},{32,4... | collective-permute-start | bytes 276488 | tf_op jit(solution)/shard_map/ppermute | solution.py:46
  155.1 11.4 %collective-permute-start.27 = (bf16[40,1152]{1,0:T(8,128)(2,1)S(1)}, bf16[40,1152]{1,0:T(8,128)(2,1)S(1)}, u32[]{:S(2)}, u32[]{:S(2)}) collective-permute-start(bf16[40,1152]{1,0:T(8,128)(2,1)S(1)} %get-tuple-element.71), channel_id=1, source_target_pairs={{0,24},{4,28},{8,32},{12,36},{16,40},{20,44},{24,48},{28,52},{32,5... | collective-permute-start | bytes 276488 | tf_op jit(solution)/shard_map/ppermute | solution.py:46
  157.2 15.0 %collective-permute-start.28 = (bf16[40,1152]{1,0:T(8,128)(2,1)S(1)}, bf16[40,1152]{1,0:T(8,128)(2,1)S(1)}, u32[]{:S(2)}, u32[]{:S(2)}) collective-permute-start(bf16[40,1152]{1,0:T(8,128)(2,1)S(1)} %get-tuple-element.72), channel_id=1, source_target_pairs={{0,32},{4,36},{8,40},{12,44},{16,48},{20,52},{24,56},{28,60},{32,0... | collective-permute-start | bytes 276488 | tf_op jit(solution)/shard_map/ppermute | solution.py:46
  159.8 13.4 %collective-permute-start.29 = (bf16[40,1152]{1,0:T(8,128)(2,1)S(1)}, bf16[40,1152]{1,0:T(8,128)(2,1)S(1)}, u32[]{:S(2)}, u32[]{:S(2)}) collective-permute-start(bf16[40,1152]{1,0:T(8,128)(2,1)S(1)} %get-tuple-element.73), channel_id=1, source_target_pairs={{0,40},{4,44},{8,48},{12,52},{16,56},{20,60},{24,0},{28,4},{32,8},... | collective-permute-start | bytes 276488 | tf_op jit(solution)/shard_map/ppermute | solution.py:46
  164.2 11.6 %collective-permute-start.30 = (bf16[40,1152]{1,0:T(8,128)(2,1)S(1)}, bf16[40,1152]{1,0:T(8,128)(2,1)S(1)}, u32[]{:S(2)}, u32[]{:S(2)}) collective-permute-start(bf16[40,1152]{1,0:T(8,128)(2,1)S(1)} %get-tuple-element.74), channel_id=1, source_target_pairs={{0,48},{4,52},{8,56},{12,60},{16,0},{20,4},{24,8},{28,12},{32,16},... | collective-permute-start | bytes 276488 | tf_op jit(solution)/shard_map/ppermute | solution.py:46
  165.0 13.3 %collective-permute-start.31 = (bf16[40,1152]{1,0:T(8,128)(2,1)S(1)}, bf16[40,1152]{1,0:T(8,128)(2,1)S(1)}, u32[]{:S(2)}, u32[]{:S(2)}) collective-permute-start(bf16[40,1152]{1,0:T(8,128)(2,1)S(1)} %get-tuple-element.75), channel_id=1, source_target_pairs={{0,56},{4,60},{8,0},{12,4},{16,8},{20,12},{24,16},{28,20},{32,24},... | collective-permute-start | bytes 276488 | tf_op jit(solution)/shard_map/ppermute | solution.py:46
  178.3 2.1 %collective-permute-start.32 = (bf16[8,16,1024]{2,1,0:T(8,128)(2,1)S(1)}, bf16[8,16,1024]{2,1,0:T(8,128)(2,1)S(1)}, u32[]{:S(2)}, u32[]{:S(2)}) collective-permute-start(bf16[8,16,1024]{2,1,0:T(8,128)(2,1)S(1)} %get-tuple-element.87), channel_id=1, source_target_pairs={{0,4},{4,0},{8,12},{12,8},{16,20},{20,16},{24,28},{28,24},{32,36},... | collective-permute-start | bytes 786440 | tf_op jit(solution)/shard_map/ppermute | solution.py:46

commit v5 on v4

--- a/solution.py
+++ b/solution.py
@@ -152,17 +152,17 @@
 
 
 def stacked(place, values, after):
-    shape = values[0].shape
+    rows, cols = values[0].shape
 
     def body(place, *refs):
         for i in range(len(values)):
-            refs[-1][i] = refs[i][...]
+            refs[-1][:, i * cols : (i + 1) * cols] = refs[i][...]
 
     return call(
         body,
         place,
         local(values),
-        [like((len(values),) + shape, BF)],
+        [like((rows, len(values) * cols), BF)],
         after=after,
         moved=4 * len(values) * values[0].size,
     )[0]
@@ -218,9 +218,10 @@
     size, width = own.shape
     groups, wide = sums.shape
 
-    def body(place, own, c1, c2, c3, sums, total, long, below):
+    def body(place, own, c1, c2, c3, sums, total, low, long, below):
         value = own[...] + c1[...].astype(F32) + c2[...].astype(F32) + c3[...].astype(F32)
         total[...] = value
+        low[...] = value.astype(BF)
         long[:size, :] = value.astype(BF)
         below[...] = jnp.zeros((EXTRA, width), F32)
         for i in range(TAPS):
@@ -232,27 +233,12 @@
         body,
         place,
         local([own] + came + [sums]),
-        [like((size, width), F32), like((size + EXTRA, width), BF)],
+        [like((size, width), F32), like((size, width), BF), like((size + EXTRA, width), BF)],
         scratch=[pltpu.VMEM((EXTRA, width), F32)],
         after=after,
         flops=4 * own.size,
         moved=16 * own.size,
     )
-
-
-def rounded(place, value, after):
-    def body(place, value, out):
-        out[...] = value[...].astype(BF)
-
-    return call(
-        body,
-        place,
-        local([value]),
-        [like(value.shape, BF)],
-        after=after,
-        flops=value.size,
-        moved=200 * value.size,
-    )[0]
 
 
 def back_products(place, around, conv_weight, after):
@@ -282,15 +268,15 @@
 
 
 def kernel_terms(place, earlier, own, later, cots, groups, after):
-    _, width, size = own.shape
+    width, size = own.shape[0], own.shape[1] // NY
     half = width // 2
     cols = TAPS * width
 
-    def body(place, earlier, own, later, d0, d1, d2, d3, kept, sent, cover, below):
+    def body(place, earlier, own, later, d0, d1, d2, d3, kept, sent, cover, done, below, joined):
         y, z, core = place[1], place[2], place[3]
         first, last = z == 0, z == NZ - 1
+        done[...] = jnp.zeros_like(done)
         for k, left in enumerate((earlier, own, later)):
-            total = jnp.zeros((width, width), F32)
             for m, right in enumerate((d0, d1, d2, d3)):
                 if k == 0:
                     index = jnp.where(first, (m + 1) % NY, m)
@@ -299,9 +285,20 @@
                     index = jnp.where(last, (m + NY - 1) % NY, m)
                     valid = jnp.logical_not(jnp.logical_and(last, y == (m + NY - 1) % NY))
                 else:
-                    index, valid = m, None
-                product = jnp.dot(left[index], right[:size, :], preferred_element_type=F32)
-                total += product if valid is None else jnp.where(valid, product, 0.0)
+                    joined[k, m * size : (m + 1) * size, :] = right[:size, :]
+                    continue
+                at = pl.ds(pl.multiple_of(index * size, size), size)
+
+                @pl.when(valid)
+                def _():
+                    joined[k, at, :] = right[:size, :]
+
+                @pl.when(jnp.logical_not(valid))
+                def _():
+                    joined[k, at, :] = jnp.zeros((size, width), BF)
+
+        for k, left in enumerate((earlier, own, later)):
+            total = jnp.dot(left[...], joined[k], preferred_element_type=F32)
             pairs = total.reshape(half // GROUP, 2, GROUP, width)
             one, two = (pairs[:, i].reshape(half, width) for i in range(2))
             at = slice(k * width, (k + 1) * width)
@@ -318,8 +315,8 @@
         body,
         place,
         local([earlier, own, later] + cots),
-        [like((half, cols), F32), like((half, cols), BF), like((NY * groups, cols), F32)],
-        scratch=[pltpu.VMEM((EXTRA, width), F32)],
+        [like((half, cols), F32), like((half, cols), BF), like((NY * groups, cols), F32), like((8, 128), F32)],
+        scratch=[pltpu.VMEM((EXTRA, width), F32), pltpu.VMEM((TAPS, NY * size, width), BF)],
         after=after,
         flops=2 * size * NY * width * cols,
         moved=8 * NY * width * size,
@@ -353,6 +350,31 @@
     )
 
 
+def summed(place, kept, cover, parts, wide):
+    rows, cols = kept.shape
+    width = cols // TAPS
+
+    def body(place, kept, cover, *refs):
+        parts, (out, blocks, done) = refs[: NZ - 1], refs[NZ - 1 :]
+        done[...] = jnp.zeros_like(done)
+        total = kept[...]
+        blocks[0] = cover[:, :wide].astype(BF)
+        for m, part in enumerate(parts):
+            total += part[...].astype(F32)[EXTRA:]
+            blocks[m + 1] = part[:EXTRA, :wide]
+        for k in range(TAPS):
+            out[k] = total[:, k * width : (k + 1) * width]
+
+    return call(
+        body,
+        place,
+        local([kept, cover] + parts),
+        [like((TAPS, rows, width), F32), like((NZ, EXTRA, wide), BF), like((8, 128), F32)],
+        flops=NZ * rows * cols,
+        moved=2 * NZ * (rows + EXTRA) * cols,
+    )
+
+
 def input_gradient(place, inputs, grad, own, came, after):
     def body(place, state, grad, own, c1, c2, c3, out, done):
         back_u = own[...] + c1[...].astype(F32) + c2[...].astype(F32) + c3[...].astype(F32)
@@ -411,25 +433,20 @@
     behind = along_seq(turned, 0, NZ - 1, 0)
     came = [along_x(blocks[r], r) for r in range(1, NX)]
     (taps,) = load(place, [conv_weight], (done,))
-    grad, long = add_up(place, blocks[0], came, sums, ())
-
-    low = rounded(place, grad, (token(long),))
+    grad, low, long = add_up(place, blocks[0], came, sums, ())
+
     cots = [long] + [along_seq(long, m, 0, 0) for m in range(1, NY)]
     around = [shifted(low, -steps), low, shifted(low, steps)]
-    *blocks, done = back_products(place, around, taps, (token(before), token(behind)))
+    kept, sent, cover, done = kernel_terms(place, before, turned, behind, cots, own, ())
+    *blocks, done = back_products(place, around, taps, (done,))
     came = [along_x(blocks[r], r) for r in range(1, NX)]
-    kept, sent, cover = kernel_terms(place, before, turned, behind, cots, own, (done,))
-    out, done = input_gradient(place, inputs, grad, blocks[0], came, ())
     kept, *parts = over_z(place, kept, along_seq(sent, 0, 0, 1), cover, (done,))
     parts = [along_seq(part, 0, m + 1, 0) for m, part in enumerate(parts)]
-    for part in parts:
-        kept = kept + part[EXTRA:].astype(F32)
-    kernel_gradient = kept.reshape(GROUP, TAPS, width).transpose(1, 0, 2)[None]
-
-    cover = jnp.stack([cover.astype(BF)] + [part[:EXTRA] for part in parts])[:, :, :wide]
+    kernel_gradient, cover, done = summed(place, kept, cover, parts, wide)
+    out, _ = input_gradient(place, inputs, grad, blocks[0], came, (done,))
     cover = jnp.stack([cover, along_seq(cover, 0, 0, 1)])
     coverage = coverage_of(cover, place, exon_blocks, own)
-    return (tracks, coverage, out, kernel_gradient)
+    return (tracks, coverage, out, kernel_gradient[None])
 
 
 def solution(mesh):

time: 182 us -> 186 us (1.022)
  waiting for transfers between devices: 79.5 us -> 71.3 us
  local copies, waits for them, and re-layouts: 4.88 us -> 12.5 us
  starting transfers between devices: 61.8 us -> 65.4 us
  other arithmetic: 1.79 us -> 4.12 us
    unnamed x29 -> x36, local copies, waits for them, and re-layouts: 2.75 us -> 8.22 us
    ppermute x17, waiting for transfers between devices: 23.6 us -> 18.2 us  [along_seq(): return lax.ppermute(value, 'seq', pairs)]
    ppermute x12, starting transfers between devices: 11.7 us -> 16.2 us  [along_x(): lax.ppermute(value, 'chan', [(i, (i + steps) % NX) for i in range(NX)])]
    broadcast_in_dim x8, local copies, waits for them, and re-layouts: 0.68 us -> 4.25 us  [coverage_of(): jnp.meshgrid(*(jnp.arange(n, dtype=jnp.int32) for n in (2, NZ, NY, own)),...]
    ppermute x4, waiting for transfers between devices: 14.2 us -> 10.8 us  [shifted(): lax.ppermute(value, 'seq', [(s, s + steps) for s in range(leading, last)])]
  transfers between devices with their start and end apart: 33 -> 33, of which waited for: 18 -> 13; matrix products, arithmetic and copies ran while one was open for 2% -> 4% of each run, Pallas kernels for 14% -> 14%
where the time goes in v5:
time: 186 us
  waiting for transfers between devices  71.3 us (38%)
  starting transfers between devices  65.4 us (35%)
  Pallas kernels  30.9 us (17%)
  local copies, waits for them, and re-layouts  12.5 us (7%)
  other arithmetic  4.12 us (2%)
    ppermute x12, waiting for transfers between devices, along_x(): lax.ppermute(value, 'chan', [(i, (i + steps) % NX) for i in range(NX)])  42.3 us
    ppermute x17, starting transfers between devices, along_seq(): return lax.ppermute(value, 'seq', pairs)  40.5 us
    pallas_call x13, Pallas kernels, call(): pl.pallas_call(kernel, in_specs=[pl.BlockSpec(memory_space=pltpu.SMEM)] +...  30.9 us
    ppermute x17, waiting for transfers between devices, along_seq(): return lax.ppermute(value, 'seq', pairs)  18.2 us
    ppermute x12, starting transfers between devices, along_x(): lax.ppermute(value, 'chan', [(i, (i + steps) % NX) for i in range(NX)])  16.2 us
    ppermute x4, waiting for transfers between devices, shifted(): lax.ppermute(value, 'seq', [(s, s + steps) for s in range(leading, last)])  10.8 us
    ppermute x4, starting transfers between devices, shifted(): lax.ppermute(value, 'seq', [(s, s + steps) for s in range(leading, last)])  8.71 us
    unnamed x36, local copies, waits for them, and re-layouts  8.22 us
  transfers between devices with their start and end apart: 33, of which 13 were waited for; matrix products, arithmetic and copies ran while one was open for 4% of the time, Pallas kernels for 14%

profile of v5, /device:TPU:1, one launch (start us, length us, event | category | flops | bytes accessed | tf_op | source)
XLA Modules:
  0.0 185.9 jit_solution(18418157468650905723)
XLA Ops:
  0.6 1.3 fusion.5.refs_1_
  1.9 3.4 %collective-permute-start = (bf16[512,384]{1,0:T(8,128)(2,1)S(1)}, bf16[512,384]{1,0:T(8,128)(2,1)S(1)}, u32[]{:S(2)}, u32[]{:S(2)}) collective-permute-start(bf16[512,384]{1,0:T(8,128)(2,1)S(1)} %fusion.5.refs_1_), channel_id=1, source_target_pairs={{0,3},{1,0},{2,1},{3,2},{4,7},{5,4},{6,5},{7,6},{8,11},{9,8},{10,9... | collective-permute-start | bytes 1179656 | tf_op jit(solution)/shard_map/ppermute | solution.py:33
  6.5 2.0 %copy-done = bf16[1,3,1536,384]{3,2,1,0:T(8,128)(2,1)S(1)} copy-done((bf16[1,3,1536,384]{3,2,1,0:T(8,128)(2,1)S(1)}, bf16[1,3,1536,384]{3,2,1,0:T(8,128)(2,1)}, u32[]{:S(2)}) %copy-start) | copy-done | bytes 3538968
  8.5 1.0 shard_map.84.refs_5_
  9.5 6.7 %collective-permute-done.refs_2_ = bf16[512,384]{1,0:T(8,128)(2,1)S(1)} collective-permute-done((bf16[512,384]{1,0:T(8,128)(2,1)S(1)}, bf16[512,384]{1,0:T(8,128)(2,1)S(1)}, u32[]{:S(2)}, u32[]{:S(2)}) %collective-permute-start) | collective-permute-done | bytes 393248 | tf_op jit(solution)/shard_map/ppermute | solution.py:33
  16.5 9.8 %collective-permute-done.2.refs_4_ = bf16[512,384]{1,0:T(8,128)(2,1)S(1)} collective-permute-done((bf16[512,384]{1,0:T(8,128)(2,1)S(1)}, bf16[512,384]{1,0:T(8,128)(2,1)S(1)}, u32[]{:S(2)}, u32[]{:S(2)}) %collective-permute-start.2) | collective-permute-done | bytes 393248 | tf_op jit(solution)/shard_map/ppermute | solution.py:33
  26.3 3.2 %shard_map.85 = (bf16[512,384]{1,0:T(8,128)(2,1)S(1)}, f32[512,384]{1,0:T(8,128)S(1)}, bf16[512,384]{1,0:T(8,128)(2,1)S(1)}, bf16[512,1536]{1,0:T(8,128)(2,1)S(1)}) custom-call(s32[4]{0:T(128)S(1)} %pad_add_fusion.refs_0_, bf16[512,384]{1,0:T(8,128)(2,1)S(1)} %fusion.5.refs_1_, bf16[512,384]{1,0:T(8,128)(2,1)S(1)} %collective-permute-done.refs_2_, ...), custom_call_target="tpu_custom_call" | custom-call | flops 1811939328 | bytes 3538944 | tf_op jit(solution)/shard_map/pallas_call | solution.py:64
  29.5 3.8 %collective-permute-start.3 = (bf16[512,384]{1,0:T(8,128)(2,1)S(1)}, bf16[512,384]{1,0:T(8,128)(2,1)S(1)}, u32[]{:S(2)}, u32[]{:S(2)}) collective-permute-start(bf16[512,384]{1,0:T(8,128)(2,1)S(1)} %get-tuple-element.46), channel_id=1, source_target_pairs={{0,8},{4,12},{8,16},{12,20},{16,24},{20,28},{24,32},{28,36},{32,40... | collective-permute-start | bytes 1179656 | tf_op jit(solution)/shard_map/ppermute | solution.py:29
  33.3 1.3 collective-permute-start.4
  34.6 6.6 %collective-permute-done.3 = bf16[512,384]{1,0:T(8,128)(2,1)S(1)} collective-permute-done((bf16[512,384]{1,0:T(8,128)(2,1)S(1)}, bf16[512,384]{1,0:T(8,128)(2,1)S(1)}, u32[]{:S(2)}, u32[]{:S(2)}) %collective-permute-start.3) | collective-permute-done | bytes 393248 | tf_op jit(solution)/shard_map/ppermute | solution.py:29
  41.3 4.2 %collective-permute-done.4 = bf16[512,384]{1,0:T(8,128)(2,1)S(1)} collective-permute-done((bf16[512,384]{1,0:T(8,128)(2,1)S(1)}, bf16[512,384]{1,0:T(8,128)(2,1)S(1)}, u32[]{:S(2)}, u32[]{:S(2)}) %collective-permute-start.4) | collective-permute-done | bytes 393248 | tf_op jit(solution)/shard_map/ppermute | solution.py:29
  46.3 0.9 collective-permute-start.7
  47.2 1.0 shard_map.88
  48.2 4.7 %collective-permute-start.10 = (bf16[384,512]{1,0:T(8,128)(2,1)S(1)}, bf16[384,512]{1,0:T(8,128)(2,1)S(1)}, u32[]{:S(2)}, u32[]{:S(2)}) collective-permute-start(bf16[384,512]{1,0:T(8,128)(2,1)S(1)} %get-tuple-element.55), channel_id=1, source_target_pairs={{0,192},{4,196},{8,200},{12,204},{16,208},{20,212},{24,216},{28,22... | collective-permute-start | bytes 1179656 | tf_op jit(solution)/shard_map/ppermute | solution.py:46
  52.9 2.0 %collective-permute-done.5.refs_2_ = bf16[512,384]{1,0:T(8,128)(2,1)S(1)} collective-permute-done((bf16[512,384]{1,0:T(8,128)(2,1)S(1)}, bf16[512,384]{1,0:T(8,128)(2,1)S(1)}, u32[]{:S(2)}, u32[]{:S(2)}) %collective-permute-start.5) | collective-permute-done | bytes 393248 | tf_op jit(solution)/shard_map/ppermute | solution.py:33
  54.8 4.6 %collective-permute-start.9 = (bf16[384,512]{1,0:T(8,128)(2,1)S(1)}, bf16[384,512]{1,0:T(8,128)(2,1)S(1)}, u32[]{:S(2)}, u32[]{:S(2)}) collective-permute-start(bf16[384,512]{1,0:T(8,128)(2,1)S(1)} %get-tuple-element.54), channel_id=1, source_target_pairs={{0,128},{4,132},{8,136},{12,140},{16,144},{20,148},{24,152},{28,15... | collective-permute-start | bytes 1179656 | tf_op jit(solution)/shard_map/ppermute | solution.py:46
  59.5 0.8 shard_map.86
  60.3 6.4 %collective-permute-done.7.refs_4_ = bf16[512,384]{1,0:T(8,128)(2,1)S(1)} collective-permute-done((bf16[512,384]{1,0:T(8,128)(2,1)S(1)}, bf16[512,384]{1,0:T(8,128)(2,1)S(1)}, u32[]{:S(2)}, u32[]{:S(2)}) %collective-permute-start.7) | collective-permute-done | bytes 393248 | tf_op jit(solution)/shard_map/ppermute | solution.py:33
  66.8 6.2 %shard_map.87 = (bf16[512,1024]{1,0:T(8,128)(2,1)}, f32[4,1024]{1,0:T(4,128)S(1)}, f32[512,384]{1,0:T(8,128)S(1)}, bf16[512,384]{1,0:T(8,128)(2,1)S(1)}, bf16[51...) custom-call(s32[4]{0:T(128)S(1)} %pad_add_fusion.refs_0_, ...), custom_call_target="tpu_custom_call" | custom-call | flops 3221225472 | bytes 3145728 | tf_op jit(solution)/shard_map/pallas_call | solution.py:64
  73.0 0.7 shard_map.89.refs_2_
  73.7 1.7 collective-permute-start.11
  75.4 4.4 %collective-permute-start.12 = (bf16[384,2048]{1,0:T(8,128)(2,1)S(1)}, bf16[384,2048]{1,0:T(8,128)(2,1)S(1)}, u32[]{:S(2)}, u32[]{:S(2)}) collective-permute-start(bf16[384,2048]{1,0:T(8,128)(2,1)S(1)} %shard_map.89.refs_2_), channel_id=1, source_target_pairs={{0,56},{4,60},{8,0},{12,4},{16,8},{20,12},{24,16},{28,20},{32,24},... | collective-permute-start | bytes 4718600 | tf_op jit(solution)/shard_map/ppermute | solution.py:46
  80.4 2.2 %collective-permute-start.15 = (bf16[512,384]{1,0:T(8,128)(2,1)S(1)}, bf16[512,384]{1,0:T(8,128)(2,1)S(1)}, u32[]{:S(2)}, u32[]{:S(2)}) collective-permute-start(bf16[512,384]{1,0:T(8,128)(2,1)S(1)} %get-tuple-element.60), channel_id=1, source_target_pairs={{0,3},{1,0},{2,1},{3,2},{4,7},{5,4},{6,5},{7,6},{8,11},{9,8},{10,9... | collective-permute-start | bytes 1179656 | tf_op jit(solution)/shard_map/ppermute | solution.py:33
  82.5 16.8 %collective-permute-done.13.refs_2_ = bf16[512,384]{1,0:T(8,128)(2,1)S(1)} collective-permute-done((bf16[512,384]{1,0:T(8,128)(2,1)S(1)}, bf16[512,384]{1,0:T(8,128)(2,1)S(1)}, u32[]{:S(2)}, u32[]{:S(2)}) %collective-permute-start.13) | collective-permute-done | bytes 393248 | tf_op jit(solution)/shard_map/ppermute | solution.py:33
  99.7 1.7 shard_map.90
  101.4 1.3 collective-permute-start.16
  102.7 1.7 collective-permute-start.17
  104.3 2.1 %collective-permute-start.18 = (bf16[528,384]{1,0:T(8,128)(2,1)S(1)}, bf16[528,384]{1,0:T(8,128)(2,1)S(1)}, u32[]{:S(2)}, u32[]{:S(2)}) collective-permute-start(bf16[528,384]{1,0:T(8,128)(2,1)S(1)} %get-tuple-element.62.refs_4_), channel_id=1, source_target_pairs={{0,192},{4,196},{8,200},{12,204},{16,208},{20,212},{24,216},{28,22... | collective-permute-start | bytes 1216520 | tf_op jit(solution)/shard_map/ppermute | solution.py:46
  106.4 5.1 %collective-permute-done.16.refs_5_ = bf16[528,384]{1,0:T(8,128)(2,1)S(1)} collective-permute-done((bf16[528,384]{1,0:T(8,128)(2,1)S(1)}, bf16[528,384]{1,0:T(8,128)(2,1)S(1)}, u32[]{:S(2)}, u32[]{:S(2)}) %collective-permute-start.16) | collective-permute-done | bytes 405536 | tf_op jit(solution)/shard_map/ppermute | solution.py:46
  111.5 1.5 collective-permute-start.20
  113.0 7.8 %collective-permute-done.17.refs_6_ = bf16[528,384]{1,0:T(8,128)(2,1)S(1)} collective-permute-done((bf16[528,384]{1,0:T(8,128)(2,1)S(1)}, bf16[528,384]{1,0:T(8,128)(2,1)S(1)}, u32[]{:S(2)}, u32[]{:S(2)}) %collective-permute-start.17) | collective-permute-done | bytes 405536 | tf_op jit(solution)/shard_map/ppermute | solution.py:46
  120.8 2.0 %collective-permute-start.21 = (bf16[512,384]{1,0:T(8,128)(2,1)}, bf16[512,384]{1,0:T(8,128)(2,1)}, u32[]{:S(2)}, u32[]{:S(2)}) collective-permute-start(bf16[512,384]{1,0:T(8,128)(2,1)} %get-tuple-element.66.refs_2_), channel_id=1, source_target_pairs={{0,8},{4,12},{8,16},{12,20},{16,24},{20,28},{24,32},{28,36},{32,40... | collective-permute-start | bytes 1179656 | tf_op jit(solution)/shard_map/ppermute | solution.py:29
  122.9 4.7 %shard_map.91 = (f32[192,1152]{1,0:T(8,128)S(1)}, bf16[192,1152]{1,0:T(8,128)(2,1)}, f32[16,1152]{1,0:T(8,128)S(1)}, f32[8,128]{1,0:T(8,128)S(1)}) custom-call(s32[4]{0:T(128)S(1)} %pad_add_fusion.refs_0_, bf16[384,2048]{1,0:T(8,128)(2,1)S(1)} %collective-permute-done.11.refs_1_, bf16[384,2048]{1,0:T(8,128)(2,1)S(1)} %shard_map.89.refs_2_, ...), custom_call_target="tpu_custom_call" | custom-call | flops 1811939328 | bytes 6291456 | tf_op jit(solution)/shard_map/pallas_call | solution.py:64
  127.5 1.0 copy-done.6
  129.1 2.9 %collective-permute-start.19 = (bf16[192,1152]{1,0:T(8,128)(2,1)}, bf16[192,1152]{1,0:T(8,128)(2,1)}, u32[]{:S(2)}, u32[]{:S(2)}) collective-permute-start(bf16[192,1152]{1,0:T(8,128)(2,1)} %get-tuple-element.64), channel_id=1, source_target_pairs={{0,4},{4,0},{8,12},{12,8},{16,20},{20,16},{24,28},{28,24},{32,36},... | collective-permute-start | bytes 1327112 | tf_op jit(solution)/shard_map/ppermute | solution.py:46
  132.6 1.0 shard_map.92.refs_4_
  133.6 5.2 %shard_map.93 = (f32[512,384]{1,0:T(8,128)S(1)}, bf16[512,384]{1,0:T(8,128)(2,1)}, bf16[512,384]{1,0:T(8,128)(2,1)}, bf16[512,384]{1,0:T(8,128)(2,1)}, f32[8,128]{1,0:T(8,128)S(1)}) custom-call(s32[4]{0:T(128)S(1)} %pad_add_fusion.refs_0_, bf16[512,384]{1,0:T(8,128)(2,1)} %collective-permute-done.20.refs_1_, bf16[512,384]{1,0:T(8,128)(2,1)} %get-tuple-element.66.refs_2_, ...), custom_call_target="tpu_custom_call" | custom-call | flops 1811939328 | bytes 3538944 | tf_op jit(solution)/shard_map/pallas_call | solution.py:64
  138.8 1.9 shard_map.94
  140.6 1.6 collective-permute-start.22
  142.2 2.5 %collective-permute-start.23 = (bf16[40,1152]{1,0:T(8,128)(2,1)S(1)}, bf16[40,1152]{1,0:T(8,128)(2,1)S(1)}, u32[]{:S(2)}, u32[]{:S(2)}) collective-permute-start(bf16[40,1152]{1,0:T(8,128)(2,1)S(1)} %get-tuple-element.71), channel_id=1, source_target_pairs={{0,16},{4,20},{8,24},{12,28},{16,32},{20,36},{24,40},{28,44},{32,4... | collective-permute-start | bytes 276488 | tf_op jit(solution)/shard_map/ppermute | solution.py:46
  145.1 6.3 %collective-permute-start.25 = (bf16[40,1152]{1,0:T(8,128)(2,1)S(1)}, bf16[40,1152]{1,0:T(8,128)(2,1)S(1)}, u32[]{:S(2)}, u32[]{:S(2)}) collective-permute-start(bf16[40,1152]{1,0:T(8,128)(2,1)S(1)} %get-tuple-element.73), channel_id=1, source_target_pairs={{0,32},{4,36},{8,40},{12,44},{16,48},{20,52},{24,56},{28,60},{32,0... | collective-permute-start | bytes 276488 | tf_op jit(solution)/shard_map/ppermute | solution.py:46
  151.3 4.5 %collective-permute-start.26 = (bf16[40,1152]{1,0:T(8,128)(2,1)S(1)}, bf16[40,1152]{1,0:T(8,128)(2,1)S(1)}, u32[]{:S(2)}, u32[]{:S(2)}) collective-permute-start(bf16[40,1152]{1,0:T(8,128)(2,1)S(1)} %get-tuple-element.74), channel_id=1, source_target_pairs={{0,40},{4,44},{8,48},{12,52},{16,56},{20,60},{24,0},{28,4},{32,8},... | collective-permute-start | bytes 276488 | tf_op jit(solution)/shard_map/ppermute | solution.py:46
  155.8 1.7 collective-permute-start.30
  157.5 2.9 %collective-permute-start.31 = (bf16[512,384]{1,0:T(8,128)(2,1)}, bf16[512,384]{1,0:T(8,128)(2,1)S(1)}, u32[]{:S(2)}, u32[]{:S(2)}) collective-permute-start(bf16[512,384]{1,0:T(8,128)(2,1)} %get-tuple-element.81), channel_id=1, source_target_pairs={{0,2},{1,3},{2,0},{3,1},{4,6},{5,7},{6,4},{7,5},{8,10},{9,11},{10,... | collective-permute-start | bytes 1179656 | tf_op jit(solution)/shard_map/ppermute | solution.py:33
  160.4 2.4 %collective-permute-done.24.refs_5_ = bf16[40,1152]{1,0:T(8,128)(2,1)S(1)} collective-permute-done((bf16[40,1152]{1,0:T(8,128)(2,1)S(1)}, bf16[40,1152]{1,0:T(8,128)(2,1)S(1)}, u32[]{:S(2)}, u32[]{:S(2)}) %collective-permute-start.24) | collective-permute-done | bytes 92192 | tf_op jit(solution)/shard_map/ppermute | solution.py:46
  162.8 0.6 copy-done.12
  163.4 2.9 %collective-permute-start.32 = (bf16[512,384]{1,0:T(8,128)(2,1)}, bf16[512,384]{1,0:T(8,128)(2,1)S(1)}, u32[]{:S(2)}, u32[]{:S(2)}) collective-permute-start(bf16[512,384]{1,0:T(8,128)(2,1)} %get-tuple-element.82), channel_id=1, source_target_pairs={{0,3},{1,0},{2,1},{3,2},{4,7},{5,4},{6,5},{7,6},{8,11},{9,8},{10,9... | collective-permute-start | bytes 1179656 | tf_op jit(solution)/shard_map/ppermute | solution.py:33
  167.2 0.6 copy-done.16
  169.0 0.7 broadcast_in_dim.27
  169.7 0.7 broadcast_in_dim.28
  170.4 0.7 broadcast_in_dim.29
  171.1 0.7 broadcast_in_dim.24
  171.8 0.7 broadcast_in_dim.25
  172.5 0.7 broadcast_in_dim.31
  173.2 2.9 %collective-permute-done.28.refs_9_ = bf16[40,1152]{1,0:T(8,128)(2,1)} collective-permute-done((bf16[40,1152]{1,0:T(8,128)(2,1)}, bf16[40,1152]{1,0:T(8,128)(2,1)}, u32[]{:S(2)}, u32[]{:S(2)}) %collective-permute-start.28) | collective-permute-done | bytes 92192 | tf_op jit(solution)/shard_map/ppermute | solution.py:46
  176.1 0.9 copy-done.13
  177.0 0.9 copy-done.15
  177.9 0.9 copy-done.17
  178.8 1.7 shard_map.95
  180.5 1.0 collective-permute-start.29
  181.5 0.7 multiply_add_fusion
  182.2 0.8 convert_reduce_fusion
  183.0 2.0 %shard_map.96 = (bf16[512,384]{1,0:T(8,128)(2,1)}, f32[8,128]{1,0:T(8,128)}) custom-call(s32[4]{0:T(128)S(1)} %pad_add_fusion.refs_0_, bf16[512,384]{1,0:T(8,128)(2,1)S(1)} %copy-done.3, f32[512,384]{1,0:T(8,128)S(1)} %copy-done.9, f32[512,384]{1,0:T(8,128)S(1)} %get-tuple-element.79.refs_3_, bf16[512,384]{1,0:T(8,128)(2,1)S(1)} %collective-permute-done.30.refs_4_, ...), custom_call_target="tpu_custom_call" | custom-call | flops 3932160 | bytes 3145728 | tf_op jit(solution)/shard_map/pallas_call | solution.py:64
  185.1 0.8 convolution_multiply_fusion
  (71 shorter events, 7.1 us)
Async XLA Ops:
  1.9 14.2 %collective-permute-start = (bf16[512,384]{1,0:T(8,128)(2,1)S(1)}, bf16[512,384]{1,0:T(8,128)(2,1)S(1)}, u32[]{:S(2)}, u32[]{:S(2)}) collective-permute-start(bf16[512,384]{1,0:T(8,128)(2,1)S(1)} %fusion.5.refs_1_), channel_id=1, source_target_pairs={{0,3},{1,0},{2,1},{3,2},{4,7},{5,4},{6,5},{7,6},{8,11},{9,8},{10,9... | collective-permute-start | bytes 1179656 | tf_op jit(solution)/shard_map/ppermute | solution.py:33
  5.3 11.2 %collective-permute-start.1 = (bf16[512,384]{1,0:T(8,128)(2,1)S(1)}, bf16[512,384]{1,0:T(8,128)(2,1)S(1)}, u32[]{:S(2)}, u32[]{:S(2)}) collective-permute-start(bf16[512,384]{1,0:T(8,128)(2,1)S(1)} %fusion.5.refs_1_), channel_id=1, source_target_pairs={{0,2},{1,3},{2,0},{3,1},{4,6},{5,7},{6,4},{7,5},{8,10},{9,11},{10,... | collective-permute-start | bytes 1179656 | tf_op jit(solution)/shard_map/ppermute | solution.py:33
  5.8 20.4 %collective-permute-start.2 = (bf16[512,384]{1,0:T(8,128)(2,1)S(1)}, bf16[512,384]{1,0:T(8,128)(2,1)S(1)}, u32[]{:S(2)}, u32[]{:S(2)}) collective-permute-start(bf16[512,384]{1,0:T(8,128)(2,1)S(1)} %fusion.5.refs_1_), channel_id=1, source_target_pairs={{0,1},{1,2},{2,3},{3,0},{4,5},{5,6},{6,7},{7,4},{8,9},{9,10},{10,1... | collective-permute-start | bytes 1179656 | tf_op jit(solution)/shard_map/ppermute | solution.py:33
  6.5 2.0 %copy-start = (bf16[1,3,1536,384]{3,2,1,0:T(8,128)(2,1)S(1)}, bf16[1,3,1536,384]{3,2,1,0:T(8,128)(2,1)}, u32[]{:S(2)}) copy-start(bf16[1,3,1536,384]{3,2,1,0:T(8,128)(2,1)} %refs_1_.6) | copy-start | bytes 10616836
  9.5 36.0 %copy-start.2 = (bf16[512,384]{1,0:T(8,128)(2,1)S(1)}, bf16[512,384]{1,0:T(8,128)(2,1)}, u32[]{:S(2)}) copy-start(bf16[512,384]{1,0:T(8,128)(2,1)} %refs_1_.7) | copy-start | bytes 1179652
  26.3 33.2 %copy-start.5 = (bf16[512,1024]{1,0:T(8,128)(2,1)S(1)}, bf16[512,1024]{1,0:T(8,128)(2,1)}, u32[]{:S(2)}) copy-start(bf16[512,1024]{1,0:T(8,128)(2,1)} %refs_2_.1) | copy-start | bytes 3145732
  29.5 30.0 %copy-start.4 = (bf16[1536,1024]{1,0:T(8,128)(2,1)S(1)}, bf16[1536,1024]{1,0:T(8,128)(2,1)}, u32[]{:S(2)}) copy-start(bf16[1536,1024]{1,0:T(8,128)(2,1)} %refs_1_.5) | copy-start | bytes 9437188
  29.5 11.8 %collective-permute-start.3 = (bf16[512,384]{1,0:T(8,128)(2,1)S(1)}, bf16[512,384]{1,0:T(8,128)(2,1)S(1)}, u32[]{:S(2)}, u32[]{:S(2)}) collective-permute-start(bf16[512,384]{1,0:T(8,128)(2,1)S(1)} %get-tuple-element.46), channel_id=1, source_target_pairs={{0,8},{4,12},{8,16},{12,20},{16,24},{20,28},{24,32},{28,36},{32,40... | collective-permute-start | bytes 1179656 | tf_op jit(solution)/shard_map/ppermute | solution.py:29
  33.3 12.1 %collective-permute-start.4 = (bf16[512,384]{1,0:T(8,128)(2,1)S(1)}, bf16[512,384]{1,0:T(8,128)(2,1)S(1)}, u32[]{:S(2)}, u32[]{:S(2)}) collective-permute-start(bf16[512,384]{1,0:T(8,128)(2,1)S(1)} %get-tuple-element.47), channel_id=1, source_target_pairs={{8,0},{12,4},{16,8},{20,12},{24,16},{28,20},{32,24},{36,28},{40,32... | collective-permute-start | bytes 1179656 | tf_op jit(solution)/shard_map/ppermute | solution.py:29
  45.6 9.2 %collective-permute-start.5 = (bf16[512,384]{1,0:T(8,128)(2,1)S(1)}, bf16[512,384]{1,0:T(8,128)(2,1)S(1)}, u32[]{:S(2)}, u32[]{:S(2)}) collective-permute-start(bf16[512,384]{1,0:T(8,128)(2,1)S(1)} %fusion.6.refs_1_), channel_id=1, source_target_pairs={{0,3},{1,0},{2,1},{3,2},{4,7},{5,4},{6,5},{7,6},{8,11},{9,8},{10,9... | collective-permute-start | bytes 1179656 | tf_op jit(solution)/shard_map/ppermute | solution.py:33
  45.7 14.6 %collective-permute-start.6 = (bf16[512,384]{1,0:T(8,128)(2,1)S(1)}, bf16[512,384]{1,0:T(8,128)(2,1)S(1)}, u32[]{:S(2)}, u32[]{:S(2)}) collective-permute-start(bf16[512,384]{1,0:T(8,128)(2,1)S(1)} %fusion.6.refs_1_), channel_id=1, source_target_pairs={{0,2},{1,3},{2,0},{3,1},{4,6},{5,7},{6,4},{7,5},{8,10},{9,11},{10,... | collective-permute-start | bytes 1179656 | tf_op jit(solution)/shard_map/ppermute | solution.py:33
  46.3 20.5 %collective-permute-start.7 = (bf16[512,384]{1,0:T(8,128)(2,1)S(1)}, bf16[512,384]{1,0:T(8,128)(2,1)S(1)}, u32[]{:S(2)}, u32[]{:S(2)}) collective-permute-start(bf16[512,384]{1,0:T(8,128)(2,1)S(1)} %fusion.6.refs_1_), channel_id=1, source_target_pairs={{0,1},{1,2},{2,3},{3,0},{4,5},{5,6},{6,7},{7,4},{8,9},{9,10},{10,1... | collective-permute-start | bytes 1179656 | tf_op jit(solution)/shard_map/ppermute | solution.py:33
  48.2 24.8 %collective-permute-start.10 = (bf16[384,512]{1,0:T(8,128)(2,1)S(1)}, bf16[384,512]{1,0:T(8,128)(2,1)S(1)}, u32[]{:S(2)}, u32[]{:S(2)}) collective-permute-start(bf16[384,512]{1,0:T(8,128)(2,1)S(1)} %get-tuple-element.55), channel_id=1, source_target_pairs={{0,192},{4,196},{8,200},{12,204},{16,208},{20,212},{24,216},{28,22... | collective-permute-start | bytes 1179656 | tf_op jit(solution)/shard_map/ppermute | solution.py:46
  52.9 20.2 %collective-permute-start.8 = (bf16[384,512]{1,0:T(8,128)(2,1)S(1)}, bf16[384,512]{1,0:T(8,128)(2,1)S(1)}, u32[]{:S(2)}, u32[]{:S(2)}) collective-permute-start(bf16[384,512]{1,0:T(8,128)(2,1)S(1)} %get-tuple-element.53), channel_id=1, source_target_pairs={{0,64},{4,68},{8,72},{12,76},{16,80},{20,84},{24,88},{28,92},{32,9... | collective-permute-start | bytes 1179656 | tf_op jit(solution)/shard_map/ppermute | solution.py:46
  54.8 18.2 %collective-permute-start.9 = (bf16[384,512]{1,0:T(8,128)(2,1)S(1)}, bf16[384,512]{1,0:T(8,128)(2,1)S(1)}, u32[]{:S(2)}, u32[]{:S(2)}) collective-permute-start(bf16[384,512]{1,0:T(8,128)(2,1)S(1)} %get-tuple-element.54), channel_id=1, source_target_pairs={{0,128},{4,132},{8,136},{12,140},{16,144},{20,148},{24,152},{28,15... | collective-permute-start | bytes 1179656 | tf_op jit(solution)/shard_map/ppermute | solution.py:46
  73.7 49.2 %collective-permute-start.11 = (bf16[384,2048]{1,0:T(8,128)(2,1)S(1)}, bf16[384,2048]{1,0:T(8,128)(2,1)S(1)}, u32[]{:S(2)}, u32[]{:S(2)}) collective-permute-start(bf16[384,2048]{1,0:T(8,128)(2,1)S(1)} %shard_map.89.refs_2_), channel_id=1, source_target_pairs={{0,8},{4,12},{8,16},{12,20},{16,24},{20,28},{24,32},{28,36},{32,40... | collective-permute-start | bytes 4718600 | tf_op jit(solution)/shard_map/ppermute | solution.py:46
  75.4 47.5 %collective-permute-start.12 = (bf16[384,2048]{1,0:T(8,128)(2,1)S(1)}, bf16[384,2048]{1,0:T(8,128)(2,1)S(1)}, u32[]{:S(2)}, u32[]{:S(2)}) collective-permute-start(bf16[384,2048]{1,0:T(8,128)(2,1)S(1)} %shard_map.89.refs_2_), channel_id=1, source_target_pairs={{0,56},{4,60},{8,0},{12,4},{16,8},{20,12},{24,16},{28,20},{32,24},... | collective-permute-start | bytes 4718600 | tf_op jit(solution)/shard_map/ppermute | solution.py:46
  79.9 19.5 %collective-permute-start.13 = (bf16[512,384]{1,0:T(8,128)(2,1)S(1)}, bf16[512,384]{1,0:T(8,128)(2,1)S(1)}, u32[]{:S(2)}, u32[]{:S(2)}) collective-permute-start(bf16[512,384]{1,0:T(8,128)(2,1)S(1)} %get-tuple-element.58), channel_id=1, source_target_pairs={{0,1},{1,2},{2,3},{3,0},{4,5},{5,6},{6,7},{7,4},{8,9},{9,10},{10,1... | collective-permute-start | bytes 1179656 | tf_op jit(solution)/shard_map/ppermute | solution.py:33
  79.9 19.5 %collective-permute-start.14 = (bf16[512,384]{1,0:T(8,128)(2,1)S(1)}, bf16[512,384]{1,0:T(8,128)(2,1)S(1)}, u32[]{:S(2)}, u32[]{:S(2)}) collective-permute-start(bf16[512,384]{1,0:T(8,128)(2,1)S(1)} %get-tuple-element.59), channel_id=1, source_target_pairs={{0,2},{1,3},{2,0},{3,1},{4,6},{5,7},{6,4},{7,5},{8,10},{9,11},{10,... | collective-permute-start | bytes 1179656 | tf_op jit(solution)/shard_map/ppermute | solution.py:33
  80.4 19.3 %collective-permute-start.15 = (bf16[512,384]{1,0:T(8,128)(2,1)S(1)}, bf16[512,384]{1,0:T(8,128)(2,1)S(1)}, u32[]{:S(2)}, u32[]{:S(2)}) collective-permute-start(bf16[512,384]{1,0:T(8,128)(2,1)S(1)} %get-tuple-element.60), channel_id=1, source_target_pairs={{0,3},{1,0},{2,1},{3,2},{4,7},{5,4},{6,5},{7,6},{8,11},{9,8},{10,9... | collective-permute-start | bytes 1179656 | tf_op jit(solution)/shard_map/ppermute | solution.py:33
  101.3 26.2 %copy-start.8 = (f32[512,384]{1,0:T(8,128)}, f32[512,384]{1,0:T(8,128)S(1)}, u32[]{:S(2)}) copy-start(f32[512,384]{1,0:T(8,128)S(1)} %get-tuple-element.78.refs_2_) | copy-start | bytes 2359300
  101.4 10.1 %collective-permute-start.16 = (bf16[528,384]{1,0:T(8,128)(2,1)S(1)}, bf16[528,384]{1,0:T(8,128)(2,1)S(1)}, u32[]{:S(2)}, u32[]{:S(2)}) collective-permute-start(bf16[528,384]{1,0:T(8,128)(2,1)S(1)} %get-tuple-element.62.refs_4_), channel_id=1, source_target_pairs={{0,64},{4,68},{8,72},{12,76},{16,80},{20,84},{24,88},{28,92},{32,9... | collective-permute-start | bytes 1216520 | tf_op jit(solution)/shard_map/ppermute | solution.py:46
  102.7 18.1 %collective-permute-start.17 = (bf16[528,384]{1,0:T(8,128)(2,1)S(1)}, bf16[528,384]{1,0:T(8,128)(2,1)S(1)}, u32[]{:S(2)}, u32[]{:S(2)}) collective-permute-start(bf16[528,384]{1,0:T(8,128)(2,1)S(1)} %get-tuple-element.62.refs_4_), channel_id=1, source_target_pairs={{0,128},{4,132},{8,136},{12,140},{16,144},{20,148},{24,152},{28,15... | collective-permute-start | bytes 1216520 | tf_op jit(solution)/shard_map/ppermute | solution.py:46
  104.3 18.5 %collective-permute-start.18 = (bf16[528,384]{1,0:T(8,128)(2,1)S(1)}, bf16[528,384]{1,0:T(8,128)(2,1)S(1)}, u32[]{:S(2)}, u32[]{:S(2)}) collective-permute-start(bf16[528,384]{1,0:T(8,128)(2,1)S(1)} %get-tuple-element.62.refs_4_), channel_id=1, source_target_pairs={{0,192},{4,196},{8,200},{12,204},{16,208},{20,212},{24,216},{28,22... | collective-permute-start | bytes 1216520 | tf_op jit(solution)/shard_map/ppermute | solution.py:46
  111.5 21.1 %copy-start.1 = (bf16[1,3,1536,384]{3,2,1,0:T(8,128)(2,1)S(1)}, bf16[1,3,1536,384]{3,2,1,0:T(8,128)(2,1)}, u32[]{:S(2)}) copy-start(bf16[1,3,1536,384]{3,2,1,0:T(8,128)(2,1)} %refs_1_.6) | copy-start | bytes 10616836
  111.5 22.1 %collective-permute-start.20 = (bf16[512,384]{1,0:T(8,128)(2,1)}, bf16[512,384]{1,0:T(8,128)(2,1)}, u32[]{:S(2)}, u32[]{:S(2)}) collective-permute-start(bf16[512,384]{1,0:T(8,128)(2,1)} %get-tuple-element.66.refs_2_), channel_id=1, source_target_pairs={{8,0},{12,4},{16,8},{20,12},{24,16},{28,20},{32,24},{36,28},{40,32... | collective-permute-start | bytes 1179656 | tf_op jit(solution)/shard_map/ppermute | solution.py:29
  120.8 12.7 %collective-permute-start.21 = (bf16[512,384]{1,0:T(8,128)(2,1)}, bf16[512,384]{1,0:T(8,128)(2,1)}, u32[]{:S(2)}, u32[]{:S(2)}) collective-permute-start(bf16[512,384]{1,0:T(8,128)(2,1)} %get-tuple-element.66.refs_2_), channel_id=1, source_target_pairs={{0,8},{4,12},{8,16},{12,20},{16,24},{20,28},{24,32},{28,36},{32,40... | collective-permute-start | bytes 1179656 | tf_op jit(solution)/shard_map/ppermute | solution.py:29
  127.5 1.0 copy-start.6
  128.5 0.6 copy-start.10
  129.1 9.7 %collective-permute-start.19 = (bf16[192,1152]{1,0:T(8,128)(2,1)}, bf16[192,1152]{1,0:T(8,128)(2,1)}, u32[]{:S(2)}, u32[]{:S(2)}) collective-permute-start(bf16[192,1152]{1,0:T(8,128)(2,1)} %get-tuple-element.64), channel_id=1, source_target_pairs={{0,4},{4,0},{8,12},{12,8},{16,20},{20,16},{24,28},{28,24},{32,36},... | collective-permute-start | bytes 1327112 | tf_op jit(solution)/shard_map/ppermute | solution.py:46
  133.6 5.2 %copy-start.7 = (f32[192,1152]{1,0:T(8,128)S(1)}, f32[192,1152]{1,0:T(8,128)}, u32[]{:S(2)}) copy-start(f32[192,1152]{1,0:T(8,128)} %copy-done.6) | copy-start | bytes 2654212
  133.6 5.2 %copy-start.11 = (f32[16,1152]{1,0:T(8,128)S(1)}, f32[16,1152]{1,0:T(8,128)}, u32[]{:S(2)}) copy-start(f32[16,1152]{1,0:T(8,128)} %copy-done.10) | copy-start | bytes 221188
  133.6 49.4 %copy-start.3 = (bf16[512,384]{1,0:T(8,128)(2,1)S(1)}, bf16[512,384]{1,0:T(8,128)(2,1)}, u32[]{:S(2)}) copy-start(bf16[512,384]{1,0:T(8,128)(2,1)} %refs_1_.7) | copy-start | bytes 1179652
  133.6 49.4 %copy-start.9 = (f32[512,384]{1,0:T(8,128)S(1)}, f32[512,384]{1,0:T(8,128)}, u32[]{:S(2)}) copy-start(f32[512,384]{1,0:T(8,128)} %copy-done.8) | copy-start | bytes 2359300
  140.6 15.2 %collective-permute-start.22 = (bf16[40,1152]{1,0:T(8,128)(2,1)S(1)}, bf16[40,1152]{1,0:T(8,128)(2,1)S(1)}, u32[]{:S(2)}, u32[]{:S(2)}) collective-permute-start(bf16[40,1152]{1,0:T(8,128)(2,1)S(1)} %get-tuple-element.70), channel_id=1, source_target_pairs={{0,8},{4,12},{8,16},{12,20},{16,24},{20,28},{24,32},{28,36},{32,40... | collective-permute-start | bytes 276488 | tf_op jit(solution)/shard_map/ppermute | solution.py:46
  142.2 15.3 %collective-permute-start.23 = (bf16[40,1152]{1,0:T(8,128)(2,1)S(1)}, bf16[40,1152]{1,0:T(8,128)(2,1)S(1)}, u32[]{:S(2)}, u32[]{:S(2)}) collective-permute-start(bf16[40,1152]{1,0:T(8,128)(2,1)S(1)} %get-tuple-element.71), channel_id=1, source_target_pairs={{0,16},{4,20},{8,24},{12,28},{16,32},{20,36},{24,40},{28,44},{32,4... | collective-permute-start | bytes 276488 | tf_op jit(solution)/shard_map/ppermute | solution.py:46
  144.7 18.1 %collective-permute-start.24 = (bf16[40,1152]{1,0:T(8,128)(2,1)S(1)}, bf16[40,1152]{1,0:T(8,128)(2,1)S(1)}, u32[]{:S(2)}, u32[]{:S(2)}) collective-permute-start(bf16[40,1152]{1,0:T(8,128)(2,1)S(1)} %get-tuple-element.72), channel_id=1, source_target_pairs={{0,24},{4,28},{8,32},{12,36},{16,40},{20,44},{24,48},{28,52},{32,5... | collective-permute-start | bytes 276488 | tf_op jit(solution)/shard_map/ppermute | solution.py:46
  145.1 21.2 %collective-permute-start.25 = (bf16[40,1152]{1,0:T(8,128)(2,1)S(1)}, bf16[40,1152]{1,0:T(8,128)(2,1)S(1)}, u32[]{:S(2)}, u32[]{:S(2)}) collective-permute-start(bf16[40,1152]{1,0:T(8,128)(2,1)S(1)} %get-tuple-element.73), channel_id=1, source_target_pairs={{0,32},{4,36},{8,40},{12,44},{16,48},{20,52},{24,56},{28,60},{32,0... | collective-permute-start | bytes 276488 | tf_op jit(solution)/shard_map/ppermute | solution.py:46
  151.3 15.9 %collective-permute-start.26 = (bf16[40,1152]{1,0:T(8,128)(2,1)S(1)}, bf16[40,1152]{1,0:T(8,128)(2,1)S(1)}, u32[]{:S(2)}, u32[]{:S(2)}) collective-permute-start(bf16[40,1152]{1,0:T(8,128)(2,1)S(1)} %get-tuple-element.74), channel_id=1, source_target_pairs={{0,40},{4,44},{8,48},{12,52},{16,56},{20,60},{24,0},{28,4},{32,8},... | collective-permute-start | bytes 276488 | tf_op jit(solution)/shard_map/ppermute | solution.py:46
  155.8 27.2 %collective-permute-start.30 = (bf16[512,384]{1,0:T(8,128)(2,1)}, bf16[512,384]{1,0:T(8,128)(2,1)S(1)}, u32[]{:S(2)}, u32[]{:S(2)}) collective-permute-start(bf16[512,384]{1,0:T(8,128)(2,1)} %get-tuple-element.80), channel_id=1, source_target_pairs={{0,1},{1,2},{2,3},{3,0},{4,5},{5,6},{6,7},{7,4},{8,9},{9,10},{10,1... | collective-permute-start | bytes 1179656 | tf_op jit(solution)/shard_map/ppermute | solution.py:33
  157.5 25.5 %collective-permute-start.31 = (bf16[512,384]{1,0:T(8,128)(2,1)}, bf16[512,384]{1,0:T(8,128)(2,1)S(1)}, u32[]{:S(2)}, u32[]{:S(2)}) collective-permute-start(bf16[512,384]{1,0:T(8,128)(2,1)} %get-tuple-element.81), channel_id=1, source_target_pairs={{0,2},{1,3},{2,0},{3,1},{4,6},{5,7},{6,4},{7,5},{8,10},{9,11},{10,... | collective-permute-start | bytes 1179656 | tf_op jit(solution)/shard_map/ppermute | solution.py:33
  162.8 0.6 copy-start.12
  163.4 19.6 %collective-permute-start.32 = (bf16[512,384]{1,0:T(8,128)(2,1)}, bf16[512,384]{1,0:T(8,128)(2,1)S(1)}, u32[]{:S(2)}, u32[]{:S(2)}) collective-permute-start(bf16[512,384]{1,0:T(8,128)(2,1)} %get-tuple-element.82), channel_id=1, source_target_pairs={{0,3},{1,0},{2,1},{3,2},{4,7},{5,4},{6,5},{7,6},{8,11},{9,8},{10,9... | collective-permute-start | bytes 1179656 | tf_op jit(solution)/shard_map/ppermute | solution.py:33
  166.3 0.6 copy-start.14
  166.9 6.3 %collective-permute-start.27 = (bf16[40,1152]{1,0:T(8,128)(2,1)}, bf16[40,1152]{1,0:T(8,128)(2,1)}, u32[]{:S(2)}, u32[]{:S(2)}) collective-permute-start(bf16[40,1152]{1,0:T(8,128)(2,1)} %get-tuple-element.75), channel_id=1, source_target_pairs={{0,48},{4,52},{8,56},{12,60},{16,0},{20,4},{24,8},{28,12},{32,16},... | collective-permute-start | bytes 276488 | tf_op jit(solution)/shard_map/ppermute | solution.py:46
  167.2 0.7 copy-start.16
  167.9 8.3 %collective-permute-start.28 = (bf16[40,1152]{1,0:T(8,128)(2,1)}, bf16[40,1152]{1,0:T(8,128)(2,1)}, u32[]{:S(2)}, u32[]{:S(2)}) collective-permute-start(bf16[40,1152]{1,0:T(8,128)(2,1)} %get-tuple-element.76), channel_id=1, source_target_pairs={{0,56},{4,60},{8,0},{12,4},{16,8},{20,12},{24,16},{28,20},{32,24},... | collective-permute-start | bytes 276488 | tf_op jit(solution)/shard_map/ppermute | solution.py:46
  176.1 0.9 copy-start.13
  177.0 0.9 copy-start.15
  177.9 0.9 copy-start.17
  180.5 4.6 %collective-permute-start.29 = (bf16[8,16,1024]{2,1,0:T(8,128)(2,1)S(1)}, bf16[8,16,1024]{2,1,0:T(8,128)(2,1)S(1)}, u32[]{:S(2)}, u32[]{:S(2)}) collective-permute-start(bf16[8,16,1024]{2,1,0:T(8,128)(2,1)S(1)} %get-tuple-element.77), channel_id=1, source_target_pairs={{0,4},{4,0},{8,12},{12,8},{16,20},{20,16},{24,28},{28,24},{32,36},... | collective-permute-start | bytes 786440 | tf_op jit(solution)/shard_map/ppermute | solution.py:46

commit v6 on v5

--- a/solution.py
+++ b/solution.py
@@ -54,7 +54,7 @@
     return lax.dot_general(left, right, (((1,), (1,)), ((), ())), preferred_element_type=F32)
 
 
-def call(body, place, operands, outs, scratch=(), after=(), limit=16, flops=0, moved=0):
+def call(body, place, operands, outs, scratch=(), after=(), limit=12, flops=0, moved=0):
     count = len(operands)
 
     def kernel(*refs):
@@ -127,6 +127,7 @@
         [like(value.shape, value.dtype) for value in values],
         scratch=[pltpu.SemaphoreType.DMA((count,))],
         after=after,
+        limit=4,
         moved=sum(4 * value.size for value in values),
     )
 
@@ -147,6 +148,7 @@
         [like((width, size), BF)] * NY,
         after=after,
         flops=size * tall,
+        limit=4,
         moved=4 * size * tall,
     )
 
@@ -164,6 +166,7 @@
         local(values),
         [like((rows, len(values) * cols), BF)],
         after=after,
+        limit=4,
         moved=4 * len(values) * values[0].size,
     )[0]
 
@@ -237,6 +240,7 @@
         scratch=[pltpu.VMEM((EXTRA, width), F32)],
         after=after,
         flops=4 * own.size,
+        limit=4,
         moved=16 * own.size,
     )
 
@@ -346,11 +350,12 @@
         scratch=[pltpu.VMEM((rows, cols), F32), pltpu.VMEM((EXTRA + GROUP, cols), F32)],
         after=after,
         flops=4 * rows * cols,
+        limit=4,
         moved=6 * rows * cols,
     )
 
 
-def summed(place, kept, cover, parts, wide):
+def summed(place, kept, cover, parts, wide, after):
     rows, cols = kept.shape
     width = cols // TAPS
 
@@ -370,7 +375,9 @@
         place,
         local([kept, cover] + parts),
         [like((TAPS, rows, width), F32), like((NZ, EXTRA, wide), BF), like((8, 128), F32)],
+        after=after,
         flops=NZ * rows * cols,
+        limit=4,
         moved=2 * NZ * (rows + EXTRA) * cols,
     )
 
@@ -388,21 +395,24 @@
         [like(inputs.shape, BF), like((8, 128), F32)],
         after=after,
         flops=20 * inputs.size,
+        limit=4,
         moved=16 * inputs.size,
     )
 
 
-def coverage_of(blocks, place, exon_blocks, own):
+def counts_of(place, exon_blocks, own):
     _, y, z, core = (place[i] for i in range(4))
     flip, dz, dy, part = jnp.meshgrid(
         *(jnp.arange(n, dtype=jnp.int32) for n in (2, NZ, NY, own)), indexing="ij"
     )
     labels = seq_index((y + NY - dy) % NY, (z + NZ - dz) % NZ, core ^ flip) * own + part
     labels = labels.reshape(-1)
-    counts = (exon_blocks[:, :, None] == labels[None, None]).astype(F32).sum(axis=1)
-    total = jnp.dot(
-        counts.astype(BF), blocks.reshape(labels.shape[0], -1), preferred_element_type=F32
-    )
+    return (exon_blocks[:, :, None] == labels[None, None]).astype(F32).sum(axis=1).astype(BF)
+
+
+def coverage_of(blocks, counts):
+    blocks = blocks.reshape(counts.shape[1], -1)
+    total = jnp.dot(counts, blocks, preferred_element_type=F32)
     return total / jnp.sqrt(F32(EXONS * BLOCK))
 
 
@@ -418,7 +428,8 @@
 
     state = inputs.astype(F32)
     acted = from_all_x(jax.nn.gelu(state).astype(BF))
-    (taps,) = load(place, [conv_weight], (token(acted[0]),))
+    counts = counts_of(place, exon_blocks, own)
+    (taps,) = load(place, [conv_weight], (token(acted[0]), counts))
     low, mid, up, whole = conv_products(place, acted, taps, ())
     low, up = shifted(low, steps), shifted(up, -steps)
     after_conv = (state + (mid + low.astype(F32) + up.astype(F32))).astype(BF)
@@ -442,10 +453,10 @@
     came = [along_x(blocks[r], r) for r in range(1, NX)]
     kept, *parts = over_z(place, kept, along_seq(sent, 0, 0, 1), cover, (done,))
     parts = [along_seq(part, 0, m + 1, 0) for m, part in enumerate(parts)]
-    kernel_gradient, cover, done = summed(place, kept, cover, parts, wide)
-    out, _ = input_gradient(place, inputs, grad, blocks[0], came, (done,))
+    out, done = input_gradient(place, inputs, grad, blocks[0], came, ())
+    kernel_gradient, cover, _ = summed(place, kept, cover, parts, wide, (done,))
     cover = jnp.stack([cover, along_seq(cover, 0, 0, 1)])
-    coverage = coverage_of(cover, place, exon_blocks, own)
+    coverage = coverage_of(cover, counts)
     return (tracks, coverage, out, kernel_gradient[None])
 
 

time: 186 us -> 182 us (0.978)
  local copies, waits for them, and re-layouts: 12.5 us -> 2.71 us
  starting transfers between devices: 65.4 us -> 71.8 us
  waiting for transfers between devices: 71.3 us -> 76.9 us
  Pallas kernels: 30.9 us -> 26.3 us
    ppermute x17, starting transfers between devices: 40.5 us -> 50.6 us  [along_seq(): return lax.ppermute(value, 'seq', pairs)]
    unnamed x36 -> x10, local copies, waits for them, and re-layouts: 8.22 us -> 2.02 us
    pallas_call x13, Pallas kernels: 30.9 us -> 26.3 us  [call(): pl.pallas_call(kernel, in_specs=[pl.BlockSpec(memory_space=pltpu.SMEM)] +...]
    broadcast_in_dim x8, local copies, waits for them, and re-layouts: 4.25 us -> 0.69 us  [counts_of(): jnp.meshgrid(*(jnp.arange(n, dtype=jnp.int32) for n in (2, NZ, NY, own)),...]
    ppermute x12, waiting for transfers between devices: 42.3 us -> 45.3 us  [along_x(): lax.ppermute(value, 'chan', [(i, (i + steps) % NX) for i in range(NX)])]
    ppermute x12, starting transfers between devices: 16.2 us -> 13.5 us  [along_x(): lax.ppermute(value, 'chan', [(i, (i + steps) % NX) for i in range(NX)])]
    ppermute x17, waiting for transfers between devices: 18.2 us -> 20.8 us  [along_seq(): return lax.ppermute(value, 'seq', pairs)]
  transfers between devices with their start and end apart: 33 -> 33, of which waited for: 13 -> 15; matrix products, arithmetic and copies ran while one was open for 4% -> 1% of each run, Pallas kernels for 14% -> 12%
where the time goes in v6:
time: 182 us
  waiting for transfers between devices  76.9 us (42%)
  starting transfers between devices  71.8 us (39%)
  Pallas kernels  26.3 us (14%)
  local copies, waits for them, and re-layouts  2.71 us (1%)
  other arithmetic  2.44 us (1%)
    ppermute x17, starting transfers between devices, along_seq(): return lax.ppermute(value, 'seq', pairs)  50.6 us
    ppermute x12, waiting for transfers between devices, along_x(): lax.ppermute(value, 'chan', [(i, (i + steps) % NX) for i in range(NX)])  45.3 us
    pallas_call x13, Pallas kernels, call(): pl.pallas_call(kernel, in_specs=[pl.BlockSpec(memory_space=pltpu.SMEM)] +...  26.3 us
    ppermute x17, waiting for transfers between devices, along_seq(): return lax.ppermute(value, 'seq', pairs)  20.8 us
    ppermute x12, starting transfers between devices, along_x(): lax.ppermute(value, 'chan', [(i, (i + steps) % NX) for i in range(NX)])  13.5 us
    ppermute x4, waiting for transfers between devices, shifted(): lax.ppermute(value, 'seq', [(s, s + steps) for s in range(leading, last)])  10.8 us
    ppermute x4, starting transfers between devices, shifted(): lax.ppermute(value, 'seq', [(s, s + steps) for s in range(leading, last)])  7.7 us
  transfers between devices with their start and end apart: 33, of which 15 were waited for; matrix products, arithmetic and copies ran while one was open for 1% of the time, Pallas kernels for 12%

profile of v6, /device:TPU:1, one launch (start us, length us, event | category | flops | bytes accessed | tf_op | source)
XLA Modules:
  0.0 181.8 jit_solution(14822616021376199020)
XLA Ops:
  0.6 1.3 fusion.5.refs_1_
  1.9 3.4 %collective-permute-start = (bf16[512,384]{1,0:T(8,128)(2,1)S(1)}, bf16[512,384]{1,0:T(8,128)(2,1)S(1)}, u32[]{:S(2)}, u32[]{:S(2)}) collective-permute-start(bf16[512,384]{1,0:T(8,128)(2,1)S(1)} %fusion.5.refs_1_), channel_id=1, source_target_pairs={{0,3},{1,0},{2,1},{3,2},{4,7},{5,4},{6,5},{7,6},{8,11},{9,8},{10,9... | collective-permute-start | bytes 1179656 | tf_op jit(solution)/shard_map/ppermute | solution.py:33
  5.3 0.5 collective-permute-start.1
  5.8 0.6 collective-permute-start.2
  6.6 0.1 broadcast_in_dim.27
  6.8 0.1 broadcast_in_dim.29
  7.0 0.1 broadcast_in_dim.25
  7.2 0.8 convert_reduce_fusion.refs_3_
  8.0 2.0 %copy-done = bf16[1,3,1536,384]{3,2,1,0:T(8,128)(2,1)S(1)} copy-done((bf16[1,3,1536,384]{3,2,1,0:T(8,128)(2,1)S(1)}, bf16[1,3,1536,384]{3,2,1,0:T(8,128)(2,1)}, u32[]{:S(2)}) %copy-start) | copy-done | bytes 3538968
  10.0 1.0 shard_map.84.refs_5_
  11.0 5.1 %collective-permute-done.refs_2_ = bf16[512,384]{1,0:T(8,128)(2,1)S(1)} collective-permute-done((bf16[512,384]{1,0:T(8,128)(2,1)S(1)}, bf16[512,384]{1,0:T(8,128)(2,1)S(1)}, u32[]{:S(2)}, u32[]{:S(2)}) %collective-permute-start) | collective-permute-done | bytes 393248 | tf_op jit(solution)/shard_map/ppermute | solution.py:33
  16.1 0.4 collective-permute-done.1.refs_3_
  16.5 9.8 %collective-permute-done.2.refs_4_ = bf16[512,384]{1,0:T(8,128)(2,1)S(1)} collective-permute-done((bf16[512,384]{1,0:T(8,128)(2,1)S(1)}, bf16[512,384]{1,0:T(8,128)(2,1)S(1)}, u32[]{:S(2)}, u32[]{:S(2)}) %collective-permute-start.2) | collective-permute-done | bytes 393248 | tf_op jit(solution)/shard_map/ppermute | solution.py:33
  26.3 3.2 %shard_map.85 = (bf16[512,384]{1,0:T(8,128)(2,1)S(1)}, f32[512,384]{1,0:T(8,128)S(1)}, bf16[512,384]{1,0:T(8,128)(2,1)S(1)}, bf16[512,1536]{1,0:T(8,128)(2,1)S(1)}) custom-call(s32[4]{0:T(128)S(1)} %pad_add_fusion.refs_0_, bf16[512,384]{1,0:T(8,128)(2,1)S(1)} %fusion.5.refs_1_, bf16[512,384]{1,0:T(8,128)(2,1)S(1)} %collective-permute-done.refs_2_, ...), custom_call_target="tpu_custom_call" | custom-call | flops 1811939328 | bytes 3538944 | tf_op jit(solution)/shard_map/pallas_call | solution.py:64
  29.5 3.8 %collective-permute-start.3 = (bf16[512,384]{1,0:T(8,128)(2,1)S(1)}, bf16[512,384]{1,0:T(8,128)(2,1)S(1)}, u32[]{:S(2)}, u32[]{:S(2)}) collective-permute-start(bf16[512,384]{1,0:T(8,128)(2,1)S(1)} %get-tuple-element.46), channel_id=1, source_target_pairs={{0,8},{4,12},{8,16},{12,20},{16,24},{20,28},{24,32},{28,36},{32,40... | collective-permute-start | bytes 1179656 | tf_op jit(solution)/shard_map/ppermute | solution.py:29
  33.3 1.3 collective-permute-start.4
  34.6 6.6 %collective-permute-done.3 = bf16[512,384]{1,0:T(8,128)(2,1)S(1)} collective-permute-done((bf16[512,384]{1,0:T(8,128)(2,1)S(1)}, bf16[512,384]{1,0:T(8,128)(2,1)S(1)}, u32[]{:S(2)}, u32[]{:S(2)}) %collective-permute-start.3) | collective-permute-done | bytes 393248 | tf_op jit(solution)/shard_map/ppermute | solution.py:29
  41.3 4.2 %collective-permute-done.4 = bf16[512,384]{1,0:T(8,128)(2,1)S(1)} collective-permute-done((bf16[512,384]{1,0:T(8,128)(2,1)S(1)}, bf16[512,384]{1,0:T(8,128)(2,1)S(1)}, u32[]{:S(2)}, u32[]{:S(2)}) %collective-permute-start.4) | collective-permute-done | bytes 393248 | tf_op jit(solution)/shard_map/ppermute | solution.py:29
  45.5 0.2 fusion.6.refs_1_
  45.8 0.6 collective-permute-start.6
  46.4 0.8 collective-permute-start.7
  47.2 1.0 shard_map.88
  48.2 4.7 %collective-permute-start.10 = (bf16[384,512]{1,0:T(8,128)(2,1)S(1)}, bf16[384,512]{1,0:T(8,128)(2,1)S(1)}, u32[]{:S(2)}, u32[]{:S(2)}) collective-permute-start(bf16[384,512]{1,0:T(8,128)(2,1)S(1)} %get-tuple-element.55), channel_id=1, source_target_pairs={{0,192},{4,196},{8,200},{12,204},{16,208},{20,212},{24,216},{28,22... | collective-permute-start | bytes 1179656 | tf_op jit(solution)/shard_map/ppermute | solution.py:46
  52.9 2.0 %collective-permute-done.5.refs_2_ = bf16[512,384]{1,0:T(8,128)(2,1)S(1)} collective-permute-done((bf16[512,384]{1,0:T(8,128)(2,1)S(1)}, bf16[512,384]{1,0:T(8,128)(2,1)S(1)}, u32[]{:S(2)}, u32[]{:S(2)}) %collective-permute-start.5) | collective-permute-done | bytes 393248 | tf_op jit(solution)/shard_map/ppermute | solution.py:33
  54.9 4.6 %collective-permute-start.9 = (bf16[384,512]{1,0:T(8,128)(2,1)S(1)}, bf16[384,512]{1,0:T(8,128)(2,1)S(1)}, u32[]{:S(2)}, u32[]{:S(2)}) collective-permute-start(bf16[384,512]{1,0:T(8,128)(2,1)S(1)} %get-tuple-element.54), channel_id=1, source_target_pairs={{0,128},{4,132},{8,136},{12,140},{16,144},{20,148},{24,152},{28,15... | collective-permute-start | bytes 1179656 | tf_op jit(solution)/shard_map/ppermute | solution.py:46
  59.5 0.8 shard_map.86
  60.4 6.4 %collective-permute-done.7.refs_4_ = bf16[512,384]{1,0:T(8,128)(2,1)S(1)} collective-permute-done((bf16[512,384]{1,0:T(8,128)(2,1)S(1)}, bf16[512,384]{1,0:T(8,128)(2,1)S(1)}, u32[]{:S(2)}, u32[]{:S(2)}) %collective-permute-start.7) | collective-permute-done | bytes 393248 | tf_op jit(solution)/shard_map/ppermute | solution.py:33
  66.8 6.2 %shard_map.87 = (bf16[512,1024]{1,0:T(8,128)(2,1)}, f32[4,1024]{1,0:T(4,128)S(1)}, f32[512,384]{1,0:T(8,128)S(1)}, bf16[512,384]{1,0:T(8,128)(2,1)S(1)}, bf16[51...) custom-call(s32[4]{0:T(128)S(1)} %pad_add_fusion.refs_0_, ...), custom_call_target="tpu_custom_call" | custom-call | flops 3221225472 | bytes 3145728 | tf_op jit(solution)/shard_map/pallas_call | solution.py:64
  73.1 0.7 shard_map.89.refs_2_
  73.8 1.7 collective-permute-start.11
  75.5 4.4 %collective-permute-start.12 = (bf16[384,2048]{1,0:T(8,128)(2,1)S(1)}, bf16[384,2048]{1,0:T(8,128)(2,1)S(1)}, u32[]{:S(2)}, u32[]{:S(2)}) collective-permute-start(bf16[384,2048]{1,0:T(8,128)(2,1)S(1)} %shard_map.89.refs_2_), channel_id=1, source_target_pairs={{0,56},{4,60},{8,0},{12,4},{16,8},{20,12},{24,16},{28,20},{32,24},... | collective-permute-start | bytes 4718600 | tf_op jit(solution)/shard_map/ppermute | solution.py:46
  79.9 0.5 collective-permute-start.14
  80.5 2.1 %collective-permute-start.15 = (bf16[512,384]{1,0:T(8,128)(2,1)S(1)}, bf16[512,384]{1,0:T(8,128)(2,1)S(1)}, u32[]{:S(2)}, u32[]{:S(2)}) collective-permute-start(bf16[512,384]{1,0:T(8,128)(2,1)S(1)} %get-tuple-element.60), channel_id=1, source_target_pairs={{0,3},{1,0},{2,1},{3,2},{4,7},{5,4},{6,5},{7,6},{8,11},{9,8},{10,9... | collective-permute-start | bytes 1179656 | tf_op jit(solution)/shard_map/ppermute | solution.py:33
  82.6 16.8 %collective-permute-done.13.refs_2_ = bf16[512,384]{1,0:T(8,128)(2,1)S(1)} collective-permute-done((bf16[512,384]{1,0:T(8,128)(2,1)S(1)}, bf16[512,384]{1,0:T(8,128)(2,1)S(1)}, u32[]{:S(2)}, u32[]{:S(2)}) %collective-permute-start.13) | collective-permute-done | bytes 393248 | tf_op jit(solution)/shard_map/ppermute | solution.py:33
  99.4 0.3 collective-permute-done.15.refs_4_
  99.8 0.9 shard_map.90
  100.7 1.4 collective-permute-start.16
  102.1 1.7 collective-permute-start.17
  103.8 2.0 %collective-permute-start.18 = (bf16[528,384]{1,0:T(8,128)(2,1)S(1)}, bf16[528,384]{1,0:T(8,128)(2,1)S(1)}, u32[]{:S(2)}, u32[]{:S(2)}) collective-permute-start(bf16[528,384]{1,0:T(8,128)(2,1)S(1)} %get-tuple-element.62.refs_4_), channel_id=1, source_target_pairs={{0,192},{4,196},{8,200},{12,204},{16,208},{20,212},{24,216},{28,22... | collective-permute-start | bytes 1216520 | tf_op jit(solution)/shard_map/ppermute | solution.py:46
  105.8 5.2 %collective-permute-done.16.refs_5_ = bf16[528,384]{1,0:T(8,128)(2,1)S(1)} collective-permute-done((bf16[528,384]{1,0:T(8,128)(2,1)S(1)}, bf16[528,384]{1,0:T(8,128)(2,1)S(1)}, u32[]{:S(2)}, u32[]{:S(2)}) %collective-permute-start.16) | collective-permute-done | bytes 405536 | tf_op jit(solution)/shard_map/ppermute | solution.py:46
  110.9 1.3 collective-permute-start.20
  112.2 7.9 %collective-permute-done.17.refs_6_ = bf16[528,384]{1,0:T(8,128)(2,1)S(1)} collective-permute-done((bf16[528,384]{1,0:T(8,128)(2,1)S(1)}, bf16[528,384]{1,0:T(8,128)(2,1)S(1)}, u32[]{:S(2)}, u32[]{:S(2)}) %collective-permute-start.17) | collective-permute-done | bytes 405536 | tf_op jit(solution)/shard_map/ppermute | solution.py:46
  120.2 1.3 collective-permute-start.21
  121.5 1.0 shard_map.92.refs_4_
  122.5 3.9 %shard_map.91 = (f32[192,1152]{1,0:T(8,128)S(1)}, bf16[192,1152]{1,0:T(8,128)(2,1)S(1)}, f32[16,1152]{1,0:T(8,128)S(1)}, f32[8,128]{1,0:T(8,128)S(1)}) custom-call(s32[4]{0:T(128)S(1)} %pad_add_fusion.refs_0_, bf16[384,2048]{1,0:T(8,128)(2,1)S(1)} %collective-permute-done.11.refs_1_, bf16[384,2048]{1,0:T(8,128)(2,1)S(1)} %shard_map.89.refs_2_, ...), custom_call_target="tpu_custom_call" | custom-call | flops 1811939328 | bytes 6291456 | tf_op jit(solution)/shard_map/pallas_call | solution.py:64
  126.3 3.1 %collective-permute-start.19 = (bf16[192,1152]{1,0:T(8,128)(2,1)S(1)}, bf16[192,1152]{1,0:T(8,128)(2,1)S(1)}, u32[]{:S(2)}, u32[]{:S(2)}) collective-permute-start(bf16[192,1152]{1,0:T(8,128)(2,1)S(1)} %get-tuple-element.64), channel_id=1, source_target_pairs={{0,4},{4,0},{8,12},{12,8},{16,20},{20,16},{24,28},{28,24},{32,36},... | collective-permute-start | bytes 1327112 | tf_op jit(solution)/shard_map/ppermute | solution.py:46
  129.5 3.6 %shard_map.93 = (f32[512,384]{1,0:T(8,128)S(1)}, bf16[512,384]{1,0:T(8,128)(2,1)S(1)}, bf16[512,384]{1,0:T(8,128)(2,1)S(1)}, bf16[512,384]{1,0:T(8,128)(2,1)S(1)}, f32[8,128]{1,0:T(8,128)S(1)}) custom-call(s32[4]{0:T(128)S(1)} %pad_add_fusion.refs_0_, bf16[512,384]{1,0:T(8,128)(2,1)S(1)} %collective-permute-done.20.refs_1_, ...), custom_call_target="tpu_custom_call" | custom-call | flops 1811939328 | bytes 3538944 | tf_op jit(solution)/shard_map/pallas_call | solution.py:64
  133.1 2.3 %collective-permute-start.29 = (bf16[512,384]{1,0:T(8,128)(2,1)S(1)}, bf16[512,384]{1,0:T(8,128)(2,1)S(1)}, u32[]{:S(2)}, u32[]{:S(2)}) collective-permute-start(bf16[512,384]{1,0:T(8,128)(2,1)S(1)} %get-tuple-element.79), channel_id=1, source_target_pairs={{0,1},{1,2},{2,3},{3,0},{4,5},{5,6},{6,7},{7,4},{8,9},{9,10},{10,1... | collective-permute-start | bytes 1179656 | tf_op jit(solution)/shard_map/ppermute | solution.py:33
  135.4 2.1 %collective-permute-start.30 = (bf16[512,384]{1,0:T(8,128)(2,1)S(1)}, bf16[512,384]{1,0:T(8,128)(2,1)S(1)}, u32[]{:S(2)}, u32[]{:S(2)}) collective-permute-start(bf16[512,384]{1,0:T(8,128)(2,1)S(1)} %get-tuple-element.80), channel_id=1, source_target_pairs={{0,2},{1,3},{2,0},{3,1},{4,6},{5,7},{6,4},{7,5},{8,10},{9,11},{10,... | collective-permute-start | bytes 1179656 | tf_op jit(solution)/shard_map/ppermute | solution.py:33
  137.5 0.4 collective-permute-start.31
  137.9 0.7 shard_map.94
  138.6 2.3 %collective-permute-start.22 = (bf16[40,1152]{1,0:T(8,128)(2,1)S(1)}, bf16[40,1152]{1,0:T(8,128)(2,1)S(1)}, u32[]{:S(2)}, u32[]{:S(2)}) collective-permute-start(bf16[40,1152]{1,0:T(8,128)(2,1)S(1)} %get-tuple-element.70), channel_id=1, source_target_pairs={{0,8},{4,12},{8,16},{12,20},{16,24},{20,28},{24,32},{28,36},{32,40... | collective-permute-start | bytes 276488 | tf_op jit(solution)/shard_map/ppermute | solution.py:46
  140.9 3.2 %collective-permute-start.23 = (bf16[40,1152]{1,0:T(8,128)(2,1)S(1)}, bf16[40,1152]{1,0:T(8,128)(2,1)S(1)}, u32[]{:S(2)}, u32[]{:S(2)}) collective-permute-start(bf16[40,1152]{1,0:T(8,128)(2,1)S(1)} %get-tuple-element.71), channel_id=1, source_target_pairs={{0,16},{4,20},{8,24},{12,28},{16,32},{20,36},{24,40},{28,44},{32,4... | collective-permute-start | bytes 276488 | tf_op jit(solution)/shard_map/ppermute | solution.py:46
  144.0 4.1 %collective-permute-start.24 = (bf16[40,1152]{1,0:T(8,128)(2,1)S(1)}, bf16[40,1152]{1,0:T(8,128)(2,1)S(1)}, u32[]{:S(2)}, u32[]{:S(2)}) collective-permute-start(bf16[40,1152]{1,0:T(8,128)(2,1)S(1)} %get-tuple-element.72), channel_id=1, source_target_pairs={{0,24},{4,28},{8,32},{12,36},{16,40},{20,44},{24,48},{28,52},{32,5... | collective-permute-start | bytes 276488 | tf_op jit(solution)/shard_map/ppermute | solution.py:46
  148.1 4.5 %collective-permute-done.30.refs_5_ = bf16[512,384]{1,0:T(8,128)(2,1)S(1)} collective-permute-done((bf16[512,384]{1,0:T(8,128)(2,1)S(1)}, bf16[512,384]{1,0:T(8,128)(2,1)S(1)}, u32[]{:S(2)}, u32[]{:S(2)}) %collective-permute-start.30) | collective-permute-done | bytes 393248 | tf_op jit(solution)/shard_map/ppermute | solution.py:33
  152.6 7.1 %collective-permute-start.25 = (bf16[40,1152]{1,0:T(8,128)(2,1)S(1)}, bf16[40,1152]{1,0:T(8,128)(2,1)S(1)}, u32[]{:S(2)}, u32[]{:S(2)}) collective-permute-start(bf16[40,1152]{1,0:T(8,128)(2,1)S(1)} %get-tuple-element.73), channel_id=1, source_target_pairs={{0,32},{4,36},{8,40},{12,44},{16,48},{20,52},{24,56},{28,60},{32,0... | collective-permute-start | bytes 276488 | tf_op jit(solution)/shard_map/ppermute | solution.py:46
  159.7 8.3 %collective-permute-start.27 = (bf16[40,1152]{1,0:T(8,128)(2,1)S(1)}, bf16[40,1152]{1,0:T(8,128)(2,1)S(1)}, u32[]{:S(2)}, u32[]{:S(2)}) collective-permute-start(bf16[40,1152]{1,0:T(8,128)(2,1)S(1)} %get-tuple-element.75), channel_id=1, source_target_pairs={{0,48},{4,52},{8,56},{12,60},{16,0},{20,4},{24,8},{28,12},{32,16},... | collective-permute-start | bytes 276488 | tf_op jit(solution)/shard_map/ppermute | solution.py:46
  168.0 2.0 %shard_map.95 = (bf16[512,384]{1,0:T(8,128)(2,1)}, f32[8,128]{1,0:T(8,128)S(1)}) custom-call(s32[4]{0:T(128)S(1)} %pad_add_fusion.refs_0_, bf16[512,384]{1,0:T(8,128)(2,1)S(1)} %copy-done.2, f32[512,384]{1,0:T(8,128)S(1)} %get-tuple-element.77.refs_2_, f32[512,384]{1,0:T(8,128)S(1)} %get-tuple-element.78.refs_3_, ...), custom_call_target="tpu_custom_call" | custom-call | flops 3932160 | bytes 3145728 | tf_op jit(solution)/shard_map/pallas_call | solution.py:64
  170.1 1.3 collective-permute-done.26.refs_7_
  171.4 5.2 %collective-permute-done.27.refs_8_ = bf16[40,1152]{1,0:T(8,128)(2,1)S(1)} collective-permute-done((bf16[40,1152]{1,0:T(8,128)(2,1)S(1)}, bf16[40,1152]{1,0:T(8,128)(2,1)S(1)}, u32[]{:S(2)}, u32[]{:S(2)}) %collective-permute-start.27) | collective-permute-done | bytes 92192 | tf_op jit(solution)/shard_map/ppermute | solution.py:46
  176.6 1.3 shard_map.96
  177.8 2.0 %collective-permute-start.32 = (bf16[8,16,1024]{2,1,0:T(8,128)(2,1)S(1)}, bf16[8,16,1024]{2,1,0:T(8,128)(2,1)S(1)}, u32[]{:S(2)}, u32[]{:S(2)}) collective-permute-start(bf16[8,16,1024]{2,1,0:T(8,128)(2,1)S(1)} %get-tuple-element.83), channel_id=1, source_target_pairs={{0,4},{4,0},{8,12},{12,8},{16,20},{20,16},{24,28},{28,24},{32,36},... | collective-permute-start | bytes 786440 | tf_op jit(solution)/shard_map/ppermute | solution.py:46
  179.8 1.2 collective-permute-done.32
  181.0 0.8 convolution_multiply_fusion
  (45 shorter events, 0.7 us)
Async XLA Ops:
  1.9 14.2 %collective-permute-start = (bf16[512,384]{1,0:T(8,128)(2,1)S(1)}, bf16[512,384]{1,0:T(8,128)(2,1)S(1)}, u32[]{:S(2)}, u32[]{:S(2)}) collective-permute-start(bf16[512,384]{1,0:T(8,128)(2,1)S(1)} %fusion.5.refs_1_), channel_id=1, source_target_pairs={{0,3},{1,0},{2,1},{3,2},{4,7},{5,4},{6,5},{7,6},{8,11},{9,8},{10,9... | collective-permute-start | bytes 1179656 | tf_op jit(solution)/shard_map/ppermute | solution.py:33
  5.3 11.2 %collective-permute-start.1 = (bf16[512,384]{1,0:T(8,128)(2,1)S(1)}, bf16[512,384]{1,0:T(8,128)(2,1)S(1)}, u32[]{:S(2)}, u32[]{:S(2)}) collective-permute-start(bf16[512,384]{1,0:T(8,128)(2,1)S(1)} %fusion.5.refs_1_), channel_id=1, source_target_pairs={{0,2},{1,3},{2,0},{3,1},{4,6},{5,7},{6,4},{7,5},{8,10},{9,11},{10,... | collective-permute-start | bytes 1179656 | tf_op jit(solution)/shard_map/ppermute | solution.py:33
  5.8 20.4 %collective-permute-start.2 = (bf16[512,384]{1,0:T(8,128)(2,1)S(1)}, bf16[512,384]{1,0:T(8,128)(2,1)S(1)}, u32[]{:S(2)}, u32[]{:S(2)}) collective-permute-start(bf16[512,384]{1,0:T(8,128)(2,1)S(1)} %fusion.5.refs_1_), channel_id=1, source_target_pairs={{0,1},{1,2},{2,3},{3,0},{4,5},{5,6},{6,7},{7,4},{8,9},{9,10},{10,1... | collective-permute-start | bytes 1179656 | tf_op jit(solution)/shard_map/ppermute | solution.py:33
  8.0 2.0 %copy-start = (bf16[1,3,1536,384]{3,2,1,0:T(8,128)(2,1)S(1)}, bf16[1,3,1536,384]{3,2,1,0:T(8,128)(2,1)}, u32[]{:S(2)}) copy-start(bf16[1,3,1536,384]{3,2,1,0:T(8,128)(2,1)} %refs_1_.6) | copy-start | bytes 10616836
  11.0 34.5 %copy-start.2 = (bf16[512,384]{1,0:T(8,128)(2,1)S(1)}, bf16[512,384]{1,0:T(8,128)(2,1)}, u32[]{:S(2)}) copy-start(bf16[512,384]{1,0:T(8,128)(2,1)} %refs_1_.7) | copy-start | bytes 1179652
  26.3 33.3 %copy-start.4 = (bf16[512,1024]{1,0:T(8,128)(2,1)S(1)}, bf16[512,1024]{1,0:T(8,128)(2,1)}, u32[]{:S(2)}) copy-start(bf16[512,1024]{1,0:T(8,128)(2,1)} %refs_2_.1) | copy-start | bytes 3145732
  29.5 30.0 %copy-start.3 = (bf16[1536,1024]{1,0:T(8,128)(2,1)S(1)}, bf16[1536,1024]{1,0:T(8,128)(2,1)}, u32[]{:S(2)}) copy-start(bf16[1536,1024]{1,0:T(8,128)(2,1)} %refs_1_.5) | copy-start | bytes 9437188
  29.5 11.8 %collective-permute-start.3 = (bf16[512,384]{1,0:T(8,128)(2,1)S(1)}, bf16[512,384]{1,0:T(8,128)(2,1)S(1)}, u32[]{:S(2)}, u32[]{:S(2)}) collective-permute-start(bf16[512,384]{1,0:T(8,128)(2,1)S(1)} %get-tuple-element.46), channel_id=1, source_target_pairs={{0,8},{4,12},{8,16},{12,20},{16,24},{20,28},{24,32},{28,36},{32,40... | collective-permute-start | bytes 1179656 | tf_op jit(solution)/shard_map/ppermute | solution.py:29
  33.3 12.1 %collective-permute-start.4 = (bf16[512,384]{1,0:T(8,128)(2,1)S(1)}, bf16[512,384]{1,0:T(8,128)(2,1)S(1)}, u32[]{:S(2)}, u32[]{:S(2)}) collective-permute-start(bf16[512,384]{1,0:T(8,128)(2,1)S(1)} %get-tuple-element.47), channel_id=1, source_target_pairs={{8,0},{12,4},{16,8},{20,12},{24,16},{28,20},{32,24},{36,28},{40,32... | collective-permute-start | bytes 1179656 | tf_op jit(solution)/shard_map/ppermute | solution.py:29
  45.7 9.2 %collective-permute-start.5 = (bf16[512,384]{1,0:T(8,128)(2,1)S(1)}, bf16[512,384]{1,0:T(8,128)(2,1)S(1)}, u32[]{:S(2)}, u32[]{:S(2)}) collective-permute-start(bf16[512,384]{1,0:T(8,128)(2,1)S(1)} %fusion.6.refs_1_), channel_id=1, source_target_pairs={{0,3},{1,0},{2,1},{3,2},{4,7},{5,4},{6,5},{7,6},{8,11},{9,8},{10,9... | collective-permute-start | bytes 1179656 | tf_op jit(solution)/shard_map/ppermute | solution.py:33
  45.8 14.6 %collective-permute-start.6 = (bf16[512,384]{1,0:T(8,128)(2,1)S(1)}, bf16[512,384]{1,0:T(8,128)(2,1)S(1)}, u32[]{:S(2)}, u32[]{:S(2)}) collective-permute-start(bf16[512,384]{1,0:T(8,128)(2,1)S(1)} %fusion.6.refs_1_), channel_id=1, source_target_pairs={{0,2},{1,3},{2,0},{3,1},{4,6},{5,7},{6,4},{7,5},{8,10},{9,11},{10,... | collective-permute-start | bytes 1179656 | tf_op jit(solution)/shard_map/ppermute | solution.py:33
  46.4 20.4 %collective-permute-start.7 = (bf16[512,384]{1,0:T(8,128)(2,1)S(1)}, bf16[512,384]{1,0:T(8,128)(2,1)S(1)}, u32[]{:S(2)}, u32[]{:S(2)}) collective-permute-start(bf16[512,384]{1,0:T(8,128)(2,1)S(1)} %fusion.6.refs_1_), channel_id=1, source_target_pairs={{0,1},{1,2},{2,3},{3,0},{4,5},{5,6},{6,7},{7,4},{8,9},{9,10},{10,1... | collective-permute-start | bytes 1179656 | tf_op jit(solution)/shard_map/ppermute | solution.py:33
  48.2 24.8 %collective-permute-start.10 = (bf16[384,512]{1,0:T(8,128)(2,1)S(1)}, bf16[384,512]{1,0:T(8,128)(2,1)S(1)}, u32[]{:S(2)}, u32[]{:S(2)}) collective-permute-start(bf16[384,512]{1,0:T(8,128)(2,1)S(1)} %get-tuple-element.55), channel_id=1, source_target_pairs={{0,192},{4,196},{8,200},{12,204},{16,208},{20,212},{24,216},{28,22... | collective-permute-start | bytes 1179656 | tf_op jit(solution)/shard_map/ppermute | solution.py:46
  52.9 20.2 %collective-permute-start.8 = (bf16[384,512]{1,0:T(8,128)(2,1)S(1)}, bf16[384,512]{1,0:T(8,128)(2,1)S(1)}, u32[]{:S(2)}, u32[]{:S(2)}) collective-permute-start(bf16[384,512]{1,0:T(8,128)(2,1)S(1)} %get-tuple-element.53), channel_id=1, source_target_pairs={{0,64},{4,68},{8,72},{12,76},{16,80},{20,84},{24,88},{28,92},{32,9... | collective-permute-start | bytes 1179656 | tf_op jit(solution)/shard_map/ppermute | solution.py:46
  54.9 18.2 %collective-permute-start.9 = (bf16[384,512]{1,0:T(8,128)(2,1)S(1)}, bf16[384,512]{1,0:T(8,128)(2,1)S(1)}, u32[]{:S(2)}, u32[]{:S(2)}) collective-permute-start(bf16[384,512]{1,0:T(8,128)(2,1)S(1)} %get-tuple-element.54), channel_id=1, source_target_pairs={{0,128},{4,132},{8,136},{12,140},{16,144},{20,148},{24,152},{28,15... | collective-permute-start | bytes 1179656 | tf_op jit(solution)/shard_map/ppermute | solution.py:46
  73.1 48.4 %copy-start.1 = (bf16[1,3,1536,384]{3,2,1,0:T(8,128)(2,1)S(1)}, bf16[1,3,1536,384]{3,2,1,0:T(8,128)(2,1)}, u32[]{:S(2)}) copy-start(bf16[1,3,1536,384]{3,2,1,0:T(8,128)(2,1)} %refs_1_.6) | copy-start | bytes 10616836
  73.8 48.7 %collective-permute-start.11 = (bf16[384,2048]{1,0:T(8,128)(2,1)S(1)}, bf16[384,2048]{1,0:T(8,128)(2,1)S(1)}, u32[]{:S(2)}, u32[]{:S(2)}) collective-permute-start(bf16[384,2048]{1,0:T(8,128)(2,1)S(1)} %shard_map.89.refs_2_), channel_id=1, source_target_pairs={{0,8},{4,12},{8,16},{12,20},{16,24},{20,28},{24,32},{28,36},{32,40... | collective-permute-start | bytes 4718600 | tf_op jit(solution)/shard_map/ppermute | solution.py:46
  75.5 47.0 %collective-permute-start.12 = (bf16[384,2048]{1,0:T(8,128)(2,1)S(1)}, bf16[384,2048]{1,0:T(8,128)(2,1)S(1)}, u32[]{:S(2)}, u32[]{:S(2)}) collective-permute-start(bf16[384,2048]{1,0:T(8,128)(2,1)S(1)} %shard_map.89.refs_2_), channel_id=1, source_target_pairs={{0,56},{4,60},{8,0},{12,4},{16,8},{20,12},{24,16},{28,20},{32,24},... | collective-permute-start | bytes 4718600 | tf_op jit(solution)/shard_map/ppermute | solution.py:46
  79.9 19.5 %collective-permute-start.13 = (bf16[512,384]{1,0:T(8,128)(2,1)S(1)}, bf16[512,384]{1,0:T(8,128)(2,1)S(1)}, u32[]{:S(2)}, u32[]{:S(2)}) collective-permute-start(bf16[512,384]{1,0:T(8,128)(2,1)S(1)} %get-tuple-element.58), channel_id=1, source_target_pairs={{0,1},{1,2},{2,3},{3,0},{4,5},{5,6},{6,7},{7,4},{8,9},{9,10},{10,1... | collective-permute-start | bytes 1179656 | tf_op jit(solution)/shard_map/ppermute | solution.py:33
  79.9 19.5 %collective-permute-start.14 = (bf16[512,384]{1,0:T(8,128)(2,1)S(1)}, bf16[512,384]{1,0:T(8,128)(2,1)S(1)}, u32[]{:S(2)}, u32[]{:S(2)}) collective-permute-start(bf16[512,384]{1,0:T(8,128)(2,1)S(1)} %get-tuple-element.59), channel_id=1, source_target_pairs={{0,2},{1,3},{2,0},{3,1},{4,6},{5,7},{6,4},{7,5},{8,10},{9,11},{10,... | collective-permute-start | bytes 1179656 | tf_op jit(solution)/shard_map/ppermute | solution.py:33
  80.5 19.3 %collective-permute-start.15 = (bf16[512,384]{1,0:T(8,128)(2,1)S(1)}, bf16[512,384]{1,0:T(8,128)(2,1)S(1)}, u32[]{:S(2)}, u32[]{:S(2)}) collective-permute-start(bf16[512,384]{1,0:T(8,128)(2,1)S(1)} %get-tuple-element.60), channel_id=1, source_target_pairs={{0,3},{1,0},{2,1},{3,2},{4,7},{5,4},{6,5},{7,6},{8,11},{9,8},{10,9... | collective-permute-start | bytes 1179656 | tf_op jit(solution)/shard_map/ppermute | solution.py:33
  100.7 10.2 %collective-permute-start.16 = (bf16[528,384]{1,0:T(8,128)(2,1)S(1)}, bf16[528,384]{1,0:T(8,128)(2,1)S(1)}, u32[]{:S(2)}, u32[]{:S(2)}) collective-permute-start(bf16[528,384]{1,0:T(8,128)(2,1)S(1)} %get-tuple-element.62.refs_4_), channel_id=1, source_target_pairs={{0,64},{4,68},{8,72},{12,76},{16,80},{20,84},{24,88},{28,92},{32,9... | collective-permute-start | bytes 1216520 | tf_op jit(solution)/shard_map/ppermute | solution.py:46
  102.1 18.1 %collective-permute-start.17 = (bf16[528,384]{1,0:T(8,128)(2,1)S(1)}, bf16[528,384]{1,0:T(8,128)(2,1)S(1)}, u32[]{:S(2)}, u32[]{:S(2)}) collective-permute-start(bf16[528,384]{1,0:T(8,128)(2,1)S(1)} %get-tuple-element.62.refs_4_), channel_id=1, source_target_pairs={{0,128},{4,132},{8,136},{12,140},{16,144},{20,148},{24,152},{28,15... | collective-permute-start | bytes 1216520 | tf_op jit(solution)/shard_map/ppermute | solution.py:46
  103.8 18.6 %collective-permute-start.18 = (bf16[528,384]{1,0:T(8,128)(2,1)S(1)}, bf16[528,384]{1,0:T(8,128)(2,1)S(1)}, u32[]{:S(2)}, u32[]{:S(2)}) collective-permute-start(bf16[528,384]{1,0:T(8,128)(2,1)S(1)} %get-tuple-element.62.refs_4_), channel_id=1, source_target_pairs={{0,192},{4,196},{8,200},{12,204},{16,208},{20,212},{24,216},{28,22... | collective-permute-start | bytes 1216520 | tf_op jit(solution)/shard_map/ppermute | solution.py:46
  110.9 18.5 %collective-permute-start.20 = (bf16[512,384]{1,0:T(8,128)(2,1)S(1)}, bf16[512,384]{1,0:T(8,128)(2,1)S(1)}, u32[]{:S(2)}, u32[]{:S(2)}) collective-permute-start(bf16[512,384]{1,0:T(8,128)(2,1)S(1)} %get-tuple-element.66.refs_2_), channel_id=1, source_target_pairs={{8,0},{12,4},{16,8},{20,12},{24,16},{28,20},{32,24},{36,28},{40,32... | collective-permute-start | bytes 1179656 | tf_op jit(solution)/shard_map/ppermute | solution.py:29
  120.2 9.3 %collective-permute-start.21 = (bf16[512,384]{1,0:T(8,128)(2,1)S(1)}, bf16[512,384]{1,0:T(8,128)(2,1)S(1)}, u32[]{:S(2)}, u32[]{:S(2)}) collective-permute-start(bf16[512,384]{1,0:T(8,128)(2,1)S(1)} %get-tuple-element.66.refs_2_), channel_id=1, source_target_pairs={{0,8},{4,12},{8,16},{12,20},{16,24},{20,28},{24,32},{28,36},{32,40... | collective-permute-start | bytes 1179656 | tf_op jit(solution)/shard_map/ppermute | solution.py:29
  126.3 11.5 %collective-permute-start.19 = (bf16[192,1152]{1,0:T(8,128)(2,1)S(1)}, bf16[192,1152]{1,0:T(8,128)(2,1)S(1)}, u32[]{:S(2)}, u32[]{:S(2)}) collective-permute-start(bf16[192,1152]{1,0:T(8,128)(2,1)S(1)} %get-tuple-element.64), channel_id=1, source_target_pairs={{0,4},{4,0},{8,12},{12,8},{16,20},{20,16},{24,28},{28,24},{32,36},... | collective-permute-start | bytes 1327112 | tf_op jit(solution)/shard_map/ppermute | solution.py:46
  133.1 10.9 %collective-permute-start.29 = (bf16[512,384]{1,0:T(8,128)(2,1)S(1)}, bf16[512,384]{1,0:T(8,128)(2,1)S(1)}, u32[]{:S(2)}, u32[]{:S(2)}) collective-permute-start(bf16[512,384]{1,0:T(8,128)(2,1)S(1)} %get-tuple-element.79), channel_id=1, source_target_pairs={{0,1},{1,2},{2,3},{3,0},{4,5},{5,6},{6,7},{7,4},{8,9},{9,10},{10,1... | collective-permute-start | bytes 1179656 | tf_op jit(solution)/shard_map/ppermute | solution.py:33
  135.4 17.2 %collective-permute-start.30 = (bf16[512,384]{1,0:T(8,128)(2,1)S(1)}, bf16[512,384]{1,0:T(8,128)(2,1)S(1)}, u32[]{:S(2)}, u32[]{:S(2)}) collective-permute-start(bf16[512,384]{1,0:T(8,128)(2,1)S(1)} %get-tuple-element.80), channel_id=1, source_target_pairs={{0,2},{1,3},{2,0},{3,1},{4,6},{5,7},{6,4},{7,5},{8,10},{9,11},{10,... | collective-permute-start | bytes 1179656 | tf_op jit(solution)/shard_map/ppermute | solution.py:33
  137.5 22.2 %collective-permute-start.31 = (bf16[512,384]{1,0:T(8,128)(2,1)S(1)}, bf16[512,384]{1,0:T(8,128)(2,1)S(1)}, u32[]{:S(2)}, u32[]{:S(2)}) collective-permute-start(bf16[512,384]{1,0:T(8,128)(2,1)S(1)} %get-tuple-element.81), channel_id=1, source_target_pairs={{0,3},{1,0},{2,1},{3,2},{4,7},{5,4},{6,5},{7,6},{8,11},{9,8},{10,9... | collective-permute-start | bytes 1179656 | tf_op jit(solution)/shard_map/ppermute | solution.py:33
  138.6 21.1 %collective-permute-start.22 = (bf16[40,1152]{1,0:T(8,128)(2,1)S(1)}, bf16[40,1152]{1,0:T(8,128)(2,1)S(1)}, u32[]{:S(2)}, u32[]{:S(2)}) collective-permute-start(bf16[40,1152]{1,0:T(8,128)(2,1)S(1)} %get-tuple-element.70), channel_id=1, source_target_pairs={{0,8},{4,12},{8,16},{12,20},{16,24},{20,28},{24,32},{28,36},{32,40... | collective-permute-start | bytes 276488 | tf_op jit(solution)/shard_map/ppermute | solution.py:46
  140.9 27.2 %collective-permute-start.23 = (bf16[40,1152]{1,0:T(8,128)(2,1)S(1)}, bf16[40,1152]{1,0:T(8,128)(2,1)S(1)}, u32[]{:S(2)}, u32[]{:S(2)}) collective-permute-start(bf16[40,1152]{1,0:T(8,128)(2,1)S(1)} %get-tuple-element.71), channel_id=1, source_target_pairs={{0,16},{4,20},{8,24},{12,28},{16,32},{20,36},{24,40},{28,44},{32,4... | collective-permute-start | bytes 276488 | tf_op jit(solution)/shard_map/ppermute | solution.py:46
  144.0 26.0 %collective-permute-start.24 = (bf16[40,1152]{1,0:T(8,128)(2,1)S(1)}, bf16[40,1152]{1,0:T(8,128)(2,1)S(1)}, u32[]{:S(2)}, u32[]{:S(2)}) collective-permute-start(bf16[40,1152]{1,0:T(8,128)(2,1)S(1)} %get-tuple-element.72), channel_id=1, source_target_pairs={{0,24},{4,28},{8,32},{12,36},{16,40},{20,44},{24,48},{28,52},{32,5... | collective-permute-start | bytes 276488 | tf_op jit(solution)/shard_map/ppermute | solution.py:46
  152.6 17.5 %collective-permute-start.25 = (bf16[40,1152]{1,0:T(8,128)(2,1)S(1)}, bf16[40,1152]{1,0:T(8,128)(2,1)S(1)}, u32[]{:S(2)}, u32[]{:S(2)}) collective-permute-start(bf16[40,1152]{1,0:T(8,128)(2,1)S(1)} %get-tuple-element.73), channel_id=1, source_target_pairs={{0,32},{4,36},{8,40},{12,44},{16,48},{20,52},{24,56},{28,60},{32,0... | collective-permute-start | bytes 276488 | tf_op jit(solution)/shard_map/ppermute | solution.py:46
  159.7 11.7 %collective-permute-start.26 = (bf16[40,1152]{1,0:T(8,128)(2,1)S(1)}, bf16[40,1152]{1,0:T(8,128)(2,1)S(1)}, u32[]{:S(2)}, u32[]{:S(2)}) collective-permute-start(bf16[40,1152]{1,0:T(8,128)(2,1)S(1)} %get-tuple-element.74), channel_id=1, source_target_pairs={{0,40},{4,44},{8,48},{12,52},{16,56},{20,60},{24,0},{28,4},{32,8},... | collective-permute-start | bytes 276488 | tf_op jit(solution)/shard_map/ppermute | solution.py:46
  159.7 16.9 %collective-permute-start.27 = (bf16[40,1152]{1,0:T(8,128)(2,1)S(1)}, bf16[40,1152]{1,0:T(8,128)(2,1)S(1)}, u32[]{:S(2)}, u32[]{:S(2)}) collective-permute-start(bf16[40,1152]{1,0:T(8,128)(2,1)S(1)} %get-tuple-element.75), channel_id=1, source_target_pairs={{0,48},{4,52},{8,56},{12,60},{16,0},{20,4},{24,8},{28,12},{32,16},... | collective-permute-start | bytes 276488 | tf_op jit(solution)/shard_map/ppermute | solution.py:46
  168.0 8.6 %collective-permute-start.28 = (bf16[40,1152]{1,0:T(8,128)(2,1)S(1)}, bf16[40,1152]{1,0:T(8,128)(2,1)S(1)}, u32[]{:S(2)}, u32[]{:S(2)}) collective-permute-start(bf16[40,1152]{1,0:T(8,128)(2,1)S(1)} %get-tuple-element.76), channel_id=1, source_target_pairs={{0,56},{4,60},{8,0},{12,4},{16,8},{20,12},{24,16},{28,20},{32,24},... | collective-permute-start | bytes 276488 | tf_op jit(solution)/shard_map/ppermute | solution.py:46
  177.8 3.1 %collective-permute-start.32 = (bf16[8,16,1024]{2,1,0:T(8,128)(2,1)S(1)}, bf16[8,16,1024]{2,1,0:T(8,128)(2,1)S(1)}, u32[]{:S(2)}, u32[]{:S(2)}) collective-permute-start(bf16[8,16,1024]{2,1,0:T(8,128)(2,1)S(1)} %get-tuple-element.83), channel_id=1, source_target_pairs={{0,4},{4,0},{8,12},{12,8},{16,20},{20,16},{24,28},{28,24},{32,36},... | collective-permute-start | bytes 786440 | tf_op jit(solution)/shard_map/ppermute | solution.py:46

commit v7 on v6

--- a/solution.py
+++ b/solution.py
@@ -330,55 +330,48 @@
 def over_z(place, kept, came, cover, after):
     rows, cols = kept.shape
 
-    def body(place, kept, came, cover, *refs):
-        outs, total, message = refs[:NZ], refs[NZ], refs[NZ + 1]
-        total[...] = kept[...] + came[...].astype(F32)
+    def body(place, kept, came, cover, out, message):
+        total = kept[...] + came[...].astype(F32)
         message[:EXTRA, :] = cover[...]
-        for m, ref in enumerate(outs):
-            at = pl.multiple_of(lax.rem(place[2] + m, NZ) * GROUP, 8)
-            if m == 0:
-                ref[...] = total[pl.ds(at, GROUP), :]
-            else:
-                message[EXTRA:, :] = total[pl.ds(at, GROUP), :]
-                ref[...] = message[...].astype(BF)
+        for z in range(NZ):
+            message[EXTRA:, :] = total[z * GROUP : (z + 1) * GROUP, :]
+            out[z] = message[...].astype(BF)
 
     return call(
         body,
         place,
         local([kept, came, cover]),
-        [like((GROUP, cols), F32)] + [like((EXTRA + GROUP, cols), BF)] * (NZ - 1),
-        scratch=[pltpu.VMEM((rows, cols), F32), pltpu.VMEM((EXTRA + GROUP, cols), F32)],
+        [like((NZ, EXTRA + GROUP, cols), BF)],
+        scratch=[pltpu.VMEM((EXTRA + GROUP, cols), F32)],
         after=after,
         flops=4 * rows * cols,
-        limit=4,
         moved=6 * rows * cols,
-    )
-
-
-def summed(place, kept, cover, parts, wide, after):
-    rows, cols = kept.shape
+        limit=8,
+    )[0]
+
+
+def summed(place, parts, wide, after):
+    _, rows, cols = parts.shape
+    rows = rows - EXTRA
     width = cols // TAPS
 
-    def body(place, kept, cover, *refs):
-        parts, (out, blocks, done) = refs[: NZ - 1], refs[NZ - 1 :]
-        done[...] = jnp.zeros_like(done)
-        total = kept[...]
-        blocks[0] = cover[:, :wide].astype(BF)
-        for m, part in enumerate(parts):
-            total += part[...].astype(F32)[EXTRA:]
-            blocks[m + 1] = part[:EXTRA, :wide]
+    def body(place, parts, out, blocks):
+        total = jnp.zeros((rows, cols), F32)
+        for z in range(NZ):
+            total += parts[z].astype(F32)[EXTRA:]
+            blocks[z] = parts[z, :EXTRA, :wide]
         for k in range(TAPS):
             out[k] = total[:, k * width : (k + 1) * width]
 
     return call(
         body,
         place,
-        local([kept, cover] + parts),
-        [like((TAPS, rows, width), F32), like((NZ, EXTRA, wide), BF), like((8, 128), F32)],
+        local([parts]),
+        [like((TAPS, rows, width), F32), like((NZ, EXTRA, wide), BF)],
         after=after,
         flops=NZ * rows * cols,
-        limit=4,
         moved=2 * NZ * (rows + EXTRA) * cols,
+        limit=8,
     )
 
 
@@ -401,11 +394,11 @@
 
 
 def counts_of(place, exon_blocks, own):
-    _, y, z, core = (place[i] for i in range(4))
+    y, core = place[1], place[3]
     flip, dz, dy, part = jnp.meshgrid(
         *(jnp.arange(n, dtype=jnp.int32) for n in (2, NZ, NY, own)), indexing="ij"
     )
-    labels = seq_index((y + NY - dy) % NY, (z + NZ - dz) % NZ, core ^ flip) * own + part
+    labels = seq_index((y + NY - dy) % NY, dz, core ^ flip) * own + part
     labels = labels.reshape(-1)
     return (exon_blocks[:, :, None] == labels[None, None]).astype(F32).sum(axis=1).astype(BF)
 
@@ -451,10 +444,11 @@
     kept, sent, cover, done = kernel_terms(place, before, turned, behind, cots, own, ())
     *blocks, done = back_products(place, around, taps, (done,))
     came = [along_x(blocks[r], r) for r in range(1, NX)]
-    kept, *parts = over_z(place, kept, along_seq(sent, 0, 0, 1), cover, (done,))
-    parts = [along_seq(part, 0, m + 1, 0) for m, part in enumerate(parts)]
+    parts = over_z(place, kept, along_seq(sent, 0, 0, 1), cover, (done,))
+    groups = [[seq_index(j, i, c) for i in range(NZ)] for j in range(NY) for c in range(2)]
+    parts = lax.all_to_all(parts, "seq", 0, 0, axis_index_groups=groups)
     out, done = input_gradient(place, inputs, grad, blocks[0], came, ())
-    kernel_gradient, cover, _ = summed(place, kept, cover, parts, wide, (done,))
+    kernel_gradient, cover = summed(place, parts, wide, (done,))
     cover = jnp.stack([cover, along_seq(cover, 0, 0, 1)])
     coverage = coverage_of(cover, counts)
     return (tracks, coverage, out, kernel_gradient[None])

time: 182 us -> 174 us (0.956)
  starting transfers between devices: 71.8 us -> 56.5 us
  waiting for transfers between devices: 76.9 us -> 82.3 us
    ppermute x17 -> x10, starting transfers between devices: 50.6 us -> 25.8 us  [along_seq(): return lax.ppermute(value, 'seq', pairs)]
    ppermute x12, waiting for transfers between devices: 45.3 us -> 57.4 us  [along_x(): lax.ppermute(value, 'chan', [(i, (i + steps) % NX) for i in range(NX)])]
    all_to_all x0 -> x1, starting transfers between devices: none -> 9.43 us  [shards(): parts = lax.all_to_all(parts, 'seq', 0, 0, axis_index_groups=groups)]
    ppermute x17 -> x10, waiting for transfers between devices: 20.8 us -> 14.1 us  [along_seq(): return lax.ppermute(value, 'seq', pairs)]
  transfers between devices with their start and end apart: 33 -> 27, of which waited for: 15 -> 16; matrix products, arithmetic and copies ran while one was open for 1% -> 1% of each run, Pallas kernels for 12% -> 12%
where the time goes in v7:
time: 174 us; the launch traced here: 173 us
  waiting for transfers between devices  82.3 us (47%)
  starting transfers between devices  56.5 us (32%)
  Pallas kernels  27.1 us (16%)
  local copies, waits for them, and re-layouts  3.37 us (2%)
  other arithmetic  2.4 us (1%)
    ppermute x12, waiting for transfers between devices, along_x(): lax.ppermute(value, 'chan', [(i, (i + steps) % NX) for i in range(NX)])  57.4 us
    pallas_call x13, Pallas kernels, call(): pl.pallas_call(kernel, in_specs=[pl.BlockSpec(memory_space=pltpu.SMEM)] +...  27.1 us
    ppermute x10, starting transfers between devices, along_seq(): return lax.ppermute(value, 'seq', pairs)  25.8 us
    ppermute x10, waiting for transfers between devices, along_seq(): return lax.ppermute(value, 'seq', pairs)  14.1 us
    ppermute x12, starting transfers between devices, along_x(): lax.ppermute(value, 'chan', [(i, (i + steps) % NX) for i in range(NX)])  13.3 us
    ppermute x4, waiting for transfers between devices, shifted(): lax.ppermute(value, 'seq', [(s, s + steps) for s in range(leading, last)])  10.8 us
    all_to_all x1, starting transfers between devices, shards(): parts = lax.all_to_all(parts, 'seq', 0, 0, axis_index_groups=groups)  9.43 us
    ppermute x4, starting transfers between devices, shifted(): lax.ppermute(value, 'seq', [(s, s + steps) for s in range(leading, last)])  7.97 us
  transfers between devices with their start and end apart: 27, of which 16 were waited for; matrix products, arithmetic and copies ran while one was open for 1% of the time, Pallas kernels for 12%

profile of v7, /device:TPU:1, one launch (start us, length us, event | category | flops | bytes accessed | tf_op | source)
XLA Modules:
  0.0 173.4 jit_solution(2418685798080801370)
XLA Ops:
  0.6 1.3 fusion.5.refs_1_
  1.9 3.4 %collective-permute-start = (bf16[512,384]{1,0:T(8,128)(2,1)S(1)}, bf16[512,384]{1,0:T(8,128)(2,1)S(1)}, u32[]{:S(2)}, u32[]{:S(2)}) collective-permute-start(bf16[512,384]{1,0:T(8,128)(2,1)S(1)} %fusion.5.refs_1_), channel_id=1, source_target_pairs={{0,3},{1,0},{2,1},{3,2},{4,7},{5,4},{6,5},{7,6},{8,11},{9,8},{10,9... | collective-permute-start | bytes 1179656 | tf_op jit(solution)/shard_map/ppermute | solution.py:33
  5.3 0.5 collective-permute-start.1
  5.8 0.6 collective-permute-start.2
  6.4 0.1 pad_add_fusion.refs_0_
  6.6 0.1 broadcast_in_dim.29
  6.8 0.1 broadcast_in_dim.25
  6.9 0.1 broadcast_in_dim.27
  7.0 0.1 broadcast_in_dim.31
  7.2 0.8 convert_reduce_fusion.refs_3_
  8.0 2.0 %copy-done = bf16[1,3,1536,384]{3,2,1,0:T(8,128)(2,1)S(1)} copy-done((bf16[1,3,1536,384]{3,2,1,0:T(8,128)(2,1)S(1)}, bf16[1,3,1536,384]{3,2,1,0:T(8,128)(2,1)}, u32[]{:S(2)}) %copy-start) | copy-done | bytes 3538968
  10.0 1.0 shard_map.84.refs_5_
  10.9 5.2 %collective-permute-done.refs_2_ = bf16[512,384]{1,0:T(8,128)(2,1)S(1)} collective-permute-done((bf16[512,384]{1,0:T(8,128)(2,1)S(1)}, bf16[512,384]{1,0:T(8,128)(2,1)S(1)}, u32[]{:S(2)}, u32[]{:S(2)}) %collective-permute-start) | collective-permute-done | bytes 393248 | tf_op jit(solution)/shard_map/ppermute | solution.py:33
  16.1 0.4 collective-permute-done.1.refs_3_
  16.5 9.8 %collective-permute-done.2.refs_4_ = bf16[512,384]{1,0:T(8,128)(2,1)S(1)} collective-permute-done((bf16[512,384]{1,0:T(8,128)(2,1)S(1)}, bf16[512,384]{1,0:T(8,128)(2,1)S(1)}, u32[]{:S(2)}, u32[]{:S(2)}) %collective-permute-start.2) | collective-permute-done | bytes 393248 | tf_op jit(solution)/shard_map/ppermute | solution.py:33
  26.3 3.2 %shard_map.85 = (bf16[512,384]{1,0:T(8,128)(2,1)S(1)}, f32[512,384]{1,0:T(8,128)S(1)}, bf16[512,384]{1,0:T(8,128)(2,1)S(1)}, bf16[512,1536]{1,0:T(8,128)(2,1)S(1)}) custom-call(s32[4]{0:T(128)S(1)} %pad_add_fusion.refs_0_, bf16[512,384]{1,0:T(8,128)(2,1)S(1)} %fusion.5.refs_1_, bf16[512,384]{1,0:T(8,128)(2,1)S(1)} %collective-permute-done.refs_2_, ...), custom_call_target="tpu_custom_call" | custom-call | flops 1811939328 | bytes 3538944 | tf_op jit(solution)/shard_map/pallas_call | solution.py:64
  29.5 3.8 %collective-permute-start.3 = (bf16[512,384]{1,0:T(8,128)(2,1)S(1)}, bf16[512,384]{1,0:T(8,128)(2,1)S(1)}, u32[]{:S(2)}, u32[]{:S(2)}) collective-permute-start(bf16[512,384]{1,0:T(8,128)(2,1)S(1)} %get-tuple-element.38), channel_id=1, source_target_pairs={{0,8},{4,12},{8,16},{12,20},{16,24},{20,28},{24,32},{28,36},{32,40... | collective-permute-start | bytes 1179656 | tf_op jit(solution)/shard_map/ppermute | solution.py:29
  33.3 1.3 collective-permute-start.4
  34.6 6.6 %collective-permute-done.3 = bf16[512,384]{1,0:T(8,128)(2,1)S(1)} collective-permute-done((bf16[512,384]{1,0:T(8,128)(2,1)S(1)}, bf16[512,384]{1,0:T(8,128)(2,1)S(1)}, u32[]{:S(2)}, u32[]{:S(2)}) %collective-permute-start.3) | collective-permute-done | bytes 393248 | tf_op jit(solution)/shard_map/ppermute | solution.py:29
  41.3 4.2 %collective-permute-done.4 = bf16[512,384]{1,0:T(8,128)(2,1)S(1)} collective-permute-done((bf16[512,384]{1,0:T(8,128)(2,1)S(1)}, bf16[512,384]{1,0:T(8,128)(2,1)S(1)}, u32[]{:S(2)}, u32[]{:S(2)}) %collective-permute-start.4) | collective-permute-done | bytes 393248 | tf_op jit(solution)/shard_map/ppermute | solution.py:29
  45.4 0.2 fusion.6.refs_1_
  45.6 0.1 collective-permute-start.5
  45.7 0.6 collective-permute-start.6
  46.3 0.8 collective-permute-start.7
  47.2 1.0 shard_map.88
  48.2 4.7 %collective-permute-start.10 = (bf16[384,512]{1,0:T(8,128)(2,1)S(1)}, bf16[384,512]{1,0:T(8,128)(2,1)S(1)}, u32[]{:S(2)}, u32[]{:S(2)}) collective-permute-start(bf16[384,512]{1,0:T(8,128)(2,1)S(1)} %get-tuple-element.47), channel_id=1, source_target_pairs={{0,192},{4,196},{8,200},{12,204},{16,208},{20,212},{24,216},{28,22... | collective-permute-start | bytes 1179656 | tf_op jit(solution)/shard_map/ppermute | solution.py:46
  52.9 2.0 %collective-permute-done.5.refs_2_ = bf16[512,384]{1,0:T(8,128)(2,1)S(1)} collective-permute-done((bf16[512,384]{1,0:T(8,128)(2,1)S(1)}, bf16[512,384]{1,0:T(8,128)(2,1)S(1)}, u32[]{:S(2)}, u32[]{:S(2)}) %collective-permute-start.5) | collective-permute-done | bytes 393248 | tf_op jit(solution)/shard_map/ppermute | solution.py:33
  54.8 4.6 %collective-permute-start.9 = (bf16[384,512]{1,0:T(8,128)(2,1)S(1)}, bf16[384,512]{1,0:T(8,128)(2,1)S(1)}, u32[]{:S(2)}, u32[]{:S(2)}) collective-permute-start(bf16[384,512]{1,0:T(8,128)(2,1)S(1)} %get-tuple-element.46), channel_id=1, source_target_pairs={{0,128},{4,132},{8,136},{12,140},{16,144},{20,148},{24,152},{28,15... | collective-permute-start | bytes 1179656 | tf_op jit(solution)/shard_map/ppermute | solution.py:46
  59.5 0.8 shard_map.86
  60.4 6.4 %collective-permute-done.7.refs_4_ = bf16[512,384]{1,0:T(8,128)(2,1)S(1)} collective-permute-done((bf16[512,384]{1,0:T(8,128)(2,1)S(1)}, bf16[512,384]{1,0:T(8,128)(2,1)S(1)}, u32[]{:S(2)}, u32[]{:S(2)}) %collective-permute-start.7) | collective-permute-done | bytes 393248 | tf_op jit(solution)/shard_map/ppermute | solution.py:33
  66.8 6.2 %shard_map.87 = (bf16[512,1024]{1,0:T(8,128)(2,1)}, f32[4,1024]{1,0:T(4,128)S(1)}, f32[512,384]{1,0:T(8,128)S(1)}, bf16[512,384]{1,0:T(8,128)(2,1)S(1)}, bf16[51...) custom-call(s32[4]{0:T(128)S(1)} %pad_add_fusion.refs_0_, ...), custom_call_target="tpu_custom_call" | custom-call | flops 3221225472 | bytes 3145728 | tf_op jit(solution)/shard_map/pallas_call | solution.py:64
  73.0 0.7 shard_map.89.refs_2_
  73.7 1.7 %collective-permute-start.11 = (bf16[384,2048]{1,0:T(8,128)(2,1)S(1)}, bf16[384,2048]{1,0:T(8,128)(2,1)S(1)}, u32[]{:S(2)}, u32[]{:S(2)}) collective-permute-start(bf16[384,2048]{1,0:T(8,128)(2,1)S(1)} %shard_map.89.refs_2_), channel_id=1, source_target_pairs={{0,8},{4,12},{8,16},{12,20},{16,24},{20,28},{24,32},{28,36},{32,40... | collective-permute-start | bytes 4718600 | tf_op jit(solution)/shard_map/ppermute | solution.py:46
  75.4 4.4 %collective-permute-start.12 = (bf16[384,2048]{1,0:T(8,128)(2,1)S(1)}, bf16[384,2048]{1,0:T(8,128)(2,1)S(1)}, u32[]{:S(2)}, u32[]{:S(2)}) collective-permute-start(bf16[384,2048]{1,0:T(8,128)(2,1)S(1)} %shard_map.89.refs_2_), channel_id=1, source_target_pairs={{0,56},{4,60},{8,0},{12,4},{16,8},{20,12},{24,16},{28,20},{32,24},... | collective-permute-start | bytes 4718600 | tf_op jit(solution)/shard_map/ppermute | solution.py:46
  79.9 0.5 collective-permute-start.14
  80.4 2.2 %collective-permute-start.15 = (bf16[512,384]{1,0:T(8,128)(2,1)S(1)}, bf16[512,384]{1,0:T(8,128)(2,1)S(1)}, u32[]{:S(2)}, u32[]{:S(2)}) collective-permute-start(bf16[512,384]{1,0:T(8,128)(2,1)S(1)} %get-tuple-element.52), channel_id=1, source_target_pairs={{0,3},{1,0},{2,1},{3,2},{4,7},{5,4},{6,5},{7,6},{8,11},{9,8},{10,9... | collective-permute-start | bytes 1179656 | tf_op jit(solution)/shard_map/ppermute | solution.py:33
  82.6 16.8 %collective-permute-done.13.refs_2_ = bf16[512,384]{1,0:T(8,128)(2,1)S(1)} collective-permute-done((bf16[512,384]{1,0:T(8,128)(2,1)S(1)}, bf16[512,384]{1,0:T(8,128)(2,1)S(1)}, u32[]{:S(2)}, u32[]{:S(2)}) %collective-permute-start.13) | collective-permute-done | bytes 393248 | tf_op jit(solution)/shard_map/ppermute | solution.py:33
  99.4 0.3 collective-permute-done.15.refs_4_
  99.7 0.9 shard_map.90
  100.7 1.4 collective-permute-start.16
  102.0 1.7 collective-permute-start.17
  103.7 2.0 %collective-permute-start.18 = (bf16[528,384]{1,0:T(8,128)(2,1)S(1)}, bf16[528,384]{1,0:T(8,128)(2,1)S(1)}, u32[]{:S(2)}, u32[]{:S(2)}) collective-permute-start(bf16[528,384]{1,0:T(8,128)(2,1)S(1)} %get-tuple-element.54.refs_4_), channel_id=1, source_target_pairs={{0,192},{4,196},{8,200},{12,204},{16,208},{20,212},{24,216},{28,22... | collective-permute-start | bytes 1216520 | tf_op jit(solution)/shard_map/ppermute | solution.py:46
  105.7 5.2 %collective-permute-done.16.refs_5_ = bf16[528,384]{1,0:T(8,128)(2,1)S(1)} collective-permute-done((bf16[528,384]{1,0:T(8,128)(2,1)S(1)}, bf16[528,384]{1,0:T(8,128)(2,1)S(1)}, u32[]{:S(2)}, u32[]{:S(2)}) %collective-permute-start.16) | collective-permute-done | bytes 405536 | tf_op jit(solution)/shard_map/ppermute | solution.py:46
  110.9 1.5 collective-permute-start.20
  112.4 7.6 %collective-permute-done.17.refs_6_ = bf16[528,384]{1,0:T(8,128)(2,1)S(1)} collective-permute-done((bf16[528,384]{1,0:T(8,128)(2,1)S(1)}, bf16[528,384]{1,0:T(8,128)(2,1)S(1)}, u32[]{:S(2)}, u32[]{:S(2)}) %collective-permute-start.17) | collective-permute-done | bytes 405536 | tf_op jit(solution)/shard_map/ppermute | solution.py:46
  120.1 1.3 collective-permute-start.21
  121.4 0.1 collective-permute-done.18.refs_7_
  121.5 3.9 %shard_map.91 = (f32[192,1152]{1,0:T(8,128)S(1)}, bf16[192,1152]{1,0:T(8,128)(2,1)S(1)}, f32[16,1152]{1,0:T(8,128)S(1)}, f32[8,128]{1,0:T(8,128)S(1)}) custom-call(s32[4]{0:T(128)S(1)} %pad_add_fusion.refs_0_, bf16[384,2048]{1,0:T(8,128)(2,1)S(1)} %collective-permute-done.11.refs_1_, bf16[384,2048]{1,0:T(8,128)(2,1)S(1)} %shard_map.89.refs_2_, ...), custom_call_target="tpu_custom_call" | custom-call | flops 1811939328 | bytes 6291456 | tf_op jit(solution)/shard_map/pallas_call | solution.py:64
  125.4 3.0 %collective-permute-start.19 = (bf16[192,1152]{1,0:T(8,128)(2,1)S(1)}, bf16[192,1152]{1,0:T(8,128)(2,1)S(1)}, u32[]{:S(2)}, u32[]{:S(2)}) collective-permute-start(bf16[192,1152]{1,0:T(8,128)(2,1)S(1)} %get-tuple-element.56), channel_id=1, source_target_pairs={{0,4},{4,0},{8,12},{12,8},{16,20},{20,16},{24,28},{28,24},{32,36},... | collective-permute-start | bytes 1327112 | tf_op jit(solution)/shard_map/ppermute | solution.py:46
  128.4 1.0 shard_map.92.refs_4_
  129.4 3.6 %shard_map.93 = (f32[512,384]{1,0:T(8,128)S(1)}, bf16[512,384]{1,0:T(8,128)(2,1)S(1)}, bf16[512,384]{1,0:T(8,128)(2,1)S(1)}, bf16[512,384]{1,0:T(8,128)(2,1)S(1)}, f32[8,128]{1,0:T(8,128)S(1)}) custom-call(s32[4]{0:T(128)S(1)} %pad_add_fusion.refs_0_, bf16[512,384]{1,0:T(8,128)(2,1)S(1)} %collective-permute-done.20.refs_1_, ...), custom_call_target="tpu_custom_call" | custom-call | flops 1811939328 | bytes 3538944 | tf_op jit(solution)/shard_map/pallas_call | solution.py:64
  133.0 0.7 copy-done.5
  133.8 1.5 shard_map.94
  135.3 9.4 %all-to-all-start = ((bf16[8,40,1152]{2,1,0:T(8,128)(2,1)}), bf16[8,40,1152]{2,1,0:T(8,128)(2,1)S(1)}, u32[]{:S(2)}, u32[]{:S(2)}) async-start(bf16[8,40,1152]{2,1,0:T(8,128)(2,1)} %shard_map.94), calls=%async_computation | async-start | bytes 1474560 | tf_op jit(solution)/shard_map/all_to_all | solution.py:449
  144.7 1.7 collective-permute-start.22
  146.4 2.9 %collective-permute-start.23 = (bf16[512,384]{1,0:T(8,128)(2,1)S(1)}, bf16[512,384]{1,0:T(8,128)(2,1)S(1)}, u32[]{:S(2)}, u32[]{:S(2)}) collective-permute-start(bf16[512,384]{1,0:T(8,128)(2,1)S(1)} %get-tuple-element.64), channel_id=1, source_target_pairs={{0,2},{1,3},{2,0},{3,1},{4,6},{5,7},{6,4},{7,5},{8,10},{9,11},{10,... | collective-permute-start | bytes 1179656 | tf_op jit(solution)/shard_map/ppermute | solution.py:33
  149.3 6.7 %collective-permute-done.22.refs_4_ = bf16[512,384]{1,0:T(8,128)(2,1)S(1)} collective-permute-done((bf16[512,384]{1,0:T(8,128)(2,1)}, bf16[512,384]{1,0:T(8,128)(2,1)S(1)}, u32[]{:S(2)}, u32[]{:S(2)}) %collective-permute-start.22) | collective-permute-done | bytes 393248 | tf_op jit(solution)/shard_map/ppermute | solution.py:33
  156.0 9.3 %collective-permute-done.23.refs_5_ = bf16[512,384]{1,0:T(8,128)(2,1)S(1)} collective-permute-done((bf16[512,384]{1,0:T(8,128)(2,1)S(1)}, bf16[512,384]{1,0:T(8,128)(2,1)S(1)}, u32[]{:S(2)}, u32[]{:S(2)}) %collective-permute-start.23) | collective-permute-done | bytes 393248 | tf_op jit(solution)/shard_map/ppermute | solution.py:33
  165.3 0.5 collective-permute-done.24.refs_6_
  165.8 2.0 %shard_map.95 = (bf16[512,384]{1,0:T(8,128)(2,1)}, f32[8,128]{1,0:T(8,128)S(1)}) custom-call(s32[4]{0:T(128)S(1)} %pad_add_fusion.refs_0_, bf16[512,384]{1,0:T(8,128)(2,1)S(1)} %copy-done.2, f32[512,384]{1,0:T(8,128)S(1)} %get-tuple-element.61.refs_2_, f32[512,384]{1,0:T(8,128)S(1)} %get-tuple-element.62.refs_3_, ...), custom_call_target="tpu_custom_call" | custom-call | flops 3932160 | bytes 3145728 | tf_op jit(solution)/shard_map/pallas_call | solution.py:64
  167.9 1.2 shard_map.96
  169.1 2.2 %collective-permute-start.25 = (bf16[8,16,1024]{2,1,0:T(8,128)(2,1)S(1)}, bf16[8,16,1024]{2,1,0:T(8,128)(2,1)S(1)}, u32[]{:S(2)}, u32[]{:S(2)}) collective-permute-start(bf16[8,16,1024]{2,1,0:T(8,128)(2,1)S(1)} %get-tuple-element.67), channel_id=1, source_target_pairs={{0,4},{4,0},{8,12},{12,8},{16,20},{20,16},{24,28},{28,24},{32,36},... | collective-permute-start | bytes 786440 | tf_op jit(solution)/shard_map/ppermute | solution.py:46
  171.3 1.2 collective-permute-done.25
  172.6 0.8 convolution_multiply_fusion
  (34 shorter events, 0.3 us)
Async XLA Ops:
  1.9 14.2 %collective-permute-start = (bf16[512,384]{1,0:T(8,128)(2,1)S(1)}, bf16[512,384]{1,0:T(8,128)(2,1)S(1)}, u32[]{:S(2)}, u32[]{:S(2)}) collective-permute-start(bf16[512,384]{1,0:T(8,128)(2,1)S(1)} %fusion.5.refs_1_), channel_id=1, source_target_pairs={{0,3},{1,0},{2,1},{3,2},{4,7},{5,4},{6,5},{7,6},{8,11},{9,8},{10,9... | collective-permute-start | bytes 1179656 | tf_op jit(solution)/shard_map/ppermute | solution.py:33
  5.3 11.2 %collective-permute-start.1 = (bf16[512,384]{1,0:T(8,128)(2,1)S(1)}, bf16[512,384]{1,0:T(8,128)(2,1)S(1)}, u32[]{:S(2)}, u32[]{:S(2)}) collective-permute-start(bf16[512,384]{1,0:T(8,128)(2,1)S(1)} %fusion.5.refs_1_), channel_id=1, source_target_pairs={{0,2},{1,3},{2,0},{3,1},{4,6},{5,7},{6,4},{7,5},{8,10},{9,11},{10,... | collective-permute-start | bytes 1179656 | tf_op jit(solution)/shard_map/ppermute | solution.py:33
  5.8 20.4 %collective-permute-start.2 = (bf16[512,384]{1,0:T(8,128)(2,1)S(1)}, bf16[512,384]{1,0:T(8,128)(2,1)S(1)}, u32[]{:S(2)}, u32[]{:S(2)}) collective-permute-start(bf16[512,384]{1,0:T(8,128)(2,1)S(1)} %fusion.5.refs_1_), channel_id=1, source_target_pairs={{0,1},{1,2},{2,3},{3,0},{4,5},{5,6},{6,7},{7,4},{8,9},{9,10},{10,1... | collective-permute-start | bytes 1179656 | tf_op jit(solution)/shard_map/ppermute | solution.py:33
  8.0 2.0 %copy-start = (bf16[1,3,1536,384]{3,2,1,0:T(8,128)(2,1)S(1)}, bf16[1,3,1536,384]{3,2,1,0:T(8,128)(2,1)}, u32[]{:S(2)}) copy-start(bf16[1,3,1536,384]{3,2,1,0:T(8,128)(2,1)} %refs_1_.6) | copy-start | bytes 10616836
  10.9 34.5 %copy-start.2 = (bf16[512,384]{1,0:T(8,128)(2,1)S(1)}, bf16[512,384]{1,0:T(8,128)(2,1)}, u32[]{:S(2)}) copy-start(bf16[512,384]{1,0:T(8,128)(2,1)} %refs_1_.7) | copy-start | bytes 1179652
  26.3 33.2 %copy-start.4 = (bf16[512,1024]{1,0:T(8,128)(2,1)S(1)}, bf16[512,1024]{1,0:T(8,128)(2,1)}, u32[]{:S(2)}) copy-start(bf16[512,1024]{1,0:T(8,128)(2,1)} %refs_2_.1) | copy-start | bytes 3145732
  29.5 30.0 %copy-start.3 = (bf16[1536,1024]{1,0:T(8,128)(2,1)S(1)}, bf16[1536,1024]{1,0:T(8,128)(2,1)}, u32[]{:S(2)}) copy-start(bf16[1536,1024]{1,0:T(8,128)(2,1)} %refs_1_.5) | copy-start | bytes 9437188
  29.5 11.8 %collective-permute-start.3 = (bf16[512,384]{1,0:T(8,128)(2,1)S(1)}, bf16[512,384]{1,0:T(8,128)(2,1)S(1)}, u32[]{:S(2)}, u32[]{:S(2)}) collective-permute-start(bf16[512,384]{1,0:T(8,128)(2,1)S(1)} %get-tuple-element.38), channel_id=1, source_target_pairs={{0,8},{4,12},{8,16},{12,20},{16,24},{20,28},{24,32},{28,36},{32,40... | collective-permute-start | bytes 1179656 | tf_op jit(solution)/shard_map/ppermute | solution.py:29
  33.3 12.1 %collective-permute-start.4 = (bf16[512,384]{1,0:T(8,128)(2,1)S(1)}, bf16[512,384]{1,0:T(8,128)(2,1)S(1)}, u32[]{:S(2)}, u32[]{:S(2)}) collective-permute-start(bf16[512,384]{1,0:T(8,128)(2,1)S(1)} %get-tuple-element.39), channel_id=1, source_target_pairs={{8,0},{12,4},{16,8},{20,12},{24,16},{28,20},{32,24},{36,28},{40,32... | collective-permute-start | bytes 1179656 | tf_op jit(solution)/shard_map/ppermute | solution.py:29
  45.6 9.2 %collective-permute-start.5 = (bf16[512,384]{1,0:T(8,128)(2,1)S(1)}, bf16[512,384]{1,0:T(8,128)(2,1)S(1)}, u32[]{:S(2)}, u32[]{:S(2)}) collective-permute-start(bf16[512,384]{1,0:T(8,128)(2,1)S(1)} %fusion.6.refs_1_), channel_id=1, source_target_pairs={{0,3},{1,0},{2,1},{3,2},{4,7},{5,4},{6,5},{7,6},{8,11},{9,8},{10,9... | collective-permute-start | bytes 1179656 | tf_op jit(solution)/shard_map/ppermute | solution.py:33
  45.7 14.6 %collective-permute-start.6 = (bf16[512,384]{1,0:T(8,128)(2,1)S(1)}, bf16[512,384]{1,0:T(8,128)(2,1)S(1)}, u32[]{:S(2)}, u32[]{:S(2)}) collective-permute-start(bf16[512,384]{1,0:T(8,128)(2,1)S(1)} %fusion.6.refs_1_), channel_id=1, source_target_pairs={{0,2},{1,3},{2,0},{3,1},{4,6},{5,7},{6,4},{7,5},{8,10},{9,11},{10,... | collective-permute-start | bytes 1179656 | tf_op jit(solution)/shard_map/ppermute | solution.py:33
  46.3 20.4 %collective-permute-start.7 = (bf16[512,384]{1,0:T(8,128)(2,1)S(1)}, bf16[512,384]{1,0:T(8,128)(2,1)S(1)}, u32[]{:S(2)}, u32[]{:S(2)}) collective-permute-start(bf16[512,384]{1,0:T(8,128)(2,1)S(1)} %fusion.6.refs_1_), channel_id=1, source_target_pairs={{0,1},{1,2},{2,3},{3,0},{4,5},{5,6},{6,7},{7,4},{8,9},{9,10},{10,1... | collective-permute-start | bytes 1179656 | tf_op jit(solution)/shard_map/ppermute | solution.py:33
  48.2 24.8 %collective-permute-start.10 = (bf16[384,512]{1,0:T(8,128)(2,1)S(1)}, bf16[384,512]{1,0:T(8,128)(2,1)S(1)}, u32[]{:S(2)}, u32[]{:S(2)}) collective-permute-start(bf16[384,512]{1,0:T(8,128)(2,1)S(1)} %get-tuple-element.47), channel_id=1, source_target_pairs={{0,192},{4,196},{8,200},{12,204},{16,208},{20,212},{24,216},{28,22... | collective-permute-start | bytes 1179656 | tf_op jit(solution)/shard_map/ppermute | solution.py:46
  52.9 20.1 %collective-permute-start.8 = (bf16[384,512]{1,0:T(8,128)(2,1)S(1)}, bf16[384,512]{1,0:T(8,128)(2,1)S(1)}, u32[]{:S(2)}, u32[]{:S(2)}) collective-permute-start(bf16[384,512]{1,0:T(8,128)(2,1)S(1)} %get-tuple-element.45), channel_id=1, source_target_pairs={{0,64},{4,68},{8,72},{12,76},{16,80},{20,84},{24,88},{28,92},{32,9... | collective-permute-start | bytes 1179656 | tf_op jit(solution)/shard_map/ppermute | solution.py:46
  54.8 18.2 %collective-permute-start.9 = (bf16[384,512]{1,0:T(8,128)(2,1)S(1)}, bf16[384,512]{1,0:T(8,128)(2,1)S(1)}, u32[]{:S(2)}, u32[]{:S(2)}) collective-permute-start(bf16[384,512]{1,0:T(8,128)(2,1)S(1)} %get-tuple-element.46), channel_id=1, source_target_pairs={{0,128},{4,132},{8,136},{12,140},{16,144},{20,148},{24,152},{28,15... | collective-permute-start | bytes 1179656 | tf_op jit(solution)/shard_map/ppermute | solution.py:46
  73.7 47.8 %collective-permute-start.11 = (bf16[384,2048]{1,0:T(8,128)(2,1)S(1)}, bf16[384,2048]{1,0:T(8,128)(2,1)S(1)}, u32[]{:S(2)}, u32[]{:S(2)}) collective-permute-start(bf16[384,2048]{1,0:T(8,128)(2,1)S(1)} %shard_map.89.refs_2_), channel_id=1, source_target_pairs={{0,8},{4,12},{8,16},{12,20},{16,24},{20,28},{24,32},{28,36},{32,40... | collective-permute-start | bytes 4718600 | tf_op jit(solution)/shard_map/ppermute | solution.py:46
  75.4 46.1 %collective-permute-start.12 = (bf16[384,2048]{1,0:T(8,128)(2,1)S(1)}, bf16[384,2048]{1,0:T(8,128)(2,1)S(1)}, u32[]{:S(2)}, u32[]{:S(2)}) collective-permute-start(bf16[384,2048]{1,0:T(8,128)(2,1)S(1)} %shard_map.89.refs_2_), channel_id=1, source_target_pairs={{0,56},{4,60},{8,0},{12,4},{16,8},{20,12},{24,16},{28,20},{32,24},... | collective-permute-start | bytes 4718600 | tf_op jit(solution)/shard_map/ppermute | solution.py:46
  79.9 19.5 %collective-permute-start.13 = (bf16[512,384]{1,0:T(8,128)(2,1)S(1)}, bf16[512,384]{1,0:T(8,128)(2,1)S(1)}, u32[]{:S(2)}, u32[]{:S(2)}) collective-permute-start(bf16[512,384]{1,0:T(8,128)(2,1)S(1)} %get-tuple-element.50), channel_id=1, source_target_pairs={{0,1},{1,2},{2,3},{3,0},{4,5},{5,6},{6,7},{7,4},{8,9},{9,10},{10,1... | collective-permute-start | bytes 1179656 | tf_op jit(solution)/shard_map/ppermute | solution.py:33
  79.9 19.5 %collective-permute-start.14 = (bf16[512,384]{1,0:T(8,128)(2,1)S(1)}, bf16[512,384]{1,0:T(8,128)(2,1)S(1)}, u32[]{:S(2)}, u32[]{:S(2)}) collective-permute-start(bf16[512,384]{1,0:T(8,128)(2,1)S(1)} %get-tuple-element.51), channel_id=1, source_target_pairs={{0,2},{1,3},{2,0},{3,1},{4,6},{5,7},{6,4},{7,5},{8,10},{9,11},{10,... | collective-permute-start | bytes 1179656 | tf_op jit(solution)/shard_map/ppermute | solution.py:33
  80.4 19.3 %collective-permute-start.15 = (bf16[512,384]{1,0:T(8,128)(2,1)S(1)}, bf16[512,384]{1,0:T(8,128)(2,1)S(1)}, u32[]{:S(2)}, u32[]{:S(2)}) collective-permute-start(bf16[512,384]{1,0:T(8,128)(2,1)S(1)} %get-tuple-element.52), channel_id=1, source_target_pairs={{0,3},{1,0},{2,1},{3,2},{4,7},{5,4},{6,5},{7,6},{8,11},{9,8},{10,9... | collective-permute-start | bytes 1179656 | tf_op jit(solution)/shard_map/ppermute | solution.py:33
  100.7 10.2 %collective-permute-start.16 = (bf16[528,384]{1,0:T(8,128)(2,1)S(1)}, bf16[528,384]{1,0:T(8,128)(2,1)S(1)}, u32[]{:S(2)}, u32[]{:S(2)}) collective-permute-start(bf16[528,384]{1,0:T(8,128)(2,1)S(1)} %get-tuple-element.54.refs_4_), channel_id=1, source_target_pairs={{0,64},{4,68},{8,72},{12,76},{16,80},{20,84},{24,88},{28,92},{32,9... | collective-permute-start | bytes 1216520 | tf_op jit(solution)/shard_map/ppermute | solution.py:46
  102.0 18.0 %collective-permute-start.17 = (bf16[528,384]{1,0:T(8,128)(2,1)S(1)}, bf16[528,384]{1,0:T(8,128)(2,1)S(1)}, u32[]{:S(2)}, u32[]{:S(2)}) collective-permute-start(bf16[528,384]{1,0:T(8,128)(2,1)S(1)} %get-tuple-element.54.refs_4_), channel_id=1, source_target_pairs={{0,128},{4,132},{8,136},{12,140},{16,144},{20,148},{24,152},{28,15... | collective-permute-start | bytes 1216520 | tf_op jit(solution)/shard_map/ppermute | solution.py:46
  103.7 17.8 %collective-permute-start.18 = (bf16[528,384]{1,0:T(8,128)(2,1)S(1)}, bf16[528,384]{1,0:T(8,128)(2,1)S(1)}, u32[]{:S(2)}, u32[]{:S(2)}) collective-permute-start(bf16[528,384]{1,0:T(8,128)(2,1)S(1)} %get-tuple-element.54.refs_4_), channel_id=1, source_target_pairs={{0,192},{4,196},{8,200},{12,204},{16,208},{20,212},{24,216},{28,22... | collective-permute-start | bytes 1216520 | tf_op jit(solution)/shard_map/ppermute | solution.py:46
  110.9 17.5 %copy-start.1 = (bf16[1,3,1536,384]{3,2,1,0:T(8,128)(2,1)S(1)}, bf16[1,3,1536,384]{3,2,1,0:T(8,128)(2,1)}, u32[]{:S(2)}) copy-start(bf16[1,3,1536,384]{3,2,1,0:T(8,128)(2,1)} %refs_1_.6) | copy-start | bytes 10616836
  110.9 18.5 %collective-permute-start.20 = (bf16[512,384]{1,0:T(8,128)(2,1)S(1)}, bf16[512,384]{1,0:T(8,128)(2,1)S(1)}, u32[]{:S(2)}, u32[]{:S(2)}) collective-permute-start(bf16[512,384]{1,0:T(8,128)(2,1)S(1)} %get-tuple-element.58.refs_2_), channel_id=1, source_target_pairs={{8,0},{12,4},{16,8},{20,12},{24,16},{28,20},{32,24},{36,28},{40,32... | collective-permute-start | bytes 1179656 | tf_op jit(solution)/shard_map/ppermute | solution.py:29
  120.1 9.3 %collective-permute-start.21 = (bf16[512,384]{1,0:T(8,128)(2,1)S(1)}, bf16[512,384]{1,0:T(8,128)(2,1)S(1)}, u32[]{:S(2)}, u32[]{:S(2)}) collective-permute-start(bf16[512,384]{1,0:T(8,128)(2,1)S(1)} %get-tuple-element.58.refs_2_), channel_id=1, source_target_pairs={{0,8},{4,12},{8,16},{12,20},{16,24},{20,28},{24,32},{28,36},{32,40... | collective-permute-start | bytes 1179656 | tf_op jit(solution)/shard_map/ppermute | solution.py:29
  125.4 8.4 %collective-permute-start.19 = (bf16[192,1152]{1,0:T(8,128)(2,1)S(1)}, bf16[192,1152]{1,0:T(8,128)(2,1)S(1)}, u32[]{:S(2)}, u32[]{:S(2)}) collective-permute-start(bf16[192,1152]{1,0:T(8,128)(2,1)S(1)} %get-tuple-element.56), channel_id=1, source_target_pairs={{0,4},{4,0},{8,12},{12,8},{16,20},{20,16},{24,28},{28,24},{32,36},... | collective-permute-start | bytes 1327112 | tf_op jit(solution)/shard_map/ppermute | solution.py:46
  133.0 0.7 copy-start.5
  135.3 32.5 %all-to-all-start = ((bf16[8,40,1152]{2,1,0:T(8,128)(2,1)}), bf16[8,40,1152]{2,1,0:T(8,128)(2,1)S(1)}, u32[]{:S(2)}, u32[]{:S(2)}) async-start(bf16[8,40,1152]{2,1,0:T(8,128)(2,1)} %shard_map.94), calls=%async_computation | async-start | bytes 1474560 | tf_op jit(solution)/shard_map/all_to_all | solution.py:449
  144.7 11.3 %collective-permute-start.22 = (bf16[512,384]{1,0:T(8,128)(2,1)}, bf16[512,384]{1,0:T(8,128)(2,1)S(1)}, u32[]{:S(2)}, u32[]{:S(2)}) collective-permute-start(bf16[512,384]{1,0:T(8,128)(2,1)} %copy-done.5), channel_id=1, source_target_pairs={{0,1},{1,2},{2,3},{3,0},{4,5},{5,6},{6,7},{7,4},{8,9},{9,10},{10,1... | collective-permute-start | bytes 1179656 | tf_op jit(solution)/shard_map/ppermute | solution.py:33
  146.4 18.9 %collective-permute-start.23 = (bf16[512,384]{1,0:T(8,128)(2,1)S(1)}, bf16[512,384]{1,0:T(8,128)(2,1)S(1)}, u32[]{:S(2)}, u32[]{:S(2)}) collective-permute-start(bf16[512,384]{1,0:T(8,128)(2,1)S(1)} %get-tuple-element.64), channel_id=1, source_target_pairs={{0,2},{1,3},{2,0},{3,1},{4,6},{5,7},{6,4},{7,5},{8,10},{9,11},{10,... | collective-permute-start | bytes 1179656 | tf_op jit(solution)/shard_map/ppermute | solution.py:33
  149.3 16.5 %collective-permute-start.24 = (bf16[512,384]{1,0:T(8,128)(2,1)S(1)}, bf16[512,384]{1,0:T(8,128)(2,1)S(1)}, u32[]{:S(2)}, u32[]{:S(2)}) collective-permute-start(bf16[512,384]{1,0:T(8,128)(2,1)S(1)} %get-tuple-element.65), channel_id=1, source_target_pairs={{0,3},{1,0},{2,1},{3,2},{4,7},{5,4},{6,5},{7,6},{8,11},{9,8},{10,9... | collective-permute-start | bytes 1179656 | tf_op jit(solution)/shard_map/ppermute | solution.py:33
  169.1 3.4 %collective-permute-start.25 = (bf16[8,16,1024]{2,1,0:T(8,128)(2,1)S(1)}, bf16[8,16,1024]{2,1,0:T(8,128)(2,1)S(1)}, u32[]{:S(2)}, u32[]{:S(2)}) collective-permute-start(bf16[8,16,1024]{2,1,0:T(8,128)(2,1)S(1)} %get-tuple-element.67), channel_id=1, source_target_pairs={{0,4},{4,0},{8,12},{12,8},{16,20},{20,16},{24,28},{28,24},{32,36},... | collective-permute-start | bytes 786440 | tf_op jit(solution)/shard_map/ppermute | solution.py:46

commit v8 on v7

--- a/solution.py
+++ b/solution.py
@@ -444,7 +444,7 @@
     kept, sent, cover, done = kernel_terms(place, before, turned, behind, cots, own, ())
     *blocks, done = back_products(place, around, taps, (done,))
     came = [along_x(blocks[r], r) for r in range(1, NX)]
-    parts = over_z(place, kept, along_seq(sent, 0, 0, 1), cover, (done,))
+    parts = over_z(place, kept, along_seq(sent, 0, 0, 1), cover, (token(came[0]),))
     groups = [[seq_index(j, i, c) for i in range(NZ)] for j in range(NY) for c in range(2)]
     parts = lax.all_to_all(parts, "seq", 0, 0, axis_index_groups=groups)
     out, done = input_gradient(place, inputs, grad, blocks[0], came, ())

time: 174 us -> 184 us (1.057)
  waiting for transfers between devices: 82.3 us -> 92.5 us
    ppermute x12, waiting for transfers between devices: 57.4 us -> 66 us  [along_x(): lax.ppermute(value, 'chan', [(i, (i + steps) % NX) for i in range(NX)])]
  transfers between devices with their start and end apart: 27 -> 27, of which waited for: 16 -> 16; matrix products, arithmetic and copies ran while one was open for 1% -> 1% of each run, Pallas kernels for 12% -> 11%
where the time goes in v8:
time: 184 us; the launch traced here: 183 us
  waiting for transfers between devices  92.5 us (50%)
  starting transfers between devices  55.9 us (30%)
  Pallas kernels  27.6 us (15%)
  local copies, waits for them, and re-layouts  3.38 us (2%)
  other arithmetic  2.4 us (1%)
    ppermute x12, waiting for transfers between devices, along_x(): lax.ppermute(value, 'chan', [(i, (i + steps) % NX) for i in range(NX)])  66 us
    pallas_call x13, Pallas kernels, call(): pl.pallas_call(kernel, in_specs=[pl.BlockSpec(memory_space=pltpu.SMEM)] +...  27.6 us
    ppermute x10, starting transfers between devices, along_seq(): return lax.ppermute(value, 'seq', pairs)  24.2 us
    ppermute x10, waiting for transfers between devices, along_seq(): return lax.ppermute(value, 'seq', pairs)  14.3 us
    ppermute x12, starting transfers between devices, along_x(): lax.ppermute(value, 'chan', [(i, (i + steps) % NX) for i in range(NX)])  12.8 us
    all_to_all x1, starting transfers between devices, shards(): parts = lax.all_to_all(parts, 'seq', 0, 0, axis_index_groups=groups)  11.2 us
    ppermute x4, waiting for transfers between devices, shifted(): lax.ppermute(value, 'seq', [(s, s + steps) for s in range(leading, last)])  10.8 us
    ppermute x4, starting transfers between devices, shifted(): lax.ppermute(value, 'seq', [(s, s + steps) for s in range(leading, last)])  7.7 us
  transfers between devices with their start and end apart: 27, of which 16 were waited for; matrix products, arithmetic and copies ran while one was open for 1% of the time, Pallas kernels for 11%

profile of v8, /device:TPU:1, one launch (start us, length us, event | category | flops | bytes accessed | tf_op | source)
XLA Modules:
  0.0 183.4 jit_solution(14534211090941238964)
XLA Ops:
  0.6 1.3 fusion.5.refs_1_
  1.9 3.4 %collective-permute-start = (bf16[512,384]{1,0:T(8,128)(2,1)S(1)}, bf16[512,384]{1,0:T(8,128)(2,1)S(1)}, u32[]{:S(2)}, u32[]{:S(2)}) collective-permute-start(bf16[512,384]{1,0:T(8,128)(2,1)S(1)} %fusion.5.refs_1_), channel_id=1, source_target_pairs={{0,3},{1,0},{2,1},{3,2},{4,7},{5,4},{6,5},{7,6},{8,11},{9,8},{10,9... | collective-permute-start | bytes 1179656 | tf_op jit(solution)/shard_map/ppermute | solution.py:33
  5.3 0.5 collective-permute-start.1
  5.8 0.6 collective-permute-start.2
  6.6 0.1 broadcast_in_dim.29
  6.8 0.1 broadcast_in_dim.25
  6.9 0.1 broadcast_in_dim.27
  7.0 0.1 broadcast_in_dim.31
  7.2 0.8 convert_reduce_fusion.refs_3_
  8.0 2.0 %copy-done = bf16[1,3,1536,384]{3,2,1,0:T(8,128)(2,1)S(1)} copy-done((bf16[1,3,1536,384]{3,2,1,0:T(8,128)(2,1)S(1)}, bf16[1,3,1536,384]{3,2,1,0:T(8,128)(2,1)}, u32[]{:S(2)}) %copy-start) | copy-done | bytes 3538968
  10.0 1.0 shard_map.84.refs_5_
  10.9 5.2 %collective-permute-done.refs_2_ = bf16[512,384]{1,0:T(8,128)(2,1)S(1)} collective-permute-done((bf16[512,384]{1,0:T(8,128)(2,1)S(1)}, bf16[512,384]{1,0:T(8,128)(2,1)S(1)}, u32[]{:S(2)}, u32[]{:S(2)}) %collective-permute-start) | collective-permute-done | bytes 393248 | tf_op jit(solution)/shard_map/ppermute | solution.py:33
  16.1 0.4 collective-permute-done.1.refs_3_
  16.5 9.8 %collective-permute-done.2.refs_4_ = bf16[512,384]{1,0:T(8,128)(2,1)S(1)} collective-permute-done((bf16[512,384]{1,0:T(8,128)(2,1)S(1)}, bf16[512,384]{1,0:T(8,128)(2,1)S(1)}, u32[]{:S(2)}, u32[]{:S(2)}) %collective-permute-start.2) | collective-permute-done | bytes 393248 | tf_op jit(solution)/shard_map/ppermute | solution.py:33
  26.3 3.2 %shard_map.85 = (bf16[512,384]{1,0:T(8,128)(2,1)S(1)}, f32[512,384]{1,0:T(8,128)S(1)}, bf16[512,384]{1,0:T(8,128)(2,1)S(1)}, bf16[512,1536]{1,0:T(8,128)(2,1)S(1)}) custom-call(s32[4]{0:T(128)S(1)} %pad_add_fusion.refs_0_, bf16[512,384]{1,0:T(8,128)(2,1)S(1)} %fusion.5.refs_1_, bf16[512,384]{1,0:T(8,128)(2,1)S(1)} %collective-permute-done.refs_2_, ...), custom_call_target="tpu_custom_call" | custom-call | flops 1811939328 | bytes 3538944 | tf_op jit(solution)/shard_map/pallas_call | solution.py:64
  29.5 3.8 %collective-permute-start.3 = (bf16[512,384]{1,0:T(8,128)(2,1)S(1)}, bf16[512,384]{1,0:T(8,128)(2,1)S(1)}, u32[]{:S(2)}, u32[]{:S(2)}) collective-permute-start(bf16[512,384]{1,0:T(8,128)(2,1)S(1)} %get-tuple-element.37), channel_id=1, source_target_pairs={{0,8},{4,12},{8,16},{12,20},{16,24},{20,28},{24,32},{28,36},{32,40... | collective-permute-start | bytes 1179656 | tf_op jit(solution)/shard_map/ppermute | solution.py:29
  33.3 1.3 collective-permute-start.4
  34.6 6.6 %collective-permute-done.3 = bf16[512,384]{1,0:T(8,128)(2,1)S(1)} collective-permute-done((bf16[512,384]{1,0:T(8,128)(2,1)S(1)}, bf16[512,384]{1,0:T(8,128)(2,1)S(1)}, u32[]{:S(2)}, u32[]{:S(2)}) %collective-permute-start.3) | collective-permute-done | bytes 393248 | tf_op jit(solution)/shard_map/ppermute | solution.py:29
  41.3 4.2 %collective-permute-done.4 = bf16[512,384]{1,0:T(8,128)(2,1)S(1)} collective-permute-done((bf16[512,384]{1,0:T(8,128)(2,1)S(1)}, bf16[512,384]{1,0:T(8,128)(2,1)S(1)}, u32[]{:S(2)}, u32[]{:S(2)}) %collective-permute-start.4) | collective-permute-done | bytes 393248 | tf_op jit(solution)/shard_map/ppermute | solution.py:29
  45.4 0.2 fusion.6.refs_1_
  45.6 0.1 collective-permute-start.5
  45.7 0.6 collective-permute-start.6
  46.3 0.8 collective-permute-start.7
  47.2 1.0 shard_map.88
  48.2 4.7 %collective-permute-start.10 = (bf16[384,512]{1,0:T(8,128)(2,1)S(1)}, bf16[384,512]{1,0:T(8,128)(2,1)S(1)}, u32[]{:S(2)}, u32[]{:S(2)}) collective-permute-start(bf16[384,512]{1,0:T(8,128)(2,1)S(1)} %get-tuple-element.46), channel_id=1, source_target_pairs={{0,192},{4,196},{8,200},{12,204},{16,208},{20,212},{24,216},{28,22... | collective-permute-start | bytes 1179656 | tf_op jit(solution)/shard_map/ppermute | solution.py:46
  52.9 2.0 %collective-permute-done.5.refs_2_ = bf16[512,384]{1,0:T(8,128)(2,1)S(1)} collective-permute-done((bf16[512,384]{1,0:T(8,128)(2,1)S(1)}, bf16[512,384]{1,0:T(8,128)(2,1)S(1)}, u32[]{:S(2)}, u32[]{:S(2)}) %collective-permute-start.5) | collective-permute-done | bytes 393248 | tf_op jit(solution)/shard_map/ppermute | solution.py:33
  54.8 4.6 %collective-permute-start.9 = (bf16[384,512]{1,0:T(8,128)(2,1)S(1)}, bf16[384,512]{1,0:T(8,128)(2,1)S(1)}, u32[]{:S(2)}, u32[]{:S(2)}) collective-permute-start(bf16[384,512]{1,0:T(8,128)(2,1)S(1)} %get-tuple-element.45), channel_id=1, source_target_pairs={{0,128},{4,132},{8,136},{12,140},{16,144},{20,148},{24,152},{28,15... | collective-permute-start | bytes 1179656 | tf_op jit(solution)/shard_map/ppermute | solution.py:46
  59.5 0.8 shard_map.86
  60.4 6.4 %collective-permute-done.7.refs_4_ = bf16[512,384]{1,0:T(8,128)(2,1)S(1)} collective-permute-done((bf16[512,384]{1,0:T(8,128)(2,1)S(1)}, bf16[512,384]{1,0:T(8,128)(2,1)S(1)}, u32[]{:S(2)}, u32[]{:S(2)}) %collective-permute-start.7) | collective-permute-done | bytes 393248 | tf_op jit(solution)/shard_map/ppermute | solution.py:33
  66.8 6.2 %shard_map.87 = (bf16[512,1024]{1,0:T(8,128)(2,1)}, f32[4,1024]{1,0:T(4,128)S(1)}, f32[512,384]{1,0:T(8,128)S(1)}, bf16[512,384]{1,0:T(8,128)(2,1)S(1)}, bf16[51...) custom-call(s32[4]{0:T(128)S(1)} %pad_add_fusion.refs_0_, ...), custom_call_target="tpu_custom_call" | custom-call | flops 3221225472 | bytes 3145728 | tf_op jit(solution)/shard_map/pallas_call | solution.py:64
  73.0 0.7 shard_map.89.refs_2_
  73.7 1.7 collective-permute-start.11
  75.4 4.4 %collective-permute-start.12 = (bf16[384,2048]{1,0:T(8,128)(2,1)S(1)}, bf16[384,2048]{1,0:T(8,128)(2,1)S(1)}, u32[]{:S(2)}, u32[]{:S(2)}) collective-permute-start(bf16[384,2048]{1,0:T(8,128)(2,1)S(1)} %shard_map.89.refs_2_), channel_id=1, source_target_pairs={{0,56},{4,60},{8,0},{12,4},{16,8},{20,12},{24,16},{28,20},{32,24},... | collective-permute-start | bytes 4718600 | tf_op jit(solution)/shard_map/ppermute | solution.py:46
  79.9 0.5 collective-permute-start.14
  80.4 2.2 %collective-permute-start.15 = (bf16[512,384]{1,0:T(8,128)(2,1)S(1)}, bf16[512,384]{1,0:T(8,128)(2,1)S(1)}, u32[]{:S(2)}, u32[]{:S(2)}) collective-permute-start(bf16[512,384]{1,0:T(8,128)(2,1)S(1)} %get-tuple-element.51), channel_id=1, source_target_pairs={{0,3},{1,0},{2,1},{3,2},{4,7},{5,4},{6,5},{7,6},{8,11},{9,8},{10,9... | collective-permute-start | bytes 1179656 | tf_op jit(solution)/shard_map/ppermute | solution.py:33
  82.6 16.8 %collective-permute-done.13.refs_2_ = bf16[512,384]{1,0:T(8,128)(2,1)S(1)} collective-permute-done((bf16[512,384]{1,0:T(8,128)(2,1)S(1)}, bf16[512,384]{1,0:T(8,128)(2,1)S(1)}, u32[]{:S(2)}, u32[]{:S(2)}) %collective-permute-start.13) | collective-permute-done | bytes 393248 | tf_op jit(solution)/shard_map/ppermute | solution.py:33
  99.4 0.3 collective-permute-done.15.refs_4_
  99.7 0.9 shard_map.90
  100.7 1.4 collective-permute-start.16
  102.0 1.7 collective-permute-start.17
  103.7 2.0 %collective-permute-start.18 = (bf16[528,384]{1,0:T(8,128)(2,1)S(1)}, bf16[528,384]{1,0:T(8,128)(2,1)S(1)}, u32[]{:S(2)}, u32[]{:S(2)}) collective-permute-start(bf16[528,384]{1,0:T(8,128)(2,1)S(1)} %get-tuple-element.53.refs_4_), channel_id=1, source_target_pairs={{0,192},{4,196},{8,200},{12,204},{16,208},{20,212},{24,216},{28,22... | collective-permute-start | bytes 1216520 | tf_op jit(solution)/shard_map/ppermute | solution.py:46
  105.7 5.2 %collective-permute-done.16.refs_5_ = bf16[528,384]{1,0:T(8,128)(2,1)S(1)} collective-permute-done((bf16[528,384]{1,0:T(8,128)(2,1)S(1)}, bf16[528,384]{1,0:T(8,128)(2,1)S(1)}, u32[]{:S(2)}, u32[]{:S(2)}) %collective-permute-start.16) | collective-permute-done | bytes 405536 | tf_op jit(solution)/shard_map/ppermute | solution.py:46
  110.9 1.3 collective-permute-start.20
  112.2 7.9 %collective-permute-done.17.refs_6_ = bf16[528,384]{1,0:T(8,128)(2,1)S(1)} collective-permute-done((bf16[528,384]{1,0:T(8,128)(2,1)S(1)}, bf16[528,384]{1,0:T(8,128)(2,1)S(1)}, u32[]{:S(2)}, u32[]{:S(2)}) %collective-permute-start.17) | collective-permute-done | bytes 405536 | tf_op jit(solution)/shard_map/ppermute | solution.py:46
  120.1 1.3 collective-permute-start.21
  121.4 1.0 shard_map.92.refs_4_
  122.4 3.9 %shard_map.91 = (f32[192,1152]{1,0:T(8,128)S(1)}, bf16[192,1152]{1,0:T(8,128)(2,1)S(1)}, f32[16,1152]{1,0:T(8,128)S(1)}, f32[8,128]{1,0:T(8,128)S(1)}) custom-call(s32[4]{0:T(128)S(1)} %pad_add_fusion.refs_0_, bf16[384,2048]{1,0:T(8,128)(2,1)S(1)} %collective-permute-done.11.refs_1_, bf16[384,2048]{1,0:T(8,128)(2,1)S(1)} %shard_map.89.refs_2_, ...), custom_call_target="tpu_custom_call" | custom-call | flops 1811939328 | bytes 6291456 | tf_op jit(solution)/shard_map/pallas_call | solution.py:64
  126.3 3.1 %collective-permute-start.19 = (bf16[192,1152]{1,0:T(8,128)(2,1)S(1)}, bf16[192,1152]{1,0:T(8,128)(2,1)S(1)}, u32[]{:S(2)}, u32[]{:S(2)}) collective-permute-start(bf16[192,1152]{1,0:T(8,128)(2,1)S(1)} %get-tuple-element.55), channel_id=1, source_target_pairs={{0,4},{4,0},{8,12},{12,8},{16,20},{20,16},{24,28},{28,24},{32,36},... | collective-permute-start | bytes 1327112 | tf_op jit(solution)/shard_map/ppermute | solution.py:46
  129.4 4.1 %shard_map.93 = (f32[512,384]{1,0:T(8,128)S(1)}, bf16[512,384]{1,0:T(8,128)(2,1)S(1)}, bf16[512,384]{1,0:T(8,128)(2,1)S(1)}, bf16[512,384]{1,0:T(8,128)(2,1)S(1)}, f32[8,128]{1,0:T(8,128)}) custom-call(s32[4]{0:T(128)S(1)} %pad_add_fusion.refs_0_, bf16[512,384]{1,0:T(8,128)(2,1)S(1)} %collective-permute-done.20.refs_1_, ...), custom_call_target="tpu_custom_call" | custom-call | flops 1811939328 | bytes 3538944 | tf_op jit(solution)/shard_map/pallas_call | solution.py:64
  133.5 0.7 copy-done.5
  134.3 2.2 %collective-permute-start.22 = (bf16[512,384]{1,0:T(8,128)(2,1)S(1)}, bf16[512,384]{1,0:T(8,128)(2,1)S(1)}, u32[]{:S(2)}, u32[]{:S(2)}) collective-permute-start(bf16[512,384]{1,0:T(8,128)(2,1)S(1)} %get-tuple-element.59), channel_id=1, source_target_pairs={{0,1},{1,2},{2,3},{3,0},{4,5},{5,6},{6,7},{7,4},{8,9},{9,10},{10,1... | collective-permute-start | bytes 1179656 | tf_op jit(solution)/shard_map/ppermute | solution.py:33
  136.4 8.0 %collective-permute-done.22.refs_4_ = bf16[512,384]{1,0:T(8,128)(2,1)S(1)} collective-permute-done((bf16[512,384]{1,0:T(8,128)(2,1)S(1)}, bf16[512,384]{1,0:T(8,128)(2,1)S(1)}, u32[]{:S(2)}, u32[]{:S(2)}) %collective-permute-start.22) | collective-permute-done | bytes 393248 | tf_op jit(solution)/shard_map/ppermute | solution.py:33
  144.4 1.5 shard_map.94
  145.9 11.2 %all-to-all-start = ((bf16[8,40,1152]{2,1,0:T(8,128)(2,1)}), bf16[8,40,1152]{2,1,0:T(8,128)(2,1)S(1)}, u32[]{:S(2)}, u32[]{:S(2)}) async-start(bf16[8,40,1152]{2,1,0:T(8,128)(2,1)} %shard_map.94), calls=%async_computation | async-start | bytes 1474560 | tf_op jit(solution)/shard_map/all_to_all | solution.py:449
  157.1 0.2 collective-permute-start.23
  157.4 1.7 collective-permute-start.24
  159.0 9.5 %collective-permute-done.23.refs_5_ = bf16[512,384]{1,0:T(8,128)(2,1)S(1)} collective-permute-done((bf16[512,384]{1,0:T(8,128)(2,1)}, bf16[512,384]{1,0:T(8,128)(2,1)S(1)}, u32[]{:S(2)}, u32[]{:S(2)}) %collective-permute-start.23) | collective-permute-done | bytes 393248 | tf_op jit(solution)/shard_map/ppermute | solution.py:33
  168.6 7.6 %collective-permute-done.24.refs_6_ = bf16[512,384]{1,0:T(8,128)(2,1)S(1)} collective-permute-done((bf16[512,384]{1,0:T(8,128)(2,1)S(1)}, bf16[512,384]{1,0:T(8,128)(2,1)S(1)}, u32[]{:S(2)}, u32[]{:S(2)}) %collective-permute-start.24) | collective-permute-done | bytes 393248 | tf_op jit(solution)/shard_map/ppermute | solution.py:33
  176.2 2.0 %shard_map.95 = (bf16[512,384]{1,0:T(8,128)(2,1)}, f32[8,128]{1,0:T(8,128)S(1)}) custom-call(s32[4]{0:T(128)S(1)} %pad_add_fusion.refs_0_, bf16[512,384]{1,0:T(8,128)(2,1)S(1)} %copy-done.2, f32[512,384]{1,0:T(8,128)S(1)} %get-tuple-element.60.refs_2_, f32[512,384]{1,0:T(8,128)S(1)} %get-tuple-element.61.refs_3_, ...), custom_call_target="tpu_custom_call" | custom-call | flops 3932160 | bytes 3145728 | tf_op jit(solution)/shard_map/pallas_call | solution.py:64
  178.2 1.5 all-to-all-done.refs_1_
  179.7 1.2 shard_map.96
  180.9 0.5 collective-permute-start.25
  181.4 1.2 collective-permute-done.25
  182.6 0.8 convolution_multiply_fusion
  (35 shorter events, 0.4 us)
Async XLA Ops:
  1.9 14.2 %collective-permute-start = (bf16[512,384]{1,0:T(8,128)(2,1)S(1)}, bf16[512,384]{1,0:T(8,128)(2,1)S(1)}, u32[]{:S(2)}, u32[]{:S(2)}) collective-permute-start(bf16[512,384]{1,0:T(8,128)(2,1)S(1)} %fusion.5.refs_1_), channel_id=1, source_target_pairs={{0,3},{1,0},{2,1},{3,2},{4,7},{5,4},{6,5},{7,6},{8,11},{9,8},{10,9... | collective-permute-start | bytes 1179656 | tf_op jit(solution)/shard_map/ppermute | solution.py:33
  5.3 11.2 %collective-permute-start.1 = (bf16[512,384]{1,0:T(8,128)(2,1)S(1)}, bf16[512,384]{1,0:T(8,128)(2,1)S(1)}, u32[]{:S(2)}, u32[]{:S(2)}) collective-permute-start(bf16[512,384]{1,0:T(8,128)(2,1)S(1)} %fusion.5.refs_1_), channel_id=1, source_target_pairs={{0,2},{1,3},{2,0},{3,1},{4,6},{5,7},{6,4},{7,5},{8,10},{9,11},{10,... | collective-permute-start | bytes 1179656 | tf_op jit(solution)/shard_map/ppermute | solution.py:33
  5.8 20.4 %collective-permute-start.2 = (bf16[512,384]{1,0:T(8,128)(2,1)S(1)}, bf16[512,384]{1,0:T(8,128)(2,1)S(1)}, u32[]{:S(2)}, u32[]{:S(2)}) collective-permute-start(bf16[512,384]{1,0:T(8,128)(2,1)S(1)} %fusion.5.refs_1_), channel_id=1, source_target_pairs={{0,1},{1,2},{2,3},{3,0},{4,5},{5,6},{6,7},{7,4},{8,9},{9,10},{10,1... | collective-permute-start | bytes 1179656 | tf_op jit(solution)/shard_map/ppermute | solution.py:33
  8.0 2.0 %copy-start = (bf16[1,3,1536,384]{3,2,1,0:T(8,128)(2,1)S(1)}, bf16[1,3,1536,384]{3,2,1,0:T(8,128)(2,1)}, u32[]{:S(2)}) copy-start(bf16[1,3,1536,384]{3,2,1,0:T(8,128)(2,1)} %refs_1_.6) | copy-start | bytes 10616836
  10.9 34.5 %copy-start.2 = (bf16[512,384]{1,0:T(8,128)(2,1)S(1)}, bf16[512,384]{1,0:T(8,128)(2,1)}, u32[]{:S(2)}) copy-start(bf16[512,384]{1,0:T(8,128)(2,1)} %refs_1_.7) | copy-start | bytes 1179652
  26.3 33.2 %copy-start.4 = (bf16[512,1024]{1,0:T(8,128)(2,1)S(1)}, bf16[512,1024]{1,0:T(8,128)(2,1)}, u32[]{:S(2)}) copy-start(bf16[512,1024]{1,0:T(8,128)(2,1)} %refs_2_.1) | copy-start | bytes 3145732
  29.5 30.0 %copy-start.3 = (bf16[1536,1024]{1,0:T(8,128)(2,1)S(1)}, bf16[1536,1024]{1,0:T(8,128)(2,1)}, u32[]{:S(2)}) copy-start(bf16[1536,1024]{1,0:T(8,128)(2,1)} %refs_1_.5) | copy-start | bytes 9437188
  29.5 11.8 %collective-permute-start.3 = (bf16[512,384]{1,0:T(8,128)(2,1)S(1)}, bf16[512,384]{1,0:T(8,128)(2,1)S(1)}, u32[]{:S(2)}, u32[]{:S(2)}) collective-permute-start(bf16[512,384]{1,0:T(8,128)(2,1)S(1)} %get-tuple-element.37), channel_id=1, source_target_pairs={{0,8},{4,12},{8,16},{12,20},{16,24},{20,28},{24,32},{28,36},{32,40... | collective-permute-start | bytes 1179656 | tf_op jit(solution)/shard_map/ppermute | solution.py:29
  33.3 12.1 %collective-permute-start.4 = (bf16[512,384]{1,0:T(8,128)(2,1)S(1)}, bf16[512,384]{1,0:T(8,128)(2,1)S(1)}, u32[]{:S(2)}, u32[]{:S(2)}) collective-permute-start(bf16[512,384]{1,0:T(8,128)(2,1)S(1)} %get-tuple-element.38), channel_id=1, source_target_pairs={{8,0},{12,4},{16,8},{20,12},{24,16},{28,20},{32,24},{36,28},{40,32... | collective-permute-start | bytes 1179656 | tf_op jit(solution)/shard_map/ppermute | solution.py:29
  45.6 9.2 %collective-permute-start.5 = (bf16[512,384]{1,0:T(8,128)(2,1)S(1)}, bf16[512,384]{1,0:T(8,128)(2,1)S(1)}, u32[]{:S(2)}, u32[]{:S(2)}) collective-permute-start(bf16[512,384]{1,0:T(8,128)(2,1)S(1)} %fusion.6.refs_1_), channel_id=1, source_target_pairs={{0,3},{1,0},{2,1},{3,2},{4,7},{5,4},{6,5},{7,6},{8,11},{9,8},{10,9... | collective-permute-start | bytes 1179656 | tf_op jit(solution)/shard_map/ppermute | solution.py:33
  45.7 14.6 %collective-permute-start.6 = (bf16[512,384]{1,0:T(8,128)(2,1)S(1)}, bf16[512,384]{1,0:T(8,128)(2,1)S(1)}, u32[]{:S(2)}, u32[]{:S(2)}) collective-permute-start(bf16[512,384]{1,0:T(8,128)(2,1)S(1)} %fusion.6.refs_1_), channel_id=1, source_target_pairs={{0,2},{1,3},{2,0},{3,1},{4,6},{5,7},{6,4},{7,5},{8,10},{9,11},{10,... | collective-permute-start | bytes 1179656 | tf_op jit(solution)/shard_map/ppermute | solution.py:33
  46.3 20.4 %collective-permute-start.7 = (bf16[512,384]{1,0:T(8,128)(2,1)S(1)}, bf16[512,384]{1,0:T(8,128)(2,1)S(1)}, u32[]{:S(2)}, u32[]{:S(2)}) collective-permute-start(bf16[512,384]{1,0:T(8,128)(2,1)S(1)} %fusion.6.refs_1_), channel_id=1, source_target_pairs={{0,1},{1,2},{2,3},{3,0},{4,5},{5,6},{6,7},{7,4},{8,9},{9,10},{10,1... | collective-permute-start | bytes 1179656 | tf_op jit(solution)/shard_map/ppermute | solution.py:33
  48.2 24.8 %collective-permute-start.10 = (bf16[384,512]{1,0:T(8,128)(2,1)S(1)}, bf16[384,512]{1,0:T(8,128)(2,1)S(1)}, u32[]{:S(2)}, u32[]{:S(2)}) collective-permute-start(bf16[384,512]{1,0:T(8,128)(2,1)S(1)} %get-tuple-element.46), channel_id=1, source_target_pairs={{0,192},{4,196},{8,200},{12,204},{16,208},{20,212},{24,216},{28,22... | collective-permute-start | bytes 1179656 | tf_op jit(solution)/shard_map/ppermute | solution.py:46
  52.9 20.1 %collective-permute-start.8 = (bf16[384,512]{1,0:T(8,128)(2,1)S(1)}, bf16[384,512]{1,0:T(8,128)(2,1)S(1)}, u32[]{:S(2)}, u32[]{:S(2)}) collective-permute-start(bf16[384,512]{1,0:T(8,128)(2,1)S(1)} %get-tuple-element.44), channel_id=1, source_target_pairs={{0,64},{4,68},{8,72},{12,76},{16,80},{20,84},{24,88},{28,92},{32,9... | collective-permute-start | bytes 1179656 | tf_op jit(solution)/shard_map/ppermute | solution.py:46
  54.8 18.2 %collective-permute-start.9 = (bf16[384,512]{1,0:T(8,128)(2,1)S(1)}, bf16[384,512]{1,0:T(8,128)(2,1)S(1)}, u32[]{:S(2)}, u32[]{:S(2)}) collective-permute-start(bf16[384,512]{1,0:T(8,128)(2,1)S(1)} %get-tuple-element.45), channel_id=1, source_target_pairs={{0,128},{4,132},{8,136},{12,140},{16,144},{20,148},{24,152},{28,15... | collective-permute-start | bytes 1179656 | tf_op jit(solution)/shard_map/ppermute | solution.py:46
  73.0 48.4 %copy-start.1 = (bf16[1,3,1536,384]{3,2,1,0:T(8,128)(2,1)S(1)}, bf16[1,3,1536,384]{3,2,1,0:T(8,128)(2,1)}, u32[]{:S(2)}) copy-start(bf16[1,3,1536,384]{3,2,1,0:T(8,128)(2,1)} %refs_1_.6) | copy-start | bytes 10616836
  73.7 48.7 %collective-permute-start.11 = (bf16[384,2048]{1,0:T(8,128)(2,1)S(1)}, bf16[384,2048]{1,0:T(8,128)(2,1)S(1)}, u32[]{:S(2)}, u32[]{:S(2)}) collective-permute-start(bf16[384,2048]{1,0:T(8,128)(2,1)S(1)} %shard_map.89.refs_2_), channel_id=1, source_target_pairs={{0,8},{4,12},{8,16},{12,20},{16,24},{20,28},{24,32},{28,36},{32,40... | collective-permute-start | bytes 4718600 | tf_op jit(solution)/shard_map/ppermute | solution.py:46
  75.4 46.9 %collective-permute-start.12 = (bf16[384,2048]{1,0:T(8,128)(2,1)S(1)}, bf16[384,2048]{1,0:T(8,128)(2,1)S(1)}, u32[]{:S(2)}, u32[]{:S(2)}) collective-permute-start(bf16[384,2048]{1,0:T(8,128)(2,1)S(1)} %shard_map.89.refs_2_), channel_id=1, source_target_pairs={{0,56},{4,60},{8,0},{12,4},{16,8},{20,12},{24,16},{28,20},{32,24},... | collective-permute-start | bytes 4718600 | tf_op jit(solution)/shard_map/ppermute | solution.py:46
  79.9 19.5 %collective-permute-start.13 = (bf16[512,384]{1,0:T(8,128)(2,1)S(1)}, bf16[512,384]{1,0:T(8,128)(2,1)S(1)}, u32[]{:S(2)}, u32[]{:S(2)}) collective-permute-start(bf16[512,384]{1,0:T(8,128)(2,1)S(1)} %get-tuple-element.49), channel_id=1, source_target_pairs={{0,1},{1,2},{2,3},{3,0},{4,5},{5,6},{6,7},{7,4},{8,9},{9,10},{10,1... | collective-permute-start | bytes 1179656 | tf_op jit(solution)/shard_map/ppermute | solution.py:33
  79.9 19.5 %collective-permute-start.14 = (bf16[512,384]{1,0:T(8,128)(2,1)S(1)}, bf16[512,384]{1,0:T(8,128)(2,1)S(1)}, u32[]{:S(2)}, u32[]{:S(2)}) collective-permute-start(bf16[512,384]{1,0:T(8,128)(2,1)S(1)} %get-tuple-element.50), channel_id=1, source_target_pairs={{0,2},{1,3},{2,0},{3,1},{4,6},{5,7},{6,4},{7,5},{8,10},{9,11},{10,... | collective-permute-start | bytes 1179656 | tf_op jit(solution)/shard_map/ppermute | solution.py:33
  80.4 19.3 %collective-permute-start.15 = (bf16[512,384]{1,0:T(8,128)(2,1)S(1)}, bf16[512,384]{1,0:T(8,128)(2,1)S(1)}, u32[]{:S(2)}, u32[]{:S(2)}) collective-permute-start(bf16[512,384]{1,0:T(8,128)(2,1)S(1)} %get-tuple-element.51), channel_id=1, source_target_pairs={{0,3},{1,0},{2,1},{3,2},{4,7},{5,4},{6,5},{7,6},{8,11},{9,8},{10,9... | collective-permute-start | bytes 1179656 | tf_op jit(solution)/shard_map/ppermute | solution.py:33
  100.7 10.2 %collective-permute-start.16 = (bf16[528,384]{1,0:T(8,128)(2,1)S(1)}, bf16[528,384]{1,0:T(8,128)(2,1)S(1)}, u32[]{:S(2)}, u32[]{:S(2)}) collective-permute-start(bf16[528,384]{1,0:T(8,128)(2,1)S(1)} %get-tuple-element.53.refs_4_), channel_id=1, source_target_pairs={{0,64},{4,68},{8,72},{12,76},{16,80},{20,84},{24,88},{28,92},{32,9... | collective-permute-start | bytes 1216520 | tf_op jit(solution)/shard_map/ppermute | solution.py:46
  102.0 18.0 %collective-permute-start.17 = (bf16[528,384]{1,0:T(8,128)(2,1)S(1)}, bf16[528,384]{1,0:T(8,128)(2,1)S(1)}, u32[]{:S(2)}, u32[]{:S(2)}) collective-permute-start(bf16[528,384]{1,0:T(8,128)(2,1)S(1)} %get-tuple-element.53.refs_4_), channel_id=1, source_target_pairs={{0,128},{4,132},{8,136},{12,140},{16,144},{20,148},{24,152},{28,15... | collective-permute-start | bytes 1216520 | tf_op jit(solution)/shard_map/ppermute | solution.py:46
  103.7 18.6 %collective-permute-start.18 = (bf16[528,384]{1,0:T(8,128)(2,1)S(1)}, bf16[528,384]{1,0:T(8,128)(2,1)S(1)}, u32[]{:S(2)}, u32[]{:S(2)}) collective-permute-start(bf16[528,384]{1,0:T(8,128)(2,1)S(1)} %get-tuple-element.53.refs_4_), channel_id=1, source_target_pairs={{0,192},{4,196},{8,200},{12,204},{16,208},{20,212},{24,216},{28,22... | collective-permute-start | bytes 1216520 | tf_op jit(solution)/shard_map/ppermute | solution.py:46
  110.9 18.5 %collective-permute-start.20 = (bf16[512,384]{1,0:T(8,128)(2,1)S(1)}, bf16[512,384]{1,0:T(8,128)(2,1)S(1)}, u32[]{:S(2)}, u32[]{:S(2)}) collective-permute-start(bf16[512,384]{1,0:T(8,128)(2,1)S(1)} %get-tuple-element.57.refs_2_), channel_id=1, source_target_pairs={{8,0},{12,4},{16,8},{20,12},{24,16},{28,20},{32,24},{36,28},{40,32... | collective-permute-start | bytes 1179656 | tf_op jit(solution)/shard_map/ppermute | solution.py:29
  120.1 9.3 %collective-permute-start.21 = (bf16[512,384]{1,0:T(8,128)(2,1)S(1)}, bf16[512,384]{1,0:T(8,128)(2,1)S(1)}, u32[]{:S(2)}, u32[]{:S(2)}) collective-permute-start(bf16[512,384]{1,0:T(8,128)(2,1)S(1)} %get-tuple-element.57.refs_2_), channel_id=1, source_target_pairs={{0,8},{4,12},{8,16},{12,20},{16,24},{20,28},{24,32},{28,36},{32,40... | collective-permute-start | bytes 1179656 | tf_op jit(solution)/shard_map/ppermute | solution.py:29
  126.3 18.1 %collective-permute-start.19 = (bf16[192,1152]{1,0:T(8,128)(2,1)S(1)}, bf16[192,1152]{1,0:T(8,128)(2,1)S(1)}, u32[]{:S(2)}, u32[]{:S(2)}) collective-permute-start(bf16[192,1152]{1,0:T(8,128)(2,1)S(1)} %get-tuple-element.55), channel_id=1, source_target_pairs={{0,4},{4,0},{8,12},{12,8},{16,20},{20,16},{24,28},{28,24},{32,36},... | collective-permute-start | bytes 1327112 | tf_op jit(solution)/shard_map/ppermute | solution.py:46
  133.5 0.7 copy-start.5
  134.3 10.1 %collective-permute-start.22 = (bf16[512,384]{1,0:T(8,128)(2,1)S(1)}, bf16[512,384]{1,0:T(8,128)(2,1)S(1)}, u32[]{:S(2)}, u32[]{:S(2)}) collective-permute-start(bf16[512,384]{1,0:T(8,128)(2,1)S(1)} %get-tuple-element.59), channel_id=1, source_target_pairs={{0,1},{1,2},{2,3},{3,0},{4,5},{5,6},{6,7},{7,4},{8,9},{9,10},{10,1... | collective-permute-start | bytes 1179656 | tf_op jit(solution)/shard_map/ppermute | solution.py:33
  145.9 33.7 %all-to-all-start = ((bf16[8,40,1152]{2,1,0:T(8,128)(2,1)}), bf16[8,40,1152]{2,1,0:T(8,128)(2,1)S(1)}, u32[]{:S(2)}, u32[]{:S(2)}) async-start(bf16[8,40,1152]{2,1,0:T(8,128)(2,1)} %shard_map.94), calls=%async_computation | async-start | bytes 1474560 | tf_op jit(solution)/shard_map/all_to_all | solution.py:449
  157.1 11.4 %collective-permute-start.23 = (bf16[512,384]{1,0:T(8,128)(2,1)}, bf16[512,384]{1,0:T(8,128)(2,1)S(1)}, u32[]{:S(2)}, u32[]{:S(2)}) collective-permute-start(bf16[512,384]{1,0:T(8,128)(2,1)} %copy-done.5), channel_id=1, source_target_pairs={{0,2},{1,3},{2,0},{3,1},{4,6},{5,7},{6,4},{7,5},{8,10},{9,11},{10,... | collective-permute-start | bytes 1179656 | tf_op jit(solution)/shard_map/ppermute | solution.py:33
  157.4 18.8 %collective-permute-start.24 = (bf16[512,384]{1,0:T(8,128)(2,1)S(1)}, bf16[512,384]{1,0:T(8,128)(2,1)S(1)}, u32[]{:S(2)}, u32[]{:S(2)}) collective-permute-start(bf16[512,384]{1,0:T(8,128)(2,1)S(1)} %get-tuple-element.63), channel_id=1, source_target_pairs={{0,3},{1,0},{2,1},{3,2},{4,7},{5,4},{6,5},{7,6},{8,11},{9,8},{10,9... | collective-permute-start | bytes 1179656 | tf_op jit(solution)/shard_map/ppermute | solution.py:33
  180.9 1.7 collective-permute-start.25
